TPU v7x, 32 devices: a whole 2x2x4 slice. The times are simulated.
32 devices in a mesh: rep: 2 (over y), grid: 8 (over z, x), eig: 2 (over core).
Axes of the slice: x: 2, y: 2, z: 4, core: 2. Of those that a mesh axis runs over, the one named last changes fastest.
Arguments:
- eigvecs: bfloat16 [3584, 32768], P('eig', ('rep', 'grid')), parts along dimension 1, may hold values from -0.046875 to 0.046875
- lanczos: bfloat16 [8, 32768], P(None, ('rep', 'grid')), parts along dimension 1, may hold values from -6 to 6
- bands: bfloat16 [64, 32768], P('eig', ('rep', 'grid')), parts along dimension 1, may hold values from -6 to 6
- band_order: int32 [128], P('rep'), parts along dimension 0, may hold values from 0 to 63, each once
Outputs:
- brakets: float32 [128, 8, 3584], P(('rep', 'grid'), None, 'eig'), parts along dimension 0
There are 2 independent parts, one for each index of `rep`. A program takes and returns all parts, laid end to end along the dimension named above; each array names one. Nothing has to cross between parts.
Inputs may be any that keep to these rules, and one draw needn't show every extreme that they name: `band_order`: each occupied band index appears exactly once.
All inputs are finite; a program needn't handle non-finite values.
Results may differ from a plain program's by a relative error of at most 0.0029.
Values may be sent and summed in bfloat16 or wider, within the bound.
No kernel may reach another device: no remote copies, remote signals or barrier semaphores. Data moves between devices by JAX's collectives and lax.ppermute only.
A program may use at most 64 MiB of HBM per device.

v0:
```python
import jax
import jax.numpy as jnp
from jax import lax
from jax.sharding import PartitionSpec as P


def per_device(eigvecs, lanczos, bands, band_order):
    dims_spec = (((2,), (1,)), ((), ()))
    all_bands = lax.all_gather(bands, "eig", axis=0, tiled=True)
    partial_value = lax.dot_general(
        (
            jnp.take(all_bands, band_order, axis=0)[:, None, :].astype(jnp.float32)
            * lanczos[None, :, :].astype(jnp.float32)
        ).astype(jnp.bfloat16),
        eigvecs,
        dims_spec,
        preferred_element_type=jnp.float32,
    )
    result = lax.psum_scatter(partial_value, "grid", scatter_dimension=0, tiled=True)
    return result


def solution(mesh):
    in_specs = (
        P("eig", ("rep", "grid")),
        P(None, ("rep", "grid")),
        P("eig", ("rep", "grid")),
        P("rep"),
    )
    out_specs = P(("rep", "grid"), None, "eig")
    return jax.shard_map(
        per_device, mesh=mesh, in_specs=in_specs, out_specs=out_specs, check_vma=False
    )
```

profile of v0, /device:TPU:0, one launch (start us, length us, event | category | flops | bytes accessed | tf_op | source)
XLA Modules:
  0.0 111.1 jit_solution(8668576205047408297)
XLA Ops:
  6.5 0.0 reduce-scatter.2.cloned.1.call-start
  6.5 0.7 compare_and_fusion
  7.2 0.7 compare_select_fusion
  7.9 0.8 convert_element_type.16
  8.6 2.3 %all_gather.3 = bf16[64,2048]{1,0:T(8,128)(2,1)S(1)} all-gather(bf16[32,2048]{1,0:T(8,128)(2,1)} %param.6), channel_id=1, replica_groups=mesh['rep'=2,'grid'=8,'eig'=2] {'eig'}, dimensions={0}, use_global_device_ids=true | all-gather | bytes 393216 | tf_op jit(solution)/shard_map/all_gather | solution.py:9
  10.9 0.7 gather_fusion
  11.7 0.1 select_convert_fusion
  11.8 8.9 %fusion = f32[64,8,1792]{2,1,0:T(8,128)} fusion(bf16[1792,2048]{1,0:T(8,128)(2,1)} %param.4, f32[8,2048]{1,0:T(8,128)S(1)} %convert_element_type.16, f32[64,2048]{1,0:T(8,128)S(1)} %select_convert_fusion), kind=kOutput, calls=%fused_computation.1 | convolution fusion | flops 3760193536 | bytes 11599872 | tf_op jit(solution)/shard_map/dot_general | solution.py:10
  20.7 0.0 reduce-scatter.2.cloned.1.call-update
  20.7 83.6 %reduce-scatter.2.cloned.1.call-done = f32[8,8,1792]{2,1,0:T(8,128)} async-done(((f32[64,8,1792]{2,1,0:T(8,128)}), f32[8,8,1792]{2,1,0:T(8,128)}) %reduce-scatter.2.cloned.1.call-update) | async-done | bytes 458768 | tf_op jit(solution)/shard_map/reduce_scatter | solution.py:19
  (1 shorter events, 0.0 us)
Async XLA Ops:
  6.5 97.8 %reduce-scatter.2.cloned.1.call-start = ((), (), s32[]{:S(2)}) async-start(), calls=%async_computation.1 | async-start | bytes 4128768 | tf_op jit(solution)/shard_map/reduce_scatter | solution.py:19
Sparse Core Ops, SparseCore 0:
  20.8 83.4 reduce-scatter.1
where the time goes:
time: 111 us
  waiting for transfers between devices  83.6 us (75%)
  between operations  13.4 us (12%)
  matrix products  8.88 us (8%)
  blocking collectives  2.28 us (2%)
  other arithmetic  2.2 us (2%)
    reduce_scatter x1, waiting for transfers between devices, per_device(): lax.psum_scatter(partial_value, 'grid', scatter_dimension=0, tiled=True)  83.6 us
    dot_general x1, matrix products, per_device(): lax.dot_general((jnp.take(all_bands, band_order, axis=0)[:, None, :].asty...  8.88 us
    all_gather x1, blocking collectives, per_device(): all_bands = lax.all_gather(bands, 'eig', axis=0, tiled=True)  2.28 us
  transfers between devices with their start and end apart: 1, of which 1 were waited for; matrix products, arithmetic and copies ran while one was open for 0% of the time, Pallas kernels for 0%

commit v1 on v0

v1 whole, which is shorter than its diff:
```python
import functools

import jax
import jax.numpy as jnp
from jax import lax
from jax.experimental import pallas as pl
from jax.experimental.pallas import tpu as pltpu
from jax.sharding import PartitionSpec as P

TILE = 256
VMEM_LIMIT = 40 * 1024 * 1024


def ranked(bits, fixed):
    out = [fixed]
    for b in reversed(bits):
        out = [c | (1 << b) for c in out] + out
    return out


def row_slots(n):
    rest = list(range(2, n.bit_length() - 1))
    a, b, c, d = (ranked(rest, f) for f in (1, 3, 2, 0))
    return a + b + c + d + a


def products_kernel(n, per_chunk, order_ref, own_ref, other_ref, lanc_ref, out_ref, held):
    me = lax.axis_index("grid")
    core = lax.axis_index("eig")
    half = own_ref.shape[0]
    held[:half, :] = own_ref[...].astype(jnp.float32)
    held[half:, :] = other_ref[...].astype(jnp.float32)
    lanc = lanc_ref[...].astype(jnp.float32)
    slots = [(r, j) for r in row_slots(n) for j in range(per_chunk)]

    def rows(slot):
        r, j = slot
        band = order_ref[(me ^ r) * per_chunk + j]
        band = lax.rem(band + core * half, 2 * half)
        return held[pl.ds(band, 1), :] * lanc

    step = 2 * lanc.shape[0]
    for at in range(0, len(slots), 2):
        pair = jnp.concatenate([rows(slots[at]), rows(slots[at + 1])], axis=0)
        out_ref[at // 2 * step : (at // 2 + 1) * step, :] = pair.astype(jnp.bfloat16)


def matmul_kernel(p_ref, e_ref, o_ref):
    o_ref[...] = lax.dot_general(
        p_ref[...], e_ref[...], (((1,), (1,)), ((), ())), preferred_element_type=jnp.float32
    ).astype(o_ref.dtype)


def matmul_piece(products, eigvecs, first, rows, piece, dtype):
    depth = products.shape[1]
    unit = rows // 2
    return pl.pallas_call(
        matmul_kernel,
        grid=(1,),
        out_shape=jax.ShapeDtypeStruct((rows, TILE), dtype),
        in_specs=[
            pl.BlockSpec((pl.Element(rows), pl.Element(depth)), lambda i: (first, 0)),
            pl.BlockSpec((TILE, depth), lambda i: (piece, 0)),
        ],
        out_specs=pl.BlockSpec((rows, TILE), lambda i: (0, 0)),
        compiler_params=pltpu.CompilerParams(vmem_limit_bytes=VMEM_LIMIT),
        cost_estimate=pl.CostEstimate(
            flops=2 * rows * TILE * depth,
            bytes_accessed=2 * depth * (rows + TILE) + 4 * rows * TILE,
            transcendentals=0,
        ),
    )(products, eigvecs)


def per_device(n, eigvecs, lanczos, bands, band_order):
    lanc = lanczos.shape[0]
    per_chunk = band_order.shape[0] // n
    cols, depth = eigvecs.shape
    rows = band_order.shape[0] * lanc
    other = lax.ppermute(bands, "eig", [(0, 1), (1, 0)])
    total = rows + rows // 4
    products = pl.pallas_call(
        functools.partial(products_kernel, n, per_chunk),
        out_shape=jax.ShapeDtypeStruct((total, depth), jnp.bfloat16),
        in_specs=[pl.BlockSpec(memory_space=pltpu.SMEM)]
        + [pl.BlockSpec(memory_space=pltpu.VMEM)] * 3,
        out_specs=pl.BlockSpec(memory_space=pltpu.VMEM),
        scratch_shapes=[pltpu.VMEM((2 * bands.shape[0], depth), jnp.float32)],
        compiler_params=pltpu.CompilerParams(vmem_limit_bytes=VMEM_LIMIT),
    )(band_order, bands, other, lanczos)

    def exchange(value, bit):
        return lax.ppermute(value, "grid", [(i, i ^ (1 << bit)) for i in range(n)])

    half, quarter = rows // 2, rows // 4
    pieces = cols // TILE
    z_first = {1, 4} if pieces >= 6 else set()
    sent = []
    for p in range(pieces):
        if p in z_first:
            send = matmul_piece(products, eigvecs, quarter, half, p, jnp.bfloat16)
        else:
            send = matmul_piece(products, eigvecs, 0, half, p, jnp.bfloat16)
        sent.append(exchange(send, 1 if p in z_first else 0))
    kept = []
    for p in range(pieces):
        first = 3 * quarter if p in z_first else half
        kept.append(matmul_piece(products, eigvecs, first, half, p, jnp.float32))
    outs = []
    for p in range(pieces):
        top = kept[p][:quarter] + sent[p][quarter:].astype(jnp.float32)
        low = kept[p][quarter:] + sent[p][:quarter].astype(jnp.float32)
        keep, send = (top, low) if p in z_first else (low, top)
        got = exchange(send.astype(jnp.bfloat16), 0 if p in z_first else 1)
        value = keep + got.astype(jnp.float32)
        for bit in range(2, n.bit_length() - 1):
            mid = value.shape[0] // 2
            dtype = jnp.bfloat16 if bit < 3 else jnp.float32
            got = exchange(value[:mid].astype(dtype), bit)
            value = value[mid:] + got.astype(jnp.float32)
        outs.append(value)
    result = jnp.concatenate(outs, axis=1)
    return result.reshape(per_chunk, lanc, cols)


def solution(mesh):
    in_specs = (
        P("eig", ("rep", "grid")),
        P(None, ("rep", "grid")),
        P("eig", ("rep", "grid")),
        P("rep"),
    )
    out_specs = P(("rep", "grid"), None, "eig")
    return jax.shard_map(
        functools.partial(per_device, mesh.shape["grid"]),
        mesh=mesh,
        in_specs=in_specs,
        out_specs=out_specs,
        check_vma=False,
    )
```

time: 111 us -> 50 us (0.45)
  waiting for transfers between devices: 83.6 us -> 5.5 us
  starting transfers between devices: 0.01 us -> 29.7 us
  between operations: 13.4 us -> 0.41 us
  matrix products: 8.88 us -> 0 us
  Pallas kernels: 0 us -> 7.66 us
  local copies, waits for them, and re-layouts: 0.74 us -> 6.2 us
  blocking collectives: 2.28 us -> 0 us
  other arithmetic: 2.2 us -> 0.3 us
    reduce_scatter x1 -> x0, waiting for transfers between devices: 83.6 us -> none  [per_device(): lax.psum_scatter(partial_value, 'grid', scatter_dimension=0, tiled=True)]
    ppermute x0 -> x22, starting transfers between devices: none -> 29.7 us  [the longest x21 29.2 us: exchange(): return lax.ppermute(value, 'grid', [(i, i ^ 1 << bit) for i in range(n)])]
    dot_general x1 -> x0, matrix products: 8.88 us -> none  [per_device(): lax.dot_general((jnp.take(all_bands, band_order, axis=0)[:, None, :].asty...]
    pallas_call x0 -> x15, Pallas kernels: none -> 7.66 us  [the longest x14 6.55 us: matmul_piece(): pl.pallas_call(matmul_kernel, grid=(1,), out_shape=jax.ShapeDtypeStruct((...]
    unnamed x0 -> x10, local copies, waits for them, and re-layouts: none -> 6.16 us
    ppermute x0 -> x22, waiting for transfers between devices: none -> 5.5 us  [the longest x21 4.31 us: exchange(): return lax.ppermute(value, 'grid', [(i, i ^ 1 << bit) for i in range(n)])]
    all_gather x1 -> x0, blocking collectives: 2.28 us -> none  [per_device(): all_bands = lax.all_gather(bands, 'eig', axis=0, tiled=True)]
  transfers between devices with their start and end apart: 1 -> 22, of which waited for: 1 -> 6; matrix products, arithmetic and copies ran while one was open for 0% -> 1% of each run, Pallas kernels for 0% -> 6%
where the time goes in v1:
time: 50 us; the launch traced here: 49.7 us
  starting transfers between devices  29.7 us (59%)
  Pallas kernels  7.66 us (15%)
  local copies, waits for them, and re-layouts  6.2 us (12%)
  waiting for transfers between devices  5.5 us (11%)
    ppermute x21, starting transfers between devices, exchange(): return lax.ppermute(value, 'grid', [(i, i ^ 1 << bit) for i in range(n)])  29.2 us
    pallas_call x14, Pallas kernels, matmul_piece(): pl.pallas_call(matmul_kernel, grid=(1,), out_shape=jax.ShapeDtypeStruct((...  6.55 us
    unnamed x10, local copies, waits for them, and re-layouts  6.16 us
    ppermute x21, waiting for transfers between devices, exchange(): return lax.ppermute(value, 'grid', [(i, i ^ 1 << bit) for i in range(n)])  4.31 us
    ppermute x1, waiting for transfers between devices, per_device(): other = lax.ppermute(bands, 'eig', [(0, 1), (1, 0)])  1.2 us
    pallas_call x1, Pallas kernels, per_device(): pl.pallas_call(functools.partial(products_kernel, n, per_chunk), out_shap...  1.11 us
  transfers between devices with their start and end apart: 22, of which 6 were waited for; matrix products, arithmetic and copies ran while one was open for 1% of the time, Pallas kernels for 6%

profile of v1, /device:TPU:0, one launch (start us, length us, event | category | flops | bytes accessed | tf_op | source)
XLA Modules:
  0.0 49.7 jit_solution(13368677646831995411)
XLA Ops:
  0.5 1.2 %collective-permute-done.other_ref = bf16[32,2048]{1,0:T(8,128)(2,1)S(1)} collective-permute-done((bf16[32,2048]{1,0:T(8,128)(2,1)}, bf16[32,2048]{1,0:T(8,128)(2,1)S(1)}, u32[]{:S(2)}, u32[]{:S(2)}) %collective-permute-start) | collective-permute-done | bytes 131104 | tf_op jit(solution)/shard_map/ppermute | solution.py:80
  1.7 0.9 %copy-done.1 = bf16[32,2048]{1,0:T(8,128)(2,1)S(1)} copy-done((bf16[32,2048]{1,0:T(8,128)(2,1)S(1)}, bf16[32,2048]{1,0:T(8,128)(2,1)}, u32[]{:S(2)}) %copy-start.1) | copy-done | bytes 131096
  2.6 0.8 %copy-done.2 = bf16[8,2048]{1,0:T(8,128)(2,1)S(1)} copy-done((bf16[8,2048]{1,0:T(8,128)(2,1)S(1)}, bf16[8,2048]{1,0:T(8,128)(2,1)}, u32[]{:S(2)}) %copy-start.2) | copy-done | bytes 32792
  3.3 0.7 %copy-done.3 = s32[64]{0:T(128)S(1)} copy-done((s32[64]{0:T(128)S(1)}, s32[64]{0:T(128)}, u32[]{:S(2)}) %copy-start.3) | copy-done | bytes 280
  4.0 1.1 %shard_map.46.p_ref = bf16[640,2048]{1,0:T(8,128)(2,1)S(1)} custom-call(s32[64]{0:T(128)S(1)} %copy-done.3, bf16[32,2048]{1,0:T(8,128)(2,1)S(1)} %copy-done.1, bf16[32,2048]{1,0:T(8,128)(2,1)S(1)} %collective-permute-done.other_ref, bf16[8,2048]{1,0:T(8,128)(2,1)S(1)} %copy-done.2), custom_call_target="tpu_custom_call" | custom-call | tf_op jit(solution)/shard_map/pallas_call | solution.py:82
  5.1 3.1 %copy-done = bf16[1792,2048]{1,0:T(8,128)(2,1)S(1)} copy-done((bf16[1792,2048]{1,0:T(8,128)(2,1)S(1)}, bf16[1792,2048]{1,0:T(8,128)(2,1)}, u32[]{:S(2)}) %copy-start) | copy-done | bytes 7340056
  12.0 2.9 %collective-permute-start.1 = (bf16[256,256]{1,0:T(8,128)(2,1)S(1)}, bf16[256,256]{1,0:T(8,128)(2,1)S(1)}, u32[]{:S(2)}, u32[]{:S(2)}) collective-permute-start(bf16[256,256]{1,0:T(8,128)(2,1)S(1)} %shard_map.48), channel_id=1, source_target_pairs={{0,2},{2,0},{4,6},{6,4},{8,10},{10,8},{12,14},{14,12},{1,3},{3,1},... | collective-permute-start | bytes 393224 | tf_op jit(solution)/shard_map/ppermute | solution.py:93
  15.4 1.6 %collective-permute-start.4 = (bf16[256,256]{1,0:T(8,128)(2,1)S(1)}, bf16[256,256]{1,0:T(8,128)(2,1)S(1)}, u32[]{:S(2)}, u32[]{:S(2)}) collective-permute-start(bf16[256,256]{1,0:T(8,128)(2,1)S(1)} %shard_map.50), channel_id=1, source_target_pairs={{0,4},{2,6},{4,0},{6,2},{8,12},{10,14},{12,8},{14,10},{1,5},{3,7},... | collective-permute-start | bytes 393224 | tf_op jit(solution)/shard_map/ppermute | solution.py:93
  17.0 0.5 %collective-permute-start.7 = (bf16[256,256]{1,0:T(8,128)(2,1)S(1)}, bf16[256,256]{1,0:T(8,128)(2,1)S(1)}, u32[]{:S(2)}, u32[]{:S(2)}) collective-permute-start(bf16[256,256]{1,0:T(8,128)(2,1)S(1)} %shard_map.52), channel_id=1, source_target_pairs={{0,2},{2,0},{4,6},{6,4},{8,10},{10,8},{12,14},{14,12},{1,3},{3,1},... | collective-permute-start | bytes 393224 | tf_op jit(solution)/shard_map/ppermute | solution.py:93
  17.5 1.5 %collective-permute-start.10 = (bf16[256,256]{1,0:T(8,128)(2,1)S(1)}, bf16[256,256]{1,0:T(8,128)(2,1)S(1)}, u32[]{:S(2)}, u32[]{:S(2)}) collective-permute-start(bf16[256,256]{1,0:T(8,128)(2,1)S(1)} %shard_map.54), channel_id=1, source_target_pairs={{0,2},{2,0},{4,6},{6,4},{8,10},{10,8},{12,14},{14,12},{1,3},{3,1},... | collective-permute-start | bytes 393224 | tf_op jit(solution)/shard_map/ppermute | solution.py:93
  22.1 1.9 %collective-permute-start.19 = (bf16[256,256]{1,0:T(8,128)(2,1)S(1)}, bf16[256,256]{1,0:T(8,128)(2,1)S(1)}, u32[]{:S(2)}, u32[]{:S(2)}) collective-permute-start(bf16[256,256]{1,0:T(8,128)(2,1)S(1)} %shard_map.60), channel_id=1, source_target_pairs={{0,2},{2,0},{4,6},{6,4},{8,10},{10,8},{12,14},{14,12},{1,3},{3,1},... | collective-permute-start | bytes 393224 | tf_op jit(solution)/shard_map/ppermute | solution.py:93
  24.1 1.6 %collective-permute-start.2 = (bf16[128,256]{1,0:T(8,128)(2,1)S(1)}, bf16[128,256]{1,0:T(8,128)(2,1)S(1)}, u32[]{:S(2)}, u32[]{:S(2)}) collective-permute-start(bf16[128,256]{1,0:T(8,128)(2,1)S(1)} %fusion.12), channel_id=1, source_target_pairs={{0,4},{2,6},{4,0},{6,2},{8,12},{10,14},{12,8},{14,10},{1,5},{3,7},... | collective-permute-start | bytes 196616 | tf_op jit(solution)/shard_map/ppermute | solution.py:93
  26.8 1.8 %collective-permute-start.8 = (bf16[128,256]{1,0:T(8,128)(2,1)S(1)}, bf16[128,256]{1,0:T(8,128)(2,1)S(1)}, u32[]{:S(2)}, u32[]{:S(2)}) collective-permute-start(bf16[128,256]{1,0:T(8,128)(2,1)S(1)} %fusion.8), channel_id=1, source_target_pairs={{0,4},{2,6},{4,0},{6,2},{8,12},{10,14},{12,8},{14,10},{1,5},{3,7},... | collective-permute-start | bytes 196616 | tf_op jit(solution)/shard_map/ppermute | solution.py:93
  28.5 0.5 %collective-permute-done.16 = bf16[256,256]{1,0:T(8,128)(2,1)S(1)} collective-permute-done((bf16[256,256]{1,0:T(8,128)(2,1)S(1)}, bf16[256,256]{1,0:T(8,128)(2,1)S(1)}, u32[]{:S(2)}, u32[]{:S(2)}) %collective-permute-start.16) | collective-permute-done | bytes 131104 | tf_op jit(solution)/shard_map/ppermute | solution.py:93
  29.0 0.9 %collective-permute-start.11 = (bf16[128,256]{1,0:T(8,128)(2,1)S(1)}, bf16[128,256]{1,0:T(8,128)(2,1)S(1)}, u32[]{:S(2)}, u32[]{:S(2)}) collective-permute-start(bf16[128,256]{1,0:T(8,128)(2,1)S(1)} %fusion.6), channel_id=1, source_target_pairs={{0,4},{2,6},{4,0},{6,2},{8,12},{10,14},{12,8},{14,10},{1,5},{3,7},... | collective-permute-start | bytes 196616 | tf_op jit(solution)/shard_map/ppermute | solution.py:93
  30.0 1.2 %collective-permute-done.19 = bf16[256,256]{1,0:T(8,128)(2,1)S(1)} collective-permute-done((bf16[256,256]{1,0:T(8,128)(2,1)S(1)}, bf16[256,256]{1,0:T(8,128)(2,1)S(1)}, u32[]{:S(2)}, u32[]{:S(2)}) %collective-permute-start.19) | collective-permute-done | bytes 131104 | tf_op jit(solution)/shard_map/ppermute | solution.py:93
  31.1 1.2 %collective-permute-start.14 = (bf16[128,256]{1,0:T(8,128)(2,1)S(1)}, bf16[128,256]{1,0:T(8,128)(2,1)S(1)}, u32[]{:S(2)}, u32[]{:S(2)}) collective-permute-start(bf16[128,256]{1,0:T(8,128)(2,1)S(1)} %fusion.4), channel_id=1, source_target_pairs={{0,2},{2,0},{4,6},{6,4},{8,10},{10,8},{12,14},{14,12},{1,3},{3,1},... | collective-permute-start | bytes 196616 | tf_op jit(solution)/shard_map/ppermute | solution.py:93
  32.4 1.7 %collective-permute-start.17 = (bf16[128,256]{1,0:T(8,128)(2,1)S(1)}, bf16[128,256]{1,0:T(8,128)(2,1)S(1)}, u32[]{:S(2)}, u32[]{:S(2)}) collective-permute-start(bf16[128,256]{1,0:T(8,128)(2,1)S(1)} %fusion.2), channel_id=1, source_target_pairs={{0,4},{2,6},{4,0},{6,2},{8,12},{10,14},{12,8},{14,10},{1,5},{3,7},... | collective-permute-start | bytes 196616 | tf_op jit(solution)/shard_map/ppermute | solution.py:93
  34.6 2.7 %collective-permute-start.3 = (bf16[64,256]{1,0:T(8,128)(2,1)S(1)}, bf16[64,256]{1,0:T(8,128)(2,1)S(1)}, u32[]{:S(2)}, u32[]{:S(2)}) collective-permute-start(bf16[64,256]{1,0:T(8,128)(2,1)S(1)} %slice.307), channel_id=1, source_target_pairs={{0,8},{2,10},{4,12},{6,14},{8,0},{10,2},{12,4},{14,6},{1,9},{3,11}... | collective-permute-start | bytes 98312 | tf_op jit(solution)/shard_map/ppermute | solution.py:93
  37.8 2.7 %collective-permute-start.9 = (bf16[64,256]{1,0:T(8,128)(2,1)S(1)}, bf16[64,256]{1,0:T(8,128)(2,1)S(1)}, u32[]{:S(2)}, u32[]{:S(2)}) collective-permute-start(bf16[64,256]{1,0:T(8,128)(2,1)S(1)} %slice.305), channel_id=1, source_target_pairs={{0,8},{2,10},{4,12},{6,14},{8,0},{10,2},{12,4},{14,6},{1,9},{3,11}... | collective-permute-start | bytes 98312 | tf_op jit(solution)/shard_map/ppermute | solution.py:93
  40.9 2.7 %collective-permute-start.15 = (bf16[64,256]{1,0:T(8,128)(2,1)S(1)}, bf16[64,256]{1,0:T(8,128)(2,1)S(1)}, u32[]{:S(2)}, u32[]{:S(2)}) collective-permute-start(bf16[64,256]{1,0:T(8,128)(2,1)S(1)} %slice.303), channel_id=1, source_target_pairs={{0,8},{2,10},{4,12},{6,14},{8,0},{10,2},{12,4},{14,6},{1,9},{3,11}... | collective-permute-start | bytes 98312 | tf_op jit(solution)/shard_map/ppermute | solution.py:93
  44.1 2.7 %collective-permute-start.21 = (bf16[64,256]{1,0:T(8,128)(2,1)S(1)}, bf16[64,256]{1,0:T(8,128)(2,1)S(1)}, u32[]{:S(2)}, u32[]{:S(2)}) collective-permute-start(bf16[64,256]{1,0:T(8,128)(2,1)S(1)} %slice.301), channel_id=1, source_target_pairs={{0,8},{2,10},{4,12},{6,14},{8,0},{10,2},{12,4},{14,6},{1,9},{3,11}... | collective-permute-start | bytes 98312 | tf_op jit(solution)/shard_map/ppermute | solution.py:93
  46.8 1.7 %collective-permute-done.18 = bf16[64,256]{1,0:T(8,128)(2,1)S(1)} collective-permute-done((bf16[64,256]{1,0:T(8,128)(2,1)S(1)}, bf16[64,256]{1,0:T(8,128)(2,1)S(1)}, u32[]{:S(2)}, u32[]{:S(2)}) %collective-permute-start.18) | collective-permute-done | bytes 32800 | tf_op jit(solution)/shard_map/ppermute | solution.py:93
  49.0 0.8 %copy-done.4 = f32[64,1792]{1,0:T(8,128)} copy-done((f32[64,1792]{1,0:T(8,128)}, f32[64,1792]{1,0:T(8,128)S(1)}, u32[]{:S(2)}) %copy-start.4) | copy-done | bytes 458776
  (73 shorter events, 11.1 us)
Async XLA Ops:
  0.0 1.6 %collective-permute-start = (bf16[32,2048]{1,0:T(8,128)(2,1)}, bf16[32,2048]{1,0:T(8,128)(2,1)S(1)}, u32[]{:S(2)}, u32[]{:S(2)}) collective-permute-start(bf16[32,2048]{1,0:T(8,128)(2,1)} %own_ref.1), channel_id=1, source_target_pairs={{0,1},{1,0},{2,3},{3,2},{4,5},{5,4},{6,7},{7,6},{8,9},{9,8},{10,11... | collective-permute-start | bytes 393224 | tf_op jit(solution)/shard_map/ppermute | solution.py:80
  1.7 0.9 %copy-start.1 = (bf16[32,2048]{1,0:T(8,128)(2,1)S(1)}, bf16[32,2048]{1,0:T(8,128)(2,1)}, u32[]{:S(2)}) copy-start(bf16[32,2048]{1,0:T(8,128)(2,1)} %own_ref.1) | copy-start | bytes 393220
  5.1 3.1 %copy-start = (bf16[1792,2048]{1,0:T(8,128)(2,1)S(1)}, bf16[1792,2048]{1,0:T(8,128)(2,1)}, u32[]{:S(2)}) copy-start(bf16[1792,2048]{1,0:T(8,128)(2,1)} %e_ref.27) | copy-start | bytes 22020100
  12.0 9.9 %collective-permute-start.1 = (bf16[256,256]{1,0:T(8,128)(2,1)S(1)}, bf16[256,256]{1,0:T(8,128)(2,1)S(1)}, u32[]{:S(2)}, u32[]{:S(2)}) collective-permute-start(bf16[256,256]{1,0:T(8,128)(2,1)S(1)} %shard_map.48), channel_id=1, source_target_pairs={{0,2},{2,0},{4,6},{6,4},{8,10},{10,8},{12,14},{14,12},{1,3},{3,1},... | collective-permute-start | bytes 393224 | tf_op jit(solution)/shard_map/ppermute | solution.py:93
  15.4 6.8 %collective-permute-start.4 = (bf16[256,256]{1,0:T(8,128)(2,1)S(1)}, bf16[256,256]{1,0:T(8,128)(2,1)S(1)}, u32[]{:S(2)}, u32[]{:S(2)}) collective-permute-start(bf16[256,256]{1,0:T(8,128)(2,1)S(1)} %shard_map.50), channel_id=1, source_target_pairs={{0,4},{2,6},{4,0},{6,2},{8,12},{10,14},{12,8},{14,10},{1,5},{3,7},... | collective-permute-start | bytes 393224 | tf_op jit(solution)/shard_map/ppermute | solution.py:93
  17.0 7.1 %collective-permute-start.7 = (bf16[256,256]{1,0:T(8,128)(2,1)S(1)}, bf16[256,256]{1,0:T(8,128)(2,1)S(1)}, u32[]{:S(2)}, u32[]{:S(2)}) collective-permute-start(bf16[256,256]{1,0:T(8,128)(2,1)S(1)} %shard_map.52), channel_id=1, source_target_pairs={{0,2},{2,0},{4,6},{6,4},{8,10},{10,8},{12,14},{14,12},{1,3},{3,1},... | collective-permute-start | bytes 393224 | tf_op jit(solution)/shard_map/ppermute | solution.py:93
  17.5 8.7 %collective-permute-start.10 = (bf16[256,256]{1,0:T(8,128)(2,1)S(1)}, bf16[256,256]{1,0:T(8,128)(2,1)S(1)}, u32[]{:S(2)}, u32[]{:S(2)}) collective-permute-start(bf16[256,256]{1,0:T(8,128)(2,1)S(1)} %shard_map.54), channel_id=1, source_target_pairs={{0,2},{2,0},{4,6},{6,4},{8,10},{10,8},{12,14},{14,12},{1,3},{3,1},... | collective-permute-start | bytes 393224 | tf_op jit(solution)/shard_map/ppermute | solution.py:93
  19.0 7.7 %collective-permute-start.13 = (bf16[256,256]{1,0:T(8,128)(2,1)S(1)}, bf16[256,256]{1,0:T(8,128)(2,1)S(1)}, u32[]{:S(2)}, u32[]{:S(2)}) collective-permute-start(bf16[256,256]{1,0:T(8,128)(2,1)S(1)} %shard_map.56), channel_id=1, source_target_pairs={{0,4},{2,6},{4,0},{6,2},{8,12},{10,14},{12,8},{14,10},{1,5},{3,7},... | collective-permute-start | bytes 393224 | tf_op jit(solution)/shard_map/ppermute | solution.py:93
  21.9 7.2 %collective-permute-start.16 = (bf16[256,256]{1,0:T(8,128)(2,1)S(1)}, bf16[256,256]{1,0:T(8,128)(2,1)S(1)}, u32[]{:S(2)}, u32[]{:S(2)}) collective-permute-start(bf16[256,256]{1,0:T(8,128)(2,1)S(1)} %shard_map.58), channel_id=1, source_target_pairs={{0,2},{2,0},{4,6},{6,4},{8,10},{10,8},{12,14},{14,12},{1,3},{3,1},... | collective-permute-start | bytes 393224 | tf_op jit(solution)/shard_map/ppermute | solution.py:93
  22.1 9.0 %collective-permute-start.19 = (bf16[256,256]{1,0:T(8,128)(2,1)S(1)}, bf16[256,256]{1,0:T(8,128)(2,1)S(1)}, u32[]{:S(2)}, u32[]{:S(2)}) collective-permute-start(bf16[256,256]{1,0:T(8,128)(2,1)S(1)} %shard_map.60), channel_id=1, source_target_pairs={{0,2},{2,0},{4,6},{6,4},{8,10},{10,8},{12,14},{14,12},{1,3},{3,1},... | collective-permute-start | bytes 393224 | tf_op jit(solution)/shard_map/ppermute | solution.py:93
  24.1 8.3 %collective-permute-start.2 = (bf16[128,256]{1,0:T(8,128)(2,1)S(1)}, bf16[128,256]{1,0:T(8,128)(2,1)S(1)}, u32[]{:S(2)}, u32[]{:S(2)}) collective-permute-start(bf16[128,256]{1,0:T(8,128)(2,1)S(1)} %fusion.12), channel_id=1, source_target_pairs={{0,4},{2,6},{4,0},{6,2},{8,12},{10,14},{12,8},{14,10},{1,5},{3,7},... | collective-permute-start | bytes 196616 | tf_op jit(solution)/shard_map/ppermute | solution.py:93
  26.2 7.8 %collective-permute-start.5 = (bf16[128,256]{1,0:T(8,128)(2,1)S(1)}, bf16[128,256]{1,0:T(8,128)(2,1)S(1)}, u32[]{:S(2)}, u32[]{:S(2)}) collective-permute-start(bf16[128,256]{1,0:T(8,128)(2,1)S(1)} %fusion.10), channel_id=1, source_target_pairs={{0,2},{2,0},{4,6},{6,4},{8,10},{10,8},{12,14},{14,12},{1,3},{3,1},... | collective-permute-start | bytes 196616 | tf_op jit(solution)/shard_map/ppermute | solution.py:93
  26.8 7.8 %collective-permute-start.8 = (bf16[128,256]{1,0:T(8,128)(2,1)S(1)}, bf16[128,256]{1,0:T(8,128)(2,1)S(1)}, u32[]{:S(2)}, u32[]{:S(2)}) collective-permute-start(bf16[128,256]{1,0:T(8,128)(2,1)S(1)} %fusion.8), channel_id=1, source_target_pairs={{0,4},{2,6},{4,0},{6,2},{8,12},{10,14},{12,8},{14,10},{1,5},{3,7},... | collective-permute-start | bytes 196616 | tf_op jit(solution)/shard_map/ppermute | solution.py:93
  29.0 8.3 %collective-permute-start.11 = (bf16[128,256]{1,0:T(8,128)(2,1)S(1)}, bf16[128,256]{1,0:T(8,128)(2,1)S(1)}, u32[]{:S(2)}, u32[]{:S(2)}) collective-permute-start(bf16[128,256]{1,0:T(8,128)(2,1)S(1)} %fusion.6), channel_id=1, source_target_pairs={{0,4},{2,6},{4,0},{6,2},{8,12},{10,14},{12,8},{14,10},{1,5},{3,7},... | collective-permute-start | bytes 196616 | tf_op jit(solution)/shard_map/ppermute | solution.py:93
  31.1 6.6 %collective-permute-start.14 = (bf16[128,256]{1,0:T(8,128)(2,1)S(1)}, bf16[128,256]{1,0:T(8,128)(2,1)S(1)}, u32[]{:S(2)}, u32[]{:S(2)}) collective-permute-start(bf16[128,256]{1,0:T(8,128)(2,1)S(1)} %fusion.4), channel_id=1, source_target_pairs={{0,2},{2,0},{4,6},{6,4},{8,10},{10,8},{12,14},{14,12},{1,3},{3,1},... | collective-permute-start | bytes 196616 | tf_op jit(solution)/shard_map/ppermute | solution.py:93
  32.4 8.1 %collective-permute-start.17 = (bf16[128,256]{1,0:T(8,128)(2,1)S(1)}, bf16[128,256]{1,0:T(8,128)(2,1)S(1)}, u32[]{:S(2)}, u32[]{:S(2)}) collective-permute-start(bf16[128,256]{1,0:T(8,128)(2,1)S(1)} %fusion.2), channel_id=1, source_target_pairs={{0,4},{2,6},{4,0},{6,2},{8,12},{10,14},{12,8},{14,10},{1,5},{3,7},... | collective-permute-start | bytes 196616 | tf_op jit(solution)/shard_map/ppermute | solution.py:93
  34.1 6.8 %collective-permute-start.20 = (bf16[128,256]{1,0:T(8,128)(2,1)S(1)}, bf16[128,256]{1,0:T(8,128)(2,1)S(1)}, u32[]{:S(2)}, u32[]{:S(2)}) collective-permute-start(bf16[128,256]{1,0:T(8,128)(2,1)S(1)} %fusion), channel_id=1, source_target_pairs={{0,4},{2,6},{4,0},{6,2},{8,12},{10,14},{12,8},{14,10},{1,5},{3,7},... | collective-permute-start | bytes 196616 | tf_op jit(solution)/shard_map/ppermute | solution.py:93
  34.6 9.0 %collective-permute-start.3 = (bf16[64,256]{1,0:T(8,128)(2,1)S(1)}, bf16[64,256]{1,0:T(8,128)(2,1)S(1)}, u32[]{:S(2)}, u32[]{:S(2)}) collective-permute-start(bf16[64,256]{1,0:T(8,128)(2,1)S(1)} %slice.307), channel_id=1, source_target_pairs={{0,8},{2,10},{4,12},{6,14},{8,0},{10,2},{12,4},{14,6},{1,9},{3,11}... | collective-permute-start | bytes 98312 | tf_op jit(solution)/shard_map/ppermute | solution.py:93
  37.3 6.7 %collective-permute-start.6 = (bf16[64,256]{1,0:T(8,128)(2,1)S(1)}, bf16[64,256]{1,0:T(8,128)(2,1)S(1)}, u32[]{:S(2)}, u32[]{:S(2)}) collective-permute-start(bf16[64,256]{1,0:T(8,128)(2,1)S(1)} %slice.306), channel_id=1, source_target_pairs={{0,8},{2,10},{4,12},{6,14},{8,0},{10,2},{12,4},{14,6},{1,9},{3,11}... | collective-permute-start | bytes 98312 | tf_op jit(solution)/shard_map/ppermute | solution.py:93
  37.8 9.0 %collective-permute-start.9 = (bf16[64,256]{1,0:T(8,128)(2,1)S(1)}, bf16[64,256]{1,0:T(8,128)(2,1)S(1)}, u32[]{:S(2)}, u32[]{:S(2)}) collective-permute-start(bf16[64,256]{1,0:T(8,128)(2,1)S(1)} %slice.305), channel_id=1, source_target_pairs={{0,8},{2,10},{4,12},{6,14},{8,0},{10,2},{12,4},{14,6},{1,9},{3,11}... | collective-permute-start | bytes 98312 | tf_op jit(solution)/shard_map/ppermute | solution.py:93
  40.5 6.3 %collective-permute-start.12 = (bf16[64,256]{1,0:T(8,128)(2,1)S(1)}, bf16[64,256]{1,0:T(8,128)(2,1)S(1)}, u32[]{:S(2)}, u32[]{:S(2)}) collective-permute-start(bf16[64,256]{1,0:T(8,128)(2,1)S(1)} %slice.304), channel_id=1, source_target_pairs={{0,8},{2,10},{4,12},{6,14},{8,0},{10,2},{12,4},{14,6},{1,9},{3,11}... | collective-permute-start | bytes 98312 | tf_op jit(solution)/shard_map/ppermute | solution.py:93
  40.9 5.9 %collective-permute-start.15 = (bf16[64,256]{1,0:T(8,128)(2,1)S(1)}, bf16[64,256]{1,0:T(8,128)(2,1)S(1)}, u32[]{:S(2)}, u32[]{:S(2)}) collective-permute-start(bf16[64,256]{1,0:T(8,128)(2,1)S(1)} %slice.303), channel_id=1, source_target_pairs={{0,8},{2,10},{4,12},{6,14},{8,0},{10,2},{12,4},{14,6},{1,9},{3,11}... | collective-permute-start | bytes 98312 | tf_op jit(solution)/shard_map/ppermute | solution.py:93
  43.6 4.9 %collective-permute-start.18 = (bf16[64,256]{1,0:T(8,128)(2,1)S(1)}, bf16[64,256]{1,0:T(8,128)(2,1)S(1)}, u32[]{:S(2)}, u32[]{:S(2)}) collective-permute-start(bf16[64,256]{1,0:T(8,128)(2,1)S(1)} %slice.302), channel_id=1, source_target_pairs={{0,8},{2,10},{4,12},{6,14},{8,0},{10,2},{12,4},{14,6},{1,9},{3,11}... | collective-permute-start | bytes 98312 | tf_op jit(solution)/shard_map/ppermute | solution.py:93
  44.1 4.9 %collective-permute-start.21 = (bf16[64,256]{1,0:T(8,128)(2,1)S(1)}, bf16[64,256]{1,0:T(8,128)(2,1)S(1)}, u32[]{:S(2)}, u32[]{:S(2)}) collective-permute-start(bf16[64,256]{1,0:T(8,128)(2,1)S(1)} %slice.301), channel_id=1, source_target_pairs={{0,8},{2,10},{4,12},{6,14},{8,0},{10,2},{12,4},{14,6},{1,9},{3,11}... | collective-permute-start | bytes 98312 | tf_op jit(solution)/shard_map/ppermute | solution.py:93
  (3 other events, 2.2 us)

commit v2 on v0

v2 whole, which is shorter than its diff:
```python
import functools

import jax
import jax.numpy as jnp
from jax import lax
from jax.experimental import pallas as pl
from jax.experimental.pallas import tpu as pltpu
from jax.sharding import PartitionSpec as P

TILE = 256
VMEM_LIMIT = 24 * 1024 * 1024


def ranked(bits, fixed):
    out = [fixed]
    for b in reversed(bits):
        out = [c | (1 << b) for c in out] + out
    return out


def project_kernel(
    n, per_chunk, sets, pieces, order_hbm, own_hbm, lanc_hbm, other_ref, eig_hbm, *rest
):
    outs = rest[: len(pieces)]
    order, own, lanc16, held, prod, eig, small_sem, eig_sem = rest[len(pieces) :]
    small = [
        pltpu.make_async_copy(src, dst, small_sem.at[i])
        for i, (src, dst) in enumerate(
            [(order_hbm, order), (own_hbm, own), (lanc_hbm, lanc16)]
        )
    ]
    for copy in small:
        copy.start()
    loads = []
    at = 0
    for i, (width, _) in enumerate(pieces):
        loads.append(
            pltpu.make_async_copy(
                eig_hbm.at[pl.ds(at, width)], eig.at[pl.ds(at, width)], eig_sem.at[i]
            )
        )
        loads[-1].start()
        at += width
    me = lax.axis_index("grid")
    core = lax.axis_index("eig")
    half = own.shape[0]
    held[half:, :] = other_ref[...].astype(jnp.float32)
    for copy in small:
        copy.wait()
    held[:half, :] = own[...].astype(jnp.float32)
    lanc = lanc16[...].astype(jnp.float32)
    rest_bits = list(range(2, n.bit_length() - 1))
    slots = [(r, j) for s in sets for r in ranked(rest_bits, s) for j in range(per_chunk)]

    def rows(slot):
        r, j = slot
        band = order[(me ^ r) * per_chunk + j]
        band = lax.rem(band + core * half, 2 * half)
        return held[pl.ds(band, 1), :] * lanc

    step = 2 * lanc.shape[0]
    for i in range(0, len(slots), 2):
        pair = jnp.concatenate([rows(slots[i]), rows(slots[i + 1])], axis=0)
        prod[i // 2 * step : (i // 2 + 1) * step, :] = pair.astype(jnp.bfloat16)

    quarter = prod.shape[0] // 3
    at = 0
    for i, (width, z_first) in enumerate(pieces):
        loads[i].wait()
        first = quarter if z_first else 0
        for col in range(0, width, TILE):
            size = min(TILE, width - col)
            outs[i][:, col : col + size] = lax.dot_general(
                prod[first : first + 2 * quarter, :],
                eig[at + col : at + col + size, :],
                (((1,), (1,)), ((), ())),
                preferred_element_type=jnp.float32,
            ).astype(outs[i].dtype)
        at += width


def project(n, sets, pieces, dtype, order, own, lanczos, other, eigvecs):
    lanc = lanczos.shape[0]
    per_chunk = order.shape[0] // n
    cols, depth = eigvecs.shape
    half = order.shape[0] * lanc // 2
    any_spec = pl.BlockSpec(memory_space=pl.ANY)
    vmem_spec = pl.BlockSpec(memory_space=pltpu.VMEM)
    return pl.pallas_call(
        functools.partial(project_kernel, n, per_chunk, sets, pieces),
        out_shape=[jax.ShapeDtypeStruct((half, w), dtype) for w, _ in pieces],
        in_specs=[any_spec, any_spec, any_spec, vmem_spec, any_spec],
        out_specs=[vmem_spec] * len(pieces),
        scratch_shapes=[
            pltpu.SMEM(order.shape, jnp.int32),
            pltpu.VMEM(own.shape, jnp.bfloat16),
            pltpu.VMEM(lanczos.shape, jnp.bfloat16),
            pltpu.VMEM((2 * own.shape[0], depth), jnp.float32),
            pltpu.VMEM((half // 2 * 3, depth), jnp.bfloat16),
            pltpu.VMEM((cols, depth), jnp.bfloat16),
            pltpu.SemaphoreType.DMA((3,)),
            pltpu.SemaphoreType.DMA((len(pieces),)),
        ],
        compiler_params=pltpu.CompilerParams(vmem_limit_bytes=VMEM_LIMIT),
        cost_estimate=pl.CostEstimate(
            flops=2 * half * cols * depth,
            bytes_accessed=2 * depth * cols + 4 * half * cols,
            transcendentals=0,
        ),
    )(order, own, lanczos, other, eigvecs)


def per_device(n, eigvecs, lanczos, bands, band_order):
    lanc = lanczos.shape[0]
    per_chunk = band_order.shape[0] // n
    cols = eigvecs.shape[0]
    quarter = band_order.shape[0] * lanc // 4
    unit = cols // 7 // 128 * 128
    pieces = [(2 * unit, False), (2 * unit, True), (2 * unit, False)]
    pieces.append((cols - 6 * unit, False))

    def exchange(value, bit):
        return lax.ppermute(value, "grid", [(i, i ^ (1 << bit)) for i in range(n)])

    other = lax.ppermute(bands, "eig", [(0, 1), (1, 0)])
    args = (band_order, bands, lanczos, other, eigvecs)
    send = project(n, (1, 3, 2), pieces, jnp.bfloat16, *args)
    got = [exchange(s, 1 if z else 0) for s, (_, z) in zip(send, pieces)]
    kept = project(n, (2, 0, 1), pieces, jnp.float32, *args)
    outs = []
    for p, (_, z_first) in enumerate(pieces):
        top = kept[p][:quarter] + got[p][quarter:].astype(jnp.float32)
        low = kept[p][quarter:] + got[p][:quarter].astype(jnp.float32)
        keep, leave = (top, low) if z_first else (low, top)
        came = exchange(leave.astype(jnp.bfloat16), 0 if z_first else 1)
        value = keep + came.astype(jnp.float32)
        for bit in range(2, n.bit_length() - 1):
            mid = value.shape[0] // 2
            dtype = jnp.bfloat16 if bit < 3 else jnp.float32
            came = exchange(value[:mid].astype(dtype), bit)
            value = value[mid:] + came.astype(jnp.float32)
        outs.append(value)
    result = jnp.concatenate(outs, axis=1)
    return result.reshape(per_chunk, lanc, cols)


def solution(mesh):
    in_specs = (
        P("eig", ("rep", "grid")),
        P(None, ("rep", "grid")),
        P("eig", ("rep", "grid")),
        P("rep"),
    )
    out_specs = P(("rep", "grid"), None, "eig")
    return jax.shard_map(
        functools.partial(per_device, mesh.shape["grid"]),
        mesh=mesh,
        in_specs=in_specs,
        out_specs=out_specs,
        check_vma=False,
    )
```

time: 111 us -> 48.3 us (0.44)
  waiting for transfers between devices: 83.6 us -> 12.8 us
  starting transfers between devices: 0.01 us -> 20 us
  between operations: 13.4 us -> 0.14 us
  matrix products: 8.88 us -> 0 us
  Pallas kernels: 0 us -> 8.63 us
  local copies, waits for them, and re-layouts: 0.74 us -> 5.44 us
  blocking collectives: 2.28 us -> 0 us
  other arithmetic: 2.2 us -> 1.09 us
    reduce_scatter x1 -> x0, waiting for transfers between devices: 83.6 us -> none  [per_device(): lax.psum_scatter(partial_value, 'grid', scatter_dimension=0, tiled=True)]
    ppermute x0 -> x13, starting transfers between devices: none -> 20 us  [the longest x12 19.5 us: exchange(): return lax.ppermute(value, 'grid', [(i, i ^ 1 << bit) for i in range(n)])]
    ppermute x0 -> x13, waiting for transfers between devices: none -> 12.8 us  [the longest x12 11.6 us: exchange(): return lax.ppermute(value, 'grid', [(i, i ^ 1 << bit) for i in range(n)])]
    dot_general x1 -> x0, matrix products: 8.88 us -> none  [per_device(): lax.dot_general((jnp.take(all_bands, band_order, axis=0)[:, None, :].asty...]
    pallas_call x0 -> x2, Pallas kernels: none -> 8.63 us  [project(): pl.pallas_call(functools.partial(project_kernel, n, per_chunk, sets, piec...]
    unnamed x0 -> x8, local copies, waits for them, and re-layouts: none -> 5.4 us
    all_gather x1 -> x0, blocking collectives: 2.28 us -> none  [per_device(): all_bands = lax.all_gather(bands, 'eig', axis=0, tiled=True)]
  transfers between devices with their start and end apart: 1 -> 13, of which waited for: 1 -> 9; matrix products, arithmetic and copies ran while one was open for 0% -> 1% of each run, Pallas kernels for 0% -> 9%
where the time goes in v2:
time: 48.3 us; the launch traced here: 48.1 us
  starting transfers between devices  20 us (41%)
  waiting for transfers between devices  12.8 us (27%)
  Pallas kernels  8.63 us (18%)
  local copies, waits for them, and re-layouts  5.44 us (11%)
  other arithmetic  1.09 us (2%)
    ppermute x12, starting transfers between devices, exchange(): return lax.ppermute(value, 'grid', [(i, i ^ 1 << bit) for i in range(n)])  19.5 us
    ppermute x12, waiting for transfers between devices, exchange(): return lax.ppermute(value, 'grid', [(i, i ^ 1 << bit) for i in range(n)])  11.6 us
    pallas_call x2, Pallas kernels, project(): pl.pallas_call(functools.partial(project_kernel, n, per_chunk, sets, piec...  8.63 us
    unnamed x8, local copies, waits for them, and re-layouts  5.4 us
    ppermute x1, waiting for transfers between devices, per_device(): other = lax.ppermute(bands, 'eig', [(0, 1), (1, 0)])  1.2 us
  transfers between devices with their start and end apart: 13, of which 9 were waited for; matrix products, arithmetic and copies ran while one was open for 1% of the time, Pallas kernels for 9%

profile of v2, /device:TPU:0, one launch (start us, length us, event | category | flops | bytes accessed | tf_op | source)
XLA Modules:
  0.0 48.1 jit_solution(1228175878252074020)
XLA Ops:
  0.5 1.2 %collective-permute-done.other_ref = bf16[32,2048]{1,0:T(8,128)(2,1)S(1)} collective-permute-done((bf16[32,2048]{1,0:T(8,128)(2,1)}, bf16[32,2048]{1,0:T(8,128)(2,1)S(1)}, u32[]{:S(2)}, u32[]{:S(2)}) %collective-permute-start) | collective-permute-done | bytes 131104 | tf_op jit(solution)/shard_map/ppermute | solution.py:125
  1.7 3.1 %copy-done = bf16[1792,2048]{1,0:T(8,128)(2,1)S(1)} copy-done((bf16[1792,2048]{1,0:T(8,128)(2,1)S(1)}, bf16[1792,2048]{1,0:T(8,128)(2,1)}, u32[]{:S(2)}) %copy-start) | copy-done | bytes 7340056
  4.7 0.9 %copy-done.1 = bf16[32,2048]{1,0:T(8,128)(2,1)S(1)} copy-done((bf16[32,2048]{1,0:T(8,128)(2,1)S(1)}, bf16[32,2048]{1,0:T(8,128)(2,1)}, u32[]{:S(2)}) %copy-start.1) | copy-done | bytes 131096
  5.6 0.8 %copy-done.2 = bf16[8,2048]{1,0:T(8,128)(2,1)S(1)} copy-done((bf16[8,2048]{1,0:T(8,128)(2,1)S(1)}, bf16[8,2048]{1,0:T(8,128)(2,1)}, u32[]{:S(2)}) %copy-start.2) | copy-done | bytes 32792
  6.4 0.7 %copy-done.3 = s32[64]{0:T(128)S(1)} copy-done((s32[64]{0:T(128)S(1)}, s32[64]{0:T(128)}, u32[]{:S(2)}) %copy-start.3) | copy-done | bytes 280
  7.1 4.3 %shard_map.47 = (bf16[256,512]{1,0:T(8,128)(2,1)S(1)}, bf16[256,512]{1,0:T(8,128)(2,1)S(1)}, bf16[256,512]{1,0:T(8,128)(2,1)S(1)}, bf16[256,256]{1,0:T(8,128)(2,1)S(1)}) custom-call(s32[64]{0:T(128)S(1)} %copy-done.3, bf16[32,2048]{1,0:T(8,128)(2,1)S(1)} %copy-done.1, bf16[8,2048]{1,0:T(8,128)(2,1)S(1)} %copy-done.2, ...), custom_call_target="tpu_custom_call" | custom-call | flops 1879048192 | bytes 9175040 | tf_op jit(solution)/shard_map/pallas_call | solution.py:89
  11.4 2.9 %collective-permute-start.10 = (bf16[256,256]{1,0:T(8,128)(2,1)S(1)}, bf16[256,256]{1,0:T(8,128)(2,1)S(1)}, u32[]{:S(2)}, u32[]{:S(2)}) collective-permute-start(bf16[256,256]{1,0:T(8,128)(2,1)S(1)} %get-tuple-element.20), channel_id=1, source_target_pairs={{0,2},{2,0},{4,6},{6,4},{8,10},{10,8},{12,14},{14,12},{1,3},{3,1},... | collective-permute-start | bytes 393224 | tf_op jit(solution)/shard_map/ppermute | solution.py:123
  14.3 4.3 %shard_map.46 = (f32[256,512]{1,0:T(8,128)S(1)}, f32[256,512]{1,0:T(8,128)S(1)}, f32[256,512]{1,0:T(8,128)S(1)}, f32[256,256]{1,0:T(8,128)S(1)}) custom-call(s32[64]{0:T(128)S(1)} %copy-done.3, bf16[32,2048]{1,0:T(8,128)(2,1)S(1)} %copy-done.1, bf16[8,2048]{1,0:T(8,128)(2,1)S(1)} %copy-done.2, bf16[32,2048]{1,0:T(8,128)(2,1)S(1)} %collective-permute-done.other_ref, ...), custom_call_target="tpu_custom_call" | custom-call | flops 1879048192 | bytes 9175040 | tf_op jit(solution)/shard_map/pallas_call | solution.py:89
  18.7 1.6 %collective-permute-start.11 = (bf16[128,256]{1,0:T(8,128)(2,1)S(1)}, bf16[128,256]{1,0:T(8,128)(2,1)S(1)}, u32[]{:S(2)}, u32[]{:S(2)}) collective-permute-start(bf16[128,256]{1,0:T(8,128)(2,1)S(1)} %add_convert_fusion.3), channel_id=1, source_target_pairs={{0,4},{2,6},{4,0},{6,2},{8,12},{10,14},{12,8},{14,10},{1,5},{3,7},... | collective-permute-start | bytes 196616 | tf_op jit(solution)/shard_map/ppermute | solution.py:123
  20.3 1.2 %collective-permute-start.7 = (bf16[256,512]{1,0:T(8,128)(2,1)S(1)}, bf16[256,512]{1,0:T(8,128)(2,1)S(1)}, u32[]{:S(2)}, u32[]{:S(2)}) collective-permute-start(bf16[256,512]{1,0:T(8,128)(2,1)S(1)} %get-tuple-element.18), channel_id=1, source_target_pairs={{0,2},{2,0},{4,6},{6,4},{8,10},{10,8},{12,14},{14,12},{1,3},{3,1},... | collective-permute-start | bytes 786440 | tf_op jit(solution)/shard_map/ppermute | solution.py:123
  21.5 1.5 %collective-permute-done.11 = bf16[128,256]{1,0:T(8,128)(2,1)S(1)} collective-permute-done((bf16[128,256]{1,0:T(8,128)(2,1)S(1)}, bf16[128,256]{1,0:T(8,128)(2,1)S(1)}, u32[]{:S(2)}, u32[]{:S(2)}) %collective-permute-start.11) | collective-permute-done | bytes 65568 | tf_op jit(solution)/shard_map/ppermute | solution.py:123
  23.0 2.6 %collective-permute-start.12 = (bf16[64,256]{1,0:T(8,128)(2,1)S(1)}, bf16[64,256]{1,0:T(8,128)(2,1)S(1)}, u32[]{:S(2)}, u32[]{:S(2)}) collective-permute-start(bf16[64,256]{1,0:T(8,128)(2,1)S(1)} %slice.143), channel_id=1, source_target_pairs={{0,8},{2,10},{4,12},{6,14},{8,0},{10,2},{12,4},{14,6},{1,9},{3,11}... | collective-permute-start | bytes 98312 | tf_op jit(solution)/shard_map/ppermute | solution.py:123
  25.7 1.6 %collective-permute-start.4 = (bf16[256,512]{1,0:T(8,128)(2,1)S(1)}, bf16[256,512]{1,0:T(8,128)(2,1)S(1)}, u32[]{:S(2)}, u32[]{:S(2)}) collective-permute-start(bf16[256,512]{1,0:T(8,128)(2,1)S(1)} %get-tuple-element.16), channel_id=1, source_target_pairs={{0,4},{2,6},{4,0},{6,2},{8,12},{10,14},{12,8},{14,10},{1,5},{3,7},... | collective-permute-start | bytes 786440 | tf_op jit(solution)/shard_map/ppermute | solution.py:123
  27.3 1.2 %collective-permute-start.1 = (bf16[256,512]{1,0:T(8,128)(2,1)S(1)}, bf16[256,512]{1,0:T(8,128)(2,1)S(1)}, u32[]{:S(2)}, u32[]{:S(2)}) collective-permute-start(bf16[256,512]{1,0:T(8,128)(2,1)S(1)} %get-tuple-element.14), channel_id=1, source_target_pairs={{0,2},{2,0},{4,6},{6,4},{8,10},{10,8},{12,14},{14,12},{1,3},{3,1},... | collective-permute-start | bytes 786440 | tf_op jit(solution)/shard_map/ppermute | solution.py:123
  28.5 1.5 %collective-permute-start.8 = (bf16[128,512]{1,0:T(8,128)(2,1)S(1)}, bf16[128,512]{1,0:T(8,128)(2,1)S(1)}, u32[]{:S(2)}, u32[]{:S(2)}) collective-permute-start(bf16[128,512]{1,0:T(8,128)(2,1)S(1)} %add_convert_fusion), channel_id=1, source_target_pairs={{0,4},{2,6},{4,0},{6,2},{8,12},{10,14},{12,8},{14,10},{1,5},{3,7},... | collective-permute-start | bytes 393224 | tf_op jit(solution)/shard_map/ppermute | solution.py:123
  30.0 4.4 %collective-permute-done.4 = bf16[256,512]{1,0:T(8,128)(2,1)S(1)} collective-permute-done((bf16[256,512]{1,0:T(8,128)(2,1)S(1)}, bf16[256,512]{1,0:T(8,128)(2,1)S(1)}, u32[]{:S(2)}, u32[]{:S(2)}) %collective-permute-start.4) | collective-permute-done | bytes 262176 | tf_op jit(solution)/shard_map/ppermute | solution.py:123
  34.9 1.7 %collective-permute-start.2 = (bf16[128,512]{1,0:T(8,128)(2,1)S(1)}, bf16[128,512]{1,0:T(8,128)(2,1)S(1)}, u32[]{:S(2)}, u32[]{:S(2)}) collective-permute-start(bf16[128,512]{1,0:T(8,128)(2,1)S(1)} %add_convert_fusion.2), channel_id=1, source_target_pairs={{0,4},{2,6},{4,0},{6,2},{8,12},{10,14},{12,8},{14,10},{1,5},{3,7},... | collective-permute-start | bytes 393224 | tf_op jit(solution)/shard_map/ppermute | solution.py:123
  37.0 1.2 %collective-permute-start.9 = (bf16[64,512]{1,0:T(8,128)(2,1)S(1)}, bf16[64,512]{1,0:T(8,128)(2,1)S(1)}, u32[]{:S(2)}, u32[]{:S(2)}) collective-permute-start(bf16[64,512]{1,0:T(8,128)(2,1)S(1)} %slice.140), channel_id=1, source_target_pairs={{0,8},{2,10},{4,12},{6,14},{8,0},{10,2},{12,4},{14,6},{1,9},{3,11}... | collective-permute-start | bytes 196616 | tf_op jit(solution)/shard_map/ppermute | solution.py:123
  38.1 1.3 %collective-permute-done.5 = bf16[128,512]{1,0:T(8,128)(2,1)S(1)} collective-permute-done((bf16[128,512]{1,0:T(8,128)(2,1)S(1)}, bf16[128,512]{1,0:T(8,128)(2,1)S(1)}, u32[]{:S(2)}, u32[]{:S(2)}) %collective-permute-start.5) | collective-permute-done | bytes 131104 | tf_op jit(solution)/shard_map/ppermute | solution.py:123
  39.5 0.6 %collective-permute-start.6 = (bf16[64,512]{1,0:T(8,128)(2,1)S(1)}, bf16[64,512]{1,0:T(8,128)(2,1)S(1)}, u32[]{:S(2)}, u32[]{:S(2)}) collective-permute-start(bf16[64,512]{1,0:T(8,128)(2,1)S(1)} %slice.141), channel_id=1, source_target_pairs={{0,8},{2,10},{4,12},{6,14},{8,0},{10,2},{12,4},{14,6},{1,9},{3,11}... | collective-permute-start | bytes 196616 | tf_op jit(solution)/shard_map/ppermute | solution.py:123
  40.6 3.0 %collective-permute-start.3 = (bf16[64,512]{1,0:T(8,128)(2,1)S(1)}, bf16[64,512]{1,0:T(8,128)(2,1)S(1)}, u32[]{:S(2)}, u32[]{:S(2)}) collective-permute-start(bf16[64,512]{1,0:T(8,128)(2,1)S(1)} %slice.142), channel_id=1, source_target_pairs={{0,8},{2,10},{4,12},{6,14},{8,0},{10,2},{12,4},{14,6},{1,9},{3,11}... | collective-permute-start | bytes 196616 | tf_op jit(solution)/shard_map/ppermute | solution.py:123
  44.0 0.8 %collective-permute-done.6 = bf16[64,512]{1,0:T(8,128)(2,1)S(1)} collective-permute-done((bf16[64,512]{1,0:T(8,128)(2,1)S(1)}, bf16[64,512]{1,0:T(8,128)(2,1)S(1)}, u32[]{:S(2)}, u32[]{:S(2)}) %collective-permute-start.6) | collective-permute-done | bytes 65568 | tf_op jit(solution)/shard_map/ppermute | solution.py:123
  44.7 2.5 %collective-permute-done.3 = bf16[64,512]{1,0:T(8,128)(2,1)S(1)} collective-permute-done((bf16[64,512]{1,0:T(8,128)(2,1)S(1)}, bf16[64,512]{1,0:T(8,128)(2,1)S(1)}, u32[]{:S(2)}, u32[]{:S(2)}) %collective-permute-start.3) | collective-permute-done | bytes 65568 | tf_op jit(solution)/shard_map/ppermute | solution.py:123
  47.3 0.8 %maximum_bitcast_fusion = f32[8,8,1792]{2,1,0:T(8,128)} fusion(f32[64,256]{1,0:T(8,128)S(1)} %slice_add_fusion.3, f32[64,512]{1,0:T(8,128)S(1)} %slice_add_fusion, f32[64,512]{1,0:T(8,128)S(1)} %slice_add_fusion.1, f32[64,512]{1,0:T(8,128)S(1)} %slice_add_fusion.2), kind=kLoop, calls=%fused_computation | loop fusion | flops 344064 | bytes 917504 | tf_op jit(solution)/shard_map/reshape | solution.py:144
  (29 shorter events, 2.4 us)
Async XLA Ops:
  0.0 1.6 %collective-permute-start = (bf16[32,2048]{1,0:T(8,128)(2,1)}, bf16[32,2048]{1,0:T(8,128)(2,1)S(1)}, u32[]{:S(2)}, u32[]{:S(2)}) collective-permute-start(bf16[32,2048]{1,0:T(8,128)(2,1)} %own_hbm.3), channel_id=1, source_target_pairs={{0,1},{1,0},{2,3},{3,2},{4,5},{5,4},{6,7},{7,6},{8,9},{9,8},{10,11... | collective-permute-start | bytes 393224 | tf_op jit(solution)/shard_map/ppermute | solution.py:125
  1.7 3.1 %copy-start = (bf16[1792,2048]{1,0:T(8,128)(2,1)S(1)}, bf16[1792,2048]{1,0:T(8,128)(2,1)}, u32[]{:S(2)}) copy-start(bf16[1792,2048]{1,0:T(8,128)(2,1)} %eig_hbm.3) | copy-start | bytes 22020100
  4.7 0.9 %copy-start.1 = (bf16[32,2048]{1,0:T(8,128)(2,1)S(1)}, bf16[32,2048]{1,0:T(8,128)(2,1)}, u32[]{:S(2)}) copy-start(bf16[32,2048]{1,0:T(8,128)(2,1)} %own_hbm.3) | copy-start | bytes 393220
  5.6 0.8 %copy-start.2 = (bf16[8,2048]{1,0:T(8,128)(2,1)S(1)}, bf16[8,2048]{1,0:T(8,128)(2,1)}, u32[]{:S(2)}) copy-start(bf16[8,2048]{1,0:T(8,128)(2,1)} %lanc_hbm.3) | copy-start | bytes 98308
  6.4 0.7 %copy-start.3 = (s32[64]{0:T(128)S(1)}, s32[64]{0:T(128)}, u32[]{:S(2)}) copy-start(s32[64]{0:T(128)} %order_hbm.3) | copy-start | bytes 772
  11.4 7.2 %collective-permute-start.10 = (bf16[256,256]{1,0:T(8,128)(2,1)S(1)}, bf16[256,256]{1,0:T(8,128)(2,1)S(1)}, u32[]{:S(2)}, u32[]{:S(2)}) collective-permute-start(bf16[256,256]{1,0:T(8,128)(2,1)S(1)} %get-tuple-element.20), channel_id=1, source_target_pairs={{0,2},{2,0},{4,6},{6,4},{8,10},{10,8},{12,14},{14,12},{1,3},{3,1},... | collective-permute-start | bytes 393224 | tf_op jit(solution)/shard_map/ppermute | solution.py:123
  18.7 4.3 %collective-permute-start.11 = (bf16[128,256]{1,0:T(8,128)(2,1)S(1)}, bf16[128,256]{1,0:T(8,128)(2,1)S(1)}, u32[]{:S(2)}, u32[]{:S(2)}) collective-permute-start(bf16[128,256]{1,0:T(8,128)(2,1)S(1)} %add_convert_fusion.3), channel_id=1, source_target_pairs={{0,4},{2,6},{4,0},{6,2},{8,12},{10,14},{12,8},{14,10},{1,5},{3,7},... | collective-permute-start | bytes 196616 | tf_op jit(solution)/shard_map/ppermute | solution.py:123
  20.3 8.2 %collective-permute-start.7 = (bf16[256,512]{1,0:T(8,128)(2,1)S(1)}, bf16[256,512]{1,0:T(8,128)(2,1)S(1)}, u32[]{:S(2)}, u32[]{:S(2)}) collective-permute-start(bf16[256,512]{1,0:T(8,128)(2,1)S(1)} %get-tuple-element.18), channel_id=1, source_target_pairs={{0,2},{2,0},{4,6},{6,4},{8,10},{10,8},{12,14},{14,12},{1,3},{3,1},... | collective-permute-start | bytes 786440 | tf_op jit(solution)/shard_map/ppermute | solution.py:123
  23.0 5.4 %collective-permute-start.12 = (bf16[64,256]{1,0:T(8,128)(2,1)S(1)}, bf16[64,256]{1,0:T(8,128)(2,1)S(1)}, u32[]{:S(2)}, u32[]{:S(2)}) collective-permute-start(bf16[64,256]{1,0:T(8,128)(2,1)S(1)} %slice.143), channel_id=1, source_target_pairs={{0,8},{2,10},{4,12},{6,14},{8,0},{10,2},{12,4},{14,6},{1,9},{3,11}... | collective-permute-start | bytes 98312 | tf_op jit(solution)/shard_map/ppermute | solution.py:123
  25.7 8.7 %collective-permute-start.4 = (bf16[256,512]{1,0:T(8,128)(2,1)S(1)}, bf16[256,512]{1,0:T(8,128)(2,1)S(1)}, u32[]{:S(2)}, u32[]{:S(2)}) collective-permute-start(bf16[256,512]{1,0:T(8,128)(2,1)S(1)} %get-tuple-element.16), channel_id=1, source_target_pairs={{0,4},{2,6},{4,0},{6,2},{8,12},{10,14},{12,8},{14,10},{1,5},{3,7},... | collective-permute-start | bytes 786440 | tf_op jit(solution)/shard_map/ppermute | solution.py:123
  27.3 7.6 %collective-permute-start.1 = (bf16[256,512]{1,0:T(8,128)(2,1)S(1)}, bf16[256,512]{1,0:T(8,128)(2,1)S(1)}, u32[]{:S(2)}, u32[]{:S(2)}) collective-permute-start(bf16[256,512]{1,0:T(8,128)(2,1)S(1)} %get-tuple-element.14), channel_id=1, source_target_pairs={{0,2},{2,0},{4,6},{6,4},{8,10},{10,8},{12,14},{14,12},{1,3},{3,1},... | collective-permute-start | bytes 786440 | tf_op jit(solution)/shard_map/ppermute | solution.py:123
  28.5 8.4 %collective-permute-start.8 = (bf16[128,512]{1,0:T(8,128)(2,1)S(1)}, bf16[128,512]{1,0:T(8,128)(2,1)S(1)}, u32[]{:S(2)}, u32[]{:S(2)}) collective-permute-start(bf16[128,512]{1,0:T(8,128)(2,1)S(1)} %add_convert_fusion), channel_id=1, source_target_pairs={{0,4},{2,6},{4,0},{6,2},{8,12},{10,14},{12,8},{14,10},{1,5},{3,7},... | collective-permute-start | bytes 393224 | tf_op jit(solution)/shard_map/ppermute | solution.py:123
  34.4 5.0 %collective-permute-start.5 = (bf16[128,512]{1,0:T(8,128)(2,1)S(1)}, bf16[128,512]{1,0:T(8,128)(2,1)S(1)}, u32[]{:S(2)}, u32[]{:S(2)}) collective-permute-start(bf16[128,512]{1,0:T(8,128)(2,1)S(1)} %add_convert_fusion.1), channel_id=1, source_target_pairs={{0,2},{2,0},{4,6},{6,4},{8,10},{10,8},{12,14},{14,12},{1,3},{3,1},... | collective-permute-start | bytes 393224 | tf_op jit(solution)/shard_map/ppermute | solution.py:123
  34.9 5.7 %collective-permute-start.2 = (bf16[128,512]{1,0:T(8,128)(2,1)S(1)}, bf16[128,512]{1,0:T(8,128)(2,1)S(1)}, u32[]{:S(2)}, u32[]{:S(2)}) collective-permute-start(bf16[128,512]{1,0:T(8,128)(2,1)S(1)} %add_convert_fusion.2), channel_id=1, source_target_pairs={{0,4},{2,6},{4,0},{6,2},{8,12},{10,14},{12,8},{14,10},{1,5},{3,7},... | collective-permute-start | bytes 393224 | tf_op jit(solution)/shard_map/ppermute | solution.py:123
  37.0 7.0 %collective-permute-start.9 = (bf16[64,512]{1,0:T(8,128)(2,1)S(1)}, bf16[64,512]{1,0:T(8,128)(2,1)S(1)}, u32[]{:S(2)}, u32[]{:S(2)}) collective-permute-start(bf16[64,512]{1,0:T(8,128)(2,1)S(1)} %slice.140), channel_id=1, source_target_pairs={{0,8},{2,10},{4,12},{6,14},{8,0},{10,2},{12,4},{14,6},{1,9},{3,11}... | collective-permute-start | bytes 196616 | tf_op jit(solution)/shard_map/ppermute | solution.py:123
  39.5 5.2 %collective-permute-start.6 = (bf16[64,512]{1,0:T(8,128)(2,1)S(1)}, bf16[64,512]{1,0:T(8,128)(2,1)S(1)}, u32[]{:S(2)}, u32[]{:S(2)}) collective-permute-start(bf16[64,512]{1,0:T(8,128)(2,1)S(1)} %slice.141), channel_id=1, source_target_pairs={{0,8},{2,10},{4,12},{6,14},{8,0},{10,2},{12,4},{14,6},{1,9},{3,11}... | collective-permute-start | bytes 196616 | tf_op jit(solution)/shard_map/ppermute | solution.py:123
  40.6 6.7 %collective-permute-start.3 = (bf16[64,512]{1,0:T(8,128)(2,1)S(1)}, bf16[64,512]{1,0:T(8,128)(2,1)S(1)}, u32[]{:S(2)}, u32[]{:S(2)}) collective-permute-start(bf16[64,512]{1,0:T(8,128)(2,1)S(1)} %slice.142), channel_id=1, source_target_pairs={{0,8},{2,10},{4,12},{6,14},{8,0},{10,2},{12,4},{14,6},{1,9},{3,11}... | collective-permute-start | bytes 196616 | tf_op jit(solution)/shard_map/ppermute | solution.py:123

commit v3 on v0

v3 whole, which is shorter than its diff:
```python
import functools

import jax
import jax.numpy as jnp
from jax import lax
from jax.experimental import pallas as pl
from jax.experimental.pallas import tpu as pltpu
from jax.sharding import PartitionSpec as P

TILE = 256
VMEM_LIMIT = 32 * 1024 * 1024
PLAN = [(2, (0, 1, 2)), (1.5, (2, 0, 1)), (2, (1, 0, 2)), (1.5, (0, 1, 2))]


def ranked(bits, fixed=0):
    out = [fixed]
    for b in reversed(bits):
        out = [c | (1 << b) for c in out] + out
    return out


def split_columns(cols):
    unit = 128
    total = sum(share for share, _ in PLAN)
    ends, done = [], 0
    for share, _ in PLAN[:-1]:
        done += share
        ends.append(int(round(cols * done / total / unit)) * unit)
    ends.append(cols)
    return list(zip([0] + ends[:-1], ends))


def halves(bits):
    keep = ranked(bits[1:])
    return keep, [c | (1 << bits[0]) for c in keep]


def dot_into(out, prod, eig, classes, at, width):
    block = prod.shape[0] // 8
    rows = jnp.concatenate([prod[c * block : (c + 1) * block, :] for c in classes], axis=0)
    for col in range(0, width, TILE):
        size = min(TILE, width - col)
        out[:, col : col + size] = lax.dot_general(
            rows,
            eig[at + col : at + col + size, :],
            (((1,), (1,)), ((), ())),
            preferred_element_type=jnp.float32,
        ).astype(out.dtype)


def send_kernel(n, per_chunk, spans, order_hbm, own_hbm, lanc_hbm, other_ref, eig_hbm, *rest):
    count = len(spans)
    outs, (prod, eig) = rest[:count], rest[count : count + 2]
    order, own, lanc16, held, small_sem, eig_sem = rest[count + 2 :]
    small = [
        pltpu.make_async_copy(src, dst, small_sem.at[i])
        for i, (src, dst) in enumerate(
            [(order_hbm, order), (own_hbm, own), (lanc_hbm, lanc16)]
        )
    ]
    for copy in small:
        copy.start()
    loads = []
    for i, (at, end) in enumerate(spans):
        part = pl.ds(at, end - at)
        loads.append(pltpu.make_async_copy(eig_hbm.at[part], eig.at[part], eig_sem.at[i]))
        loads[-1].start()
    me = lax.axis_index("grid")
    core = lax.axis_index("eig")
    half = own.shape[0]
    held[half:, :] = other_ref[...].astype(jnp.float32)
    for copy in small:
        copy.wait()
    held[:half, :] = own[...].astype(jnp.float32)
    lanc = lanc16[...].astype(jnp.float32)
    rest_bits = list(range(3, n.bit_length() - 1))

    def row_group(r, j):
        band = order[(me ^ r) * per_chunk + j]
        band = lax.rem(band + core * half, 2 * half)
        return held[pl.ds(band, 1), :] * lanc

    block = prod.shape[0] // 8
    step = 2 * lanc.shape[0]

    def make_class(c):
        slots = [(r, j) for r in ranked(rest_bits, c) for j in range(per_chunk)]
        for i in range(0, len(slots), 2):
            pair = jnp.concatenate([row_group(*slots[i]), row_group(*slots[i + 1])], axis=0)
            first = c * block + i // 2 * step
            prod[first : first + step, :] = pair.astype(jnp.bfloat16)

    made = set()
    for i, (at, end) in enumerate(spans):
        leave = halves(PLAN[i][1])[1]
        for c in leave:
            if c not in made:
                make_class(c)
                made.add(c)
        loads[i].wait()
        dot_into(outs[i], prod, eig, leave, at, end - at)
    for c in set(range(8)) - made:
        make_class(c)


def keep_kernel(classes, at, width, prod, eig, out):
    dot_into(out, prod, eig, classes, at, width)


VMEM_SPEC = pl.BlockSpec(memory_space=pltpu.VMEM)
PARAMS = pltpu.CompilerParams(vmem_limit_bytes=VMEM_LIMIT)


def cost(rows, cols, depth):
    return pl.CostEstimate(
        flops=2 * rows * cols * depth,
        bytes_accessed=2 * depth * (cols + rows) + 4 * rows * cols,
        transcendentals=0,
    )


def send_half(n, spans, order, own, lanczos, other, eigvecs):
    lanc = lanczos.shape[0]
    cols, depth = eigvecs.shape
    rows = order.shape[0] * lanc
    hbm = pl.BlockSpec(memory_space=pltpu.HBM)
    order, own, lanczos, eigvecs = (
        pltpu.with_memory_space_constraint(x, pltpu.HBM) for x in (order, own, lanczos, eigvecs)
    )
    shapes = [jax.ShapeDtypeStruct((rows // 2, end - at), jnp.bfloat16) for at, end in spans]
    shapes.append(jax.ShapeDtypeStruct((rows, depth), jnp.bfloat16))
    shapes.append(jax.ShapeDtypeStruct((cols, depth), jnp.bfloat16))
    return pl.pallas_call(
        functools.partial(send_kernel, n, order.shape[0] // n, spans),
        out_shape=shapes,
        in_specs=[hbm, hbm, hbm, VMEM_SPEC, hbm],
        out_specs=[VMEM_SPEC] * len(shapes),
        scratch_shapes=[
            pltpu.SMEM(order.shape, jnp.int32),
            pltpu.VMEM(own.shape, jnp.bfloat16),
            pltpu.VMEM(lanczos.shape, jnp.bfloat16),
            pltpu.VMEM((2 * own.shape[0], depth), jnp.float32),
            pltpu.SemaphoreType.DMA((3,)),
            pltpu.SemaphoreType.DMA((len(spans),)),
        ],
        compiler_params=PARAMS,
        cost_estimate=cost(rows // 2, cols, depth),
    )(order, own, lanczos, other, eigvecs)


def keep_half(classes, span, prod, eig):
    at, end = span
    rows, depth = prod.shape
    return pl.pallas_call(
        functools.partial(keep_kernel, classes, at, end - at),
        out_shape=jax.ShapeDtypeStruct((rows // 2, end - at), jnp.float32),
        in_specs=[VMEM_SPEC, VMEM_SPEC],
        out_specs=VMEM_SPEC,
        compiler_params=PARAMS,
        cost_estimate=cost(rows // 2, end - at, depth),
    )(prod, eig)


def per_device(n, eigvecs, lanczos, bands, band_order):
    cols = eigvecs.shape[0]
    spans = split_columns(cols)

    def exchange(value, bit):
        return lax.ppermute(value, "grid", [(i, i ^ (1 << bit)) for i in range(n)])

    other = lax.ppermute(bands, "eig", [(0, 1), (1, 0)])
    *send, prod, eig = send_half(n, spans, band_order, bands, lanczos, other, eigvecs)
    got = [exchange(s, bits[0]) for s, (_, bits) in zip(send, PLAN)]
    outs = []
    for p, (_, bits) in enumerate(PLAN):
        kept = keep_half(halves(bits)[0], spans[p], prod, eig)
        value = kept + got[p].astype(jnp.float32)
        for stage, bit in enumerate(list(bits[1:]) + list(range(3, n.bit_length() - 1))):
            mid = value.shape[0] // 2
            dtype = jnp.bfloat16 if stage < 2 else jnp.float32
            came = exchange(value[:mid].astype(dtype), bit)
            value = value[mid:] + came.astype(jnp.float32)
        outs.append(value)
    result = jnp.concatenate(outs, axis=1)
    return result.reshape(band_order.shape[0] // n, lanczos.shape[0], cols)


def solution(mesh):
    in_specs = (
        P("eig", ("rep", "grid")),
        P(None, ("rep", "grid")),
        P("eig", ("rep", "grid")),
        P("rep"),
    )
    out_specs = P(("rep", "grid"), None, "eig")
    return jax.shard_map(
        functools.partial(per_device, mesh.shape["grid"]),
        mesh=mesh,
        in_specs=in_specs,
        out_specs=out_specs,
        check_vma=False,
    )
```

time: 111 us -> 42.9 us (0.39)
  waiting for transfers between devices: 83.6 us -> 13.2 us
  starting transfers between devices: 0.01 us -> 19.4 us
  between operations: 13.4 us -> 0.21 us
  matrix products: 8.88 us -> 0 us
  Pallas kernels: 0 us -> 8.73 us
  blocking collectives: 2.28 us -> 0 us
    reduce_scatter x1 -> x0, waiting for transfers between devices: 83.6 us -> none  [per_device(): lax.psum_scatter(partial_value, 'grid', scatter_dimension=0, tiled=True)]
    ppermute x0 -> x13, starting transfers between devices: none -> 19.4 us  [the longest x12 18.9 us: exchange(): return lax.ppermute(value, 'grid', [(i, i ^ 1 << bit) for i in range(n)])]
    ppermute x0 -> x13, waiting for transfers between devices: none -> 13.2 us  [the longest x12 12 us: exchange(): return lax.ppermute(value, 'grid', [(i, i ^ 1 << bit) for i in range(n)])]
    dot_general x1 -> x0, matrix products: 8.88 us -> none  [per_device(): lax.dot_general((jnp.take(all_bands, band_order, axis=0)[:, None, :].asty...]
    pallas_call x0 -> x5, Pallas kernels: none -> 8.73 us  [the longest x1 5.81 us: send_half(): pl.pallas_call(functools.partial(send_kernel, n, order.shape[0] // n, spa...]
    all_gather x1 -> x0, blocking collectives: 2.28 us -> none  [per_device(): all_bands = lax.all_gather(bands, 'eig', axis=0, tiled=True)]
  transfers between devices with their start and end apart: 1 -> 13, of which waited for: 1 -> 6; matrix products, arithmetic and copies ran while one was open for 0% -> 1% of each run, Pallas kernels for 0% -> 7%
where the time goes in v3:
time: 42.9 us; the launch traced here: 42.7 us
  starting transfers between devices  19.4 us (45%)
  waiting for transfers between devices  13.2 us (31%)
  Pallas kernels  8.73 us (20%)
  other arithmetic  1.17 us (3%)
    ppermute x12, starting transfers between devices, exchange(): return lax.ppermute(value, 'grid', [(i, i ^ 1 << bit) for i in range(n)])  18.9 us
    ppermute x12, waiting for transfers between devices, exchange(): return lax.ppermute(value, 'grid', [(i, i ^ 1 << bit) for i in range(n)])  12 us
    pallas_call x1, Pallas kernels, send_half(): pl.pallas_call(functools.partial(send_kernel, n, order.shape[0] // n, spa...  5.81 us
    pallas_call x4, Pallas kernels, keep_half(): pl.pallas_call(functools.partial(keep_kernel, classes, at, end - at), out...  2.91 us
    ppermute x1, waiting for transfers between devices, per_device(): other = lax.ppermute(bands, 'eig', [(0, 1), (1, 0)])  1.2 us
  transfers between devices with their start and end apart: 13, of which 6 were waited for; matrix products, arithmetic and copies ran while one was open for 1% of the time, Pallas kernels for 7%

profile of v3, /device:TPU:0, one launch (start us, length us, event | category | flops | bytes accessed | tf_op | source)
XLA Modules:
  0.0 42.7 jit_solution(7902990163671773827)
XLA Ops:
  0.0 0.5 %collective-permute-start = (bf16[32,2048]{1,0:T(8,128)(2,1)}, bf16[32,2048]{1,0:T(8,128)(2,1)S(1)}, u32[]{:S(2)}, u32[]{:S(2)}) collective-permute-start(bf16[32,2048]{1,0:T(8,128)(2,1)} %own_hbm.1), channel_id=1, source_target_pairs={{0,1},{1,0},{2,3},{3,2},{4,5},{5,4},{6,7},{7,6},{8,9},{9,8},{10,11... | collective-permute-start | bytes 393224 | tf_op jit(solution)/shard_map/ppermute | solution.py:171
  0.5 1.2 %collective-permute-done.other_ref = bf16[32,2048]{1,0:T(8,128)(2,1)S(1)} collective-permute-done((bf16[32,2048]{1,0:T(8,128)(2,1)}, bf16[32,2048]{1,0:T(8,128)(2,1)S(1)}, u32[]{:S(2)}, u32[]{:S(2)}) %collective-permute-start) | collective-permute-done | bytes 131104 | tf_op jit(solution)/shard_map/ppermute | solution.py:171
  1.7 5.8 %shard_map.46 = (bf16[256,512]{1,0:T(8,128)(2,1)S(1)}, bf16[256,384]{1,0:T(8,128)(2,1)S(1)}, bf16[256,512]{1,0:T(8,128)(2,1)S(1)}, bf16[256,384]{1,0:T(8,128)(2,...) custom-call(s32[64]{0:T(128)} %order_hbm.1, bf16[32,2048]{1,0:T(8,128)(2,1)} %own_hbm.1, ...), custom_call_target="tpu_custom_call" | custom-call | flops 1879048192 | bytes 10223616 | tf_op jit(solution)/shard_map/pallas_call | solution.py:133
  7.5 2.9 %collective-permute-start.10 = (bf16[256,384]{1,0:T(8,128)(2,1)S(1)}, bf16[256,384]{1,0:T(8,128)(2,1)S(1)}, u32[]{:S(2)}, u32[]{:S(2)}) collective-permute-start(bf16[256,384]{1,0:T(8,128)(2,1)S(1)} %get-tuple-element.16), channel_id=1, source_target_pairs={{0,2},{2,0},{4,6},{6,4},{8,10},{10,8},{12,14},{14,12},{1,3},{3,1},... | collective-permute-start | bytes 589832 | tf_op jit(solution)/shard_map/ppermute | solution.py:169
  10.4 1.6 %collective-permute-start.7 = (bf16[256,512]{1,0:T(8,128)(2,1)S(1)}, bf16[256,512]{1,0:T(8,128)(2,1)S(1)}, u32[]{:S(2)}, u32[]{:S(2)}) collective-permute-start(bf16[256,512]{1,0:T(8,128)(2,1)S(1)} %get-tuple-element.15), channel_id=1, source_target_pairs={{0,4},{2,6},{4,0},{6,2},{8,12},{10,14},{12,8},{14,10},{1,5},{3,7},... | collective-permute-start | bytes 786440 | tf_op jit(solution)/shard_map/ppermute | solution.py:169
  12.0 2.6 %collective-permute-start.4 = (bf16[256,384]{1,0:T(8,128)(2,1)S(1)}, bf16[256,384]{1,0:T(8,128)(2,1)S(1)}, u32[]{:S(2)}, u32[]{:S(2)}) collective-permute-start(bf16[256,384]{1,0:T(8,128)(2,1)S(1)} %get-tuple-element.14), channel_id=1, source_target_pairs={{0,8},{2,10},{4,12},{6,14},{8,0},{10,2},{12,4},{14,6},{1,9},{3,11}... | collective-permute-start | bytes 589832 | tf_op jit(solution)/shard_map/ppermute | solution.py:169
  14.6 0.5 %collective-permute-start.1 = (bf16[256,512]{1,0:T(8,128)(2,1)S(1)}, bf16[256,512]{1,0:T(8,128)(2,1)S(1)}, u32[]{:S(2)}, u32[]{:S(2)}) collective-permute-start(bf16[256,512]{1,0:T(8,128)(2,1)S(1)} %get-tuple-element.13), channel_id=1, source_target_pairs={{0,2},{2,0},{4,6},{6,4},{8,10},{10,8},{12,14},{14,12},{1,3},{3,1},... | collective-permute-start | bytes 786440 | tf_op jit(solution)/shard_map/ppermute | solution.py:169
  15.1 0.7 %shard_map.50 = f32[256,384]{1,0:T(8,128)S(1)} custom-call(bf16[512,2048]{1,0:T(8,128)(2,1)S(1)} %get-tuple-element.11.prod, bf16[1792,2048]{1,0:T(8,128)(2,1)S(1)} %get-tuple-element.12.eig), custom_call_target="tpu_custom_call" | custom-call | flops 402653184 | bytes 3014656 | tf_op jit(solution)/shard_map/pallas_call | solution.py:154
  15.8 0.7 %shard_map.48 = f32[256,384]{1,0:T(8,128)S(1)} custom-call(bf16[512,2048]{1,0:T(8,128)(2,1)S(1)} %get-tuple-element.11.prod, bf16[1792,2048]{1,0:T(8,128)(2,1)S(1)} %get-tuple-element.12.eig), custom_call_target="tpu_custom_call" | custom-call | flops 402653184 | bytes 3014656 | tf_op jit(solution)/shard_map/pallas_call | solution.py:154
  16.5 0.7 %shard_map.49 = f32[256,512]{1,0:T(8,128)S(1)} custom-call(bf16[512,2048]{1,0:T(8,128)(2,1)S(1)} %get-tuple-element.11.prod, bf16[1792,2048]{1,0:T(8,128)(2,1)S(1)} %get-tuple-element.12.eig), custom_call_target="tpu_custom_call" | custom-call | flops 536870912 | bytes 3670016 | tf_op jit(solution)/shard_map/pallas_call | solution.py:154
  17.3 0.7 %shard_map.47 = f32[256,512]{1,0:T(8,128)S(1)} custom-call(bf16[512,2048]{1,0:T(8,128)(2,1)S(1)} %get-tuple-element.11.prod, bf16[1792,2048]{1,0:T(8,128)(2,1)S(1)} %get-tuple-element.12.eig), custom_call_target="tpu_custom_call" | custom-call | flops 536870912 | bytes 3670016 | tf_op jit(solution)/shard_map/pallas_call | solution.py:154
  18.1 0.5 %collective-permute-start.11 = (bf16[128,384]{1,0:T(8,128)(2,1)S(1)}, bf16[128,384]{1,0:T(8,128)(2,1)S(1)}, u32[]{:S(2)}, u32[]{:S(2)}) collective-permute-start(bf16[128,384]{1,0:T(8,128)(2,1)S(1)} %slice.106), channel_id=1, source_target_pairs={{0,4},{2,6},{4,0},{6,2},{8,12},{10,14},{12,8},{14,10},{1,5},{3,7},... | collective-permute-start | bytes 294920 | tf_op jit(solution)/shard_map/ppermute | solution.py:169
  18.6 4.2 %collective-permute-done.4 = bf16[256,384]{1,0:T(8,128)(2,1)S(1)} collective-permute-done((bf16[256,384]{1,0:T(8,128)(2,1)S(1)}, bf16[256,384]{1,0:T(8,128)(2,1)S(1)}, u32[]{:S(2)}, u32[]{:S(2)}) %collective-permute-start.4) | collective-permute-done | bytes 196640 | tf_op jit(solution)/shard_map/ppermute | solution.py:169
  22.9 0.6 %collective-permute-start.5 = (bf16[128,384]{1,0:T(8,128)(2,1)S(1)}, bf16[128,384]{1,0:T(8,128)(2,1)S(1)}, u32[]{:S(2)}, u32[]{:S(2)}) collective-permute-start(bf16[128,384]{1,0:T(8,128)(2,1)S(1)} %slice.107), channel_id=1, source_target_pairs={{0,2},{2,0},{4,6},{6,4},{8,10},{10,8},{12,14},{14,12},{1,3},{3,1},... | collective-permute-start | bytes 294920 | tf_op jit(solution)/shard_map/ppermute | solution.py:169
  23.5 0.2 collective-permute-done.7
  23.8 1.3 %collective-permute-start.8 = (bf16[128,512]{1,0:T(8,128)(2,1)S(1)}, bf16[128,512]{1,0:T(8,128)(2,1)S(1)}, u32[]{:S(2)}, u32[]{:S(2)}) collective-permute-start(bf16[128,512]{1,0:T(8,128)(2,1)S(1)} %slice.104), channel_id=1, source_target_pairs={{0,2},{2,0},{4,6},{6,4},{8,10},{10,8},{12,14},{14,12},{1,3},{3,1},... | collective-permute-start | bytes 393224 | tf_op jit(solution)/shard_map/ppermute | solution.py:169
  25.3 3.5 %collective-permute-start.2 = (bf16[128,512]{1,0:T(8,128)(2,1)S(1)}, bf16[128,512]{1,0:T(8,128)(2,1)S(1)}, u32[]{:S(2)}, u32[]{:S(2)}) collective-permute-start(bf16[128,512]{1,0:T(8,128)(2,1)S(1)} %slice.105), channel_id=1, source_target_pairs={{0,4},{2,6},{4,0},{6,2},{8,12},{10,14},{12,8},{14,10},{1,5},{3,7},... | collective-permute-start | bytes 393224 | tf_op jit(solution)/shard_map/ppermute | solution.py:169
  29.0 2.2 %collective-permute-start.6 = (bf16[64,384]{1,0:T(8,128)(2,1)S(1)}, bf16[64,384]{1,0:T(8,128)(2,1)S(1)}, u32[]{:S(2)}, u32[]{:S(2)}) collective-permute-start(bf16[64,384]{1,0:T(8,128)(2,1)S(1)} %slice.111), channel_id=1, source_target_pairs={{0,4},{2,6},{4,0},{6,2},{8,12},{10,14},{12,8},{14,10},{1,5},{3,7},... | collective-permute-start | bytes 147464 | tf_op jit(solution)/shard_map/ppermute | solution.py:169
  31.2 3.1 %collective-permute-done.12 = bf16[64,384]{1,0:T(8,128)(2,1)S(1)} collective-permute-done((bf16[64,384]{1,0:T(8,128)(2,1)S(1)}, bf16[64,384]{1,0:T(8,128)(2,1)S(1)}, u32[]{:S(2)}, u32[]{:S(2)}) %collective-permute-start.12) | collective-permute-done | bytes 49184 | tf_op jit(solution)/shard_map/ppermute | solution.py:169
  34.4 2.0 %collective-permute-start.9 = (bf16[64,512]{1,0:T(8,128)(2,1)S(1)}, bf16[64,512]{1,0:T(8,128)(2,1)S(1)}, u32[]{:S(2)}, u32[]{:S(2)}) collective-permute-start(bf16[64,512]{1,0:T(8,128)(2,1)S(1)} %slice.108), channel_id=1, source_target_pairs={{0,8},{2,10},{4,12},{6,14},{8,0},{10,2},{12,4},{14,6},{1,9},{3,11}... | collective-permute-start | bytes 196616 | tf_op jit(solution)/shard_map/ppermute | solution.py:169
  36.5 1.0 %collective-permute-start.3 = (bf16[64,512]{1,0:T(8,128)(2,1)S(1)}, bf16[64,512]{1,0:T(8,128)(2,1)S(1)}, u32[]{:S(2)}, u32[]{:S(2)}) collective-permute-start(bf16[64,512]{1,0:T(8,128)(2,1)S(1)} %slice.109), channel_id=1, source_target_pairs={{0,8},{2,10},{4,12},{6,14},{8,0},{10,2},{12,4},{14,6},{1,9},{3,11}... | collective-permute-start | bytes 196616 | tf_op jit(solution)/shard_map/ppermute | solution.py:169
  37.5 2.1 %collective-permute-done.9 = bf16[64,512]{1,0:T(8,128)(2,1)S(1)} collective-permute-done((bf16[64,512]{1,0:T(8,128)(2,1)S(1)}, bf16[64,512]{1,0:T(8,128)(2,1)S(1)}, u32[]{:S(2)}, u32[]{:S(2)}) %collective-permute-start.9) | collective-permute-done | bytes 65568 | tf_op jit(solution)/shard_map/ppermute | solution.py:169
  39.6 2.3 %collective-permute-done.3 = bf16[64,512]{1,0:T(8,128)(2,1)S(1)} collective-permute-done((bf16[64,512]{1,0:T(8,128)(2,1)S(1)}, bf16[64,512]{1,0:T(8,128)(2,1)S(1)}, u32[]{:S(2)}, u32[]{:S(2)}) %collective-permute-start.3) | collective-permute-done | bytes 65568 | tf_op jit(solution)/shard_map/ppermute | solution.py:169
  41.9 0.8 %maximum_bitcast_fusion = f32[8,8,1792]{2,1,0:T(8,128)} fusion(f32[64,384]{1,0:T(8,128)S(1)} %slice_add_fusion.6, f32[64,512]{1,0:T(8,128)S(1)} %slice_add_fusion.4, f32[64,384]{1,0:T(8,128)S(1)} %slice_add_fusion.7, f32[64,512]{1,0:T(8,128)S(1)} %slice_add_fusion.5), kind=kLoop, calls=%fused_computation.2 | loop fusion | flops 344064 | bytes 917504 | tf_op jit(solution)/shard_map/reshape | solution.py:185
  (28 shorter events, 0.6 us)
Async XLA Ops:
  0.0 1.6 %collective-permute-start = (bf16[32,2048]{1,0:T(8,128)(2,1)}, bf16[32,2048]{1,0:T(8,128)(2,1)S(1)}, u32[]{:S(2)}, u32[]{:S(2)}) collective-permute-start(bf16[32,2048]{1,0:T(8,128)(2,1)} %own_hbm.1), channel_id=1, source_target_pairs={{0,1},{1,0},{2,3},{3,2},{4,5},{5,4},{6,7},{7,6},{8,9},{9,8},{10,11... | collective-permute-start | bytes 393224 | tf_op jit(solution)/shard_map/ppermute | solution.py:171
  7.5 10.6 %collective-permute-start.10 = (bf16[256,384]{1,0:T(8,128)(2,1)S(1)}, bf16[256,384]{1,0:T(8,128)(2,1)S(1)}, u32[]{:S(2)}, u32[]{:S(2)}) collective-permute-start(bf16[256,384]{1,0:T(8,128)(2,1)S(1)} %get-tuple-element.16), channel_id=1, source_target_pairs={{0,2},{2,0},{4,6},{6,4},{8,10},{10,8},{12,14},{14,12},{1,3},{3,1},... | collective-permute-start | bytes 589832 | tf_op jit(solution)/shard_map/ppermute | solution.py:169
  10.4 13.3 %collective-permute-start.7 = (bf16[256,512]{1,0:T(8,128)(2,1)S(1)}, bf16[256,512]{1,0:T(8,128)(2,1)S(1)}, u32[]{:S(2)}, u32[]{:S(2)}) collective-permute-start(bf16[256,512]{1,0:T(8,128)(2,1)S(1)} %get-tuple-element.15), channel_id=1, source_target_pairs={{0,4},{2,6},{4,0},{6,2},{8,12},{10,14},{12,8},{14,10},{1,5},{3,7},... | collective-permute-start | bytes 786440 | tf_op jit(solution)/shard_map/ppermute | solution.py:169
  12.0 10.9 %collective-permute-start.4 = (bf16[256,384]{1,0:T(8,128)(2,1)S(1)}, bf16[256,384]{1,0:T(8,128)(2,1)S(1)}, u32[]{:S(2)}, u32[]{:S(2)}) collective-permute-start(bf16[256,384]{1,0:T(8,128)(2,1)S(1)} %get-tuple-element.14), channel_id=1, source_target_pairs={{0,8},{2,10},{4,12},{6,14},{8,0},{10,2},{12,4},{14,6},{1,9},{3,11}... | collective-permute-start | bytes 589832 | tf_op jit(solution)/shard_map/ppermute | solution.py:169
  14.6 10.6 %collective-permute-start.1 = (bf16[256,512]{1,0:T(8,128)(2,1)S(1)}, bf16[256,512]{1,0:T(8,128)(2,1)S(1)}, u32[]{:S(2)}, u32[]{:S(2)}) collective-permute-start(bf16[256,512]{1,0:T(8,128)(2,1)S(1)} %get-tuple-element.13), channel_id=1, source_target_pairs={{0,2},{2,0},{4,6},{6,4},{8,10},{10,8},{12,14},{14,12},{1,3},{3,1},... | collective-permute-start | bytes 786440 | tf_op jit(solution)/shard_map/ppermute | solution.py:169
  18.1 10.7 %collective-permute-start.11 = (bf16[128,384]{1,0:T(8,128)(2,1)S(1)}, bf16[128,384]{1,0:T(8,128)(2,1)S(1)}, u32[]{:S(2)}, u32[]{:S(2)}) collective-permute-start(bf16[128,384]{1,0:T(8,128)(2,1)S(1)} %slice.106), channel_id=1, source_target_pairs={{0,4},{2,6},{4,0},{6,2},{8,12},{10,14},{12,8},{14,10},{1,5},{3,7},... | collective-permute-start | bytes 294920 | tf_op jit(solution)/shard_map/ppermute | solution.py:169
  22.9 6.0 %collective-permute-start.5 = (bf16[128,384]{1,0:T(8,128)(2,1)S(1)}, bf16[128,384]{1,0:T(8,128)(2,1)S(1)}, u32[]{:S(2)}, u32[]{:S(2)}) collective-permute-start(bf16[128,384]{1,0:T(8,128)(2,1)S(1)} %slice.107), channel_id=1, source_target_pairs={{0,2},{2,0},{4,6},{6,4},{8,10},{10,8},{12,14},{14,12},{1,3},{3,1},... | collective-permute-start | bytes 294920 | tf_op jit(solution)/shard_map/ppermute | solution.py:169
  23.8 10.5 %collective-permute-start.8 = (bf16[128,512]{1,0:T(8,128)(2,1)S(1)}, bf16[128,512]{1,0:T(8,128)(2,1)S(1)}, u32[]{:S(2)}, u32[]{:S(2)}) collective-permute-start(bf16[128,512]{1,0:T(8,128)(2,1)S(1)} %slice.104), channel_id=1, source_target_pairs={{0,2},{2,0},{4,6},{6,4},{8,10},{10,8},{12,14},{14,12},{1,3},{3,1},... | collective-permute-start | bytes 393224 | tf_op jit(solution)/shard_map/ppermute | solution.py:169
  25.3 11.1 %collective-permute-start.2 = (bf16[128,512]{1,0:T(8,128)(2,1)S(1)}, bf16[128,512]{1,0:T(8,128)(2,1)S(1)}, u32[]{:S(2)}, u32[]{:S(2)}) collective-permute-start(bf16[128,512]{1,0:T(8,128)(2,1)S(1)} %slice.105), channel_id=1, source_target_pairs={{0,4},{2,6},{4,0},{6,2},{8,12},{10,14},{12,8},{14,10},{1,5},{3,7},... | collective-permute-start | bytes 393224 | tf_op jit(solution)/shard_map/ppermute | solution.py:169
  28.9 5.4 %collective-permute-start.12 = (bf16[64,384]{1,0:T(8,128)(2,1)S(1)}, bf16[64,384]{1,0:T(8,128)(2,1)S(1)}, u32[]{:S(2)}, u32[]{:S(2)}) collective-permute-start(bf16[64,384]{1,0:T(8,128)(2,1)S(1)} %slice.110), channel_id=1, source_target_pairs={{0,8},{2,10},{4,12},{6,14},{8,0},{10,2},{12,4},{14,6},{1,9},{3,11}... | collective-permute-start | bytes 147464 | tf_op jit(solution)/shard_map/ppermute | solution.py:169
  29.0 5.3 %collective-permute-start.6 = (bf16[64,384]{1,0:T(8,128)(2,1)S(1)}, bf16[64,384]{1,0:T(8,128)(2,1)S(1)}, u32[]{:S(2)}, u32[]{:S(2)}) collective-permute-start(bf16[64,384]{1,0:T(8,128)(2,1)S(1)} %slice.111), channel_id=1, source_target_pairs={{0,4},{2,6},{4,0},{6,2},{8,12},{10,14},{12,8},{14,10},{1,5},{3,7},... | collective-permute-start | bytes 147464 | tf_op jit(solution)/shard_map/ppermute | solution.py:169
  34.4 5.2 %collective-permute-start.9 = (bf16[64,512]{1,0:T(8,128)(2,1)S(1)}, bf16[64,512]{1,0:T(8,128)(2,1)S(1)}, u32[]{:S(2)}, u32[]{:S(2)}) collective-permute-start(bf16[64,512]{1,0:T(8,128)(2,1)S(1)} %slice.108), channel_id=1, source_target_pairs={{0,8},{2,10},{4,12},{6,14},{8,0},{10,2},{12,4},{14,6},{1,9},{3,11}... | collective-permute-start | bytes 196616 | tf_op jit(solution)/shard_map/ppermute | solution.py:169
  36.5 5.5 %collective-permute-start.3 = (bf16[64,512]{1,0:T(8,128)(2,1)S(1)}, bf16[64,512]{1,0:T(8,128)(2,1)S(1)}, u32[]{:S(2)}, u32[]{:S(2)}) collective-permute-start(bf16[64,512]{1,0:T(8,128)(2,1)S(1)} %slice.109), channel_id=1, source_target_pairs={{0,8},{2,10},{4,12},{6,14},{8,0},{10,2},{12,4},{14,6},{1,9},{3,11}... | collective-permute-start | bytes 196616 | tf_op jit(solution)/shard_map/ppermute | solution.py:169

commit v4 on v0

v4 whole, which is shorter than its diff:
```python
import functools

import jax
import jax.numpy as jnp
from jax import lax
from jax.experimental import pallas as pl
from jax.experimental.pallas import tpu as pltpu
from jax.sharding import PartitionSpec as P

TILE = 256
VMEM_LIMIT = 32 * 1024 * 1024
PLAN = [(1.5, (0, 1, 2)), (2, (1, 0, 2)), (2, (0, 1, 2)), (1.5, (0, 1, 2))]


def ranked(bits, fixed=0):
    out = [fixed]
    for b in reversed(bits):
        out = [c | (1 << b) for c in out] + out
    return out


def split_columns(cols):
    unit = 128
    total = sum(share for share, _ in PLAN)
    ends, done = [], 0
    for share, _ in PLAN[:-1]:
        done += share
        ends.append(int(round(cols * done / total / unit)) * unit)
    ends.append(cols)
    return list(zip([0] + ends[:-1], ends))


def halves(bits):
    keep = ranked(bits[1:])
    return keep, [c | (1 << bits[0]) for c in keep]


def dot_into(out, prod, eig, classes):
    block = prod.shape[0] // 8
    rows = jnp.concatenate([prod[c * block : (c + 1) * block, :] for c in classes], axis=0)
    width = eig.shape[0]
    for col in range(0, width, TILE):
        size = min(TILE, width - col)
        out[:, col : col + size] = lax.dot_general(
            rows,
            eig[col : col + size, :],
            (((1,), (1,)), ((), ())),
            preferred_element_type=jnp.float32,
        ).astype(out.dtype)


def setup_kernel(n, per_chunk, lanc, span, order_hbm, own_hbm, lanc_hbm, eig_hbm, *rest):
    pick, own, lanc16, eig, order, sem = rest
    copies = [
        pltpu.make_async_copy(src, dst, sem.at[i])
        for i, (src, dst) in enumerate(
            [
                (order_hbm, order),
                (own_hbm, own),
                (lanc_hbm, lanc16),
                (eig_hbm.at[pl.ds(span[0], span[1] - span[0])], eig),
            ]
        )
    ]
    for copy in copies:
        copy.start()
    me = lax.axis_index("grid")
    core = lax.axis_index("eig")
    bands = pick.shape[1]
    rest_bits = list(range(3, n.bit_length() - 1))
    slots = [(r, j) for c in range(8) for r in ranked(rest_bits, c) for j in range(per_chunk)]
    col = lax.broadcasted_iota(jnp.int32, (2 * lanc, bands), 1)
    upper = lax.broadcasted_iota(jnp.int32, (2 * lanc, bands), 0) < lanc
    copies[0].wait()
    for i in range(0, len(slots), 2):
        want = []
        for r, j in slots[i : i + 2]:
            band = order[(me ^ r) * per_chunk + j]
            want.append(lax.rem(band + core * (bands // 2), bands))
        hit = col == jnp.where(upper, want[0], want[1])
        pick[i * lanc : (i + 2) * lanc, :] = hit.astype(jnp.float32).astype(jnp.bfloat16)
    for copy in copies[1:]:
        copy.wait()


def first_kernel(bits, span, pick, own, other, lanc16, eig, eig_hbm, out, prod, eig_next, sem):
    load = pltpu.make_async_copy(
        eig_hbm.at[pl.ds(span[0], span[1] - span[0])], eig_next, sem.at[0]
    )
    load.start()
    half = own.shape[0]
    lanc = lanc16[...].astype(jnp.float32)
    block = prod.shape[0] // 8
    groups = block // lanc.shape[0]
    bands = jnp.concatenate([own[...], other[...]], axis=0)

    def make_classes(classes):
        for c in classes:
            chosen = lax.dot_general(
                pick[c * block : (c + 1) * block, :],
                bands,
                (((1,), (0,)), ((), ())),
                preferred_element_type=jnp.float32,
            )
            value = chosen.reshape(groups, lanc.shape[0], lanc.shape[1]) * lanc[None]
            prod[c * block : (c + 1) * block, :] = value.reshape(chosen.shape).astype(
                jnp.bfloat16
            )

    keep, leave = halves(bits)
    make_classes(leave)
    dot_into(out, prod, eig, leave)
    make_classes(keep)
    load.wait()


def send_kernel(plan, spans, prod, eig, eig_hbm, *rest):
    count = len(plan)
    outs, later, sem = rest[:count], rest[count:-1], rest[-1]
    loads = [
        pltpu.make_async_copy(eig_hbm.at[pl.ds(at, end - at)], ref, sem.at[i])
        for i, ((at, end), ref) in enumerate(zip(spans[1:], later))
    ]
    for load in loads:
        load.start()
    for i, bits in enumerate(plan):
        if i > 0:
            loads[i - 1].wait()
        dot_into(outs[i], prod, later[i - 1] if i > 0 else eig, halves(bits)[1])


def keep_kernel(classes, prod, eig, out):
    dot_into(out, prod, eig, classes)


VMEM_SPEC = pl.BlockSpec(memory_space=pltpu.VMEM)
HBM_SPEC = pl.BlockSpec(memory_space=pltpu.HBM)


def kernel_call(body, ins, outs, scratch, cost):
    flops, moved = cost
    return pl.pallas_call(
        body,
        out_shape=[jax.ShapeDtypeStruct(*out) for out in outs],
        in_specs=[HBM_SPEC if far else VMEM_SPEC for _, far in ins],
        out_specs=[VMEM_SPEC] * len(outs),
        scratch_shapes=scratch,
        compiler_params=pltpu.CompilerParams(vmem_limit_bytes=VMEM_LIMIT),
        cost_estimate=pl.CostEstimate(flops=flops, bytes_accessed=moved, transcendentals=0),
    )(
        *(
            pltpu.with_memory_space_constraint(x, pltpu.HBM) if far else x
            for x, far in ins
        )
    )


def per_device(n, eigvecs, lanczos, bands, band_order):
    cols, depth = eigvecs.shape
    lanc = lanczos.shape[0]
    per_chunk = band_order.shape[0] // n
    rows = band_order.shape[0] * lanc
    spans = split_columns(cols)
    widths = [end - at for at, end in spans]
    orders = [bits for _, bits in PLAN]
    bf16 = jnp.bfloat16

    def exchange(value, bit):
        return lax.ppermute(value, "grid", [(i, i ^ (1 << bit)) for i in range(n)])

    def flops(width):
        return rows * width * depth

    other = lax.ppermute(bands, "eig", [(0, 1), (1, 0)])
    pick, own, lanc16, eig = kernel_call(
        functools.partial(setup_kernel, n, per_chunk, lanc, spans[0]),
        [(band_order, True), (bands, True), (lanczos, True), (eigvecs, True)],
        [
            ((rows, 2 * bands.shape[0]), bf16),
            (bands.shape, bf16),
            (lanczos.shape, bf16),
            ((widths[0], depth), bf16),
        ],
        [pltpu.SMEM(band_order.shape, jnp.int32), pltpu.SemaphoreType.DMA((4,))],
        (0, 2 * widths[0] * depth),
    )
    eigs = [eig]
    send, prod, eig = kernel_call(
        functools.partial(first_kernel, orders[0], spans[1]),
        [(pick, False), (own, False), (other, False), (lanc16, False), (eig, False)]
        + [(eigvecs, True)],
        [((rows // 2, widths[0]), bf16), ((rows, depth), bf16), ((widths[1], depth), bf16)],
        [pltpu.SemaphoreType.DMA((1,))],
        (flops(widths[0]), 2 * widths[1] * depth),
    )
    eigs.append(eig)
    sends = [send]
    more = kernel_call(
        functools.partial(send_kernel, orders[1:], spans[1:]),
        [(prod, False), (eig, False), (eigvecs, True)],
        [((rows // 2, w), bf16) for w in widths[1:]] + [((w, depth), bf16) for w in widths[2:]],
        [pltpu.SemaphoreType.DMA((len(PLAN) - 2,))],
        (flops(sum(widths[1:])), 2 * sum(widths[2:]) * depth),
    )
    sends += more[: len(PLAN) - 1]
    eigs += more[len(PLAN) - 1 :]
    got = [exchange(s, bits[0]) for s, bits in zip(sends, orders)]
    outs = []
    for p, bits in enumerate(orders):
        (kept,) = kernel_call(
            functools.partial(keep_kernel, halves(bits)[0]),
            [(prod, False), (eigs[p], False)],
            [((rows // 2, widths[p]), jnp.float32)],
            [],
            (flops(widths[p]), 2 * widths[p] * depth),
        )
        value = kept + got[p].astype(jnp.float32)
        for stage, bit in enumerate(list(bits[1:]) + list(range(3, n.bit_length() - 1))):
            mid = value.shape[0] // 2
            dtype = bf16 if stage < 2 else jnp.float32
            came = exchange(value[:mid].astype(dtype), bit)
            value = value[mid:] + came.astype(jnp.float32)
        outs.append(value)
    result = jnp.concatenate(outs, axis=1)
    return result.reshape(per_chunk, lanc, cols)


def solution(mesh):
    in_specs = (
        P("eig", ("rep", "grid")),
        P(None, ("rep", "grid")),
        P("eig", ("rep", "grid")),
        P("rep"),
    )
    out_specs = P(("rep", "grid"), None, "eig")
    return jax.shard_map(
        functools.partial(per_device, mesh.shape["grid"]),
        mesh=mesh,
        in_specs=in_specs,
        out_specs=out_specs,
        check_vma=False,
    )
```

time: 111 us -> 40.6 us (0.37)
  waiting for transfers between devices: 83.6 us -> 11.5 us
  starting transfers between devices: 0.01 us -> 18.3 us
  between operations: 13.4 us -> 0.21 us
  Pallas kernels: 0 us -> 9.19 us
  matrix products: 8.88 us -> 0 us
  blocking collectives: 2.28 us -> 0 us
    reduce_scatter x1 -> x0, waiting for transfers between devices: 83.6 us -> none  [per_device(): lax.psum_scatter(partial_value, 'grid', scatter_dimension=0, tiled=True)]
    ppermute x0 -> x13, starting transfers between devices: none -> 18.3 us  [the longest x12 17.9 us: exchange(): return lax.ppermute(value, 'grid', [(i, i ^ 1 << bit) for i in range(n)])]
    ppermute x0 -> x13, waiting for transfers between devices: none -> 11.5 us  [the longest x12 11.5 us: exchange(): return lax.ppermute(value, 'grid', [(i, i ^ 1 << bit) for i in range(n)])]
    pallas_call x0 -> x7, Pallas kernels: none -> 9.19 us  [kernel_call(): pl.pallas_call(body, out_shape=[jax.ShapeDtypeStruct(*out) for out in out...]
    dot_general x1 -> x0, matrix products: 8.88 us -> none  [per_device(): lax.dot_general((jnp.take(all_bands, band_order, axis=0)[:, None, :].asty...]
    all_gather x1 -> x0, blocking collectives: 2.28 us -> none  [per_device(): all_bands = lax.all_gather(bands, 'eig', axis=0, tiled=True)]
  transfers between devices with their start and end apart: 1 -> 13, of which waited for: 1 -> 6; matrix products, arithmetic and copies ran while one was open for 0% -> 1% of each run, Pallas kernels for 0% -> 19%
where the time goes in v4:
time: 40.6 us; the launch traced here: 40.4 us
  starting transfers between devices  18.3 us (45%)
  waiting for transfers between devices  11.5 us (28%)
  Pallas kernels  9.19 us (23%)
  other arithmetic  1.17 us (3%)
    ppermute x12, starting transfers between devices, exchange(): return lax.ppermute(value, 'grid', [(i, i ^ 1 << bit) for i in range(n)])  17.9 us
    ppermute x12, waiting for transfers between devices, exchange(): return lax.ppermute(value, 'grid', [(i, i ^ 1 << bit) for i in range(n)])  11.5 us
    pallas_call x7, Pallas kernels, kernel_call(): pl.pallas_call(body, out_shape=[jax.ShapeDtypeStruct(*out) for out in out...  9.19 us
  transfers between devices with their start and end apart: 13, of which 6 were waited for; matrix products, arithmetic and copies ran while one was open for 1% of the time, Pallas kernels for 19%

profile of v4, /device:TPU:0, one launch (start us, length us, event | category | flops | bytes accessed | tf_op | source)
XLA Modules:
  0.0 40.4 jit_solution(4658736808829609637)
XLA Ops:
  0.0 0.5 %collective-permute-start = (bf16[32,2048]{1,0:T(8,128)(2,1)}, bf16[32,2048]{1,0:T(8,128)(2,1)S(1)}, u32[]{:S(2)}, u32[]{:S(2)}) collective-permute-start(bf16[32,2048]{1,0:T(8,128)(2,1)} %own_hbm.1), channel_id=1, source_target_pairs={{0,1},{1,0},{2,3},{3,2},{4,5},{5,4},{6,7},{7,6},{8,9},{9,8},{10,11... | collective-permute-start | bytes 393224 | tf_op jit(solution)/shard_map/ppermute | solution.py:174
  0.5 1.5 %shard_map.46 = (bf16[512,64]{1,0:T(8,128)(2,1)S(1)}, bf16[32,2048]{1,0:T(8,128)(2,1)S(1)}, bf16[8,2048]{1,0:T(8,128)(2,1)S(1)}, bf16[384,2048]{1,0:T(8,128)(2,1)S(1)}) custom-call(s32[64]{0:T(128)} %order_hbm.1, bf16[32,2048]{1,0:T(8,128)(2,1)} %own_hbm.1, bf16[8,2048]{1,0:T(8,128)(2,1)} %lanc_hbm.1, bf16[1792,2048]{1,0:T(8,128)(2,1)} %eig_hbm.5), custom_call_target="tpu_custom_call" | custom-call | bytes 1572864 | tf_op jit(solution)/shard_map/pallas_call | solution.py:142
  2.0 1.7 %shard_map.47 = (bf16[256,384]{1,0:T(8,128)(2,1)S(1)}, bf16[512,2048]{1,0:T(8,128)(2,1)S(1)}, bf16[512,2048]{1,0:T(8,128)(2,1)S(1)}) custom-call(bf16[512,64]{1,0:T(8,128)(2,1)S(1)} %get-tuple-element.17.pick, bf16[32,2048]{1,0:T(8,128)(2,1)S(1)} %get-tuple-element.18.own, bf16[32,2048]{1,0:T(8,128)(2,1)S(1)} %collective-permute-done.other, ...), custom_call_target="tpu_custom_call" | custom-call | flops 402653184 | bytes 2097152 | tf_op jit(solution)/shard_map/pallas_call | solution.py:142
  3.7 2.6 %collective-permute-start.1 = (bf16[256,384]{1,0:T(8,128)(2,1)S(1)}, bf16[256,384]{1,0:T(8,128)(2,1)S(1)}, u32[]{:S(2)}, u32[]{:S(2)}) collective-permute-start(bf16[256,384]{1,0:T(8,128)(2,1)S(1)} %get-tuple-element.22), channel_id=1, source_target_pairs={{0,2},{2,0},{4,6},{6,4},{8,10},{10,8},{12,14},{14,12},{1,3},{3,1},... | collective-permute-start | bytes 589832 | tf_op jit(solution)/shard_map/ppermute | solution.py:169
  6.2 3.1 %shard_map.50 = (bf16[256,512]{1,0:T(8,128)(2,1)S(1)}, bf16[256,512]{1,0:T(8,128)(2,1)S(1)}, bf16[256,384]{1,0:T(8,128)(2,1)S(1)}, bf16[512,2048]{1,0:T(8,128)(2,1)S(1)}, bf16[384,2048]{1,0:T(8,128)(2,1)S(1)}) custom-call(bf16[512,2048]{1,0:T(8,128)(2,1)S(1)} %get-tuple-element.21.prod, bf16[512,2048]{1,0:T(8,128)(2,1)S(1)} %get-tuple-element.23.eig, ...), custom_call_target="tpu_custom_call" | custom-call | flops 1476395008 | bytes 3670016 | tf_op jit(solution)/shard_map/pallas_call | solution.py:142
  9.4 2.1 %collective-permute-start.4 = (bf16[256,512]{1,0:T(8,128)(2,1)S(1)}, bf16[256,512]{1,0:T(8,128)(2,1)S(1)}, u32[]{:S(2)}, u32[]{:S(2)}) collective-permute-start(bf16[256,512]{1,0:T(8,128)(2,1)S(1)} %get-tuple-element.24), channel_id=1, source_target_pairs={{0,4},{2,6},{4,0},{6,2},{8,12},{10,14},{12,8},{14,10},{1,5},{3,7},... | collective-permute-start | bytes 786440 | tf_op jit(solution)/shard_map/ppermute | solution.py:169
  11.5 1.5 %collective-permute-start.7 = (bf16[256,512]{1,0:T(8,128)(2,1)S(1)}, bf16[256,512]{1,0:T(8,128)(2,1)S(1)}, u32[]{:S(2)}, u32[]{:S(2)}) collective-permute-start(bf16[256,512]{1,0:T(8,128)(2,1)S(1)} %get-tuple-element.26), channel_id=1, source_target_pairs={{0,2},{2,0},{4,6},{6,4},{8,10},{10,8},{12,14},{14,12},{1,3},{3,1},... | collective-permute-start | bytes 786440 | tf_op jit(solution)/shard_map/ppermute | solution.py:169
  13.0 0.7 %shard_map.48 = f32[256,384]{1,0:T(8,128)S(1)} custom-call(bf16[512,2048]{1,0:T(8,128)(2,1)S(1)} %get-tuple-element.21.prod, bf16[384,2048]{1,0:T(8,128)(2,1)S(1)} %get-tuple-element.20.eig), custom_call_target="tpu_custom_call" | custom-call | flops 402653184 | bytes 1572864 | tf_op jit(solution)/shard_map/pallas_call | solution.py:142
  13.7 0.7 %shard_map.52 = f32[256,384]{1,0:T(8,128)S(1)} custom-call(bf16[512,2048]{1,0:T(8,128)(2,1)S(1)} %get-tuple-element.21.prod, bf16[384,2048]{1,0:T(8,128)(2,1)S(1)} %get-tuple-element.27.eig), custom_call_target="tpu_custom_call" | custom-call | flops 402653184 | bytes 1572864 | tf_op jit(solution)/shard_map/pallas_call | solution.py:142
  14.4 0.7 %shard_map.49 = f32[256,512]{1,0:T(8,128)S(1)} custom-call(bf16[512,2048]{1,0:T(8,128)(2,1)S(1)} %get-tuple-element.21.prod, bf16[512,2048]{1,0:T(8,128)(2,1)S(1)} %get-tuple-element.23.eig), custom_call_target="tpu_custom_call" | custom-call | flops 536870912 | bytes 2097152 | tf_op jit(solution)/shard_map/pallas_call | solution.py:142
  15.2 0.7 %shard_map.51 = f32[256,512]{1,0:T(8,128)S(1)} custom-call(bf16[512,2048]{1,0:T(8,128)(2,1)S(1)} %get-tuple-element.21.prod, bf16[512,2048]{1,0:T(8,128)(2,1)S(1)} %get-tuple-element.25.eig), custom_call_target="tpu_custom_call" | custom-call | flops 536870912 | bytes 2097152 | tf_op jit(solution)/shard_map/pallas_call | solution.py:142
  16.0 0.5 %collective-permute-start.2 = (bf16[128,384]{1,0:T(8,128)(2,1)S(1)}, bf16[128,384]{1,0:T(8,128)(2,1)S(1)}, u32[]{:S(2)}, u32[]{:S(2)}) collective-permute-start(bf16[128,384]{1,0:T(8,128)(2,1)S(1)} %slice.107), channel_id=1, source_target_pairs={{0,4},{2,6},{4,0},{6,2},{8,12},{10,14},{12,8},{14,10},{1,5},{3,7},... | collective-permute-start | bytes 294920 | tf_op jit(solution)/shard_map/ppermute | solution.py:169
  16.5 0.6 %collective-permute-done.10 = bf16[256,384]{1,0:T(8,128)(2,1)S(1)} collective-permute-done((bf16[256,384]{1,0:T(8,128)(2,1)S(1)}, bf16[256,384]{1,0:T(8,128)(2,1)S(1)}, u32[]{:S(2)}, u32[]{:S(2)}) %collective-permute-start.10) | collective-permute-done | bytes 196640 | tf_op jit(solution)/shard_map/ppermute | solution.py:169
  17.2 1.6 %collective-permute-start.11 = (bf16[128,384]{1,0:T(8,128)(2,1)S(1)}, bf16[128,384]{1,0:T(8,128)(2,1)S(1)}, u32[]{:S(2)}, u32[]{:S(2)}) collective-permute-start(bf16[128,384]{1,0:T(8,128)(2,1)S(1)} %slice.106), channel_id=1, source_target_pairs={{0,4},{2,6},{4,0},{6,2},{8,12},{10,14},{12,8},{14,10},{1,5},{3,7},... | collective-permute-start | bytes 294920 | tf_op jit(solution)/shard_map/ppermute | solution.py:169
  18.9 1.7 %collective-permute-start.5 = (bf16[128,512]{1,0:T(8,128)(2,1)S(1)}, bf16[128,512]{1,0:T(8,128)(2,1)S(1)}, u32[]{:S(2)}, u32[]{:S(2)}) collective-permute-start(bf16[128,512]{1,0:T(8,128)(2,1)S(1)} %slice.105), channel_id=1, source_target_pairs={{0,2},{2,0},{4,6},{6,4},{8,10},{10,8},{12,14},{14,12},{1,3},{3,1},... | collective-permute-start | bytes 393224 | tf_op jit(solution)/shard_map/ppermute | solution.py:169
  20.7 2.1 %collective-permute-done.7 = bf16[256,512]{1,0:T(8,128)(2,1)S(1)} collective-permute-done((bf16[256,512]{1,0:T(8,128)(2,1)S(1)}, bf16[256,512]{1,0:T(8,128)(2,1)S(1)}, u32[]{:S(2)}, u32[]{:S(2)}) %collective-permute-start.7) | collective-permute-done | bytes 262176 | tf_op jit(solution)/shard_map/ppermute | solution.py:169
  22.8 1.6 %collective-permute-start.8 = (bf16[128,512]{1,0:T(8,128)(2,1)S(1)}, bf16[128,512]{1,0:T(8,128)(2,1)S(1)}, u32[]{:S(2)}, u32[]{:S(2)}) collective-permute-start(bf16[128,512]{1,0:T(8,128)(2,1)S(1)} %slice.104), channel_id=1, source_target_pairs={{0,4},{2,6},{4,0},{6,2},{8,12},{10,14},{12,8},{14,10},{1,5},{3,7},... | collective-permute-start | bytes 393224 | tf_op jit(solution)/shard_map/ppermute | solution.py:169
  24.5 2.7 %collective-permute-start.3 = (bf16[64,384]{1,0:T(8,128)(2,1)S(1)}, bf16[64,384]{1,0:T(8,128)(2,1)S(1)}, u32[]{:S(2)}, u32[]{:S(2)}) collective-permute-start(bf16[64,384]{1,0:T(8,128)(2,1)S(1)} %slice.111), channel_id=1, source_target_pairs={{0,8},{2,10},{4,12},{6,14},{8,0},{10,2},{12,4},{14,6},{1,9},{3,11}... | collective-permute-start | bytes 147464 | tf_op jit(solution)/shard_map/ppermute | solution.py:169
  27.6 2.8 %collective-permute-done.3 = bf16[64,384]{1,0:T(8,128)(2,1)S(1)} collective-permute-done((bf16[64,384]{1,0:T(8,128)(2,1)S(1)}, bf16[64,384]{1,0:T(8,128)(2,1)S(1)}, u32[]{:S(2)}, u32[]{:S(2)}) %collective-permute-start.3) | collective-permute-done | bytes 49184 | tf_op jit(solution)/shard_map/ppermute | solution.py:169
  30.4 2.2 %collective-permute-done.12 = bf16[64,384]{1,0:T(8,128)(2,1)S(1)} collective-permute-done((bf16[64,384]{1,0:T(8,128)(2,1)S(1)}, bf16[64,384]{1,0:T(8,128)(2,1)S(1)}, u32[]{:S(2)}, u32[]{:S(2)}) %collective-permute-start.12) | collective-permute-done | bytes 49184 | tf_op jit(solution)/shard_map/ppermute | solution.py:169
  33.0 2.9 %collective-permute-start.9 = (bf16[64,512]{1,0:T(8,128)(2,1)S(1)}, bf16[64,512]{1,0:T(8,128)(2,1)S(1)}, u32[]{:S(2)}, u32[]{:S(2)}) collective-permute-start(bf16[64,512]{1,0:T(8,128)(2,1)S(1)} %slice.108), channel_id=1, source_target_pairs={{0,8},{2,10},{4,12},{6,14},{8,0},{10,2},{12,4},{14,6},{1,9},{3,11}... | collective-permute-start | bytes 196616 | tf_op jit(solution)/shard_map/ppermute | solution.py:169
  35.9 2.3 %collective-permute-done.6 = bf16[64,512]{1,0:T(8,128)(2,1)S(1)} collective-permute-done((bf16[64,512]{1,0:T(8,128)(2,1)S(1)}, bf16[64,512]{1,0:T(8,128)(2,1)S(1)}, u32[]{:S(2)}, u32[]{:S(2)}) %collective-permute-start.6) | collective-permute-done | bytes 65568 | tf_op jit(solution)/shard_map/ppermute | solution.py:169
  38.2 1.4 %collective-permute-done.9 = bf16[64,512]{1,0:T(8,128)(2,1)S(1)} collective-permute-done((bf16[64,512]{1,0:T(8,128)(2,1)S(1)}, bf16[64,512]{1,0:T(8,128)(2,1)S(1)}, u32[]{:S(2)}, u32[]{:S(2)}) %collective-permute-start.9) | collective-permute-done | bytes 65568 | tf_op jit(solution)/shard_map/ppermute | solution.py:169
  39.6 0.8 %maximum_bitcast_fusion = f32[8,8,1792]{2,1,0:T(8,128)} fusion(f32[64,384]{1,0:T(8,128)S(1)} %slice_add_fusion.6, f32[64,512]{1,0:T(8,128)S(1)} %slice_add_fusion.4, f32[64,512]{1,0:T(8,128)S(1)} %slice_add_fusion.5, f32[64,384]{1,0:T(8,128)S(1)} %slice_add_fusion.7), kind=kLoop, calls=%fused_computation.2 | loop fusion | flops 344064 | bytes 917504 | tf_op jit(solution)/shard_map/reshape | solution.py:225
  (30 shorter events, 1.1 us)
Async XLA Ops:
  0.0 2.0 %collective-permute-start = (bf16[32,2048]{1,0:T(8,128)(2,1)}, bf16[32,2048]{1,0:T(8,128)(2,1)S(1)}, u32[]{:S(2)}, u32[]{:S(2)}) collective-permute-start(bf16[32,2048]{1,0:T(8,128)(2,1)} %own_hbm.1), channel_id=1, source_target_pairs={{0,1},{1,0},{2,3},{3,2},{4,5},{5,4},{6,7},{7,6},{8,9},{9,8},{10,11... | collective-permute-start | bytes 393224 | tf_op jit(solution)/shard_map/ppermute | solution.py:174
  3.7 12.3 %collective-permute-start.1 = (bf16[256,384]{1,0:T(8,128)(2,1)S(1)}, bf16[256,384]{1,0:T(8,128)(2,1)S(1)}, u32[]{:S(2)}, u32[]{:S(2)}) collective-permute-start(bf16[256,384]{1,0:T(8,128)(2,1)S(1)} %get-tuple-element.22), channel_id=1, source_target_pairs={{0,2},{2,0},{4,6},{6,4},{8,10},{10,8},{12,14},{14,12},{1,3},{3,1},... | collective-permute-start | bytes 589832 | tf_op jit(solution)/shard_map/ppermute | solution.py:169
  9.3 7.8 %collective-permute-start.10 = (bf16[256,384]{1,0:T(8,128)(2,1)S(1)}, bf16[256,384]{1,0:T(8,128)(2,1)S(1)}, u32[]{:S(2)}, u32[]{:S(2)}) collective-permute-start(bf16[256,384]{1,0:T(8,128)(2,1)S(1)} %get-tuple-element.28), channel_id=1, source_target_pairs={{0,2},{2,0},{4,6},{6,4},{8,10},{10,8},{12,14},{14,12},{1,3},{3,1},... | collective-permute-start | bytes 589832 | tf_op jit(solution)/shard_map/ppermute | solution.py:169
  9.4 9.4 %collective-permute-start.4 = (bf16[256,512]{1,0:T(8,128)(2,1)S(1)}, bf16[256,512]{1,0:T(8,128)(2,1)S(1)}, u32[]{:S(2)}, u32[]{:S(2)}) collective-permute-start(bf16[256,512]{1,0:T(8,128)(2,1)S(1)} %get-tuple-element.24), channel_id=1, source_target_pairs={{0,4},{2,6},{4,0},{6,2},{8,12},{10,14},{12,8},{14,10},{1,5},{3,7},... | collective-permute-start | bytes 786440 | tf_op jit(solution)/shard_map/ppermute | solution.py:169
  11.5 11.2 %collective-permute-start.7 = (bf16[256,512]{1,0:T(8,128)(2,1)S(1)}, bf16[256,512]{1,0:T(8,128)(2,1)S(1)}, u32[]{:S(2)}, u32[]{:S(2)}) collective-permute-start(bf16[256,512]{1,0:T(8,128)(2,1)S(1)} %get-tuple-element.26), channel_id=1, source_target_pairs={{0,2},{2,0},{4,6},{6,4},{8,10},{10,8},{12,14},{14,12},{1,3},{3,1},... | collective-permute-start | bytes 786440 | tf_op jit(solution)/shard_map/ppermute | solution.py:169
  16.0 8.5 %collective-permute-start.2 = (bf16[128,384]{1,0:T(8,128)(2,1)S(1)}, bf16[128,384]{1,0:T(8,128)(2,1)S(1)}, u32[]{:S(2)}, u32[]{:S(2)}) collective-permute-start(bf16[128,384]{1,0:T(8,128)(2,1)S(1)} %slice.107), channel_id=1, source_target_pairs={{0,4},{2,6},{4,0},{6,2},{8,12},{10,14},{12,8},{14,10},{1,5},{3,7},... | collective-permute-start | bytes 294920 | tf_op jit(solution)/shard_map/ppermute | solution.py:169
  17.2 10.0 %collective-permute-start.11 = (bf16[128,384]{1,0:T(8,128)(2,1)S(1)}, bf16[128,384]{1,0:T(8,128)(2,1)S(1)}, u32[]{:S(2)}, u32[]{:S(2)}) collective-permute-start(bf16[128,384]{1,0:T(8,128)(2,1)S(1)} %slice.106), channel_id=1, source_target_pairs={{0,4},{2,6},{4,0},{6,2},{8,12},{10,14},{12,8},{14,10},{1,5},{3,7},... | collective-permute-start | bytes 294920 | tf_op jit(solution)/shard_map/ppermute | solution.py:169
  18.9 13.8 %collective-permute-start.5 = (bf16[128,512]{1,0:T(8,128)(2,1)S(1)}, bf16[128,512]{1,0:T(8,128)(2,1)S(1)}, u32[]{:S(2)}, u32[]{:S(2)}) collective-permute-start(bf16[128,512]{1,0:T(8,128)(2,1)S(1)} %slice.105), channel_id=1, source_target_pairs={{0,2},{2,0},{4,6},{6,4},{8,10},{10,8},{12,14},{14,12},{1,3},{3,1},... | collective-permute-start | bytes 393224 | tf_op jit(solution)/shard_map/ppermute | solution.py:169
  22.8 10.1 %collective-permute-start.8 = (bf16[128,512]{1,0:T(8,128)(2,1)S(1)}, bf16[128,512]{1,0:T(8,128)(2,1)S(1)}, u32[]{:S(2)}, u32[]{:S(2)}) collective-permute-start(bf16[128,512]{1,0:T(8,128)(2,1)S(1)} %slice.104), channel_id=1, source_target_pairs={{0,4},{2,6},{4,0},{6,2},{8,12},{10,14},{12,8},{14,10},{1,5},{3,7},... | collective-permute-start | bytes 393224 | tf_op jit(solution)/shard_map/ppermute | solution.py:169
  24.5 5.9 %collective-permute-start.3 = (bf16[64,384]{1,0:T(8,128)(2,1)S(1)}, bf16[64,384]{1,0:T(8,128)(2,1)S(1)}, u32[]{:S(2)}, u32[]{:S(2)}) collective-permute-start(bf16[64,384]{1,0:T(8,128)(2,1)S(1)} %slice.111), channel_id=1, source_target_pairs={{0,8},{2,10},{4,12},{6,14},{8,0},{10,2},{12,4},{14,6},{1,9},{3,11}... | collective-permute-start | bytes 147464 | tf_op jit(solution)/shard_map/ppermute | solution.py:169
  27.2 5.5 %collective-permute-start.12 = (bf16[64,384]{1,0:T(8,128)(2,1)S(1)}, bf16[64,384]{1,0:T(8,128)(2,1)S(1)}, u32[]{:S(2)}, u32[]{:S(2)}) collective-permute-start(bf16[64,384]{1,0:T(8,128)(2,1)S(1)} %slice.110), channel_id=1, source_target_pairs={{0,8},{2,10},{4,12},{6,14},{8,0},{10,2},{12,4},{14,6},{1,9},{3,11}... | collective-permute-start | bytes 147464 | tf_op jit(solution)/shard_map/ppermute | solution.py:169
  32.8 5.4 %collective-permute-start.6 = (bf16[64,512]{1,0:T(8,128)(2,1)S(1)}, bf16[64,512]{1,0:T(8,128)(2,1)S(1)}, u32[]{:S(2)}, u32[]{:S(2)}) collective-permute-start(bf16[64,512]{1,0:T(8,128)(2,1)S(1)} %slice.109), channel_id=1, source_target_pairs={{0,8},{2,10},{4,12},{6,14},{8,0},{10,2},{12,4},{14,6},{1,9},{3,11}... | collective-permute-start | bytes 196616 | tf_op jit(solution)/shard_map/ppermute | solution.py:169
  33.0 6.6 %collective-permute-start.9 = (bf16[64,512]{1,0:T(8,128)(2,1)S(1)}, bf16[64,512]{1,0:T(8,128)(2,1)S(1)}, u32[]{:S(2)}, u32[]{:S(2)}) collective-permute-start(bf16[64,512]{1,0:T(8,128)(2,1)S(1)} %slice.108), channel_id=1, source_target_pairs={{0,8},{2,10},{4,12},{6,14},{8,0},{10,2},{12,4},{14,6},{1,9},{3,11}... | collective-permute-start | bytes 196616 | tf_op jit(solution)/shard_map/ppermute | solution.py:169

commit v5 on v4

v5 whole, which is shorter than its diff:
```python
import functools

import jax
import jax.numpy as jnp
from jax import lax
from jax.experimental import pallas as pl
from jax.experimental.pallas import tpu as pltpu
from jax.sharding import PartitionSpec as P

TILE = 256
VMEM_LIMIT = 32 * 1024 * 1024
PLAN = [1.5, 2, 2, 1.5]


def split_columns(cols):
    unit = 128
    ends, done = [], 0
    for share in PLAN[:-1]:
        done += share
        ends.append(int(round(cols * done / sum(PLAN) / unit)) * unit)
    ends.append(cols)
    return list(zip([0] + ends[:-1], ends))


def dot_into(out, prod, eig, first):
    rows = prod[first : first + out.shape[0], :]
    width = eig.shape[0]
    for col in range(0, width, TILE):
        size = min(TILE, width - col)
        out[:, col : col + size] = lax.dot_general(
            rows,
            eig[col : col + size, :],
            (((1,), (1,)), ((), ())),
            preferred_element_type=jnp.float32,
        ).astype(out.dtype)


def setup_kernel(n, per_chunk, lanc, span, order_hbm, own_hbm, lanc_hbm, eig_hbm, *rest):
    pick, own, lanc16, eig, order, sem = rest
    copies = [
        pltpu.make_async_copy(src, dst, sem.at[i])
        for i, (src, dst) in enumerate(
            [
                (order_hbm, order),
                (own_hbm, own),
                (lanc_hbm, lanc16),
                (eig_hbm.at[pl.ds(span[0], span[1] - span[0])], eig),
            ]
        )
    ]
    for copy in copies:
        copy.start()
    me = lax.axis_index("grid")
    core = lax.axis_index("eig")
    bands = pick.shape[1]
    slots = [(r, j) for half in (1, 0) for r in range(half, n, 2) for j in range(per_chunk)]
    col = lax.broadcasted_iota(jnp.int32, (2 * lanc, bands), 1)
    upper = lax.broadcasted_iota(jnp.int32, (2 * lanc, bands), 0) < lanc
    copies[0].wait()
    for i in range(0, len(slots), 2):
        want = []
        for r, j in slots[i : i + 2]:
            band = order[((me & 1) ^ r) * per_chunk + j]
            want.append(lax.rem(band + core * (bands // 2), bands))
        hit = col == jnp.where(upper, want[0], want[1])
        pick[i * lanc : (i + 2) * lanc, :] = hit.astype(jnp.float32).astype(jnp.bfloat16)
    for copy in copies[1:]:
        copy.wait()


def first_kernel(span, pick, own, other, lanc16, eig, eig_hbm, out, prod, eig_next, sem):
    load = pltpu.make_async_copy(
        eig_hbm.at[pl.ds(span[0], span[1] - span[0])], eig_next, sem.at[0]
    )
    load.start()
    half = own.shape[0]
    lanc = lanc16[...].astype(jnp.float32)
    block = prod.shape[0] // 2
    groups = block // lanc.shape[0]
    bands = jnp.concatenate([own[...], other[...]], axis=0)

    def make_rows(first):
        chosen = lax.dot_general(
            pick[first : first + block, :],
            bands,
            (((1,), (0,)), ((), ())),
            preferred_element_type=jnp.float32,
        )
        value = chosen.reshape(groups, lanc.shape[0], lanc.shape[1]) * lanc[None]
        prod[first : first + block, :] = value.reshape(chosen.shape).astype(jnp.bfloat16)

    make_rows(0)
    dot_into(out, prod, eig, 0)
    make_rows(block)
    load.wait()


def send_kernel(spans, prod, eig, eig_hbm, *rest):
    count = len(spans)
    outs, later, sem = rest[:count], rest[count:-1], rest[-1]
    loads = [
        pltpu.make_async_copy(eig_hbm.at[pl.ds(at, end - at)], ref, sem.at[i])
        for i, ((at, end), ref) in enumerate(zip(spans[1:], later))
    ]
    for load in loads:
        load.start()
    for i in range(count):
        if i > 0:
            loads[i - 1].wait()
        dot_into(outs[i], prod, later[i - 1] if i > 0 else eig, 0)


def keep_kernel(prod, eig, out):
    dot_into(out, prod, eig, out.shape[0])


def finish_kernel(spans, *refs):
    came, out = refs[:-1], refs[-1]
    rows = out.shape[0]
    for (at, end), ref in zip(spans, came):
        total = ref[:rows, :].astype(jnp.float32)
        for i in range(1, ref.shape[0] // rows):
            total += ref[i * rows : (i + 1) * rows, :].astype(jnp.float32)
        out[:, at:end] = total


VMEM_SPEC = pl.BlockSpec(memory_space=pltpu.VMEM)
HBM_SPEC = pl.BlockSpec(memory_space=pltpu.HBM)


def kernel_call(body, ins, outs, scratch, cost):
    flops, moved = cost
    return pl.pallas_call(
        body,
        out_shape=[jax.ShapeDtypeStruct(*out) for out in outs],
        in_specs=[HBM_SPEC if far else VMEM_SPEC for _, far in ins],
        out_specs=[VMEM_SPEC] * len(outs),
        scratch_shapes=scratch,
        compiler_params=pltpu.CompilerParams(vmem_limit_bytes=VMEM_LIMIT),
        cost_estimate=pl.CostEstimate(flops=flops, bytes_accessed=moved, transcendentals=0),
    )(
        *(
            pltpu.with_memory_space_constraint(x, pltpu.HBM) if far else x
            for x, far in ins
        )
    )


def per_device(n, eigvecs, lanczos, bands, band_order):
    cols, depth = eigvecs.shape
    lanc = lanczos.shape[0]
    per_chunk = band_order.shape[0] // n
    rows = band_order.shape[0] * lanc
    spans = split_columns(cols)
    widths = [end - at for at, end in spans]
    lines = [list(range(first, n, 2)) for first in (0, 1)]
    bf16 = jnp.bfloat16

    def exchange(value):
        return lax.ppermute(value, "grid", [(i, i ^ 1) for i in range(n)])

    def spread(value):
        return lax.all_to_all(value, "grid", 0, 0, axis_index_groups=lines, tiled=True)

    def flops(width):
        return rows * width * depth

    other = lax.ppermute(bands, "eig", [(0, 1), (1, 0)])
    pick, own, lanc16, eig = kernel_call(
        functools.partial(setup_kernel, n, per_chunk, lanc, spans[0]),
        [(band_order, True), (bands, True), (lanczos, True), (eigvecs, True)],
        [
            ((rows, 2 * bands.shape[0]), bf16),
            (bands.shape, bf16),
            (lanczos.shape, bf16),
            ((widths[0], depth), bf16),
        ],
        [pltpu.SMEM(band_order.shape, jnp.int32), pltpu.SemaphoreType.DMA((4,))],
        (0, 2 * widths[0] * depth),
    )
    eigs = [eig]
    send, prod, eig = kernel_call(
        functools.partial(first_kernel, spans[1]),
        [(pick, False), (own, False), (other, False), (lanc16, False), (eig, False)]
        + [(eigvecs, True)],
        [((rows // 2, widths[0]), bf16), ((rows, depth), bf16), ((widths[1], depth), bf16)],
        [pltpu.SemaphoreType.DMA((1,))],
        (flops(widths[0]), 2 * widths[1] * depth),
    )
    eigs.append(eig)
    sends = [send]
    more = kernel_call(
        functools.partial(send_kernel, spans[1:]),
        [(prod, False), (eig, False), (eigvecs, True)],
        [((rows // 2, w), bf16) for w in widths[1:]] + [((w, depth), bf16) for w in widths[2:]],
        [pltpu.SemaphoreType.DMA((len(PLAN) - 2,))],
        (flops(sum(widths[1:])), 2 * sum(widths[2:]) * depth),
    )
    sends += more[: len(PLAN) - 1]
    eigs += more[len(PLAN) - 1 :]
    got = [exchange(s) for s in sends]
    came = []
    for p, width in enumerate(widths):
        (kept,) = kernel_call(
            keep_kernel,
            [(prod, False), (eigs[p], False)],
            [((rows // 2, width), jnp.float32)],
            [],
            (flops(width), 2 * width * depth),
        )
        came.append(spread((kept + got[p].astype(jnp.float32)).astype(bf16)))
    (result,) = kernel_call(
        functools.partial(finish_kernel, spans),
        [(c, False) for c in came],
        [((rows // n, cols), jnp.float32)],
        [],
        (rows * cols // 2, (rows + 4 * rows // n) * cols),
    )
    return result.reshape(per_chunk, lanc, cols)


def solution(mesh):
    in_specs = (
        P("eig", ("rep", "grid")),
        P(None, ("rep", "grid")),
        P("eig", ("rep", "grid")),
        P("rep"),
    )
    out_specs = P(("rep", "grid"), None, "eig")
    return jax.shard_map(
        functools.partial(per_device, mesh.shape["grid"]),
        mesh=mesh,
        in_specs=in_specs,
        out_specs=out_specs,
        check_vma=False,
    )
```

time: 40.6 us -> 56.7 us (1.40)
  blocking collectives: 0 us -> 10.3 us
  local copies, waits for them, and re-layouts: 0.11 us -> 4.59 us
  other arithmetic: 1.17 us -> 3.2 us
  waiting for transfers between devices: 11.5 us -> 9.97 us
  Pallas kernels: 9.19 us -> 10 us
    ppermute x12 -> x4, starting transfers between devices: 17.9 us -> 5.34 us  [exchange(): return lax.ppermute(value, 'grid', [(i, i ^ 1) for i in range(n)])]
    all_to_all x0 -> x3, starting transfers between devices: none -> 12.1 us  [spread(): lax.all_to_all(value, 'grid', 0, 0, axis_index_groups=lines, tiled=True)]
    ppermute x12 -> x4, waiting for transfers between devices: 11.5 us -> 0.98 us  [exchange(): return lax.ppermute(value, 'grid', [(i, i ^ 1) for i in range(n)])]
    all_to_all x0 -> x1, blocking collectives: none -> 10.3 us  [spread(): lax.all_to_all(value, 'grid', 0, 0, axis_index_groups=lines, tiled=True)]
    all_to_all x0 -> x3, waiting for transfers between devices: none -> 8.99 us  [spread(): lax.all_to_all(value, 'grid', 0, 0, axis_index_groups=lines, tiled=True)]
    unnamed x0 -> x12, local copies, waits for them, and re-layouts: none -> 4.59 us
    convert_element_type x0 -> x4, other arithmetic: none -> 3.2 us  [per_device(): came.append(spread((kept + got[p].astype(jnp.float32)).astype(bf16)))]
    pallas_call x7 -> x8, Pallas kernels: 9.19 us -> 10 us  [kernel_call(): pl.pallas_call(body, out_shape=[jax.ShapeDtypeStruct(*out) for out in out...]
  transfers between devices with their start and end apart: 13 -> 8, of which waited for: 6 -> 4; matrix products, arithmetic and copies ran while one was open for 1% -> 6% of each run, Pallas kernels for 19% -> 13%
where the time goes in v5:
time: 56.7 us; the launch traced here: 56.2 us
  starting transfers between devices  17.9 us (32%)
  blocking collectives  10.3 us (18%)
  Pallas kernels  10 us (18%)
  waiting for transfers between devices  9.97 us (18%)
  local copies, waits for them, and re-layouts  4.59 us (8%)
  other arithmetic  3.2 us (6%)
    all_to_all x3, starting transfers between devices, spread(): lax.all_to_all(value, 'grid', 0, 0, axis_index_groups=lines, tiled=True)  12.1 us
    all_to_all x1, blocking collectives, spread(): lax.all_to_all(value, 'grid', 0, 0, axis_index_groups=lines, tiled=True)  10.3 us
    pallas_call x8, Pallas kernels, kernel_call(): pl.pallas_call(body, out_shape=[jax.ShapeDtypeStruct(*out) for out in out...  10 us
    all_to_all x3, waiting for transfers between devices, spread(): lax.all_to_all(value, 'grid', 0, 0, axis_index_groups=lines, tiled=True)  8.99 us
    ppermute x4, starting transfers between devices, exchange(): return lax.ppermute(value, 'grid', [(i, i ^ 1) for i in range(n)])  5.34 us
    unnamed x12, local copies, waits for them, and re-layouts  4.59 us
    convert_element_type x4, other arithmetic, per_device(): came.append(spread((kept + got[p].astype(jnp.float32)).astype(bf16)))  3.2 us
  transfers between devices with their start and end apart: 8, of which 4 were waited for; matrix products, arithmetic and copies ran while one was open for 6% of the time, Pallas kernels for 13%

profile of v5, /device:TPU:0, one launch (start us, length us, event | category | flops | bytes accessed | tf_op | source)
XLA Modules:
  0.0 56.2 jit_solution(6303453580709083829)
XLA Ops:
  0.5 1.5 %shard_map.46 = (bf16[512,64]{1,0:T(8,128)(2,1)S(1)}, bf16[32,2048]{1,0:T(8,128)(2,1)S(1)}, bf16[8,2048]{1,0:T(8,128)(2,1)S(1)}, bf16[384,2048]{1,0:T(8,128)(2,1)S(1)}) custom-call(s32[64]{0:T(128)} %order_hbm.1, bf16[32,2048]{1,0:T(8,128)(2,1)} %own_hbm.1, bf16[8,2048]{1,0:T(8,128)(2,1)} %lanc_hbm.1, bf16[1792,2048]{1,0:T(8,128)(2,1)} %eig_hbm.5), custom_call_target="tpu_custom_call" | custom-call | bytes 1572864 | tf_op jit(solution)/shard_map/pallas_call | solution.py:133
  2.0 1.6 %shard_map.47 = (bf16[256,384]{1,0:T(8,128)(2,1)S(1)}, bf16[512,2048]{1,0:T(8,128)(2,1)S(1)}, bf16[512,2048]{1,0:T(8,128)(2,1)S(1)}) custom-call(bf16[512,64]{1,0:T(8,128)(2,1)S(1)} %get-tuple-element.17.pick, bf16[32,2048]{1,0:T(8,128)(2,1)S(1)} %get-tuple-element.18.own, bf16[32,2048]{1,0:T(8,128)(2,1)S(1)} %collective-permute-done.other, ...), custom_call_target="tpu_custom_call" | custom-call | flops 402653184 | bytes 2097152 | tf_op jit(solution)/shard_map/pallas_call | solution.py:133
  3.6 2.6 %collective-permute-start.1 = (bf16[256,384]{1,0:T(8,128)(2,1)S(1)}, bf16[256,384]{1,0:T(8,128)(2,1)S(1)}, u32[]{:S(2)}, u32[]{:S(2)}) collective-permute-start(bf16[256,384]{1,0:T(8,128)(2,1)S(1)} %get-tuple-element.22), channel_id=1, source_target_pairs={{0,2},{2,0},{4,6},{6,4},{8,10},{10,8},{12,14},{14,12},{1,3},{3,1},... | collective-permute-start | bytes 589832 | tf_op jit(solution)/shard_map/ppermute | solution.py:160
  6.2 3.1 %shard_map.50 = (bf16[256,512]{1,0:T(8,128)(2,1)S(1)}, bf16[256,512]{1,0:T(8,128)(2,1)S(1)}, bf16[256,384]{1,0:T(8,128)(2,1)S(1)}, bf16[512,2048]{1,0:T(8,128)(2,1)S(1)}, bf16[384,2048]{1,0:T(8,128)(2,1)S(1)}) custom-call(bf16[512,2048]{1,0:T(8,128)(2,1)S(1)} %get-tuple-element.21.prod, bf16[512,2048]{1,0:T(8,128)(2,1)S(1)} %get-tuple-element.23.eig, ...), custom_call_target="tpu_custom_call" | custom-call | flops 1476395008 | bytes 3670016 | tf_op jit(solution)/shard_map/pallas_call | solution.py:133
  9.3 0.8 %collective-permute-start.4 = (bf16[256,384]{1,0:T(8,128)(2,1)S(1)}, bf16[256,384]{1,0:T(8,128)(2,1)}, u32[]{:S(2)}, u32[]{:S(2)}) collective-permute-start(bf16[256,384]{1,0:T(8,128)(2,1)S(1)} %get-tuple-element.28), channel_id=1, source_target_pairs={{0,2},{2,0},{4,6},{6,4},{8,10},{10,8},{12,14},{14,12},{1,3},{3,1},... | collective-permute-start | bytes 589832 | tf_op jit(solution)/shard_map/ppermute | solution.py:160
  10.1 0.7 %shard_map.48 = f32[256,384]{1,0:T(8,128)S(1)} custom-call(bf16[512,2048]{1,0:T(8,128)(2,1)S(1)} %get-tuple-element.21.prod, bf16[384,2048]{1,0:T(8,128)(2,1)S(1)} %get-tuple-element.20.eig), custom_call_target="tpu_custom_call" | custom-call | flops 402653184 | bytes 1572864 | tf_op jit(solution)/shard_map/pallas_call | solution.py:133
  10.8 1.0 %collective-permute-done.1 = bf16[256,384]{1,0:T(8,128)(2,1)S(1)} collective-permute-done((bf16[256,384]{1,0:T(8,128)(2,1)S(1)}, bf16[256,384]{1,0:T(8,128)(2,1)S(1)}, u32[]{:S(2)}, u32[]{:S(2)}) %collective-permute-start.1) | collective-permute-done | bytes 196640 | tf_op jit(solution)/shard_map/ppermute | solution.py:160
  12.5 5.1 %all-to-all-start = ((bf16[4,64,384]{2,1,0:T(8,128)(2,1)}), bf16[4,64,384]{2,1,0:T(8,128)(2,1)S(1)}, u32[]{:S(2)}, u32[]{:S(2)}) async-start(bf16[4,64,384]{2,1,0:T(8,128)(2,1)} %bitcast), calls=%async_computation | async-start | bytes 393216 | tf_op jit(solution)/shard_map/all_to_all | solution.py:163
  17.6 1.8 %collective-permute-start.2 = (bf16[256,512]{1,0:T(8,128)(2,1)S(1)}, bf16[256,512]{1,0:T(8,128)(2,1)S(1)}, u32[]{:S(2)}, u32[]{:S(2)}) collective-permute-start(bf16[256,512]{1,0:T(8,128)(2,1)S(1)} %get-tuple-element.24), channel_id=1, source_target_pairs={{0,2},{2,0},{4,6},{6,4},{8,10},{10,8},{12,14},{14,12},{1,3},{3,1},... | collective-permute-start | bytes 786440 | tf_op jit(solution)/shard_map/ppermute | solution.py:160
  19.6 1.4 %copy-done.5 = bf16[384,2048]{1,0:T(8,128)(2,1)S(1)} copy-done((bf16[384,2048]{1,0:T(8,128)(2,1)S(1)}, bf16[384,2048]{1,0:T(8,128)(2,1)}, u32[]{:S(2)}) %copy-start.5) | copy-done | bytes 1572888
  21.0 0.7 %shard_map.52 = f32[256,384]{1,0:T(8,128)S(1)} custom-call(bf16[512,2048]{1,0:T(8,128)(2,1)S(1)} %get-tuple-element.21.prod, bf16[384,2048]{1,0:T(8,128)(2,1)S(1)} %copy-done.5), custom_call_target="tpu_custom_call" | custom-call | flops 402653184 | bytes 1572864 | tf_op jit(solution)/shard_map/pallas_call | solution.py:133
  21.8 1.6 %add_convert_fusion.2 = bf16[256,384]{1,0:T(8,128)(2,1)} fusion(f32[256,384]{1,0:T(8,128)S(1)} %shard_map.52, bf16[256,384]{1,0:T(8,128)(2,1)} %collective-permute-done.4), kind=kLoop, calls=%fused_computation.2 | loop fusion | flops 294912 | bytes 786432 | tf_op jit(solution)/shard_map/convert_element_type | solution.py:211
  23.4 1.5 %all-to-all-done = bf16[4,64,384]{2,1,0:T(8,128)(2,1)S(1)} async-done(((bf16[4,64,384]{2,1,0:T(8,128)(2,1)}), bf16[4,64,384]{2,1,0:T(8,128)(2,1)S(1)}, u32[]{:S(2)}, u32[]{:S(2)}) %all-to-all-start) | async-done | bytes 196640 | tf_op jit(solution)/shard_map/all_to_all | solution.py:163
  25.0 3.6 %all-to-all-start.3 = ((bf16[4,64,384]{2,1,0:T(8,128)(2,1)}), bf16[4,64,384]{2,1,0:T(8,128)(2,1)S(1)}, u32[]{:S(2)}, u32[]{:S(2)}) async-start(bf16[4,64,384]{2,1,0:T(8,128)(2,1)} %bitcast.6), calls=%async_computation.3 | async-start | bytes 393216 | tf_op jit(solution)/shard_map/all_to_all | solution.py:163
  28.5 1.6 %copy-done.1 = bf16[512,2048]{1,0:T(8,128)(2,1)S(1)} copy-done((bf16[512,2048]{1,0:T(8,128)(2,1)S(1)}, bf16[512,2048]{1,0:T(8,128)(2,1)}, u32[]{:S(2)}) %copy-start.1) | copy-done | bytes 2097176
  30.1 0.7 %shard_map.49 = f32[256,512]{1,0:T(8,128)S(1)} custom-call(bf16[512,2048]{1,0:T(8,128)(2,1)S(1)} %get-tuple-element.21.prod, bf16[512,2048]{1,0:T(8,128)(2,1)S(1)} %copy-done.1), custom_call_target="tpu_custom_call" | custom-call | flops 536870912 | bytes 2097152 | tf_op jit(solution)/shard_map/pallas_call | solution.py:133
  30.9 0.8 %add_convert_fusion.1 = bf16[256,512]{1,0:T(8,128)(2,1)} fusion(f32[256,512]{1,0:T(8,128)S(1)} %shard_map.49, bf16[256,512]{1,0:T(8,128)(2,1)S(1)} %collective-permute-done.2), kind=kLoop, calls=%fused_computation.1 | loop fusion | flops 393216 | bytes 1048576 | tf_op jit(solution)/shard_map/convert_element_type | solution.py:211
  31.6 3.1 %all-to-all-done.3 = bf16[4,64,384]{2,1,0:T(8,128)(2,1)S(1)} async-done(((bf16[4,64,384]{2,1,0:T(8,128)(2,1)}), bf16[4,64,384]{2,1,0:T(8,128)(2,1)S(1)}, u32[]{:S(2)}, u32[]{:S(2)}) %all-to-all-start.3) | async-done | bytes 196640 | tf_op jit(solution)/shard_map/all_to_all | solution.py:163
  34.8 3.4 %all-to-all-start.1 = ((bf16[4,64,512]{2,1,0:T(8,128)(2,1)}), bf16[4,64,512]{2,1,0:T(8,128)(2,1)S(1)}, u32[]{:S(2)}, u32[]{:S(2)}) async-start(bf16[4,64,512]{2,1,0:T(8,128)(2,1)} %bitcast.2), calls=%async_computation.1 | async-start | bytes 524288 | tf_op jit(solution)/shard_map/all_to_all | solution.py:163
  38.2 1.6 %copy-done.3 = bf16[512,2048]{1,0:T(8,128)(2,1)S(1)} copy-done((bf16[512,2048]{1,0:T(8,128)(2,1)S(1)}, bf16[512,2048]{1,0:T(8,128)(2,1)}, u32[]{:S(2)}) %copy-start.3) | copy-done | bytes 2097176
  39.8 0.7 %shard_map.51 = f32[256,512]{1,0:T(8,128)S(1)} custom-call(bf16[512,2048]{1,0:T(8,128)(2,1)S(1)} %get-tuple-element.21.prod, bf16[512,2048]{1,0:T(8,128)(2,1)S(1)} %copy-done.3), custom_call_target="tpu_custom_call" | custom-call | flops 536870912 | bytes 2097152 | tf_op jit(solution)/shard_map/pallas_call | solution.py:133
  40.6 4.3 %all-to-all-done.1 = bf16[4,64,512]{2,1,0:T(8,128)(2,1)S(1)} async-done(((bf16[4,64,512]{2,1,0:T(8,128)(2,1)}), bf16[4,64,512]{2,1,0:T(8,128)(2,1)S(1)}, u32[]{:S(2)}, u32[]{:S(2)}) %all-to-all-start.1) | async-done | bytes 262176 | tf_op jit(solution)/shard_map/all_to_all | solution.py:163
  44.9 10.3 %all_to_all.44 = bf16[4,64,512]{2,1,0:T(8,128)(2,1)S(1)} all-to-all(bf16[4,64,512]{2,1,0:T(8,128)(2,1)S(1)} %bitcast.13), channel_id=1, replica_groups={{0,4,8,12},{2,6,10,14},{1,5,9,13},{3,7,11,15},{16,20,24,28},{18,22,26,3..., dimensions={0} | all-to-all | bytes 524288 | tf_op jit(solution)/shard_map/all_to_all | solution.py:163
  55.3 0.9 %shard_map.53 = f32[64,1792]{1,0:T(8,128)} custom-call(bf16[256,384]{1,0:T(8,128)(2,1)S(1)} %bitcast.11, bf16[256,512]{1,0:T(8,128)(2,1)S(1)} %bitcast.9, bf16[256,512]{1,0:T(8,128)(2,1)S(1)} %bitcast.10, bf16[256,384]{1,0:T(8,128)(2,1)S(1)} %bitcast.12), custom_call_target="tpu_custom_call" | custom-call | flops 458752 | bytes 1376256 | tf_op jit(solution)/shard_map/pallas_call | solution.py:133
  (17 shorter events, 1.5 us)
Async XLA Ops:
  0.0 2.0 %collective-permute-start = (bf16[32,2048]{1,0:T(8,128)(2,1)}, bf16[32,2048]{1,0:T(8,128)(2,1)S(1)}, u32[]{:S(2)}, u32[]{:S(2)}) collective-permute-start(bf16[32,2048]{1,0:T(8,128)(2,1)} %own_hbm.1), channel_id=1, source_target_pairs={{0,1},{1,0},{2,3},{3,2},{4,5},{5,4},{6,7},{7,6},{8,9},{9,8},{10,11... | collective-permute-start | bytes 393224 | tf_op jit(solution)/shard_map/ppermute | solution.py:168
  3.6 5.7 %copy-start = (bf16[512,2048]{1,0:T(8,128)(2,1)}, bf16[512,2048]{1,0:T(8,128)(2,1)S(1)}, u32[]{:S(2)}) copy-start(bf16[512,2048]{1,0:T(8,128)(2,1)S(1)} %get-tuple-element.23.eig) | copy-start | bytes 6291460
  3.6 8.1 %collective-permute-start.1 = (bf16[256,384]{1,0:T(8,128)(2,1)S(1)}, bf16[256,384]{1,0:T(8,128)(2,1)S(1)}, u32[]{:S(2)}, u32[]{:S(2)}) collective-permute-start(bf16[256,384]{1,0:T(8,128)(2,1)S(1)} %get-tuple-element.22), channel_id=1, source_target_pairs={{0,2},{2,0},{4,6},{6,4},{8,10},{10,8},{12,14},{14,12},{1,3},{3,1},... | collective-permute-start | bytes 589832 | tf_op jit(solution)/shard_map/ppermute | solution.py:160
  9.3 3.2 %copy-start.2 = (bf16[512,2048]{1,0:T(8,128)(2,1)}, bf16[512,2048]{1,0:T(8,128)(2,1)S(1)}, u32[]{:S(2)}) copy-start(bf16[512,2048]{1,0:T(8,128)(2,1)S(1)} %get-tuple-element.25.eig) | copy-start | bytes 6291460
  9.3 3.2 %copy-start.4 = (bf16[384,2048]{1,0:T(8,128)(2,1)}, bf16[384,2048]{1,0:T(8,128)(2,1)S(1)}, u32[]{:S(2)}) copy-start(bf16[384,2048]{1,0:T(8,128)(2,1)S(1)} %get-tuple-element.27.eig) | copy-start | bytes 4718596
  9.3 12.5 %collective-permute-start.4 = (bf16[256,384]{1,0:T(8,128)(2,1)S(1)}, bf16[256,384]{1,0:T(8,128)(2,1)}, u32[]{:S(2)}, u32[]{:S(2)}) collective-permute-start(bf16[256,384]{1,0:T(8,128)(2,1)S(1)} %get-tuple-element.28), channel_id=1, source_target_pairs={{0,2},{2,0},{4,6},{6,4},{8,10},{10,8},{12,14},{14,12},{1,3},{3,1},... | collective-permute-start | bytes 589832 | tf_op jit(solution)/shard_map/ppermute | solution.py:160
  12.5 12.5 %all-to-all-start = ((bf16[4,64,384]{2,1,0:T(8,128)(2,1)}), bf16[4,64,384]{2,1,0:T(8,128)(2,1)S(1)}, u32[]{:S(2)}, u32[]{:S(2)}) async-start(bf16[4,64,384]{2,1,0:T(8,128)(2,1)} %bitcast), calls=%async_computation | async-start | bytes 393216 | tf_op jit(solution)/shard_map/all_to_all | solution.py:163
  17.6 13.3 %collective-permute-start.2 = (bf16[256,512]{1,0:T(8,128)(2,1)S(1)}, bf16[256,512]{1,0:T(8,128)(2,1)S(1)}, u32[]{:S(2)}, u32[]{:S(2)}) collective-permute-start(bf16[256,512]{1,0:T(8,128)(2,1)S(1)} %get-tuple-element.24), channel_id=1, source_target_pairs={{0,2},{2,0},{4,6},{6,4},{8,10},{10,8},{12,14},{14,12},{1,3},{3,1},... | collective-permute-start | bytes 786440 | tf_op jit(solution)/shard_map/ppermute | solution.py:160
  19.4 21.1 %collective-permute-start.3 = (bf16[256,512]{1,0:T(8,128)(2,1)S(1)}, bf16[256,512]{1,0:T(8,128)(2,1)S(1)}, u32[]{:S(2)}, u32[]{:S(2)}) collective-permute-start(bf16[256,512]{1,0:T(8,128)(2,1)S(1)} %get-tuple-element.26), channel_id=1, source_target_pairs={{0,2},{2,0},{4,6},{6,4},{8,10},{10,8},{12,14},{14,12},{1,3},{3,1},... | collective-permute-start | bytes 786440 | tf_op jit(solution)/shard_map/ppermute | solution.py:160
  19.6 1.4 %copy-start.5 = (bf16[384,2048]{1,0:T(8,128)(2,1)S(1)}, bf16[384,2048]{1,0:T(8,128)(2,1)}, u32[]{:S(2)}) copy-start(bf16[384,2048]{1,0:T(8,128)(2,1)} %copy-done.4) | copy-start | bytes 4718596
  25.0 9.8 %all-to-all-start.3 = ((bf16[4,64,384]{2,1,0:T(8,128)(2,1)}), bf16[4,64,384]{2,1,0:T(8,128)(2,1)S(1)}, u32[]{:S(2)}, u32[]{:S(2)}) async-start(bf16[4,64,384]{2,1,0:T(8,128)(2,1)} %bitcast.6), calls=%async_computation.3 | async-start | bytes 393216 | tf_op jit(solution)/shard_map/all_to_all | solution.py:163
  28.5 1.6 %copy-start.1 = (bf16[512,2048]{1,0:T(8,128)(2,1)S(1)}, bf16[512,2048]{1,0:T(8,128)(2,1)}, u32[]{:S(2)}) copy-start(bf16[512,2048]{1,0:T(8,128)(2,1)} %copy-done) | copy-start | bytes 6291460
  34.8 10.2 %all-to-all-start.1 = ((bf16[4,64,512]{2,1,0:T(8,128)(2,1)}), bf16[4,64,512]{2,1,0:T(8,128)(2,1)S(1)}, u32[]{:S(2)}, u32[]{:S(2)}) async-start(bf16[4,64,512]{2,1,0:T(8,128)(2,1)} %bitcast.2), calls=%async_computation.1 | async-start | bytes 524288 | tf_op jit(solution)/shard_map/all_to_all | solution.py:163
  38.2 1.6 %copy-start.3 = (bf16[512,2048]{1,0:T(8,128)(2,1)S(1)}, bf16[512,2048]{1,0:T(8,128)(2,1)}, u32[]{:S(2)}) copy-start(bf16[512,2048]{1,0:T(8,128)(2,1)} %copy-done.2) | copy-start | bytes 6291460

commit v6 on v4

--- a/solution.py
+++ b/solution.py
@@ -9,7 +9,8 @@
 
 TILE = 256
 VMEM_LIMIT = 32 * 1024 * 1024
-PLAN = [(1.5, (0, 1, 2)), (2, (1, 0, 2)), (2, (0, 1, 2)), (1.5, (0, 1, 2))]
+WAYS = ((1, 0, 2), (0, 2, 1))
+PLAN = [(3.5, (0, 1, 2)), (2, (1, 0, 2)), (1.5, (0, 1, 2))]
 
 
 def ranked(bits, fixed=0):
@@ -33,6 +34,10 @@
 def halves(bits):
     keep = ranked(bits[1:])
     return keep, [c | (1 << bits[0]) for c in keep]
+
+
+def grid_offset(c, core):
+    return sum(((c >> s) & 1) << bit for s, bit in enumerate(WAYS[core])) + (c >> 3 << 3)
 
 
 def dot_into(out, prod, eig, classes):
@@ -75,7 +80,8 @@
     for i in range(0, len(slots), 2):
         want = []
         for r, j in slots[i : i + 2]:
-            band = order[(me ^ r) * per_chunk + j]
+            offset = jnp.where(core == 0, grid_offset(r, 0), grid_offset(r, 1))
+            band = order[(me ^ offset) * per_chunk + j]
             want.append(lax.rem(band + core * (bands // 2), bands))
         hit = col == jnp.where(upper, want[0], want[1])
         pick[i * lanc : (i + 2) * lanc, :] = hit.astype(jnp.float32).astype(jnp.bfloat16)
@@ -133,8 +139,25 @@
     dot_into(out, prod, eig, classes)
 
 
+def add_kernel(kept, got, _, leave, keep):
+    mid = leave.shape[0]
+    leave[...] = (kept[:mid, :] + got[:mid, :].astype(jnp.float32)).astype(leave.dtype)
+    keep[...] = kept[mid:, :] + got[mid:, :].astype(jnp.float32)
+
+
+def finish_kernel(spans, *refs):
+    count = len(spans)
+    kept, came, out = refs[:count], refs[count : 2 * count], refs[-1]
+    for (at, end), a, b in zip(spans, kept, came):
+        out[:, at:end] = a[a.shape[0] - out.shape[0] :, :] + b[...].astype(jnp.float32)
+
+
 VMEM_SPEC = pl.BlockSpec(memory_space=pltpu.VMEM)
-HBM_SPEC = pl.BlockSpec(memory_space=pltpu.HBM)
+SPECS = {
+    True: pl.BlockSpec(memory_space=pltpu.HBM),
+    False: VMEM_SPEC,
+    None: pl.BlockSpec(memory_space=pl.ANY),
+}
 
 
 def kernel_call(body, ins, outs, scratch, cost):
@@ -142,7 +165,7 @@
     return pl.pallas_call(
         body,
         out_shape=[jax.ShapeDtypeStruct(*out) for out in outs],
-        in_specs=[HBM_SPEC if far else VMEM_SPEC for _, far in ins],
+        in_specs=[SPECS[far] for _, far in ins],
         out_specs=[VMEM_SPEC] * len(outs),
         scratch_shapes=scratch,
         compiler_params=pltpu.CompilerParams(vmem_limit_bytes=VMEM_LIMIT),
@@ -165,8 +188,13 @@
     orders = [bits for _, bits in PLAN]
     bf16 = jnp.bfloat16
 
-    def exchange(value, bit):
-        return lax.ppermute(value, "grid", [(i, i ^ (1 << bit)) for i in range(n)])
+    def exchange(value, stage):
+        pairs = []
+        for i in range(n):
+            for core in range(2):
+                bit = WAYS[core][stage] if stage < 3 else stage
+                pairs.append((2 * i + core, 2 * (i ^ (1 << bit)) + core))
+        return lax.ppermute(value, ("grid", "eig"), pairs)
 
     def flops(width):
         return rows * width * depth
@@ -205,23 +233,39 @@
     sends += more[: len(PLAN) - 1]
     eigs += more[len(PLAN) - 1 :]
     got = [exchange(s, bits[0]) for s, bits in zip(sends, orders)]
-    outs = []
+    value = []
     for p, bits in enumerate(orders):
-        (kept,) = kernel_call(
+        value += kernel_call(
             functools.partial(keep_kernel, halves(bits)[0]),
             [(prod, False), (eigs[p], False)],
             [((rows // 2, widths[p]), jnp.float32)],
             [],
             (flops(widths[p]), 2 * widths[p] * depth),
         )
-        value = kept + got[p].astype(jnp.float32)
-        for stage, bit in enumerate(list(bits[1:]) + list(range(3, n.bit_length() - 1))):
-            mid = value.shape[0] // 2
-            dtype = bf16 if stage < 2 else jnp.float32
-            came = exchange(value[:mid].astype(dtype), bit)
-            value = value[mid:] + came.astype(jnp.float32)
-        outs.append(value)
-    result = jnp.concatenate(outs, axis=1)
+    later = range(3, n.bit_length() - 1)
+    token = prod
+    for stage in range(1, 3 + len(later)):
+        for p, bits in enumerate(orders):
+            half = value[p].shape[0] // 2
+            size = half * widths[p]
+            leave, value[p] = kernel_call(
+                add_kernel,
+                [(value[p], False), (got[p], False), (token, None)],
+                [((half, widths[p]), bf16 if stage < 3 else jnp.float32)]
+                + [((half, widths[p]), jnp.float32)],
+                [],
+                (2 * size, 18 * size),
+            )
+            token = leave
+            got[p] = exchange(leave, (*bits, *later)[stage])
+    outs = list(zip(value, got))
+    (result,) = kernel_call(
+        functools.partial(finish_kernel, spans),
+        [(value, False) for value, _ in outs] + [(came, False) for _, came in outs],
+        [((rows // n, cols), jnp.float32)],
+        [],
+        (rows // n * cols, 12 * rows // n * cols),
+    )
     return result.reshape(per_chunk, lanc, cols)
 
 

time: 40.6 us -> 35.3 us (0.87)
  waiting for transfers between devices: 11.5 us -> 7.24 us
  Pallas kernels: 9.19 us -> 11.1 us
  starting transfers between devices: 18.3 us -> 16.7 us
  other arithmetic: 1.17 us -> 0 us
    ppermute x12 -> x9, waiting for transfers between devices: 11.5 us -> 7.24 us  [exchange(): return lax.ppermute(value, ('grid', 'eig'), pairs)]
    pallas_call x7 -> x13, Pallas kernels: 9.19 us -> 11.1 us  [kernel_call(): pl.pallas_call(body, out_shape=[jax.ShapeDtypeStruct(*out) for out in out...]
    ppermute x12 -> x9, starting transfers between devices: 17.9 us -> 16.2 us  [exchange(): return lax.ppermute(value, ('grid', 'eig'), pairs)]
    reshape x1 -> x0, other arithmetic: 0.8 us -> none  [per_device(): return result.reshape(per_chunk, lanc, cols)]
  transfers between devices with their start and end apart: 13 -> 10, of which waited for: 6 -> 3; matrix products, arithmetic and copies ran while one was open for 1% -> 0% of each run, Pallas kernels for 19% -> 21%
where the time goes in v6:
time: 35.3 us; the launch traced here: 35.1 us
  starting transfers between devices  16.7 us (47%)
  Pallas kernels  11.1 us (31%)
  waiting for transfers between devices  7.24 us (21%)
    ppermute x9, starting transfers between devices, exchange(): return lax.ppermute(value, ('grid', 'eig'), pairs)  16.2 us
    pallas_call x13, Pallas kernels, kernel_call(): pl.pallas_call(body, out_shape=[jax.ShapeDtypeStruct(*out) for out in out...  11.1 us
    ppermute x9, waiting for transfers between devices, exchange(): return lax.ppermute(value, ('grid', 'eig'), pairs)  7.24 us
  transfers between devices with their start and end apart: 10, of which 3 were waited for; matrix products, arithmetic and copies ran while one was open for 0% of the time, Pallas kernels for 21%

profile of v6, /device:TPU:0, one launch (start us, length us, event | category | flops | bytes accessed | tf_op | source)
XLA Modules:
  0.0 35.1 jit_solution(1441309417884328687)
XLA Ops:
  0.0 0.5 %collective-permute-start = (bf16[32,2048]{1,0:T(8,128)(2,1)}, bf16[32,2048]{1,0:T(8,128)(2,1)S(1)}, u32[]{:S(2)}, u32[]{:S(2)}) collective-permute-start(bf16[32,2048]{1,0:T(8,128)(2,1)} %own_hbm.1), channel_id=1, source_target_pairs={{0,1},{1,0},{2,3},{3,2},{4,5},{5,4},{6,7},{7,6},{8,9},{9,8},{10,11... | collective-permute-start | bytes 393224 | tf_op jit(solution)/shard_map/ppermute | solution.py:202
  0.5 2.2 %shard_map.46 = (bf16[512,64]{1,0:T(8,128)(2,1)S(1)}, bf16[32,2048]{1,0:T(8,128)(2,1)S(1)}, bf16[8,2048]{1,0:T(8,128)(2,1)S(1)}, bf16[896,2048]{1,0:T(8,128)(2,1)S(1)}) custom-call(s32[64]{0:T(128)} %order_hbm.1, bf16[32,2048]{1,0:T(8,128)(2,1)} %own_hbm.1, bf16[8,2048]{1,0:T(8,128)(2,1)} %lanc_hbm.1, bf16[1792,2048]{1,0:T(8,128)(2,1)} %eig_hbm.5), custom_call_target="tpu_custom_call" | custom-call | bytes 3670016 | tf_op jit(solution)/shard_map/pallas_call | solution.py:165
  2.6 3.0 %shard_map.47 = (bf16[256,896]{1,0:T(8,128)(2,1)S(1)}, bf16[512,2048]{1,0:T(8,128)(2,1)S(1)}, bf16[512,2048]{1,0:T(8,128)(2,1)S(1)}) custom-call(bf16[512,64]{1,0:T(8,128)(2,1)S(1)} %get-tuple-element.27.pick, bf16[32,2048]{1,0:T(8,128)(2,1)S(1)} %get-tuple-element.28.own, bf16[32,2048]{1,0:T(8,128)(2,1)S(1)} %collective-permute-done.other, ...), custom_call_target="tpu_custom_call" | custom-call | flops 939524096 | bytes 2097152 | tf_op jit(solution)/shard_map/pallas_call | solution.py:165
  5.6 2.6 %collective-permute-start.1 = (bf16[256,896]{1,0:T(8,128)(2,1)S(1)}, bf16[256,896]{1,0:T(8,128)(2,1)S(1)}, u32[]{:S(2)}, u32[]{:S(2)}) collective-permute-start(bf16[256,896]{1,0:T(8,128)(2,1)S(1)} %get-tuple-element.32), channel_id=1, source_target_pairs={{0,4},{1,3},{2,6},{3,1},{4,0},{5,7},{6,2},{7,5},{8,12},{9,11},{10,... | collective-permute-start | bytes 1376264 | tf_op jit(solution)/shard_map/ppermute | solution.py:197
  8.2 2.1 %shard_map.50 = (bf16[256,512]{1,0:T(8,128)(2,1)S(1)}, bf16[256,384]{1,0:T(8,128)(2,1)S(1)}, bf16[384,2048]{1,0:T(8,128)(2,1)S(1)}) custom-call(bf16[512,2048]{1,0:T(8,128)(2,1)S(1)} %get-tuple-element.31.prod._, bf16[512,2048]{1,0:T(8,128)(2,1)S(1)} %get-tuple-element.35.eig, bf16[1792,2048]{1,0:T(8,128)(2,1)} %eig_hbm.5), custom_call_target="tpu_custom_call" | custom-call | flops 939524096 | bytes 1572864 | tf_op jit(solution)/shard_map/pallas_call | solution.py:165
  10.4 1.6 %collective-permute-start.4 = (bf16[256,512]{1,0:T(8,128)(2,1)S(1)}, bf16[256,512]{1,0:T(8,128)(2,1)S(1)}, u32[]{:S(2)}, u32[]{:S(2)}) collective-permute-start(bf16[256,512]{1,0:T(8,128)(2,1)S(1)} %get-tuple-element.38), channel_id=1, source_target_pairs={{0,2},{1,9},{2,0},{3,11},{4,6},{5,13},{6,4},{7,15},{8,10},{9,1},{1... | collective-permute-start | bytes 786440 | tf_op jit(solution)/shard_map/ppermute | solution.py:197
  12.0 0.4 %collective-permute-start.3 = (bf16[256,384]{1,0:T(8,128)(2,1)S(1)}, bf16[256,384]{1,0:T(8,128)(2,1)S(1)}, u32[]{:S(2)}, u32[]{:S(2)}) collective-permute-start(bf16[256,384]{1,0:T(8,128)(2,1)S(1)} %get-tuple-element.37), channel_id=1, source_target_pairs={{0,4},{1,3},{2,6},{3,1},{4,0},{5,7},{6,2},{7,5},{8,12},{9,11},{10,... | collective-permute-start | bytes 589832 | tf_op jit(solution)/shard_map/ppermute | solution.py:197
  12.4 1.3 %shard_map.48.kept = f32[256,896]{1,0:T(8,128)S(1)} custom-call(bf16[512,2048]{1,0:T(8,128)(2,1)S(1)} %get-tuple-element.31.prod._, bf16[896,2048]{1,0:T(8,128)(2,1)S(1)} %get-tuple-element.30.eig), custom_call_target="tpu_custom_call" | custom-call | flops 939524096 | bytes 3670016 | tf_op jit(solution)/shard_map/pallas_call | solution.py:165
  13.7 2.6 %collective-permute-done.1.got = bf16[256,896]{1,0:T(8,128)(2,1)S(1)} collective-permute-done((bf16[256,896]{1,0:T(8,128)(2,1)S(1)}, bf16[256,896]{1,0:T(8,128)(2,1)S(1)}, u32[]{:S(2)}, u32[]{:S(2)}) %collective-permute-start.1) | collective-permute-done | bytes 458784 | tf_op jit(solution)/shard_map/ppermute | solution.py:197
  16.3 0.1 shard_map.49
  16.4 3.2 %collective-permute-start.2 = (bf16[128,896]{1,0:T(8,128)(2,1)S(1)}, bf16[128,896]{1,0:T(8,128)(2,1)S(1)}, u32[]{:S(2)}, u32[]{:S(2)}) collective-permute-start(bf16[128,896]{1,0:T(8,128)(2,1)S(1)} %get-tuple-element.34._), channel_id=1, source_target_pairs={{0,2},{1,9},{2,0},{3,11},{4,6},{5,13},{6,4},{7,15},{8,10},{9,1},{1... | collective-permute-start | bytes 688136 | tf_op jit(solution)/shard_map/ppermute | solution.py:197
  19.6 0.7 %shard_map.52.kept = f32[256,512]{1,0:T(8,128)S(1)} custom-call(bf16[512,2048]{1,0:T(8,128)(2,1)S(1)} %get-tuple-element.31.prod._, bf16[512,2048]{1,0:T(8,128)(2,1)S(1)} %get-tuple-element.35.eig), custom_call_target="tpu_custom_call" | custom-call | flops 536870912 | bytes 2097152 | tf_op jit(solution)/shard_map/pallas_call | solution.py:165
  20.3 0.0 collective-permute-done.4.got
  20.4 0.7 %collective-permute-start.5 = (bf16[128,512]{1,0:T(8,128)(2,1)S(1)}, bf16[128,512]{1,0:T(8,128)(2,1)S(1)}, u32[]{:S(2)}, u32[]{:S(2)}) collective-permute-start(bf16[128,512]{1,0:T(8,128)(2,1)S(1)} %get-tuple-element.39._), channel_id=1, source_target_pairs={{0,4},{1,3},{2,6},{3,1},{4,0},{5,7},{6,2},{7,5},{8,12},{9,11},{10,... | collective-permute-start | bytes 393224 | tf_op jit(solution)/shard_map/ppermute | solution.py:197
  21.1 0.7 %shard_map.51.kept = f32[256,384]{1,0:T(8,128)S(1)} custom-call(bf16[512,2048]{1,0:T(8,128)(2,1)S(1)} %get-tuple-element.31.prod._, bf16[384,2048]{1,0:T(8,128)(2,1)S(1)} %get-tuple-element.36.eig), custom_call_target="tpu_custom_call" | custom-call | flops 402653184 | bytes 1572864 | tf_op jit(solution)/shard_map/pallas_call | solution.py:165
  21.8 0.0 collective-permute-done.3.got
  21.8 2.2 %collective-permute-start.6 = (bf16[128,384]{1,0:T(8,128)(2,1)S(1)}, bf16[128,384]{1,0:T(8,128)(2,1)S(1)}, u32[]{:S(2)}, u32[]{:S(2)}) collective-permute-start(bf16[128,384]{1,0:T(8,128)(2,1)S(1)} %get-tuple-element.40._), channel_id=1, source_target_pairs={{0,2},{1,9},{2,0},{3,11},{4,6},{5,13},{6,4},{7,15},{8,10},{9,1},{1... | collective-permute-start | bytes 294920 | tf_op jit(solution)/shard_map/ppermute | solution.py:197
  24.0 1.0 %collective-permute-done.2.got = bf16[128,896]{1,0:T(8,128)(2,1)S(1)} collective-permute-done((bf16[128,896]{1,0:T(8,128)(2,1)S(1)}, bf16[128,896]{1,0:T(8,128)(2,1)S(1)}, u32[]{:S(2)}, u32[]{:S(2)}) %collective-permute-start.2) | collective-permute-done | bytes 229408 | tf_op jit(solution)/shard_map/ppermute | solution.py:197
  25.1 2.5 %collective-permute-start.7 = (bf16[64,896]{1,0:T(8,128)(2,1)S(1)}, bf16[64,896]{1,0:T(8,128)(2,1)S(1)}, u32[]{:S(2)}, u32[]{:S(2)}) collective-permute-start(bf16[64,896]{1,0:T(8,128)(2,1)S(1)} %get-tuple-element.43._), channel_id=1, source_target_pairs={{0,8},{1,5},{2,10},{3,7},{4,12},{5,1},{6,14},{7,3},{8,0},{9,13},{1... | collective-permute-start | bytes 344072 | tf_op jit(solution)/shard_map/ppermute | solution.py:197
  27.6 1.6 %collective-permute-start.8 = (bf16[64,512]{1,0:T(8,128)(2,1)S(1)}, bf16[64,512]{1,0:T(8,128)(2,1)S(1)}, u32[]{:S(2)}, u32[]{:S(2)}) collective-permute-start(bf16[64,512]{1,0:T(8,128)(2,1)S(1)} %get-tuple-element.46._), channel_id=1, source_target_pairs={{0,8},{1,5},{2,10},{3,7},{4,12},{5,1},{6,14},{7,3},{8,0},{9,13},{1... | collective-permute-start | bytes 196616 | tf_op jit(solution)/shard_map/ppermute | solution.py:197
  29.2 0.0 collective-permute-done.6.got
  29.2 1.5 %collective-permute-start.9 = (bf16[64,384]{1,0:T(8,128)(2,1)S(1)}, bf16[64,384]{1,0:T(8,128)(2,1)S(1)}, u32[]{:S(2)}, u32[]{:S(2)}) collective-permute-start(bf16[64,384]{1,0:T(8,128)(2,1)S(1)} %get-tuple-element.48), channel_id=1, source_target_pairs={{0,8},{1,5},{2,10},{3,7},{4,12},{5,1},{6,14},{7,3},{8,0},{9,13},{1... | collective-permute-start | bytes 147464 | tf_op jit(solution)/shard_map/ppermute | solution.py:197
  30.7 3.6 %collective-permute-done.9.refs_5_ = bf16[64,384]{1,0:T(8,128)(2,1)S(1)} collective-permute-done((bf16[64,384]{1,0:T(8,128)(2,1)S(1)}, bf16[64,384]{1,0:T(8,128)(2,1)S(1)}, u32[]{:S(2)}, u32[]{:S(2)}) %collective-permute-start.9) | collective-permute-done | bytes 49184 | tf_op jit(solution)/shard_map/ppermute | solution.py:197
  34.3 0.8 %shard_map.58 = f32[64,1792]{1,0:T(8,128)} custom-call(f32[64,896]{1,0:T(8,128)S(1)} %get-tuple-element.41.refs_0_, f32[64,512]{1,0:T(8,128)S(1)} %get-tuple-element.44.refs_1_, f32[64,384]{1,0:T(8,128)S(1)} %get-tuple-element.47.refs_2_, bf16[64,896]{1,0:T(8,128)(2,1)S(1)} %collective-permute-done.7.refs_3_, ...), custom_call_target="tpu_custom_call" | custom-call | flops 114688 | bytes 1376256 | tf_op jit(solution)/shard_map/pallas_call | solution.py:165
  (9 shorter events, 0.2 us)
Async XLA Ops:
  0.0 2.6 %collective-permute-start = (bf16[32,2048]{1,0:T(8,128)(2,1)}, bf16[32,2048]{1,0:T(8,128)(2,1)S(1)}, u32[]{:S(2)}, u32[]{:S(2)}) collective-permute-start(bf16[32,2048]{1,0:T(8,128)(2,1)} %own_hbm.1), channel_id=1, source_target_pairs={{0,1},{1,0},{2,3},{3,2},{4,5},{5,4},{6,7},{7,6},{8,9},{9,8},{10,11... | collective-permute-start | bytes 393224 | tf_op jit(solution)/shard_map/ppermute | solution.py:202
  5.6 10.7 %collective-permute-start.1 = (bf16[256,896]{1,0:T(8,128)(2,1)S(1)}, bf16[256,896]{1,0:T(8,128)(2,1)S(1)}, u32[]{:S(2)}, u32[]{:S(2)}) collective-permute-start(bf16[256,896]{1,0:T(8,128)(2,1)S(1)} %get-tuple-element.32), channel_id=1, source_target_pairs={{0,4},{1,3},{2,6},{3,1},{4,0},{5,7},{6,2},{7,5},{8,12},{9,11},{10,... | collective-permute-start | bytes 1376264 | tf_op jit(solution)/shard_map/ppermute | solution.py:197
  10.4 10.0 %collective-permute-start.4 = (bf16[256,512]{1,0:T(8,128)(2,1)S(1)}, bf16[256,512]{1,0:T(8,128)(2,1)S(1)}, u32[]{:S(2)}, u32[]{:S(2)}) collective-permute-start(bf16[256,512]{1,0:T(8,128)(2,1)S(1)} %get-tuple-element.38), channel_id=1, source_target_pairs={{0,2},{1,9},{2,0},{3,11},{4,6},{5,13},{6,4},{7,15},{8,10},{9,1},{1... | collective-permute-start | bytes 786440 | tf_op jit(solution)/shard_map/ppermute | solution.py:197
  12.0 9.8 %collective-permute-start.3 = (bf16[256,384]{1,0:T(8,128)(2,1)S(1)}, bf16[256,384]{1,0:T(8,128)(2,1)S(1)}, u32[]{:S(2)}, u32[]{:S(2)}) collective-permute-start(bf16[256,384]{1,0:T(8,128)(2,1)S(1)} %get-tuple-element.37), channel_id=1, source_target_pairs={{0,4},{1,3},{2,6},{3,1},{4,0},{5,7},{6,2},{7,5},{8,12},{9,11},{10,... | collective-permute-start | bytes 589832 | tf_op jit(solution)/shard_map/ppermute | solution.py:197
  16.4 8.6 %collective-permute-start.2 = (bf16[128,896]{1,0:T(8,128)(2,1)S(1)}, bf16[128,896]{1,0:T(8,128)(2,1)S(1)}, u32[]{:S(2)}, u32[]{:S(2)}) collective-permute-start(bf16[128,896]{1,0:T(8,128)(2,1)S(1)} %get-tuple-element.34._), channel_id=1, source_target_pairs={{0,2},{1,9},{2,0},{3,11},{4,6},{5,13},{6,4},{7,15},{8,10},{9,1},{1... | collective-permute-start | bytes 688136 | tf_op jit(solution)/shard_map/ppermute | solution.py:197
  20.4 7.1 %collective-permute-start.5 = (bf16[128,512]{1,0:T(8,128)(2,1)S(1)}, bf16[128,512]{1,0:T(8,128)(2,1)S(1)}, u32[]{:S(2)}, u32[]{:S(2)}) collective-permute-start(bf16[128,512]{1,0:T(8,128)(2,1)S(1)} %get-tuple-element.39._), channel_id=1, source_target_pairs={{0,4},{1,3},{2,6},{3,1},{4,0},{5,7},{6,2},{7,5},{8,12},{9,11},{10,... | collective-permute-start | bytes 393224 | tf_op jit(solution)/shard_map/ppermute | solution.py:197
  21.8 7.3 %collective-permute-start.6 = (bf16[128,384]{1,0:T(8,128)(2,1)S(1)}, bf16[128,384]{1,0:T(8,128)(2,1)S(1)}, u32[]{:S(2)}, u32[]{:S(2)}) collective-permute-start(bf16[128,384]{1,0:T(8,128)(2,1)S(1)} %get-tuple-element.40._), channel_id=1, source_target_pairs={{0,2},{1,9},{2,0},{3,11},{4,6},{5,13},{6,4},{7,15},{8,10},{9,1},{1... | collective-permute-start | bytes 294920 | tf_op jit(solution)/shard_map/ppermute | solution.py:197
  25.1 9.2 %collective-permute-start.7 = (bf16[64,896]{1,0:T(8,128)(2,1)S(1)}, bf16[64,896]{1,0:T(8,128)(2,1)S(1)}, u32[]{:S(2)}, u32[]{:S(2)}) collective-permute-start(bf16[64,896]{1,0:T(8,128)(2,1)S(1)} %get-tuple-element.43._), channel_id=1, source_target_pairs={{0,8},{1,5},{2,10},{3,7},{4,12},{5,1},{6,14},{7,3},{8,0},{9,13},{1... | collective-permute-start | bytes 344072 | tf_op jit(solution)/shard_map/ppermute | solution.py:197
  27.6 6.7 %collective-permute-start.8 = (bf16[64,512]{1,0:T(8,128)(2,1)S(1)}, bf16[64,512]{1,0:T(8,128)(2,1)S(1)}, u32[]{:S(2)}, u32[]{:S(2)}) collective-permute-start(bf16[64,512]{1,0:T(8,128)(2,1)S(1)} %get-tuple-element.46._), channel_id=1, source_target_pairs={{0,8},{1,5},{2,10},{3,7},{4,12},{5,1},{6,14},{7,3},{8,0},{9,13},{1... | collective-permute-start | bytes 196616 | tf_op jit(solution)/shard_map/ppermute | solution.py:197
  29.2 5.1 %collective-permute-start.9 = (bf16[64,384]{1,0:T(8,128)(2,1)S(1)}, bf16[64,384]{1,0:T(8,128)(2,1)S(1)}, u32[]{:S(2)}, u32[]{:S(2)}) collective-permute-start(bf16[64,384]{1,0:T(8,128)(2,1)S(1)} %get-tuple-element.48), channel_id=1, source_target_pairs={{0,8},{1,5},{2,10},{3,7},{4,12},{5,1},{6,14},{7,3},{8,0},{9,13},{1... | collective-permute-start | bytes 147464 | tf_op jit(solution)/shard_map/ppermute | solution.py:197

commit v7 on v6

--- a/solution.py
+++ b/solution.py
@@ -9,8 +9,9 @@
 
 TILE = 256
 VMEM_LIMIT = 32 * 1024 * 1024
-WAYS = ((1, 0, 2), (0, 2, 1))
-PLAN = [(3.5, (0, 1, 2)), (2, (1, 0, 2)), (1.5, (0, 1, 2))]
+WAYS = ((0, 1, 2), (1, 2, 0))
+PLAN = [(3, (0, 2, 1)), (2, (2, 0, 1)), (2, (0, 1, 2))]
+ORDER = [(piece, stage) for stage in range(3) for piece in range(len(PLAN))]
 
 
 def ranked(bits, fixed=0):
@@ -40,18 +41,55 @@
     return sum(((c >> s) & 1) << bit for s, bit in enumerate(WAYS[core])) + (c >> 3 << 3)
 
 
-def dot_into(out, prod, eig, classes):
-    block = prod.shape[0] // 8
-    rows = jnp.concatenate([prod[c * block : (c + 1) * block, :] for c in classes], axis=0)
-    width = eig.shape[0]
-    for col in range(0, width, TILE):
-        size = min(TILE, width - col)
-        out[:, col : col + size] = lax.dot_general(
-            rows,
-            eig[col : col + size, :],
-            (((1,), (1,)), ((), ())),
-            preferred_element_type=jnp.float32,
-        ).astype(out.dtype)
+def tiles_of(spans, p):
+    at, end = spans[p]
+    head = min(TILE, end - at)
+    before = end_of_rest(spans, p - 1) if p else 0
+    tiles = [(p, before, head, 0)]
+    for col in range(head, end - at, TILE):
+        tiles.append((p + 1, col - head, min(TILE, end - at - col), col))
+    return tiles
+
+
+def end_of_rest(spans, p):
+    return max(0, spans[p][1] - spans[p][0] - TILE)
+
+
+def fetched(spans, p):
+    first = spans[p][1] - end_of_rest(spans, p)
+    head = min(TILE, spans[p + 1][1] - spans[p + 1][0]) if p + 1 < len(spans) else 0
+    return first, spans[p][1] + head
+
+
+def dot_tile(out, rows, eig, tile):
+    _, first, size, col = tile
+    out[:, col : col + size] = lax.dot_general(
+        rows,
+        eig[first : first + size, :],
+        (((1,), (1,)), ((), ())),
+        preferred_element_type=jnp.float32,
+    ).astype(out.dtype)
+
+
+def classes_made(orders):
+    last = next(i for i, (_, stage) in enumerate(ORDER) if stage > 0) - 1
+    made, seen = [], []
+    for i, bits in enumerate(orders):
+        new = [c for c in halves(bits)[1] if c not in seen]
+        if i == last:
+            new += [c for c in range(8) if c not in seen + new]
+        seen += new
+        made.append(new)
+    return made
+
+
+def pick_rows(prods, made, classes, block):
+    parts = []
+    for c in classes:
+        i = next(i for i, group in enumerate(made) if c in group)
+        at = made[i].index(c) * block
+        parts.append(prods[i][at : at + block, :])
+    return jnp.concatenate(parts, axis=0)
 
 
 def setup_kernel(n, per_chunk, lanc, span, order_hbm, own_hbm, lanc_hbm, eig_hbm, *rest):
@@ -89,54 +127,73 @@
         copy.wait()
 
 
-def first_kernel(bits, span, pick, own, other, lanc16, eig, eig_hbm, out, prod, eig_next, sem):
-    load = pltpu.make_async_copy(
-        eig_hbm.at[pl.ds(span[0], span[1] - span[0])], eig_next, sem.at[0]
-    )
-    load.start()
-    half = own.shape[0]
+def send_kernel(spans, orders, p, pick, own, other, lanc16, eig_hbm, _, head, *rest):
+    made = classes_made(orders)
+    prods = rest[: sum(1 for group in made[:p] if group)]
+    out, *rest = rest[len(prods) :]
+    block = pick.shape[0] // 8
+    new = rest.pop(0) if made[p] else None
+    loads = []
+    if len(rest) > 1:
+        eig, sem = rest
+        first, last = fetched(spans, p)
+        cuts = [t[1:3] for t in tiles_of(spans, p)[1:]]
+        rest_end = end_of_rest(spans, p)
+        if last - first > rest_end:
+            cuts.append((rest_end, last - first - rest_end))
+        for i, (at, size) in enumerate(cuts):
+            loads.append(
+                pltpu.make_async_copy(
+                    eig_hbm.at[pl.ds(first + at, size)], eig.at[pl.ds(at, size)], sem.at[i]
+                )
+            )
+            loads[-1].start()
     lanc = lanc16[...].astype(jnp.float32)
-    block = prod.shape[0] // 8
-    groups = block // lanc.shape[0]
     bands = jnp.concatenate([own[...], other[...]], axis=0)
 
-    def make_classes(classes):
-        for c in classes:
-            chosen = lax.dot_general(
-                pick[c * block : (c + 1) * block, :],
-                bands,
-                (((1,), (0,)), ((), ())),
-                preferred_element_type=jnp.float32,
-            )
-            value = chosen.reshape(groups, lanc.shape[0], lanc.shape[1]) * lanc[None]
-            prod[c * block : (c + 1) * block, :] = value.reshape(chosen.shape).astype(
-                jnp.bfloat16
-            )
-
-    keep, leave = halves(bits)
-    make_classes(leave)
-    dot_into(out, prod, eig, leave)
-    make_classes(keep)
-    load.wait()
-
-
-def send_kernel(plan, spans, prod, eig, eig_hbm, *rest):
-    count = len(plan)
-    outs, later, sem = rest[:count], rest[count:-1], rest[-1]
-    loads = [
-        pltpu.make_async_copy(eig_hbm.at[pl.ds(at, end - at)], ref, sem.at[i])
-        for i, ((at, end), ref) in enumerate(zip(spans[1:], later))
-    ]
-    for load in loads:
-        load.start()
-    for i, bits in enumerate(plan):
+    def make(classes, at):
+        rows = [pick[c * block : (c + 1) * block, :] for c in classes]
+        chosen = lax.dot_general(
+            jnp.concatenate(rows, axis=0),
+            bands,
+            (((1,), (0,)), ((), ())),
+            preferred_element_type=jnp.float32,
+        )
+        value = chosen.reshape(-1, *lanc.shape) * lanc[None]
+        new[at * block : (at + len(classes)) * block, :] = value.reshape(chosen.shape).astype(
+            jnp.bfloat16
+        )
+
+    needed = [c for c in made[p] if c in halves(orders[p])[1]]
+    if needed:
+        make(needed, 0)
+    found, at = [], 0
+    for i, group in enumerate(made[: p + 1]):
+        found.append(new if i == p else prods[at] if group else None)
+        at += 1 if group else 0
+    rows = pick_rows(found, made, halves(orders[p])[1], block)
+    for i, tile in enumerate(tiles_of(spans, p)):
         if i > 0:
             loads[i - 1].wait()
-        dot_into(outs[i], prod, later[i - 1] if i > 0 else eig, halves(bits)[1])
-
-
-def keep_kernel(classes, prod, eig, out):
-    dot_into(out, prod, eig, classes)
+        dot_tile(out, rows, head if i == 0 else eig, tile)
+    if len(made[p]) > len(needed):
+        make(made[p][len(needed) :], len(needed))
+    for load in loads[len(tiles_of(spans, p)) - 1 :]:
+        load.wait()
+
+
+def keep_kernel(spans, orders, p, *refs):
+    made = classes_made(orders)
+    out = refs[-1]
+    found, at = [], 0
+    for group in made:
+        found.append(refs[at] if group else None)
+        at += 1 if group else 0
+    eigs = refs[at:-1]
+    block = out.shape[0] // 4
+    rows = pick_rows(found, made, halves(orders[p])[0], block)
+    for tile in tiles_of(spans, p):
+        dot_tile(out, rows, eigs[tile[0] - p], tile)
 
 
 def add_kernel(kept, got, _, leave, keep):
@@ -200,65 +257,70 @@
         return rows * width * depth
 
     other = lax.ppermute(bands, "eig", [(0, 1), (1, 0)])
+    head = min(TILE, widths[0])
     pick, own, lanc16, eig = kernel_call(
-        functools.partial(setup_kernel, n, per_chunk, lanc, spans[0]),
+        functools.partial(setup_kernel, n, per_chunk, lanc, (0, head)),
         [(band_order, True), (bands, True), (lanczos, True), (eigvecs, True)],
         [
             ((rows, 2 * bands.shape[0]), bf16),
             (bands.shape, bf16),
             (lanczos.shape, bf16),
-            ((widths[0], depth), bf16),
+            ((head, depth), bf16),
         ],
         [pltpu.SMEM(band_order.shape, jnp.int32), pltpu.SemaphoreType.DMA((4,))],
-        (0, 2 * widths[0] * depth),
-    )
-    eigs = [eig]
-    send, prod, eig = kernel_call(
-        functools.partial(first_kernel, orders[0], spans[1]),
-        [(pick, False), (own, False), (other, False), (lanc16, False), (eig, False)]
-        + [(eigvecs, True)],
-        [((rows // 2, widths[0]), bf16), ((rows, depth), bf16), ((widths[1], depth), bf16)],
-        [pltpu.SemaphoreType.DMA((1,))],
-        (flops(widths[0]), 2 * widths[1] * depth),
-    )
-    eigs.append(eig)
-    sends = [send]
-    more = kernel_call(
-        functools.partial(send_kernel, orders[1:], spans[1:]),
-        [(prod, False), (eig, False), (eigvecs, True)],
-        [((rows // 2, w), bf16) for w in widths[1:]] + [((w, depth), bf16) for w in widths[2:]],
-        [pltpu.SemaphoreType.DMA((len(PLAN) - 2,))],
-        (flops(sum(widths[1:])), 2 * sum(widths[2:]) * depth),
-    )
-    sends += more[: len(PLAN) - 1]
-    eigs += more[len(PLAN) - 1 :]
-    got = [exchange(s, bits[0]) for s, bits in zip(sends, orders)]
-    value = []
-    for p, bits in enumerate(orders):
-        value += kernel_call(
-            functools.partial(keep_kernel, halves(bits)[0]),
-            [(prod, False), (eigs[p], False)],
+        (0, 2 * head * depth),
+    )
+    made = classes_made(orders)
+    eigs, prods, value, got = [eig], [], {}, {}
+    token = other
+    later = range(3, n.bit_length() - 1)
+
+    def kept(p):
+        tiles = sorted({tile[0] for tile in tiles_of(spans, p)})
+        return kernel_call(
+            functools.partial(keep_kernel, spans, orders, p),
+            [(x, False) for x in prods] + [(eigs[i], False) for i in tiles],
             [((rows // 2, widths[p]), jnp.float32)],
             [],
-            (flops(widths[p]), 2 * widths[p] * depth),
-        )
-    later = range(3, n.bit_length() - 1)
-    token = prod
-    for stage in range(1, 3 + len(later)):
-        for p, bits in enumerate(orders):
-            half = value[p].shape[0] // 2
+            (0, 0),
+        )[0]
+
+    events = ORDER + [(p, stage) for stage in later for p in range(len(PLAN))]
+    for p, stage in events:
+        if stage == 0:
+            first, last = fetched(spans, p)
+            outs = [((rows // 2, widths[p]), bf16)]
+            if made[p]:
+                outs.append(((len(made[p]) * (rows // 8), depth), bf16))
+            if last > first:
+                outs.append(((last - first, depth), bf16))
+            copies = len(tiles_of(spans, p))
+            leave, *new = kernel_call(
+                functools.partial(send_kernel, spans, orders, p),
+                [(x, False) for x in (pick, own, other, lanc16)]
+                + [(eigvecs, True), (token, None), (eigs[p], False)]
+                + [(x, False) for x in prods],
+                outs,
+                [pltpu.SemaphoreType.DMA((copies,))],
+                (0, 0),
+            )
+            if made[p]:
+                prods.append(new.pop(0))
+            eigs += new
+        else:
+            half = rows // 2 >> stage
             size = half * widths[p]
             leave, value[p] = kernel_call(
                 add_kernel,
-                [(value[p], False), (got[p], False), (token, None)],
+                [(kept(p) if stage == 1 else value[p], False), (got[p], False), (token, None)],
                 [((half, widths[p]), bf16 if stage < 3 else jnp.float32)]
                 + [((half, widths[p]), jnp.float32)],
                 [],
                 (2 * size, 18 * size),
             )
-            token = leave
-            got[p] = exchange(leave, (*bits, *later)[stage])
-    outs = list(zip(value, got))
+        token = leave
+        got[p] = exchange(leave, (*orders[p], *later)[stage])
+    outs = [(value[p], got[p]) for p in range(len(PLAN))]
     (result,) = kernel_call(
         functools.partial(finish_kernel, spans),
         [(value, False) for value, _ in outs] + [(came, False) for _, came in outs],

time: 35.3 us -> 36.4 us (1.031)
  waiting for transfers between devices: 7.24 us -> 4.82 us
  starting transfers between devices: 16.7 us -> 19.1 us
  Pallas kernels: 11.1 us -> 12.2 us
    ppermute x9, waiting for transfers between devices: 7.24 us -> 4.82 us  [exchange(): return lax.ppermute(value, ('grid', 'eig'), pairs)]
    ppermute x9, starting transfers between devices: 16.2 us -> 18.6 us  [exchange(): return lax.ppermute(value, ('grid', 'eig'), pairs)]
    pallas_call x13 -> x14, Pallas kernels: 11.1 us -> 12.2 us  [kernel_call(): pl.pallas_call(body, out_shape=[jax.ShapeDtypeStruct(*out) for out in out...]
  transfers between devices with their start and end apart: 10 -> 10, of which waited for: 3 -> 5; matrix products, arithmetic and copies ran while one was open for 0% -> 0% of each run, Pallas kernels for 21% -> 24%
where the time goes in v7:
time: 36.4 us; the launch traced here: 36.2 us
  starting transfers between devices  19.1 us (52%)
  Pallas kernels  12.2 us (34%)
  waiting for transfers between devices  4.82 us (13%)
    ppermute x9, starting transfers between devices, exchange(): return lax.ppermute(value, ('grid', 'eig'), pairs)  18.6 us
    pallas_call x14, Pallas kernels, kernel_call(): pl.pallas_call(body, out_shape=[jax.ShapeDtypeStruct(*out) for out in out...  12.2 us
    ppermute x9, waiting for transfers between devices, exchange(): return lax.ppermute(value, ('grid', 'eig'), pairs)  4.82 us
  transfers between devices with their start and end apart: 10, of which 5 were waited for; matrix products, arithmetic and copies ran while one was open for 0% of the time, Pallas kernels for 24%

profile of v7, /device:TPU:0, one launch (start us, length us, event | category | flops | bytes accessed | tf_op | source)
XLA Modules:
  0.0 36.2 jit_solution(13386629555289712679)
XLA Ops:
  0.0 0.5 %collective-permute-start = (bf16[32,2048]{1,0:T(8,128)(2,1)}, bf16[32,2048]{1,0:T(8,128)(2,1)S(1)}, u32[]{:S(2)}, u32[]{:S(2)}) collective-permute-start(bf16[32,2048]{1,0:T(8,128)(2,1)} %own_hbm.1), channel_id=1, source_target_pairs={{0,1},{1,0},{2,3},{3,2},{4,5},{5,4},{6,7},{7,6},{8,9},{9,8},{10,11... | collective-permute-start | bytes 393224 | tf_op jit(solution)/shard_map/ppermute | solution.py:259
  0.5 1.4 %shard_map.46 = (bf16[512,64]{1,0:T(8,128)(2,1)S(1)}, bf16[32,2048]{1,0:T(8,128)(2,1)S(1)}, bf16[8,2048]{1,0:T(8,128)(2,1)S(1)}, bf16[256,2048]{1,0:T(8,128)(2,1)S(1)}) custom-call(s32[64]{0:T(128)} %order_hbm.1, bf16[32,2048]{1,0:T(8,128)(2,1)} %own_hbm.1, bf16[8,2048]{1,0:T(8,128)(2,1)} %lanc_hbm.1, bf16[1792,2048]{1,0:T(8,128)(2,1)} %eig_hbm.7), custom_call_target="tpu_custom_call" | custom-call | bytes 1048576 | tf_op jit(solution)/shard_map/pallas_call | solution.py:222
  1.8 2.7 %shard_map.47 = (bf16[256,768]{1,0:T(8,128)(2,1)S(1)}, bf16[256,2048]{1,0:T(8,128)(2,1)S(1)}, bf16[768,2048]{1,0:T(8,128)(2,1)S(1)}) custom-call(bf16[512,64]{1,0:T(8,128)(2,1)S(1)} %get-tuple-element.30.pick, bf16[32,2048]{1,0:T(8,128)(2,1)S(1)} %get-tuple-element.31.own, bf16[32,2048]{1,0:T(8,128)(2,1)S(1)} %collective-permute-done.other._, ...), custom_call_target="tpu_custom_call" | custom-call | tf_op jit(solution)/shard_map/pallas_call | solution.py:222
  4.5 2.7 %collective-permute-start.1 = (bf16[256,768]{1,0:T(8,128)(2,1)S(1)}, bf16[256,768]{1,0:T(8,128)(2,1)S(1)}, u32[]{:S(2)}, u32[]{:S(2)}) collective-permute-start(bf16[256,768]{1,0:T(8,128)(2,1)S(1)} %get-tuple-element.35._), channel_id=1, source_target_pairs={{0,2},{1,5},{2,0},{3,7},{4,6},{5,1},{6,4},{7,3},{8,10},{9,13},{10,... | collective-permute-start | bytes 1179656 | tf_op jit(solution)/shard_map/ppermute | solution.py:254
  7.3 2.0 %shard_map.48 = (bf16[256,512]{1,0:T(8,128)(2,1)S(1)}, bf16[128,2048]{1,0:T(8,128)(2,1)S(1)}, bf16[512,2048]{1,0:T(8,128)(2,1)S(1)}) custom-call(bf16[512,64]{1,0:T(8,128)(2,1)S(1)} %get-tuple-element.30.pick, bf16[32,2048]{1,0:T(8,128)(2,1)S(1)} %get-tuple-element.31.own, bf16[32,2048]{1,0:T(8,128)(2,1)S(1)} %collective-permute-done.other._, ...), custom_call_target="tpu_custom_call" | custom-call | tf_op jit(solution)/shard_map/pallas_call | solution.py:222
  9.2 2.7 %collective-permute-start.4 = (bf16[256,512]{1,0:T(8,128)(2,1)S(1)}, bf16[256,512]{1,0:T(8,128)(2,1)S(1)}, u32[]{:S(2)}, u32[]{:S(2)}) collective-permute-start(bf16[256,512]{1,0:T(8,128)(2,1)S(1)} %get-tuple-element.38._), channel_id=1, source_target_pairs={{0,8},{1,3},{2,10},{3,1},{4,12},{5,7},{6,14},{7,5},{8,0},{9,11},{1... | collective-permute-start | bytes 786440 | tf_op jit(solution)/shard_map/ppermute | solution.py:254
  11.9 2.7 %shard_map.49 = (bf16[256,512]{1,0:T(8,128)(2,1)S(1)}, bf16[128,2048]{1,0:T(8,128)(2,1)S(1)}, bf16[256,2048]{1,0:T(8,128)(2,1)S(1)}) custom-call(bf16[512,64]{1,0:T(8,128)(2,1)S(1)} %get-tuple-element.30.pick, bf16[32,2048]{1,0:T(8,128)(2,1)S(1)} %get-tuple-element.31.own, bf16[32,2048]{1,0:T(8,128)(2,1)S(1)} %collective-permute-done.other._, ...), custom_call_target="tpu_custom_call" | custom-call | tf_op jit(solution)/shard_map/pallas_call | solution.py:222
  14.6 0.6 %collective-permute-start.3 = (bf16[256,512]{1,0:T(8,128)(2,1)S(1)}, bf16[256,512]{1,0:T(8,128)(2,1)S(1)}, u32[]{:S(2)}, u32[]{:S(2)}) collective-permute-start(bf16[256,512]{1,0:T(8,128)(2,1)S(1)} %get-tuple-element.41._), channel_id=1, source_target_pairs={{0,2},{1,5},{2,0},{3,7},{4,6},{5,1},{6,4},{7,3},{8,10},{9,13},{10,... | collective-permute-start | bytes 786440 | tf_op jit(solution)/shard_map/ppermute | solution.py:254
  15.2 1.0 %shard_map.50.kept = f32[256,768]{1,0:T(8,128)S(1)} custom-call(bf16[256,2048]{1,0:T(8,128)(2,1)S(1)} %get-tuple-element.34.rest_0_.refs_0_, bf16[128,2048]{1,0:T(8,128)(2,1)S(1)} %get-tuple-element.37.rest_1_.refs_1_, bf16[128,2048]{1,0:T(8,128)(2,1)S(1)} %get-tuple-element.40.refs_2_, bf16[256,2048]{1,0:T(8,128)(2,1)S(1)} %get-tuple-element.33.head.refs_3_, ...), custom_call_target="tpu_custom_call" | custom-call | tf_op jit(solution)/shard_map/pallas_call | solution.py:222
  16.2 0.1 shard_map.51
  16.3 1.4 %collective-permute-start.2 = (bf16[128,768]{1,0:T(8,128)(2,1)S(1)}, bf16[128,768]{1,0:T(8,128)(2,1)S(1)}, u32[]{:S(2)}, u32[]{:S(2)}) collective-permute-start(bf16[128,768]{1,0:T(8,128)(2,1)S(1)} %get-tuple-element.43._), channel_id=1, source_target_pairs={{0,8},{1,3},{2,10},{3,1},{4,12},{5,7},{6,14},{7,5},{8,0},{9,11},{1... | collective-permute-start | bytes 589832 | tf_op jit(solution)/shard_map/ppermute | solution.py:254
  17.7 0.7 %shard_map.53.kept = f32[256,512]{1,0:T(8,128)S(1)} custom-call(bf16[256,2048]{1,0:T(8,128)(2,1)S(1)} %get-tuple-element.34.rest_0_.refs_0_, bf16[128,2048]{1,0:T(8,128)(2,1)S(1)} %get-tuple-element.37.rest_1_.refs_1_, bf16[128,2048]{1,0:T(8,128)(2,1)S(1)} %get-tuple-element.40.refs_2_, bf16[768,2048]{1,0:T(8,128)(2,1)S(1)} %get-tuple-element.36.head.refs_4_.refs_3_, ...), custom_call_target="tpu_custom_call" | custom-call | tf_op jit(solution)/shard_map/pallas_call | solution.py:222
  18.5 1.0 %collective-permute-done.4.got = bf16[256,512]{1,0:T(8,128)(2,1)S(1)} collective-permute-done((bf16[256,512]{1,0:T(8,128)(2,1)S(1)}, bf16[256,512]{1,0:T(8,128)(2,1)S(1)}, u32[]{:S(2)}, u32[]{:S(2)}) %collective-permute-start.4) | collective-permute-done | bytes 262176 | tf_op jit(solution)/shard_map/ppermute | solution.py:254
  19.5 0.5 %collective-permute-start.5 = (bf16[128,512]{1,0:T(8,128)(2,1)S(1)}, bf16[128,512]{1,0:T(8,128)(2,1)S(1)}, u32[]{:S(2)}, u32[]{:S(2)}) collective-permute-start(bf16[128,512]{1,0:T(8,128)(2,1)S(1)} %get-tuple-element.45._), channel_id=1, source_target_pairs={{0,2},{1,5},{2,0},{3,7},{4,6},{5,1},{6,4},{7,3},{8,10},{9,13},{10,... | collective-permute-start | bytes 393224 | tf_op jit(solution)/shard_map/ppermute | solution.py:254
  20.1 0.7 %shard_map.52.kept = f32[256,512]{1,0:T(8,128)S(1)} custom-call(bf16[256,2048]{1,0:T(8,128)(2,1)S(1)} %get-tuple-element.34.rest_0_.refs_0_, bf16[128,2048]{1,0:T(8,128)(2,1)S(1)} %get-tuple-element.37.rest_1_.refs_1_, bf16[128,2048]{1,0:T(8,128)(2,1)S(1)} %get-tuple-element.40.refs_2_, bf16[512,2048]{1,0:T(8,128)(2,1)S(1)} %get-tuple-element.39.head.refs_3_.refs_4_, ...), custom_call_target="tpu_custom_call" | custom-call | tf_op jit(solution)/shard_map/pallas_call | solution.py:222
  20.8 1.4 %collective-permute-done.3.got = bf16[256,512]{1,0:T(8,128)(2,1)S(1)} collective-permute-done((bf16[256,512]{1,0:T(8,128)(2,1)S(1)}, bf16[256,512]{1,0:T(8,128)(2,1)S(1)}, u32[]{:S(2)}, u32[]{:S(2)}) %collective-permute-start.3) | collective-permute-done | bytes 262176 | tf_op jit(solution)/shard_map/ppermute | solution.py:254
  22.3 1.6 %collective-permute-start.6 = (bf16[128,512]{1,0:T(8,128)(2,1)S(1)}, bf16[128,512]{1,0:T(8,128)(2,1)S(1)}, u32[]{:S(2)}, u32[]{:S(2)}) collective-permute-start(bf16[128,512]{1,0:T(8,128)(2,1)S(1)} %get-tuple-element.46._), channel_id=1, source_target_pairs={{0,4},{1,9},{2,6},{3,11},{4,0},{5,13},{6,2},{7,15},{8,12},{9,1},{1... | collective-permute-start | bytes 393224 | tf_op jit(solution)/shard_map/ppermute | solution.py:254
  24.0 0.1 collective-permute-done.2.got
  24.1 5.5 %collective-permute-start.7 = (bf16[64,768]{1,0:T(8,128)(2,1)S(1)}, bf16[64,768]{1,0:T(8,128)(2,1)S(1)}, u32[]{:S(2)}, u32[]{:S(2)}) collective-permute-start(bf16[64,768]{1,0:T(8,128)(2,1)S(1)} %get-tuple-element.49._), channel_id=1, source_target_pairs={{0,4},{1,9},{2,6},{3,11},{4,0},{5,13},{6,2},{7,15},{8,12},{9,1},{1... | collective-permute-start | bytes 294920 | tf_op jit(solution)/shard_map/ppermute | solution.py:254
  29.6 0.1 collective-permute-start.8
  29.7 3.4 %collective-permute-start.9 = (bf16[64,512]{1,0:T(8,128)(2,1)S(1)}, bf16[64,512]{1,0:T(8,128)(2,1)S(1)}, u32[]{:S(2)}, u32[]{:S(2)}) collective-permute-start(bf16[64,512]{1,0:T(8,128)(2,1)S(1)} %get-tuple-element.54), channel_id=1, source_target_pairs={{0,8},{1,3},{2,10},{3,1},{4,12},{5,7},{6,14},{7,5},{8,0},{9,11},{1... | collective-permute-start | bytes 196616 | tf_op jit(solution)/shard_map/ppermute | solution.py:254
  33.2 0.8 %collective-permute-done.8.refs_4_ = bf16[64,512]{1,0:T(8,128)(2,1)S(1)} collective-permute-done((bf16[64,512]{1,0:T(8,128)(2,1)S(1)}, bf16[64,512]{1,0:T(8,128)(2,1)S(1)}, u32[]{:S(2)}, u32[]{:S(2)}) %collective-permute-start.8) | collective-permute-done | bytes 65568 | tf_op jit(solution)/shard_map/ppermute | solution.py:254
  34.0 1.5 %collective-permute-done.9.refs_5_ = bf16[64,512]{1,0:T(8,128)(2,1)S(1)} collective-permute-done((bf16[64,512]{1,0:T(8,128)(2,1)S(1)}, bf16[64,512]{1,0:T(8,128)(2,1)S(1)}, u32[]{:S(2)}, u32[]{:S(2)}) %collective-permute-start.9) | collective-permute-done | bytes 65568 | tf_op jit(solution)/shard_map/ppermute | solution.py:254
  35.4 0.8 %shard_map.59 = f32[64,1792]{1,0:T(8,128)} custom-call(f32[64,768]{1,0:T(8,128)S(1)} %get-tuple-element.47.refs_0_, f32[64,512]{1,0:T(8,128)S(1)} %get-tuple-element.50.refs_1_, f32[64,512]{1,0:T(8,128)S(1)} %get-tuple-element.53.refs_2_, bf16[64,768]{1,0:T(8,128)(2,1)S(1)} %collective-permute-done.7.refs_3_, ...), custom_call_target="tpu_custom_call" | custom-call | flops 114688 | bytes 1376256 | tf_op jit(solution)/shard_map/pallas_call | solution.py:222
  (10 shorter events, 0.2 us)
Async XLA Ops:
  0.0 1.8 %collective-permute-start = (bf16[32,2048]{1,0:T(8,128)(2,1)}, bf16[32,2048]{1,0:T(8,128)(2,1)S(1)}, u32[]{:S(2)}, u32[]{:S(2)}) collective-permute-start(bf16[32,2048]{1,0:T(8,128)(2,1)} %own_hbm.1), channel_id=1, source_target_pairs={{0,1},{1,0},{2,3},{3,2},{4,5},{5,4},{6,7},{7,6},{8,9},{9,8},{10,11... | collective-permute-start | bytes 393224 | tf_op jit(solution)/shard_map/ppermute | solution.py:259
  4.5 11.7 %collective-permute-start.1 = (bf16[256,768]{1,0:T(8,128)(2,1)S(1)}, bf16[256,768]{1,0:T(8,128)(2,1)S(1)}, u32[]{:S(2)}, u32[]{:S(2)}) collective-permute-start(bf16[256,768]{1,0:T(8,128)(2,1)S(1)} %get-tuple-element.35._), channel_id=1, source_target_pairs={{0,2},{1,5},{2,0},{3,7},{4,6},{5,1},{6,4},{7,3},{8,10},{9,13},{10,... | collective-permute-start | bytes 1179656 | tf_op jit(solution)/shard_map/ppermute | solution.py:254
  9.2 10.3 %collective-permute-start.4 = (bf16[256,512]{1,0:T(8,128)(2,1)S(1)}, bf16[256,512]{1,0:T(8,128)(2,1)S(1)}, u32[]{:S(2)}, u32[]{:S(2)}) collective-permute-start(bf16[256,512]{1,0:T(8,128)(2,1)S(1)} %get-tuple-element.38._), channel_id=1, source_target_pairs={{0,8},{1,3},{2,10},{3,1},{4,12},{5,7},{6,14},{7,5},{8,0},{9,11},{1... | collective-permute-start | bytes 786440 | tf_op jit(solution)/shard_map/ppermute | solution.py:254
  14.6 7.7 %collective-permute-start.3 = (bf16[256,512]{1,0:T(8,128)(2,1)S(1)}, bf16[256,512]{1,0:T(8,128)(2,1)S(1)}, u32[]{:S(2)}, u32[]{:S(2)}) collective-permute-start(bf16[256,512]{1,0:T(8,128)(2,1)S(1)} %get-tuple-element.41._), channel_id=1, source_target_pairs={{0,2},{1,5},{2,0},{3,7},{4,6},{5,1},{6,4},{7,3},{8,10},{9,13},{10,... | collective-permute-start | bytes 786440 | tf_op jit(solution)/shard_map/ppermute | solution.py:254
  16.3 7.8 %collective-permute-start.2 = (bf16[128,768]{1,0:T(8,128)(2,1)S(1)}, bf16[128,768]{1,0:T(8,128)(2,1)S(1)}, u32[]{:S(2)}, u32[]{:S(2)}) collective-permute-start(bf16[128,768]{1,0:T(8,128)(2,1)S(1)} %get-tuple-element.43._), channel_id=1, source_target_pairs={{0,8},{1,3},{2,10},{3,1},{4,12},{5,7},{6,14},{7,5},{8,0},{9,11},{1... | collective-permute-start | bytes 589832 | tf_op jit(solution)/shard_map/ppermute | solution.py:254
  19.5 10.0 %collective-permute-start.5 = (bf16[128,512]{1,0:T(8,128)(2,1)S(1)}, bf16[128,512]{1,0:T(8,128)(2,1)S(1)}, u32[]{:S(2)}, u32[]{:S(2)}) collective-permute-start(bf16[128,512]{1,0:T(8,128)(2,1)S(1)} %get-tuple-element.45._), channel_id=1, source_target_pairs={{0,2},{1,5},{2,0},{3,7},{4,6},{5,1},{6,4},{7,3},{8,10},{9,13},{10,... | collective-permute-start | bytes 393224 | tf_op jit(solution)/shard_map/ppermute | solution.py:254
  22.3 7.4 %collective-permute-start.6 = (bf16[128,512]{1,0:T(8,128)(2,1)S(1)}, bf16[128,512]{1,0:T(8,128)(2,1)S(1)}, u32[]{:S(2)}, u32[]{:S(2)}) collective-permute-start(bf16[128,512]{1,0:T(8,128)(2,1)S(1)} %get-tuple-element.46._), channel_id=1, source_target_pairs={{0,4},{1,9},{2,6},{3,11},{4,0},{5,13},{6,2},{7,15},{8,12},{9,1},{1... | collective-permute-start | bytes 393224 | tf_op jit(solution)/shard_map/ppermute | solution.py:254
  24.1 11.3 %collective-permute-start.7 = (bf16[64,768]{1,0:T(8,128)(2,1)S(1)}, bf16[64,768]{1,0:T(8,128)(2,1)S(1)}, u32[]{:S(2)}, u32[]{:S(2)}) collective-permute-start(bf16[64,768]{1,0:T(8,128)(2,1)S(1)} %get-tuple-element.49._), channel_id=1, source_target_pairs={{0,4},{1,9},{2,6},{3,11},{4,0},{5,13},{6,2},{7,15},{8,12},{9,1},{1... | collective-permute-start | bytes 294920 | tf_op jit(solution)/shard_map/ppermute | solution.py:254
  29.6 4.3 %collective-permute-start.8 = (bf16[64,512]{1,0:T(8,128)(2,1)S(1)}, bf16[64,512]{1,0:T(8,128)(2,1)S(1)}, u32[]{:S(2)}, u32[]{:S(2)}) collective-permute-start(bf16[64,512]{1,0:T(8,128)(2,1)S(1)} %get-tuple-element.52._), channel_id=1, source_target_pairs={{0,4},{1,9},{2,6},{3,11},{4,0},{5,13},{6,2},{7,15},{8,12},{9,1},{1... | collective-permute-start | bytes 196616 | tf_op jit(solution)/shard_map/ppermute | solution.py:254
  29.7 5.7 %collective-permute-start.9 = (bf16[64,512]{1,0:T(8,128)(2,1)S(1)}, bf16[64,512]{1,0:T(8,128)(2,1)S(1)}, u32[]{:S(2)}, u32[]{:S(2)}) collective-permute-start(bf16[64,512]{1,0:T(8,128)(2,1)S(1)} %get-tuple-element.54), channel_id=1, source_target_pairs={{0,8},{1,3},{2,10},{3,1},{4,12},{5,7},{6,14},{7,5},{8,0},{9,11},{1... | collective-permute-start | bytes 196616 | tf_op jit(solution)/shard_map/ppermute | solution.py:254

commit v8 on v6

--- a/solution.py
+++ b/solution.py
@@ -8,6 +8,7 @@
 from jax.sharding import PartitionSpec as P
 
 TILE = 256
+SETUP = 512
 VMEM_LIMIT = 32 * 1024 * 1024
 WAYS = ((1, 0, 2), (0, 2, 1))
 PLAN = [(3.5, (0, 1, 2)), (2, (1, 0, 2)), (1.5, (0, 1, 2))]
@@ -40,21 +41,33 @@
     return sum(((c >> s) & 1) << bit for s, bit in enumerate(WAYS[core])) + (c >> 3 << 3)
 
 
-def dot_into(out, prod, eig, classes):
-    block = prod.shape[0] // 8
-    rows = jnp.concatenate([prod[c * block : (c + 1) * block, :] for c in classes], axis=0)
-    width = eig.shape[0]
-    for col in range(0, width, TILE):
-        size = min(TILE, width - col)
-        out[:, col : col + size] = lax.dot_general(
+def rows_of(prods, made, classes):
+    if classes in made:
+        return prods[made.index(classes)][...]
+    parts = []
+    for c in classes:
+        i = next(i for i, group in enumerate(made) if c in group)
+        block = prods[i].shape[0] // len(made[i])
+        at = made[i].index(c) * block
+        parts.append(prods[i][at : at + block, :])
+    return jnp.concatenate(parts, axis=0)
+
+
+def dot_span(out, rows, eigs, cuts, span):
+    col = span[0]
+    while col < span[1]:
+        i = max(i for i, cut in enumerate(cuts) if cut <= col)
+        size = min(TILE, span[1] - col, cuts[i + 1] - col)
+        out[:, col - span[0] : col - span[0] + size] = lax.dot_general(
             rows,
-            eig[col : col + size, :],
+            eigs[i][col - cuts[i] : col - cuts[i] + size, :],
             (((1,), (1,)), ((), ())),
             preferred_element_type=jnp.float32,
-        ).astype(out.dtype)
-
-
-def setup_kernel(n, per_chunk, lanc, span, order_hbm, own_hbm, lanc_hbm, eig_hbm, *rest):
+        )
+        col += size
+
+
+def setup_kernel(n, per_chunk, lanc, classes, width, order_hbm, own_hbm, lanc_hbm, eig_hbm, *rest):
     pick, own, lanc16, eig, order, sem = rest
     copies = [
         pltpu.make_async_copy(src, dst, sem.at[i])
@@ -63,7 +76,7 @@
                 (order_hbm, order),
                 (own_hbm, own),
                 (lanc_hbm, lanc16),
-                (eig_hbm.at[pl.ds(span[0], span[1] - span[0])], eig),
+                (eig_hbm.at[pl.ds(0, width)], eig),
             ]
         )
     ]
@@ -73,7 +86,7 @@
     core = lax.axis_index("eig")
     bands = pick.shape[1]
     rest_bits = list(range(3, n.bit_length() - 1))
-    slots = [(r, j) for c in range(8) for r in ranked(rest_bits, c) for j in range(per_chunk)]
+    slots = [(r, j) for c in classes for r in ranked(rest_bits, c) for j in range(per_chunk)]
     col = lax.broadcasted_iota(jnp.int32, (2 * lanc, bands), 1)
     upper = lax.broadcasted_iota(jnp.int32, (2 * lanc, bands), 0) < lanc
     copies[0].wait()
@@ -89,54 +102,71 @@
         copy.wait()
 
 
-def first_kernel(bits, span, pick, own, other, lanc16, eig, eig_hbm, out, prod, eig_next, sem):
-    load = pltpu.make_async_copy(
-        eig_hbm.at[pl.ds(span[0], span[1] - span[0])], eig_next, sem.at[0]
-    )
-    load.start()
-    half = own.shape[0]
+def fetch(eig_hbm, eig, sem, cuts):
+    copies = []
+    for i, (at, end) in enumerate(zip(cuts, cuts[1:])):
+        if at == end:
+            copies.append(None)
+            continue
+        part = pl.ds(at - cuts[0], end - at)
+        copy = pltpu.make_async_copy(eig_hbm.at[pl.ds(at, end - at)], eig.at[part], sem.at[i])
+        copy.start()
+        copies.append(copy)
+    return copies
+
+
+def make_rows(prod, pick, own, other, lanc16, first):
     lanc = lanc16[...].astype(jnp.float32)
-    block = prod.shape[0] // 8
-    groups = block // lanc.shape[0]
-    bands = jnp.concatenate([own[...], other[...]], axis=0)
-
-    def make_classes(classes):
-        for c in classes:
-            chosen = lax.dot_general(
-                pick[c * block : (c + 1) * block, :],
-                bands,
-                (((1,), (0,)), ((), ())),
-                preferred_element_type=jnp.float32,
-            )
-            value = chosen.reshape(groups, lanc.shape[0], lanc.shape[1]) * lanc[None]
-            prod[c * block : (c + 1) * block, :] = value.reshape(chosen.shape).astype(
-                jnp.bfloat16
-            )
-
-    keep, leave = halves(bits)
-    make_classes(leave)
-    dot_into(out, prod, eig, leave)
-    make_classes(keep)
-    load.wait()
-
-
-def send_kernel(plan, spans, prod, eig, eig_hbm, *rest):
-    count = len(plan)
-    outs, later, sem = rest[:count], rest[count:-1], rest[-1]
-    loads = [
-        pltpu.make_async_copy(eig_hbm.at[pl.ds(at, end - at)], ref, sem.at[i])
-        for i, ((at, end), ref) in enumerate(zip(spans[1:], later))
-    ]
-    for load in loads:
-        load.start()
-    for i, bits in enumerate(plan):
+    chosen = lax.dot_general(
+        pick[first : first + prod.shape[0], :],
+        jnp.concatenate([own[...], other[...]], axis=0),
+        (((1,), (0,)), ((), ())),
+        preferred_element_type=jnp.float32,
+    )
+    value = chosen.reshape(-1, *lanc.shape) * lanc[None]
+    prod[...] = value.reshape(chosen.shape).astype(jnp.bfloat16)
+
+
+def first_kernel(
+    cuts, span, pick, own, other, lanc16, eig, eig_hbm, out, prod, eig_next, acc, sem
+):
+    copies = fetch(eig_hbm, eig_next, sem, [cuts[1], max(cuts[1], span[1]), cuts[2]])
+    make_rows(prod, pick, own, other, lanc16, 0)
+    rows = prod[...]
+    dot_span(acc, rows, [eig], cuts, (0, min(cuts[1], span[1])))
+    if span[1] > cuts[1]:
+        copies[0].wait()
+        late = acc.at[:, cuts[1] : span[1]]
+        dot_span(late, rows, [eig, eig_next], cuts, (cuts[1], span[1]))
+    out[...] = acc[...].astype(out.dtype)
+    copies[1].wait()
+
+
+def send_kernel(
+    cuts, orders, made, spans, pick, own, other, lanc16, prod, eig, eig_hbm, *rest
+):
+    count = len(spans)
+    outs, (more, eig_next, acc, sem) = rest[:count], rest[count:]
+    ends = [end for _, end in spans[1:]]
+    copies = fetch(eig_hbm, eig_next, sem, [cuts[2], *ends])
+    make_rows(more, pick, own, other, lanc16, prod.shape[0])
+    for i, (out, span) in enumerate(zip(outs, spans)):
         if i > 0:
-            loads[i - 1].wait()
-        dot_into(outs[i], prod, later[i - 1] if i > 0 else eig, halves(bits)[1])
-
-
-def keep_kernel(classes, prod, eig, out):
-    dot_into(out, prod, eig, classes)
+            copies[i - 1].wait()
+        rows = rows_of([prod, more], made, halves(orders[i])[1])
+        part = acc.at[:, : span[1] - span[0]]
+        dot_span(part, rows, [None, eig, eig_next], cuts, span)
+        out[...] = part[...].astype(out.dtype)
+
+
+def keep_kernel(cuts, classes, made, span, prod, more, *refs):
+    used = arrays_of(cuts, span)
+    eigs = [refs[used.index(i)] if i in used else None for i in range(len(cuts) - 1)]
+    dot_span(refs[-1], rows_of([prod, more], made, classes), eigs, cuts, span)
+
+
+def arrays_of(cuts, span):
+    return [i for i in range(len(cuts) - 1) if cuts[i] < span[1] and span[0] < cuts[i + 1]]
 
 
 def add_kernel(kept, got, _, leave, keep):
@@ -199,45 +229,51 @@
     def flops(width):
         return rows * width * depth
 
+    made = list(reversed(halves(orders[0])))
+    cuts = [0, min(SETUP, widths[0]), spans[1][1], cols]
     other = lax.ppermute(bands, "eig", [(0, 1), (1, 0)])
     pick, own, lanc16, eig = kernel_call(
-        functools.partial(setup_kernel, n, per_chunk, lanc, spans[0]),
+        functools.partial(setup_kernel, n, per_chunk, lanc, made[0] + made[1], cuts[1]),
         [(band_order, True), (bands, True), (lanczos, True), (eigvecs, True)],
         [
             ((rows, 2 * bands.shape[0]), bf16),
             (bands.shape, bf16),
             (lanczos.shape, bf16),
-            ((widths[0], depth), bf16),
+            ((cuts[1], depth), bf16),
         ],
         [pltpu.SMEM(band_order.shape, jnp.int32), pltpu.SemaphoreType.DMA((4,))],
-        (0, 2 * widths[0] * depth),
+        (0, 2 * cuts[1] * depth),
     )
     eigs = [eig]
+    sources = [(x, False) for x in (pick, own, other, lanc16)]
     send, prod, eig = kernel_call(
-        functools.partial(first_kernel, orders[0], spans[1]),
-        [(pick, False), (own, False), (other, False), (lanc16, False), (eig, False)]
-        + [(eigvecs, True)],
-        [((rows // 2, widths[0]), bf16), ((rows, depth), bf16), ((widths[1], depth), bf16)],
-        [pltpu.SemaphoreType.DMA((1,))],
+        functools.partial(first_kernel, cuts, spans[0]),
+        sources + [(eig, False), (eigvecs, True)],
+        [((rows // 2, widths[0]), bf16), ((rows // 2, depth), bf16)]
+        + [((cuts[2] - cuts[1], depth), bf16)],
+        [pltpu.VMEM((rows // 2, widths[0]), jnp.float32), pltpu.SemaphoreType.DMA((2,))],
         (flops(widths[0]), 2 * widths[1] * depth),
     )
     eigs.append(eig)
-    sends = [send]
-    more = kernel_call(
-        functools.partial(send_kernel, orders[1:], spans[1:]),
-        [(prod, False), (eig, False), (eigvecs, True)],
-        [((rows // 2, w), bf16) for w in widths[1:]] + [((w, depth), bf16) for w in widths[2:]],
-        [pltpu.SemaphoreType.DMA((len(PLAN) - 2,))],
+    *sends, more, eig = kernel_call(
+        functools.partial(send_kernel, cuts, orders[1:], made, spans[1:]),
+        sources + [(prod, False), (eig, False), (eigvecs, True)],
+        [((rows // 2, w), bf16) for w in widths[1:]]
+        + [((rows // 2, depth), bf16), ((cuts[3] - cuts[2], depth), bf16)],
+        [
+            pltpu.VMEM((rows // 2, max(widths[1:])), jnp.float32),
+            pltpu.SemaphoreType.DMA((len(PLAN) - 2,)),
+        ],
         (flops(sum(widths[1:])), 2 * sum(widths[2:]) * depth),
     )
-    sends += more[: len(PLAN) - 1]
-    eigs += more[len(PLAN) - 1 :]
-    got = [exchange(s, bits[0]) for s, bits in zip(sends, orders)]
+    eigs.append(eig)
+    got = [exchange(s, bits[0]) for s, bits in zip([send, *sends], orders)]
     value = []
     for p, bits in enumerate(orders):
         value += kernel_call(
-            functools.partial(keep_kernel, halves(bits)[0]),
-            [(prod, False), (eigs[p], False)],
+            functools.partial(keep_kernel, cuts, halves(bits)[0], made, spans[p]),
+            [(prod, False), (more, False)]
+            + [(eigs[i], False) for i in arrays_of(cuts, spans[p])],
             [((rows // 2, widths[p]), jnp.float32)],
             [],
             (flops(widths[p]), 2 * widths[p] * depth),

time: 35.3 us -> 34.9 us (0.989)
  Pallas kernels: 11.1 us -> 10.6 us
    pallas_call x13, Pallas kernels: 11.1 us -> 10.6 us  [kernel_call(): pl.pallas_call(body, out_shape=[jax.ShapeDtypeStruct(*out) for out in out...]
  transfers between devices with their start and end apart: 10 -> 10, of which waited for: 3 -> 3; matrix products, arithmetic and copies ran while one was open for 0% -> 0% of each run, Pallas kernels for 21% -> 20%
where the time goes in v8:
time: 34.9 us; the launch traced here: 34.7 us
  starting transfers between devices  16.7 us (48%)
  Pallas kernels  10.6 us (30%)
  waiting for transfers between devices  7.24 us (21%)
    ppermute x9, starting transfers between devices, exchange(): return lax.ppermute(value, ('grid', 'eig'), pairs)  16.3 us
    pallas_call x13, Pallas kernels, kernel_call(): pl.pallas_call(body, out_shape=[jax.ShapeDtypeStruct(*out) for out in out...  10.6 us
    ppermute x9, waiting for transfers between devices, exchange(): return lax.ppermute(value, ('grid', 'eig'), pairs)  7.24 us
  transfers between devices with their start and end apart: 10, of which 3 were waited for; matrix products, arithmetic and copies ran while one was open for 0% of the time, Pallas kernels for 20%

profile of v8, /device:TPU:0, one launch (start us, length us, event | category | flops | bytes accessed | tf_op | source)
XLA Modules:
  0.0 34.7 jit_solution(11935338405999627734)
XLA Ops:
  0.0 0.5 %collective-permute-start = (bf16[32,2048]{1,0:T(8,128)(2,1)}, bf16[32,2048]{1,0:T(8,128)(2,1)S(1)}, u32[]{:S(2)}, u32[]{:S(2)}) collective-permute-start(bf16[32,2048]{1,0:T(8,128)(2,1)} %own_hbm.1), channel_id=1, source_target_pairs={{0,1},{1,0},{2,3},{3,2},{4,5},{5,4},{6,7},{7,6},{8,9},{9,8},{10,11... | collective-permute-start | bytes 393224 | tf_op jit(solution)/shard_map/ppermute | solution.py:234
  0.5 1.7 %shard_map.46 = (bf16[512,64]{1,0:T(8,128)(2,1)S(1)}, bf16[32,2048]{1,0:T(8,128)(2,1)S(1)}, bf16[8,2048]{1,0:T(8,128)(2,1)S(1)}, bf16[512,2048]{1,0:T(8,128)(2,1)S(1)}) custom-call(s32[64]{0:T(128)} %order_hbm.1, bf16[32,2048]{1,0:T(8,128)(2,1)} %own_hbm.1, bf16[8,2048]{1,0:T(8,128)(2,1)} %lanc_hbm.1, bf16[1792,2048]{1,0:T(8,128)(2,1)} %eig_hbm.5), custom_call_target="tpu_custom_call" | custom-call | bytes 2097152 | tf_op jit(solution)/shard_map/pallas_call | solution.py:195
  2.2 3.0 %shard_map.47 = (bf16[256,896]{1,0:T(8,128)(2,1)S(1)}, bf16[256,2048]{1,0:T(8,128)(2,1)S(1)}, bf16[896,2048]{1,0:T(8,128)(2,1)S(1)}) custom-call(bf16[512,64]{1,0:T(8,128)(2,1)S(1)} %get-tuple-element.28.pick, bf16[32,2048]{1,0:T(8,128)(2,1)S(1)} %get-tuple-element.29.own, bf16[32,2048]{1,0:T(8,128)(2,1)S(1)} %collective-permute-done.other, ...), custom_call_target="tpu_custom_call" | custom-call | flops 939524096 | bytes 2097152 | tf_op jit(solution)/shard_map/pallas_call | solution.py:195
  5.2 2.6 %collective-permute-start.1 = (bf16[256,896]{1,0:T(8,128)(2,1)S(1)}, bf16[256,896]{1,0:T(8,128)(2,1)S(1)}, u32[]{:S(2)}, u32[]{:S(2)}) collective-permute-start(bf16[256,896]{1,0:T(8,128)(2,1)S(1)} %get-tuple-element.35), channel_id=1, source_target_pairs={{0,4},{1,3},{2,6},{3,1},{4,0},{5,7},{6,2},{7,5},{8,12},{9,11},{10,... | collective-permute-start | bytes 1376264 | tf_op jit(solution)/shard_map/ppermute | solution.py:227
  7.9 2.1 %shard_map.48 = (bf16[256,512]{1,0:T(8,128)(2,1)S(1)}, bf16[256,384]{1,0:T(8,128)(2,1)S(1)}, bf16[256,2048]{1,0:T(8,128)(2,1)S(1)}, bf16[384,2048]{1,0:T(8,128)(2,1)S(1)}) custom-call(bf16[512,64]{1,0:T(8,128)(2,1)S(1)} %get-tuple-element.28.pick, bf16[32,2048]{1,0:T(8,128)(2,1)S(1)} %get-tuple-element.29.own, ...), custom_call_target="tpu_custom_call" | custom-call | flops 939524096 | bytes 1572864 | tf_op jit(solution)/shard_map/pallas_call | solution.py:195
  10.0 1.6 %collective-permute-start.4 = (bf16[256,512]{1,0:T(8,128)(2,1)S(1)}, bf16[256,512]{1,0:T(8,128)(2,1)S(1)}, u32[]{:S(2)}, u32[]{:S(2)}) collective-permute-start(bf16[256,512]{1,0:T(8,128)(2,1)S(1)} %get-tuple-element.40), channel_id=1, source_target_pairs={{0,2},{1,9},{2,0},{3,11},{4,6},{5,13},{6,4},{7,15},{8,10},{9,1},{1... | collective-permute-start | bytes 786440 | tf_op jit(solution)/shard_map/ppermute | solution.py:227
  11.6 0.4 %collective-permute-start.3 = (bf16[256,384]{1,0:T(8,128)(2,1)S(1)}, bf16[256,384]{1,0:T(8,128)(2,1)S(1)}, u32[]{:S(2)}, u32[]{:S(2)}) collective-permute-start(bf16[256,384]{1,0:T(8,128)(2,1)S(1)} %get-tuple-element.39), channel_id=1, source_target_pairs={{0,4},{1,3},{2,6},{3,1},{4,0},{5,7},{6,2},{7,5},{8,12},{9,11},{10,... | collective-permute-start | bytes 589832 | tf_op jit(solution)/shard_map/ppermute | solution.py:227
  12.0 1.3 %shard_map.49.kept = f32[256,896]{1,0:T(8,128)S(1)} custom-call(bf16[256,2048]{1,0:T(8,128)(2,1)S(1)} %get-tuple-element.32.prod._, bf16[256,2048]{1,0:T(8,128)(2,1)S(1)} %get-tuple-element.34.more, bf16[512,2048]{1,0:T(8,128)(2,1)S(1)} %get-tuple-element.31.eig.refs_0_, bf16[896,2048]{1,0:T(8,128)(2,1)S(1)} %get-tuple-element.33.eig.refs_1_.refs_0_), custom_call_target="tpu_custom_call" | custom-call | flops 939524096 | bytes 3670016 | tf_op jit(solution)/shard_map/pallas_call | solution.py:195
  13.3 2.6 %collective-permute-done.1.got = bf16[256,896]{1,0:T(8,128)(2,1)S(1)} collective-permute-done((bf16[256,896]{1,0:T(8,128)(2,1)S(1)}, bf16[256,896]{1,0:T(8,128)(2,1)S(1)}, u32[]{:S(2)}, u32[]{:S(2)}) %collective-permute-start.1) | collective-permute-done | bytes 458784 | tf_op jit(solution)/shard_map/ppermute | solution.py:227
  15.9 0.1 shard_map.50
  16.0 3.2 %collective-permute-start.2 = (bf16[128,896]{1,0:T(8,128)(2,1)S(1)}, bf16[128,896]{1,0:T(8,128)(2,1)S(1)}, u32[]{:S(2)}, u32[]{:S(2)}) collective-permute-start(bf16[128,896]{1,0:T(8,128)(2,1)S(1)} %get-tuple-element.37._), channel_id=1, source_target_pairs={{0,2},{1,9},{2,0},{3,11},{4,6},{5,13},{6,4},{7,15},{8,10},{9,1},{1... | collective-permute-start | bytes 688136 | tf_op jit(solution)/shard_map/ppermute | solution.py:227
  19.2 0.7 %shard_map.52.kept = f32[256,512]{1,0:T(8,128)S(1)} custom-call(bf16[256,2048]{1,0:T(8,128)(2,1)S(1)} %get-tuple-element.32.prod._, bf16[256,2048]{1,0:T(8,128)(2,1)S(1)} %get-tuple-element.34.more, bf16[896,2048]{1,0:T(8,128)(2,1)S(1)} %get-tuple-element.33.eig.refs_1_.refs_0_), custom_call_target="tpu_custom_call" | custom-call | flops 536870912 | bytes 2097152 | tf_op jit(solution)/shard_map/pallas_call | solution.py:195
  20.0 0.7 %collective-permute-start.5 = (bf16[128,512]{1,0:T(8,128)(2,1)S(1)}, bf16[128,512]{1,0:T(8,128)(2,1)S(1)}, u32[]{:S(2)}, u32[]{:S(2)}) collective-permute-start(bf16[128,512]{1,0:T(8,128)(2,1)S(1)} %get-tuple-element.41._), channel_id=1, source_target_pairs={{0,4},{1,3},{2,6},{3,1},{4,0},{5,7},{6,2},{7,5},{8,12},{9,11},{10,... | collective-permute-start | bytes 393224 | tf_op jit(solution)/shard_map/ppermute | solution.py:227
  20.7 0.7 %shard_map.51.kept = f32[256,384]{1,0:T(8,128)S(1)} custom-call(bf16[256,2048]{1,0:T(8,128)(2,1)S(1)} %get-tuple-element.32.prod._, bf16[256,2048]{1,0:T(8,128)(2,1)S(1)} %get-tuple-element.34.more, bf16[384,2048]{1,0:T(8,128)(2,1)S(1)} %get-tuple-element.38.refs_0_), custom_call_target="tpu_custom_call" | custom-call | flops 402653184 | bytes 1572864 | tf_op jit(solution)/shard_map/pallas_call | solution.py:195
  21.4 0.0 collective-permute-done.3.got
  21.4 2.1 %collective-permute-start.6 = (bf16[128,384]{1,0:T(8,128)(2,1)S(1)}, bf16[128,384]{1,0:T(8,128)(2,1)S(1)}, u32[]{:S(2)}, u32[]{:S(2)}) collective-permute-start(bf16[128,384]{1,0:T(8,128)(2,1)S(1)} %get-tuple-element.42._), channel_id=1, source_target_pairs={{0,2},{1,9},{2,0},{3,11},{4,6},{5,13},{6,4},{7,15},{8,10},{9,1},{1... | collective-permute-start | bytes 294920 | tf_op jit(solution)/shard_map/ppermute | solution.py:227
  23.6 1.0 %collective-permute-done.2.got = bf16[128,896]{1,0:T(8,128)(2,1)S(1)} collective-permute-done((bf16[128,896]{1,0:T(8,128)(2,1)S(1)}, bf16[128,896]{1,0:T(8,128)(2,1)S(1)}, u32[]{:S(2)}, u32[]{:S(2)}) %collective-permute-start.2) | collective-permute-done | bytes 229408 | tf_op jit(solution)/shard_map/ppermute | solution.py:227
  24.7 2.5 %collective-permute-start.7 = (bf16[64,896]{1,0:T(8,128)(2,1)S(1)}, bf16[64,896]{1,0:T(8,128)(2,1)S(1)}, u32[]{:S(2)}, u32[]{:S(2)}) collective-permute-start(bf16[64,896]{1,0:T(8,128)(2,1)S(1)} %get-tuple-element.45._), channel_id=1, source_target_pairs={{0,8},{1,5},{2,10},{3,7},{4,12},{5,1},{6,14},{7,3},{8,0},{9,13},{1... | collective-permute-start | bytes 344072 | tf_op jit(solution)/shard_map/ppermute | solution.py:227
  27.2 0.0 collective-permute-done.5.got
  27.2 1.6 %collective-permute-start.8 = (bf16[64,512]{1,0:T(8,128)(2,1)S(1)}, bf16[64,512]{1,0:T(8,128)(2,1)S(1)}, u32[]{:S(2)}, u32[]{:S(2)}) collective-permute-start(bf16[64,512]{1,0:T(8,128)(2,1)S(1)} %get-tuple-element.48._), channel_id=1, source_target_pairs={{0,8},{1,5},{2,10},{3,7},{4,12},{5,1},{6,14},{7,3},{8,0},{9,13},{1... | collective-permute-start | bytes 196616 | tf_op jit(solution)/shard_map/ppermute | solution.py:227
  28.8 0.0 collective-permute-done.6.got
  28.8 1.5 %collective-permute-start.9 = (bf16[64,384]{1,0:T(8,128)(2,1)S(1)}, bf16[64,384]{1,0:T(8,128)(2,1)S(1)}, u32[]{:S(2)}, u32[]{:S(2)}) collective-permute-start(bf16[64,384]{1,0:T(8,128)(2,1)S(1)} %get-tuple-element.50), channel_id=1, source_target_pairs={{0,8},{1,5},{2,10},{3,7},{4,12},{5,1},{6,14},{7,3},{8,0},{9,13},{1... | collective-permute-start | bytes 147464 | tf_op jit(solution)/shard_map/ppermute | solution.py:227
  30.3 3.6 %collective-permute-done.9.refs_5_ = bf16[64,384]{1,0:T(8,128)(2,1)S(1)} collective-permute-done((bf16[64,384]{1,0:T(8,128)(2,1)S(1)}, bf16[64,384]{1,0:T(8,128)(2,1)S(1)}, u32[]{:S(2)}, u32[]{:S(2)}) %collective-permute-start.9) | collective-permute-done | bytes 49184 | tf_op jit(solution)/shard_map/ppermute | solution.py:227
  33.9 0.8 %shard_map.58 = f32[64,1792]{1,0:T(8,128)} custom-call(f32[64,896]{1,0:T(8,128)S(1)} %get-tuple-element.43.refs_0_, f32[64,512]{1,0:T(8,128)S(1)} %get-tuple-element.46.refs_1_, f32[64,384]{1,0:T(8,128)S(1)} %get-tuple-element.49.refs_2_, bf16[64,896]{1,0:T(8,128)(2,1)S(1)} %collective-permute-done.7.refs_3_, ...), custom_call_target="tpu_custom_call" | custom-call | flops 114688 | bytes 1376256 | tf_op jit(solution)/shard_map/pallas_call | solution.py:195
  (9 shorter events, 0.2 us)
Async XLA Ops:
  0.0 2.2 %collective-permute-start = (bf16[32,2048]{1,0:T(8,128)(2,1)}, bf16[32,2048]{1,0:T(8,128)(2,1)S(1)}, u32[]{:S(2)}, u32[]{:S(2)}) collective-permute-start(bf16[32,2048]{1,0:T(8,128)(2,1)} %own_hbm.1), channel_id=1, source_target_pairs={{0,1},{1,0},{2,3},{3,2},{4,5},{5,4},{6,7},{7,6},{8,9},{9,8},{10,11... | collective-permute-start | bytes 393224 | tf_op jit(solution)/shard_map/ppermute | solution.py:234
  5.2 10.7 %collective-permute-start.1 = (bf16[256,896]{1,0:T(8,128)(2,1)S(1)}, bf16[256,896]{1,0:T(8,128)(2,1)S(1)}, u32[]{:S(2)}, u32[]{:S(2)}) collective-permute-start(bf16[256,896]{1,0:T(8,128)(2,1)S(1)} %get-tuple-element.35), channel_id=1, source_target_pairs={{0,4},{1,3},{2,6},{3,1},{4,0},{5,7},{6,2},{7,5},{8,12},{9,11},{10,... | collective-permute-start | bytes 1376264 | tf_op jit(solution)/shard_map/ppermute | solution.py:227
  10.0 9.9 %collective-permute-start.4 = (bf16[256,512]{1,0:T(8,128)(2,1)S(1)}, bf16[256,512]{1,0:T(8,128)(2,1)S(1)}, u32[]{:S(2)}, u32[]{:S(2)}) collective-permute-start(bf16[256,512]{1,0:T(8,128)(2,1)S(1)} %get-tuple-element.40), channel_id=1, source_target_pairs={{0,2},{1,9},{2,0},{3,11},{4,6},{5,13},{6,4},{7,15},{8,10},{9,1},{1... | collective-permute-start | bytes 786440 | tf_op jit(solution)/shard_map/ppermute | solution.py:227
  11.6 9.8 %collective-permute-start.3 = (bf16[256,384]{1,0:T(8,128)(2,1)S(1)}, bf16[256,384]{1,0:T(8,128)(2,1)S(1)}, u32[]{:S(2)}, u32[]{:S(2)}) collective-permute-start(bf16[256,384]{1,0:T(8,128)(2,1)S(1)} %get-tuple-element.39), channel_id=1, source_target_pairs={{0,4},{1,3},{2,6},{3,1},{4,0},{5,7},{6,2},{7,5},{8,12},{9,11},{10,... | collective-permute-start | bytes 589832 | tf_op jit(solution)/shard_map/ppermute | solution.py:227
  16.0 8.6 %collective-permute-start.2 = (bf16[128,896]{1,0:T(8,128)(2,1)S(1)}, bf16[128,896]{1,0:T(8,128)(2,1)S(1)}, u32[]{:S(2)}, u32[]{:S(2)}) collective-permute-start(bf16[128,896]{1,0:T(8,128)(2,1)S(1)} %get-tuple-element.37._), channel_id=1, source_target_pairs={{0,2},{1,9},{2,0},{3,11},{4,6},{5,13},{6,4},{7,15},{8,10},{9,1},{1... | collective-permute-start | bytes 688136 | tf_op jit(solution)/shard_map/ppermute | solution.py:227
  20.0 7.2 %collective-permute-start.5 = (bf16[128,512]{1,0:T(8,128)(2,1)S(1)}, bf16[128,512]{1,0:T(8,128)(2,1)S(1)}, u32[]{:S(2)}, u32[]{:S(2)}) collective-permute-start(bf16[128,512]{1,0:T(8,128)(2,1)S(1)} %get-tuple-element.41._), channel_id=1, source_target_pairs={{0,4},{1,3},{2,6},{3,1},{4,0},{5,7},{6,2},{7,5},{8,12},{9,11},{10,... | collective-permute-start | bytes 393224 | tf_op jit(solution)/shard_map/ppermute | solution.py:227
  21.4 7.3 %collective-permute-start.6 = (bf16[128,384]{1,0:T(8,128)(2,1)S(1)}, bf16[128,384]{1,0:T(8,128)(2,1)S(1)}, u32[]{:S(2)}, u32[]{:S(2)}) collective-permute-start(bf16[128,384]{1,0:T(8,128)(2,1)S(1)} %get-tuple-element.42._), channel_id=1, source_target_pairs={{0,2},{1,9},{2,0},{3,11},{4,6},{5,13},{6,4},{7,15},{8,10},{9,1},{1... | collective-permute-start | bytes 294920 | tf_op jit(solution)/shard_map/ppermute | solution.py:227
  24.7 9.2 %collective-permute-start.7 = (bf16[64,896]{1,0:T(8,128)(2,1)S(1)}, bf16[64,896]{1,0:T(8,128)(2,1)S(1)}, u32[]{:S(2)}, u32[]{:S(2)}) collective-permute-start(bf16[64,896]{1,0:T(8,128)(2,1)S(1)} %get-tuple-element.45._), channel_id=1, source_target_pairs={{0,8},{1,5},{2,10},{3,7},{4,12},{5,1},{6,14},{7,3},{8,0},{9,13},{1... | collective-permute-start | bytes 344072 | tf_op jit(solution)/shard_map/ppermute | solution.py:227
  27.2 6.7 %collective-permute-start.8 = (bf16[64,512]{1,0:T(8,128)(2,1)S(1)}, bf16[64,512]{1,0:T(8,128)(2,1)S(1)}, u32[]{:S(2)}, u32[]{:S(2)}) collective-permute-start(bf16[64,512]{1,0:T(8,128)(2,1)S(1)} %get-tuple-element.48._), channel_id=1, source_target_pairs={{0,8},{1,5},{2,10},{3,7},{4,12},{5,1},{6,14},{7,3},{8,0},{9,13},{1... | collective-permute-start | bytes 196616 | tf_op jit(solution)/shard_map/ppermute | solution.py:227
  28.8 5.1 %collective-permute-start.9 = (bf16[64,384]{1,0:T(8,128)(2,1)S(1)}, bf16[64,384]{1,0:T(8,128)(2,1)S(1)}, u32[]{:S(2)}, u32[]{:S(2)}) collective-permute-start(bf16[64,384]{1,0:T(8,128)(2,1)S(1)} %get-tuple-element.50), channel_id=1, source_target_pairs={{0,8},{1,5},{2,10},{3,7},{4,12},{5,1},{6,14},{7,3},{8,0},{9,13},{1... | collective-permute-start | bytes 147464 | tf_op jit(solution)/shard_map/ppermute | solution.py:227

commit v9 on v8

v9 whole, which is shorter than its diff:
```python
import functools

import jax
import jax.numpy as jnp
from jax import lax
from jax.experimental import pallas as pl
from jax.experimental.pallas import tpu as pltpu
from jax.sharding import PartitionSpec as P

TILE = 256
VMEM_LIMIT = 32 * 1024 * 1024
X, NEAR, FAR = 0, 1, 2
PLAN = [
    (3, (X, FAR, NEAR), (NEAR, X, FAR)),
    (2.5, (X, NEAR, FAR), (NEAR, X, FAR)),
    (1.5, (FAR, X, NEAR), (X, FAR, NEAR)),
]
ORDER = [(piece, stage) for stage in (1, 2) for piece in range(len(PLAN))]


def ranked(bits, fixed=0):
    out = [fixed]
    for b in reversed(bits):
        out = [c | (1 << b) for c in out] + out
    return out


def split_columns(cols):
    unit = 128
    total = sum(plan[0] for plan in PLAN)
    ends, done = [], 0
    for share, *_ in PLAN[:-1]:
        done += share
        ends.append(int(round(cols * done / total / unit)) * unit)
    ends.append(cols)
    return list(zip([0] + ends[:-1], ends))


def halves(bits):
    keep = ranked(bits[1:])
    return keep, [c | (1 << bits[0]) for c in keep]


def places(p, core, kept):
    keep, leave = halves(PLAN[0][1 + core])
    return [(leave + keep).index(c) for c in halves(PLAN[p][1 + core])[0 if kept else 1]]


def rows_of(prod, p, kept):
    block = prod.shape[0] // 8
    core = lax.axis_index("eig")
    parts = []
    for a, b in zip(places(p, 0, kept), places(p, 1, kept)):
        at = a * block if a == b else pl.multiple_of(jnp.where(core == 0, a, b) * block, block)
        parts.append(prod[pl.ds(at, block), :])
    return jnp.concatenate(parts, axis=0)


def dot_span(out, rows, eigs, cuts, span):
    col = span[0]
    while col < span[1]:
        i = max(i for i, cut in enumerate(cuts) if cut <= col)
        size = min(TILE, span[1] - col, cuts[i + 1] - col)
        out[:, col - span[0] : col - span[0] + size] = lax.dot_general(
            rows,
            eigs[i][col - cuts[i] : col - cuts[i] + size, :],
            (((1,), (1,)), ((), ())),
            preferred_element_type=jnp.float32,
        )
        col += size


def setup_kernel(n, per_chunk, lanc, width, order_hbm, own_hbm, lanc_hbm, eig_hbm, *rest):
    pick, own, lanc16, eig, order, sem = rest
    copies = [
        pltpu.make_async_copy(src, dst, sem.at[i])
        for i, (src, dst) in enumerate(
            [
                (order_hbm, order),
                (own_hbm, own),
                (lanc_hbm, lanc16),
                (eig_hbm.at[pl.ds(0, width)], eig),
            ]
        )
    ]
    for copy in copies:
        copy.start()
    me = lax.axis_index("grid")
    core = lax.axis_index("eig")
    bands = pick.shape[1]
    rest_bits = list(range(3, n.bit_length() - 1))
    classes = zip(*(sum(reversed(halves(PLAN[0][1 + i])), []) for i in range(2)))
    slots = []
    for pair in classes:
        for both in zip(*(ranked(rest_bits, c) for c in pair)):
            slots += [(both, j) for j in range(per_chunk)]
    col = lax.broadcasted_iota(jnp.int32, (2 * lanc, bands), 1)
    upper = lax.broadcasted_iota(jnp.int32, (2 * lanc, bands), 0) < lanc
    copies[0].wait()
    for i in range(0, len(slots), 2):
        want = []
        for r, j in slots[i : i + 2]:
            offset = jnp.where(core == 0, r[0], r[1])
            band = order[(me ^ offset) * per_chunk + j]
            want.append(lax.rem(band + core * (bands // 2), bands))
        hit = col == jnp.where(upper, want[0], want[1])
        pick[i * lanc : (i + 2) * lanc, :] = hit.astype(jnp.float32).astype(jnp.bfloat16)
    for copy in copies[1:]:
        copy.wait()


def fetch(eig_hbm, eig, sem, cuts):
    copies = []
    for i, (at, end) in enumerate(zip(cuts, cuts[1:])):
        if at == end:
            copies.append(None)
            continue
        part = pl.ds(at - cuts[0], end - at)
        copy = pltpu.make_async_copy(eig_hbm.at[pl.ds(at, end - at)], eig.at[part], sem.at[i])
        copy.start()
        copies.append(copy)
    return copies


def make_rows(prod, pick, own, other, lanc16, first):
    lanc = lanc16[...].astype(jnp.float32)
    chosen = lax.dot_general(
        pick[first : first + prod.shape[0], :],
        jnp.concatenate([own[...], other[...]], axis=0),
        (((1,), (0,)), ((), ())),
        preferred_element_type=jnp.float32,
    )
    value = chosen.reshape(-1, *lanc.shape) * lanc[None]
    prod[...] = value.reshape(chosen.shape).astype(jnp.bfloat16)


def first_kernel(width, pick, own, other, lanc16, eig, out, prod, acc):
    make_rows(prod, pick, own, other, lanc16, 0)
    dot_span(acc, prod[...], [eig], [0, width], (0, width))
    out[...] = acc[...].astype(out.dtype)


def send_kernel(cuts, pick, own, other, lanc16, half, eig_hbm, *rest):
    count = len(cuts) - 2
    outs, (prod, eig, acc, sem) = rest[:count], rest[count:]
    copies = fetch(eig_hbm, eig, sem, cuts[1:])
    first = half.shape[0]
    prod[:first, :] = half[...]
    make_rows(prod.at[first:, :], pick, own, other, lanc16, first)
    for i, out in enumerate(outs):
        rows = rows_of(prod, i + 1, False)
        copies[i].wait()
        part = acc.at[:, : out.shape[1]]
        dot_span(part, rows, [None, eig], [0, cuts[1], cuts[-1]], (cuts[i + 1], cuts[i + 2]))
        out[...] = part[...].astype(out.dtype)


def keep_kernel(p, first, prod, eig, out):
    dot_span(
        out, rows_of(prod, p, True), [eig], [0, eig.shape[0]], (first, first + out.shape[1])
    )


def add_kernel(kept, got, _, leave, keep):
    mid = leave.shape[0]
    leave[...] = (kept[:mid, :] + got[:mid, :].astype(jnp.float32)).astype(leave.dtype)
    keep[...] = kept[mid:, :] + got[mid:, :].astype(jnp.float32)


def finish_kernel(spans, *refs):
    count = len(spans)
    kept, came, out = refs[:count], refs[count : 2 * count], refs[-1]
    for (at, end), a, b in zip(spans, kept, came):
        out[:, at:end] = a[a.shape[0] - out.shape[0] :, :] + b[...].astype(jnp.float32)


VMEM_SPEC = pl.BlockSpec(memory_space=pltpu.VMEM)
SPECS = {
    True: pl.BlockSpec(memory_space=pltpu.HBM),
    False: VMEM_SPEC,
    None: pl.BlockSpec(memory_space=pl.ANY),
}


def kernel_call(body, ins, outs, scratch, cost):
    flops, moved = cost
    return pl.pallas_call(
        body,
        out_shape=[jax.ShapeDtypeStruct(*out) for out in outs],
        in_specs=[SPECS[far] for _, far in ins],
        out_specs=[VMEM_SPEC] * len(outs),
        scratch_shapes=scratch,
        compiler_params=pltpu.CompilerParams(vmem_limit_bytes=VMEM_LIMIT),
        cost_estimate=pl.CostEstimate(flops=flops, bytes_accessed=moved, transcendentals=0),
    )(
        *(
            pltpu.with_memory_space_constraint(x, pltpu.HBM) if far else x
            for x, far in ins
        )
    )


def per_device(n, eigvecs, lanczos, bands, band_order):
    cols, depth = eigvecs.shape
    lanc = lanczos.shape[0]
    per_chunk = band_order.shape[0] // n
    rows = band_order.shape[0] * lanc
    spans = split_columns(cols)
    cuts = [0] + [end for _, end in spans]
    widths = [end - at for at, end in spans]
    bf16 = jnp.bfloat16

    def exchange(value, p, stage):
        pairs = []
        for i in range(n):
            for core in range(2):
                bit = PLAN[p][1 + core][stage] if stage < 3 else stage
                pairs.append((2 * i + core, 2 * (i ^ (1 << bit)) + core))
        return lax.ppermute(value, ("grid", "eig"), pairs)

    def flops(width):
        return rows * width * depth

    other = lax.ppermute(bands, "eig", [(0, 1), (1, 0)])
    pick, own, lanc16, eig = kernel_call(
        functools.partial(setup_kernel, n, per_chunk, lanc, widths[0]),
        [(band_order, True), (bands, True), (lanczos, True), (eigvecs, True)],
        [
            ((rows, 2 * bands.shape[0]), bf16),
            (bands.shape, bf16),
            (lanczos.shape, bf16),
            ((widths[0], depth), bf16),
        ],
        [pltpu.SMEM(band_order.shape, jnp.int32), pltpu.SemaphoreType.DMA((4,))],
        (0, 2 * widths[0] * depth),
    )
    sources = [(x, False) for x in (pick, own, other, lanc16)]
    send, half = kernel_call(
        functools.partial(first_kernel, widths[0]),
        sources + [(eig, False)],
        [((rows // 2, widths[0]), bf16), ((rows // 2, depth), bf16)],
        [pltpu.VMEM((rows // 2, widths[0]), jnp.float32)],
        (flops(widths[0]), 2 * widths[0] * depth),
    )
    *sends, prod, eig_rest = kernel_call(
        functools.partial(send_kernel, cuts),
        sources + [(half, False), (eigvecs, True)],
        [((rows // 2, w), bf16) for w in widths[1:]]
        + [((rows, depth), bf16), ((cols - widths[0], depth), bf16)],
        [
            pltpu.VMEM((rows // 2, max(widths[1:])), jnp.float32),
            pltpu.SemaphoreType.DMA((len(PLAN) - 1,)),
        ],
        (flops(sum(widths[1:])), 2 * sum(widths[1:]) * depth),
    )
    got = [exchange(s, p, 0) for p, s in enumerate([send, *sends])]
    value = []
    for p, width in enumerate(widths):
        value += kernel_call(
            functools.partial(keep_kernel, p, cuts[p] - cuts[min(p, 1)]),
            [(prod, False), (eig_rest if p else eig, False)],
            [((rows // 2, width), jnp.float32)],
            [],
            (flops(width), 2 * width * depth),
        )
    later = range(3, n.bit_length() - 1)
    token = prod
    for p, stage in ORDER + [(p, stage) for stage in later for p in range(len(PLAN))]:
        part = value[p].shape[0] // 2
        size = part * widths[p]
        leave, value[p] = kernel_call(
            add_kernel,
            [(value[p], False), (got[p], False), (token, None)],
            [((part, widths[p]), bf16 if stage < 3 else jnp.float32)]
            + [((part, widths[p]), jnp.float32)],
            [],
            (2 * size, 18 * size),
        )
        token = leave
        got[p] = exchange(leave, p, stage)
    outs = list(zip(value, got))
    (result,) = kernel_call(
        functools.partial(finish_kernel, spans),
        [(value, False) for value, _ in outs] + [(came, False) for _, came in outs],
        [((rows // n, cols), jnp.float32)],
        [],
        (rows // n * cols, 12 * rows // n * cols),
    )
    return result.reshape(per_chunk, lanc, cols)


def solution(mesh):
    in_specs = (
        P("eig", ("rep", "grid")),
        P(None, ("rep", "grid")),
        P("eig", ("rep", "grid")),
        P("rep"),
    )
    out_specs = P(("rep", "grid"), None, "eig")
    return jax.shard_map(
        functools.partial(per_device, mesh.shape["grid"]),
        mesh=mesh,
        in_specs=in_specs,
        out_specs=out_specs,
        check_vma=False,
    )
```

time: 34.9 us -> 36.4 us (1.043)
  the two profiles are of different devices: /device:TPU:0 before, /device:TPU:6 now
where the time goes in v9:
time: 36.4 us; the launch traced here: 36.2 us
  starting transfers between devices  15.3 us (42%)
  Pallas kernels  10.9 us (30%)
  waiting for transfers between devices  9.88 us (27%)
    ppermute x9, starting transfers between devices, exchange(): return lax.ppermute(value, ('grid', 'eig'), pairs)  15.3 us
    pallas_call x13, Pallas kernels, kernel_call(): pl.pallas_call(body, out_shape=[jax.ShapeDtypeStruct(*out) for out in out...  10.9 us
    ppermute x9, waiting for transfers between devices, exchange(): return lax.ppermute(value, ('grid', 'eig'), pairs)  9.88 us
  transfers between devices with their start and end apart: 10, of which 3 were waited for; matrix products, arithmetic and copies ran while one was open for 0% of the time, Pallas kernels for 24%

profile of v9, /device:TPU:6, one launch (start us, length us, event | category | flops | bytes accessed | tf_op | source)
XLA Modules:
  0.0 36.2 jit_solution(11958124618438121405)
XLA Ops:
  0.0 0.0 collective-permute-start
  0.0 2.0 %shard_map.46 = (bf16[512,64]{1,0:T(8,128)(2,1)S(1)}, bf16[32,2048]{1,0:T(8,128)(2,1)S(1)}, bf16[8,2048]{1,0:T(8,128)(2,1)S(1)}, bf16[768,2048]{1,0:T(8,128)(2,1)S(1)}) custom-call(s32[64]{0:T(128)} %order_hbm.1, bf16[32,2048]{1,0:T(8,128)(2,1)} %own_hbm.1, bf16[8,2048]{1,0:T(8,128)(2,1)} %lanc_hbm.1, bf16[1792,2048]{1,0:T(8,128)(2,1)} %eig_hbm.3), custom_call_target="tpu_custom_call" | custom-call | bytes 3145728 | tf_op jit(solution)/shard_map/pallas_call | solution.py:187
  2.0 0.0 collective-permute-done.other
  2.0 1.3 %shard_map.47 = (bf16[256,768]{1,0:T(8,128)(2,1)S(1)}, bf16[256,2048]{1,0:T(8,128)(2,1)S(1)}) custom-call(bf16[512,64]{1,0:T(8,128)(2,1)S(1)} %get-tuple-element.27.pick, bf16[32,2048]{1,0:T(8,128)(2,1)S(1)} %get-tuple-element.28.own, bf16[32,2048]{1,0:T(8,128)(2,1)S(1)} %collective-permute-done.other, bf16[8,2048]{1,0:T(8,128)(2,1)S(1)} %get-tuple-element.29.lanc16, ...), custom_call_target="tpu_custom_call" | custom-call | flops 805306368 | bytes 3145728 | tf_op jit(solution)/shard_map/pallas_call | solution.py:187
  3.4 0.6 %collective-permute-start.1 = (bf16[256,768]{1,0:T(8,128)(2,1)S(1)}, bf16[256,768]{1,0:T(8,128)(2,1)S(1)}, u32[]{:S(2)}, u32[]{:S(2)}) collective-permute-start(bf16[256,768]{1,0:T(8,128)(2,1)S(1)} %get-tuple-element.33), channel_id=1, source_target_pairs={{0,2},{1,5},{2,0},{3,7},{4,6},{5,1},{6,4},{7,3},{8,10},{9,13},{10,... | collective-permute-start | bytes 1179656 | tf_op jit(solution)/shard_map/ppermute | solution.py:219
  4.0 3.8 %shard_map.48 = (bf16[256,640]{1,0:T(8,128)(2,1)S(1)}, bf16[256,384]{1,0:T(8,128)(2,1)S(1)}, bf16[512,2048]{1,0:T(8,128)(2,1)S(1)}, bf16[1024,2048]{1,0:T(8,128)(2,1)S(1)}) custom-call(bf16[512,64]{1,0:T(8,128)(2,1)S(1)} %get-tuple-element.27.pick, bf16[32,2048]{1,0:T(8,128)(2,1)S(1)} %get-tuple-element.28.own, ...), custom_call_target="tpu_custom_call" | custom-call | flops 1073741824 | bytes 4194304 | tf_op jit(solution)/shard_map/pallas_call | solution.py:187
  7.8 1.5 %collective-permute-start.4 = (bf16[256,640]{1,0:T(8,128)(2,1)S(1)}, bf16[256,640]{1,0:T(8,128)(2,1)S(1)}, u32[]{:S(2)}, u32[]{:S(2)}) collective-permute-start(bf16[256,640]{1,0:T(8,128)(2,1)S(1)} %get-tuple-element.38), channel_id=1, source_target_pairs={{0,2},{1,5},{2,0},{3,7},{4,6},{5,1},{6,4},{7,3},{8,10},{9,13},{10,... | collective-permute-start | bytes 983048 | tf_op jit(solution)/shard_map/ppermute | solution.py:219
  9.3 2.6 %collective-permute-start.3 = (bf16[256,384]{1,0:T(8,128)(2,1)S(1)}, bf16[256,384]{1,0:T(8,128)(2,1)S(1)}, u32[]{:S(2)}, u32[]{:S(2)}) collective-permute-start(bf16[256,384]{1,0:T(8,128)(2,1)S(1)} %get-tuple-element.37), channel_id=1, source_target_pairs={{0,8},{1,3},{2,10},{3,1},{4,12},{5,7},{6,14},{7,5},{8,0},{9,11},{1... | collective-permute-start | bytes 589832 | tf_op jit(solution)/shard_map/ppermute | solution.py:219
  11.9 1.0 %shard_map.49.kept = f32[256,768]{1,0:T(8,128)S(1)} custom-call(bf16[512,2048]{1,0:T(8,128)(2,1)S(1)} %get-tuple-element.32.prod._, bf16[768,2048]{1,0:T(8,128)(2,1)S(1)} %get-tuple-element.30.eig), custom_call_target="tpu_custom_call" | custom-call | flops 805306368 | bytes 3145728 | tf_op jit(solution)/shard_map/pallas_call | solution.py:187
  12.9 0.0 collective-permute-done.1.got
  13.0 0.1 shard_map.50
  13.0 0.9 %collective-permute-start.2 = (bf16[128,768]{1,0:T(8,128)(2,1)S(1)}, bf16[128,768]{1,0:T(8,128)(2,1)S(1)}, u32[]{:S(2)}, u32[]{:S(2)}) collective-permute-start(bf16[128,768]{1,0:T(8,128)(2,1)S(1)} %get-tuple-element.35._), channel_id=1, source_target_pairs={{0,8},{1,3},{2,10},{3,1},{4,12},{5,7},{6,14},{7,5},{8,0},{9,11},{1... | collective-permute-start | bytes 589832 | tf_op jit(solution)/shard_map/ppermute | solution.py:219
  14.0 1.0 %shard_map.52.kept = f32[256,640]{1,0:T(8,128)S(1)} custom-call(bf16[512,2048]{1,0:T(8,128)(2,1)S(1)} %get-tuple-element.32.prod._, bf16[1024,2048]{1,0:T(8,128)(2,1)S(1)} %get-tuple-element.36.eig), custom_call_target="tpu_custom_call" | custom-call | flops 671088640 | bytes 2621440 | tf_op jit(solution)/shard_map/pallas_call | solution.py:187
  15.0 3.1 %collective-permute-done.4.got = bf16[256,640]{1,0:T(8,128)(2,1)S(1)} collective-permute-done((bf16[256,640]{1,0:T(8,128)(2,1)S(1)}, bf16[256,640]{1,0:T(8,128)(2,1)S(1)}, u32[]{:S(2)}, u32[]{:S(2)}) %collective-permute-start.4) | collective-permute-done | bytes 327712 | tf_op jit(solution)/shard_map/ppermute | solution.py:219
  18.1 0.1 shard_map.53
  18.1 1.6 %collective-permute-start.5 = (bf16[128,640]{1,0:T(8,128)(2,1)S(1)}, bf16[128,640]{1,0:T(8,128)(2,1)S(1)}, u32[]{:S(2)}, u32[]{:S(2)}) collective-permute-start(bf16[128,640]{1,0:T(8,128)(2,1)S(1)} %get-tuple-element.39._), channel_id=1, source_target_pairs={{0,4},{1,3},{2,6},{3,1},{4,0},{5,7},{6,2},{7,5},{8,12},{9,11},{10,... | collective-permute-start | bytes 491528 | tf_op jit(solution)/shard_map/ppermute | solution.py:219
  19.7 0.7 %shard_map.51.kept = f32[256,384]{1,0:T(8,128)S(1)} custom-call(bf16[512,2048]{1,0:T(8,128)(2,1)S(1)} %get-tuple-element.32.prod._, bf16[1024,2048]{1,0:T(8,128)(2,1)S(1)} %get-tuple-element.36.eig), custom_call_target="tpu_custom_call" | custom-call | flops 402653184 | bytes 1572864 | tf_op jit(solution)/shard_map/pallas_call | solution.py:187
  20.5 1.9 %collective-permute-start.6 = (bf16[128,384]{1,0:T(8,128)(2,1)S(1)}, bf16[128,384]{1,0:T(8,128)(2,1)S(1)}, u32[]{:S(2)}, u32[]{:S(2)}) collective-permute-start(bf16[128,384]{1,0:T(8,128)(2,1)S(1)} %get-tuple-element.40._), channel_id=1, source_target_pairs={{0,2},{1,9},{2,0},{3,11},{4,6},{5,13},{6,4},{7,15},{8,10},{9,1},{1... | collective-permute-start | bytes 294920 | tf_op jit(solution)/shard_map/ppermute | solution.py:219
  22.4 2.7 %collective-permute-done.2.got = bf16[128,768]{1,0:T(8,128)(2,1)S(1)} collective-permute-done((bf16[128,768]{1,0:T(8,128)(2,1)S(1)}, bf16[128,768]{1,0:T(8,128)(2,1)S(1)}, u32[]{:S(2)}, u32[]{:S(2)}) %collective-permute-start.2) | collective-permute-done | bytes 196640 | tf_op jit(solution)/shard_map/ppermute | solution.py:219
  25.2 1.6 %collective-permute-start.7 = (bf16[64,768]{1,0:T(8,128)(2,1)S(1)}, bf16[64,768]{1,0:T(8,128)(2,1)S(1)}, u32[]{:S(2)}, u32[]{:S(2)}) collective-permute-start(bf16[64,768]{1,0:T(8,128)(2,1)S(1)} %get-tuple-element.43._), channel_id=1, source_target_pairs={{0,4},{1,9},{2,6},{3,11},{4,0},{5,13},{6,2},{7,15},{8,12},{9,1},{1... | collective-permute-start | bytes 294920 | tf_op jit(solution)/shard_map/ppermute | solution.py:219
  26.8 4.5 %collective-permute-start.8 = (bf16[64,640]{1,0:T(8,128)(2,1)S(1)}, bf16[64,640]{1,0:T(8,128)(2,1)S(1)}, u32[]{:S(2)}, u32[]{:S(2)}) collective-permute-start(bf16[64,640]{1,0:T(8,128)(2,1)S(1)} %get-tuple-element.46._), channel_id=1, source_target_pairs={{0,8},{1,9},{2,10},{3,11},{4,12},{5,13},{6,14},{7,15},{8,0},{9,1},... | collective-permute-start | bytes 245768 | tf_op jit(solution)/shard_map/ppermute | solution.py:219
  31.3 0.1 collective-permute-start.9
  31.4 4.1 %collective-permute-done.9.refs_5_ = bf16[64,384]{1,0:T(8,128)(2,1)S(1)} collective-permute-done((bf16[64,384]{1,0:T(8,128)(2,1)S(1)}, bf16[64,384]{1,0:T(8,128)(2,1)S(1)}, u32[]{:S(2)}, u32[]{:S(2)}) %collective-permute-start.9) | collective-permute-done | bytes 49184 | tf_op jit(solution)/shard_map/ppermute | solution.py:219
  35.4 0.8 %shard_map.58 = f32[64,1792]{1,0:T(8,128)} custom-call(f32[64,768]{1,0:T(8,128)S(1)} %get-tuple-element.41.refs_0_, f32[64,640]{1,0:T(8,128)S(1)} %get-tuple-element.44.refs_1_, f32[64,384]{1,0:T(8,128)S(1)} %get-tuple-element.47.refs_2_, bf16[64,768]{1,0:T(8,128)(2,1)S(1)} %collective-permute-done.7.refs_3_, ...), custom_call_target="tpu_custom_call" | custom-call | flops 114688 | bytes 1376256 | tf_op jit(solution)/shard_map/pallas_call | solution.py:187
  (9 shorter events, 0.1 us)
Async XLA Ops:
  0.0 2.0 %collective-permute-start = (bf16[32,2048]{1,0:T(8,128)(2,1)}, bf16[32,2048]{1,0:T(8,128)(2,1)S(1)}, u32[]{:S(2)}, u32[]{:S(2)}) collective-permute-start(bf16[32,2048]{1,0:T(8,128)(2,1)} %own_hbm.1), channel_id=1, source_target_pairs={{0,1},{1,0},{2,3},{3,2},{4,5},{5,4},{6,7},{7,6},{8,9},{9,8},{10,11... | collective-permute-start | bytes 393224 | tf_op jit(solution)/shard_map/ppermute | solution.py:224
  3.4 9.5 %collective-permute-start.1 = (bf16[256,768]{1,0:T(8,128)(2,1)S(1)}, bf16[256,768]{1,0:T(8,128)(2,1)S(1)}, u32[]{:S(2)}, u32[]{:S(2)}) collective-permute-start(bf16[256,768]{1,0:T(8,128)(2,1)S(1)} %get-tuple-element.33), channel_id=1, source_target_pairs={{0,2},{1,5},{2,0},{3,7},{4,6},{5,1},{6,4},{7,3},{8,10},{9,13},{10,... | collective-permute-start | bytes 1179656 | tf_op jit(solution)/shard_map/ppermute | solution.py:219
  7.8 10.3 %collective-permute-start.4 = (bf16[256,640]{1,0:T(8,128)(2,1)S(1)}, bf16[256,640]{1,0:T(8,128)(2,1)S(1)}, u32[]{:S(2)}, u32[]{:S(2)}) collective-permute-start(bf16[256,640]{1,0:T(8,128)(2,1)S(1)} %get-tuple-element.38), channel_id=1, source_target_pairs={{0,2},{1,5},{2,0},{3,7},{4,6},{5,1},{6,4},{7,3},{8,10},{9,13},{10,... | collective-permute-start | bytes 983048 | tf_op jit(solution)/shard_map/ppermute | solution.py:219
  9.3 11.1 %collective-permute-start.3 = (bf16[256,384]{1,0:T(8,128)(2,1)S(1)}, bf16[256,384]{1,0:T(8,128)(2,1)S(1)}, u32[]{:S(2)}, u32[]{:S(2)}) collective-permute-start(bf16[256,384]{1,0:T(8,128)(2,1)S(1)} %get-tuple-element.37), channel_id=1, source_target_pairs={{0,8},{1,3},{2,10},{3,1},{4,12},{5,7},{6,14},{7,5},{8,0},{9,11},{1... | collective-permute-start | bytes 589832 | tf_op jit(solution)/shard_map/ppermute | solution.py:219
  13.0 12.1 %collective-permute-start.2 = (bf16[128,768]{1,0:T(8,128)(2,1)S(1)}, bf16[128,768]{1,0:T(8,128)(2,1)S(1)}, u32[]{:S(2)}, u32[]{:S(2)}) collective-permute-start(bf16[128,768]{1,0:T(8,128)(2,1)S(1)} %get-tuple-element.35._), channel_id=1, source_target_pairs={{0,8},{1,3},{2,10},{3,1},{4,12},{5,7},{6,14},{7,5},{8,0},{9,11},{1... | collective-permute-start | bytes 589832 | tf_op jit(solution)/shard_map/ppermute | solution.py:219
  18.1 8.6 %collective-permute-start.5 = (bf16[128,640]{1,0:T(8,128)(2,1)S(1)}, bf16[128,640]{1,0:T(8,128)(2,1)S(1)}, u32[]{:S(2)}, u32[]{:S(2)}) collective-permute-start(bf16[128,640]{1,0:T(8,128)(2,1)S(1)} %get-tuple-element.39._), channel_id=1, source_target_pairs={{0,4},{1,3},{2,6},{3,1},{4,0},{5,7},{6,2},{7,5},{8,12},{9,11},{10,... | collective-permute-start | bytes 491528 | tf_op jit(solution)/shard_map/ppermute | solution.py:219
  20.5 10.7 %collective-permute-start.6 = (bf16[128,384]{1,0:T(8,128)(2,1)S(1)}, bf16[128,384]{1,0:T(8,128)(2,1)S(1)}, u32[]{:S(2)}, u32[]{:S(2)}) collective-permute-start(bf16[128,384]{1,0:T(8,128)(2,1)S(1)} %get-tuple-element.40._), channel_id=1, source_target_pairs={{0,2},{1,9},{2,0},{3,11},{4,6},{5,13},{6,4},{7,15},{8,10},{9,1},{1... | collective-permute-start | bytes 294920 | tf_op jit(solution)/shard_map/ppermute | solution.py:219
  25.2 10.3 %collective-permute-start.7 = (bf16[64,768]{1,0:T(8,128)(2,1)S(1)}, bf16[64,768]{1,0:T(8,128)(2,1)S(1)}, u32[]{:S(2)}, u32[]{:S(2)}) collective-permute-start(bf16[64,768]{1,0:T(8,128)(2,1)S(1)} %get-tuple-element.43._), channel_id=1, source_target_pairs={{0,4},{1,9},{2,6},{3,11},{4,0},{5,13},{6,2},{7,15},{8,12},{9,1},{1... | collective-permute-start | bytes 294920 | tf_op jit(solution)/shard_map/ppermute | solution.py:219
  26.8 8.7 %collective-permute-start.8 = (bf16[64,640]{1,0:T(8,128)(2,1)S(1)}, bf16[64,640]{1,0:T(8,128)(2,1)S(1)}, u32[]{:S(2)}, u32[]{:S(2)}) collective-permute-start(bf16[64,640]{1,0:T(8,128)(2,1)S(1)} %get-tuple-element.46._), channel_id=1, source_target_pairs={{0,8},{1,9},{2,10},{3,11},{4,12},{5,13},{6,14},{7,15},{8,0},{9,1},... | collective-permute-start | bytes 245768 | tf_op jit(solution)/shard_map/ppermute | solution.py:219
  31.3 4.2 %collective-permute-start.9 = (bf16[64,384]{1,0:T(8,128)(2,1)S(1)}, bf16[64,384]{1,0:T(8,128)(2,1)S(1)}, u32[]{:S(2)}, u32[]{:S(2)}) collective-permute-start(bf16[64,384]{1,0:T(8,128)(2,1)S(1)} %get-tuple-element.48), channel_id=1, source_target_pairs={{0,4},{1,5},{2,6},{3,7},{4,0},{5,1},{6,2},{7,3},{8,12},{9,13},{10,... | collective-permute-start | bytes 147464 | tf_op jit(solution)/shard_map/ppermute | solution.py:219

commit v10 on v9

--- a/solution.py
+++ b/solution.py
@@ -11,9 +11,9 @@
 VMEM_LIMIT = 32 * 1024 * 1024
 X, NEAR, FAR = 0, 1, 2
 PLAN = [
-    (3, (X, FAR, NEAR), (NEAR, X, FAR)),
-    (2.5, (X, NEAR, FAR), (NEAR, X, FAR)),
-    (1.5, (FAR, X, NEAR), (X, FAR, NEAR)),
+    (3.5, (NEAR, X, FAR), (X, FAR, NEAR)),
+    (2, (X, NEAR, FAR), (FAR, X, NEAR)),
+    (1.5, (NEAR, X, FAR), (X, FAR, NEAR)),
 ]
 ORDER = [(piece, stage) for stage in (1, 2) for piece in range(len(PLAN))]
 
@@ -56,18 +56,20 @@
     return jnp.concatenate(parts, axis=0)
 
 
-def dot_span(out, rows, eigs, cuts, span):
-    col = span[0]
-    while col < span[1]:
-        i = max(i for i, cut in enumerate(cuts) if cut <= col)
-        size = min(TILE, span[1] - col, cuts[i + 1] - col)
-        out[:, col - span[0] : col - span[0] + size] = lax.dot_general(
+def tiles_of(width):
+    return [(at, min(TILE, width - at)) for at in range(0, width, TILE)]
+
+
+def dot_tiles(out, rows, eig, first, waits=()):
+    for i, (at, size) in enumerate(tiles_of(out.shape[1])):
+        if waits:
+            waits[i].wait()
+        out[:, at : at + size] = lax.dot_general(
             rows,
-            eigs[i][col - cuts[i] : col - cuts[i] + size, :],
+            eig[first + at : first + at + size, :],
             (((1,), (1,)), ((), ())),
             preferred_element_type=jnp.float32,
         )
-        col += size
 
 
 def setup_kernel(n, per_chunk, lanc, width, order_hbm, own_hbm, lanc_hbm, eig_hbm, *rest):
@@ -109,19 +111,6 @@
         copy.wait()
 
 
-def fetch(eig_hbm, eig, sem, cuts):
-    copies = []
-    for i, (at, end) in enumerate(zip(cuts, cuts[1:])):
-        if at == end:
-            copies.append(None)
-            continue
-        part = pl.ds(at - cuts[0], end - at)
-        copy = pltpu.make_async_copy(eig_hbm.at[pl.ds(at, end - at)], eig.at[part], sem.at[i])
-        copy.start()
-        copies.append(copy)
-    return copies
-
-
 def make_rows(prod, pick, own, other, lanc16, first):
     lanc = lanc16[...].astype(jnp.float32)
     chosen = lax.dot_general(
@@ -134,31 +123,35 @@
     prod[...] = value.reshape(chosen.shape).astype(jnp.bfloat16)
 
 
-def first_kernel(width, pick, own, other, lanc16, eig, out, prod, acc):
+def first_kernel(pick, own, other, lanc16, eig, out, prod, acc):
     make_rows(prod, pick, own, other, lanc16, 0)
-    dot_span(acc, prod[...], [eig], [0, width], (0, width))
+    dot_tiles(acc, prod[...], eig, 0)
     out[...] = acc[...].astype(out.dtype)
 
 
 def send_kernel(cuts, pick, own, other, lanc16, half, eig_hbm, *rest):
     count = len(cuts) - 2
     outs, (prod, eig, acc, sem) = rest[:count], rest[count:]
-    copies = fetch(eig_hbm, eig, sem, cuts[1:])
+    copies = []
+    for cut, end in zip(cuts[1:], cuts[2:]):
+        copies.append([])
+        for at, size in tiles_of(end - cut):
+            source = eig_hbm.at[pl.ds(cut + at, size)]
+            target = eig.at[pl.ds(cut - cuts[1] + at, size)]
+            copy = pltpu.make_async_copy(source, target, sem.at[sum(map(len, copies))])
+            copy.start()
+            copies[-1].append(copy)
     first = half.shape[0]
     prod[:first, :] = half[...]
     make_rows(prod.at[first:, :], pick, own, other, lanc16, first)
     for i, out in enumerate(outs):
-        rows = rows_of(prod, i + 1, False)
-        copies[i].wait()
         part = acc.at[:, : out.shape[1]]
-        dot_span(part, rows, [None, eig], [0, cuts[1], cuts[-1]], (cuts[i + 1], cuts[i + 2]))
+        dot_tiles(part, rows_of(prod, i + 1, False), eig, cuts[i + 1] - cuts[1], copies[i])
         out[...] = part[...].astype(out.dtype)
 
 
 def keep_kernel(p, first, prod, eig, out):
-    dot_span(
-        out, rows_of(prod, p, True), [eig], [0, eig.shape[0]], (first, first + out.shape[1])
-    )
+    dot_tiles(out, rows_of(prod, p, True), eig, first)
 
 
 def add_kernel(kept, got, _, leave, keep):
@@ -236,7 +229,7 @@
     )
     sources = [(x, False) for x in (pick, own, other, lanc16)]
     send, half = kernel_call(
-        functools.partial(first_kernel, widths[0]),
+        first_kernel,
         sources + [(eig, False)],
         [((rows // 2, widths[0]), bf16), ((rows // 2, depth), bf16)],
         [pltpu.VMEM((rows // 2, widths[0]), jnp.float32)],
@@ -249,7 +242,7 @@
         + [((rows, depth), bf16), ((cols - widths[0], depth), bf16)],
         [
             pltpu.VMEM((rows // 2, max(widths[1:])), jnp.float32),
-            pltpu.SemaphoreType.DMA((len(PLAN) - 1,)),
+            pltpu.SemaphoreType.DMA((sum(len(tiles_of(w)) for w in widths[1:]),)),
         ],
         (flops(sum(widths[1:])), 2 * sum(widths[1:]) * depth),
     )

time: 36.4 us -> 35.5 us (0.975)
  the two profiles are of different devices: /device:TPU:6 before, /device:TPU:0 now
where the time goes in v10:
time: 35.5 us; the launch traced here: 35.4 us
  starting transfers between devices  14.4 us (41%)
  Pallas kernels  11.6 us (33%)
  waiting for transfers between devices  9.2 us (26%)
    ppermute x9, starting transfers between devices, exchange(): return lax.ppermute(value, ('grid', 'eig'), pairs)  13.9 us
    pallas_call x13, Pallas kernels, kernel_call(): pl.pallas_call(body, out_shape=[jax.ShapeDtypeStruct(*out) for out in out...  11.6 us
    ppermute x9, waiting for transfers between devices, exchange(): return lax.ppermute(value, ('grid', 'eig'), pairs)  9.2 us
  transfers between devices with their start and end apart: 10, of which 3 were waited for; matrix products, arithmetic and copies ran while one was open for 0% of the time, Pallas kernels for 26%

profile of v10, /device:TPU:0, one launch (start us, length us, event | category | flops | bytes accessed | tf_op | source)
XLA Modules:
  0.0 35.4 jit_solution(5849438799681298208)
XLA Ops:
  0.0 0.5 %collective-permute-start = (bf16[32,2048]{1,0:T(8,128)(2,1)}, bf16[32,2048]{1,0:T(8,128)(2,1)S(1)}, u32[]{:S(2)}, u32[]{:S(2)}) collective-permute-start(bf16[32,2048]{1,0:T(8,128)(2,1)} %own_hbm.1), channel_id=1, source_target_pairs={{0,1},{1,0},{2,3},{3,2},{4,5},{5,4},{6,7},{7,6},{8,9},{9,8},{10,11... | collective-permute-start | bytes 393224 | tf_op jit(solution)/shard_map/ppermute | solution.py:217
  0.5 2.2 %shard_map.46 = (bf16[512,64]{1,0:T(8,128)(2,1)S(1)}, bf16[32,2048]{1,0:T(8,128)(2,1)S(1)}, bf16[8,2048]{1,0:T(8,128)(2,1)S(1)}, bf16[896,2048]{1,0:T(8,128)(2,1)S(1)}) custom-call(s32[64]{0:T(128)} %order_hbm.1, bf16[32,2048]{1,0:T(8,128)(2,1)} %own_hbm.1, bf16[8,2048]{1,0:T(8,128)(2,1)} %lanc_hbm.1, bf16[1792,2048]{1,0:T(8,128)(2,1)} %eig_hbm.3), custom_call_target="tpu_custom_call" | custom-call | bytes 3670016 | tf_op jit(solution)/shard_map/pallas_call | solution.py:180
  2.6 1.5 %shard_map.47 = (bf16[256,896]{1,0:T(8,128)(2,1)S(1)}, bf16[256,2048]{1,0:T(8,128)(2,1)S(1)}) custom-call(bf16[512,64]{1,0:T(8,128)(2,1)S(1)} %get-tuple-element.27.pick, bf16[32,2048]{1,0:T(8,128)(2,1)S(1)} %get-tuple-element.28.own, bf16[32,2048]{1,0:T(8,128)(2,1)S(1)} %collective-permute-done.other, bf16[8,2048]{1,0:T(8,128)(2,1)S(1)} %get-tuple-element.29.lanc16, ...), custom_call_target="tpu_custom_call" | custom-call | flops 939524096 | bytes 3670016 | tf_op jit(solution)/shard_map/pallas_call | solution.py:180
  4.1 2.6 %collective-permute-start.1 = (bf16[256,896]{1,0:T(8,128)(2,1)S(1)}, bf16[256,896]{1,0:T(8,128)(2,1)S(1)}, u32[]{:S(2)}, u32[]{:S(2)}) collective-permute-start(bf16[256,896]{1,0:T(8,128)(2,1)S(1)} %get-tuple-element.33), channel_id=1, source_target_pairs={{0,4},{1,3},{2,6},{3,1},{4,0},{5,7},{6,2},{7,5},{8,12},{9,11},{10,... | collective-permute-start | bytes 1376264 | tf_op jit(solution)/shard_map/ppermute | solution.py:212
  6.8 4.2 %shard_map.48 = (bf16[256,512]{1,0:T(8,128)(2,1)S(1)}, bf16[256,384]{1,0:T(8,128)(2,1)S(1)}, bf16[512,2048]{1,0:T(8,128)(2,1)S(1)}, bf16[896,2048]{1,0:T(8,128)(2,1)S(1)}) custom-call(bf16[512,64]{1,0:T(8,128)(2,1)S(1)} %get-tuple-element.27.pick, bf16[32,2048]{1,0:T(8,128)(2,1)S(1)} %get-tuple-element.28.own, ...), custom_call_target="tpu_custom_call" | custom-call | flops 939524096 | bytes 3670016 | tf_op jit(solution)/shard_map/pallas_call | solution.py:180
  11.0 1.6 %collective-permute-start.4 = (bf16[256,512]{1,0:T(8,128)(2,1)S(1)}, bf16[256,512]{1,0:T(8,128)(2,1)S(1)}, u32[]{:S(2)}, u32[]{:S(2)}) collective-permute-start(bf16[256,512]{1,0:T(8,128)(2,1)S(1)} %get-tuple-element.38), channel_id=1, source_target_pairs={{0,2},{1,9},{2,0},{3,11},{4,6},{5,13},{6,4},{7,15},{8,10},{9,1},{1... | collective-permute-start | bytes 786440 | tf_op jit(solution)/shard_map/ppermute | solution.py:212
  12.5 0.5 %collective-permute-start.3 = (bf16[256,384]{1,0:T(8,128)(2,1)S(1)}, bf16[256,384]{1,0:T(8,128)(2,1)S(1)}, u32[]{:S(2)}, u32[]{:S(2)}) collective-permute-start(bf16[256,384]{1,0:T(8,128)(2,1)S(1)} %get-tuple-element.37), channel_id=1, source_target_pairs={{0,4},{1,3},{2,6},{3,1},{4,0},{5,7},{6,2},{7,5},{8,12},{9,11},{10,... | collective-permute-start | bytes 589832 | tf_op jit(solution)/shard_map/ppermute | solution.py:212
  13.0 1.3 %shard_map.49.kept = f32[256,896]{1,0:T(8,128)S(1)} custom-call(bf16[512,2048]{1,0:T(8,128)(2,1)S(1)} %get-tuple-element.32.prod._, bf16[896,2048]{1,0:T(8,128)(2,1)S(1)} %get-tuple-element.30.eig), custom_call_target="tpu_custom_call" | custom-call | flops 939524096 | bytes 3670016 | tf_op jit(solution)/shard_map/pallas_call | solution.py:180
  14.3 0.1 shard_map.50
  14.4 0.9 %collective-permute-start.2 = (bf16[128,896]{1,0:T(8,128)(2,1)S(1)}, bf16[128,896]{1,0:T(8,128)(2,1)S(1)}, u32[]{:S(2)}, u32[]{:S(2)}) collective-permute-start(bf16[128,896]{1,0:T(8,128)(2,1)S(1)} %get-tuple-element.35._), channel_id=1, source_target_pairs={{0,2},{1,9},{2,0},{3,11},{4,6},{5,13},{6,4},{7,15},{8,10},{9,1},{1... | collective-permute-start | bytes 688136 | tf_op jit(solution)/shard_map/ppermute | solution.py:212
  15.3 0.7 %shard_map.52.kept = f32[256,512]{1,0:T(8,128)S(1)} custom-call(bf16[512,2048]{1,0:T(8,128)(2,1)S(1)} %get-tuple-element.32.prod._, bf16[896,2048]{1,0:T(8,128)(2,1)S(1)} %get-tuple-element.36.eig), custom_call_target="tpu_custom_call" | custom-call | flops 536870912 | bytes 2097152 | tf_op jit(solution)/shard_map/pallas_call | solution.py:180
  16.1 2.6 %collective-permute-done.4.got = bf16[256,512]{1,0:T(8,128)(2,1)S(1)} collective-permute-done((bf16[256,512]{1,0:T(8,128)(2,1)S(1)}, bf16[256,512]{1,0:T(8,128)(2,1)S(1)}, u32[]{:S(2)}, u32[]{:S(2)}) %collective-permute-start.4) | collective-permute-done | bytes 262176 | tf_op jit(solution)/shard_map/ppermute | solution.py:212
  18.7 0.1 collective-permute-start.5
  18.8 0.7 %shard_map.51.kept = f32[256,384]{1,0:T(8,128)S(1)} custom-call(bf16[512,2048]{1,0:T(8,128)(2,1)S(1)} %get-tuple-element.32.prod._, bf16[896,2048]{1,0:T(8,128)(2,1)S(1)} %get-tuple-element.36.eig), custom_call_target="tpu_custom_call" | custom-call | flops 402653184 | bytes 1572864 | tf_op jit(solution)/shard_map/pallas_call | solution.py:180
  19.5 0.0 collective-permute-done.3.got
  19.6 2.4 %collective-permute-start.6 = (bf16[128,384]{1,0:T(8,128)(2,1)S(1)}, bf16[128,384]{1,0:T(8,128)(2,1)S(1)}, u32[]{:S(2)}, u32[]{:S(2)}) collective-permute-start(bf16[128,384]{1,0:T(8,128)(2,1)S(1)} %get-tuple-element.40._), channel_id=1, source_target_pairs={{0,2},{1,9},{2,0},{3,11},{4,6},{5,13},{6,4},{7,15},{8,10},{9,1},{1... | collective-permute-start | bytes 294920 | tf_op jit(solution)/shard_map/ppermute | solution.py:212
  22.0 0.0 collective-permute-done.2.got
  22.0 2.8 %collective-permute-start.7 = (bf16[64,896]{1,0:T(8,128)(2,1)S(1)}, bf16[64,896]{1,0:T(8,128)(2,1)S(1)}, u32[]{:S(2)}, u32[]{:S(2)}) collective-permute-start(bf16[64,896]{1,0:T(8,128)(2,1)S(1)} %get-tuple-element.43._), channel_id=1, source_target_pairs={{0,8},{1,5},{2,10},{3,7},{4,12},{5,1},{6,14},{7,3},{8,0},{9,13},{1... | collective-permute-start | bytes 344072 | tf_op jit(solution)/shard_map/ppermute | solution.py:212
  24.9 3.2 %collective-permute-done.5.got = bf16[128,512]{1,0:T(8,128)(2,1)S(1)} collective-permute-done((bf16[128,512]{1,0:T(8,128)(2,1)S(1)}, bf16[128,512]{1,0:T(8,128)(2,1)S(1)}, u32[]{:S(2)}, u32[]{:S(2)}) %collective-permute-start.5) | collective-permute-done | bytes 131104 | tf_op jit(solution)/shard_map/ppermute | solution.py:212
  28.1 0.1 collective-permute-start.8
  28.1 0.0 collective-permute-done.6.got
  28.2 3.0 %collective-permute-start.9 = (bf16[64,384]{1,0:T(8,128)(2,1)S(1)}, bf16[64,384]{1,0:T(8,128)(2,1)S(1)}, u32[]{:S(2)}, u32[]{:S(2)}) collective-permute-start(bf16[64,384]{1,0:T(8,128)(2,1)S(1)} %get-tuple-element.48), channel_id=1, source_target_pairs={{0,8},{1,5},{2,10},{3,7},{4,12},{5,1},{6,14},{7,3},{8,0},{9,13},{1... | collective-permute-start | bytes 147464 | tf_op jit(solution)/shard_map/ppermute | solution.py:212
  31.1 3.4 %collective-permute-done.9.refs_5_ = bf16[64,384]{1,0:T(8,128)(2,1)S(1)} collective-permute-done((bf16[64,384]{1,0:T(8,128)(2,1)S(1)}, bf16[64,384]{1,0:T(8,128)(2,1)S(1)}, u32[]{:S(2)}, u32[]{:S(2)}) %collective-permute-start.9) | collective-permute-done | bytes 49184 | tf_op jit(solution)/shard_map/ppermute | solution.py:212
  34.6 0.8 %shard_map.58 = f32[64,1792]{1,0:T(8,128)} custom-call(f32[64,896]{1,0:T(8,128)S(1)} %get-tuple-element.41.refs_0_, f32[64,512]{1,0:T(8,128)S(1)} %get-tuple-element.44.refs_1_, f32[64,384]{1,0:T(8,128)S(1)} %get-tuple-element.47.refs_2_, bf16[64,896]{1,0:T(8,128)(2,1)S(1)} %collective-permute-done.7.refs_3_, ...), custom_call_target="tpu_custom_call" | custom-call | flops 114688 | bytes 1376256 | tf_op jit(solution)/shard_map/pallas_call | solution.py:180
  (9 shorter events, 0.2 us)
Async XLA Ops:
  0.0 2.6 %collective-permute-start = (bf16[32,2048]{1,0:T(8,128)(2,1)}, bf16[32,2048]{1,0:T(8,128)(2,1)S(1)}, u32[]{:S(2)}, u32[]{:S(2)}) collective-permute-start(bf16[32,2048]{1,0:T(8,128)(2,1)} %own_hbm.1), channel_id=1, source_target_pairs={{0,1},{1,0},{2,3},{3,2},{4,5},{5,4},{6,7},{7,6},{8,9},{9,8},{10,11... | collective-permute-start | bytes 393224 | tf_op jit(solution)/shard_map/ppermute | solution.py:217
  4.1 10.1 %collective-permute-start.1 = (bf16[256,896]{1,0:T(8,128)(2,1)S(1)}, bf16[256,896]{1,0:T(8,128)(2,1)S(1)}, u32[]{:S(2)}, u32[]{:S(2)}) collective-permute-start(bf16[256,896]{1,0:T(8,128)(2,1)S(1)} %get-tuple-element.33), channel_id=1, source_target_pairs={{0,4},{1,3},{2,6},{3,1},{4,0},{5,7},{6,2},{7,5},{8,12},{9,11},{10,... | collective-permute-start | bytes 1376264 | tf_op jit(solution)/shard_map/ppermute | solution.py:212
  11.0 7.7 %collective-permute-start.4 = (bf16[256,512]{1,0:T(8,128)(2,1)S(1)}, bf16[256,512]{1,0:T(8,128)(2,1)S(1)}, u32[]{:S(2)}, u32[]{:S(2)}) collective-permute-start(bf16[256,512]{1,0:T(8,128)(2,1)S(1)} %get-tuple-element.38), channel_id=1, source_target_pairs={{0,2},{1,9},{2,0},{3,11},{4,6},{5,13},{6,4},{7,15},{8,10},{9,1},{1... | collective-permute-start | bytes 786440 | tf_op jit(solution)/shard_map/ppermute | solution.py:212
  12.5 7.0 %collective-permute-start.3 = (bf16[256,384]{1,0:T(8,128)(2,1)S(1)}, bf16[256,384]{1,0:T(8,128)(2,1)S(1)}, u32[]{:S(2)}, u32[]{:S(2)}) collective-permute-start(bf16[256,384]{1,0:T(8,128)(2,1)S(1)} %get-tuple-element.37), channel_id=1, source_target_pairs={{0,4},{1,3},{2,6},{3,1},{4,0},{5,7},{6,2},{7,5},{8,12},{9,11},{10,... | collective-permute-start | bytes 589832 | tf_op jit(solution)/shard_map/ppermute | solution.py:212
  14.4 7.6 %collective-permute-start.2 = (bf16[128,896]{1,0:T(8,128)(2,1)S(1)}, bf16[128,896]{1,0:T(8,128)(2,1)S(1)}, u32[]{:S(2)}, u32[]{:S(2)}) collective-permute-start(bf16[128,896]{1,0:T(8,128)(2,1)S(1)} %get-tuple-element.35._), channel_id=1, source_target_pairs={{0,2},{1,9},{2,0},{3,11},{4,6},{5,13},{6,4},{7,15},{8,10},{9,1},{1... | collective-permute-start | bytes 688136 | tf_op jit(solution)/shard_map/ppermute | solution.py:212
  18.7 9.3 %collective-permute-start.5 = (bf16[128,512]{1,0:T(8,128)(2,1)S(1)}, bf16[128,512]{1,0:T(8,128)(2,1)S(1)}, u32[]{:S(2)}, u32[]{:S(2)}) collective-permute-start(bf16[128,512]{1,0:T(8,128)(2,1)S(1)} %get-tuple-element.39._), channel_id=1, source_target_pairs={{0,4},{1,3},{2,6},{3,1},{4,0},{5,7},{6,2},{7,5},{8,12},{9,11},{10,... | collective-permute-start | bytes 393224 | tf_op jit(solution)/shard_map/ppermute | solution.py:212
  19.6 8.6 %collective-permute-start.6 = (bf16[128,384]{1,0:T(8,128)(2,1)S(1)}, bf16[128,384]{1,0:T(8,128)(2,1)S(1)}, u32[]{:S(2)}, u32[]{:S(2)}) collective-permute-start(bf16[128,384]{1,0:T(8,128)(2,1)S(1)} %get-tuple-element.40._), channel_id=1, source_target_pairs={{0,2},{1,9},{2,0},{3,11},{4,6},{5,13},{6,4},{7,15},{8,10},{9,1},{1... | collective-permute-start | bytes 294920 | tf_op jit(solution)/shard_map/ppermute | solution.py:212
  22.0 12.5 %collective-permute-start.7 = (bf16[64,896]{1,0:T(8,128)(2,1)S(1)}, bf16[64,896]{1,0:T(8,128)(2,1)S(1)}, u32[]{:S(2)}, u32[]{:S(2)}) collective-permute-start(bf16[64,896]{1,0:T(8,128)(2,1)S(1)} %get-tuple-element.43._), channel_id=1, source_target_pairs={{0,8},{1,5},{2,10},{3,7},{4,12},{5,1},{6,14},{7,3},{8,0},{9,13},{1... | collective-permute-start | bytes 344072 | tf_op jit(solution)/shard_map/ppermute | solution.py:212
  28.1 6.5 %collective-permute-start.8 = (bf16[64,512]{1,0:T(8,128)(2,1)S(1)}, bf16[64,512]{1,0:T(8,128)(2,1)S(1)}, u32[]{:S(2)}, u32[]{:S(2)}) collective-permute-start(bf16[64,512]{1,0:T(8,128)(2,1)S(1)} %get-tuple-element.46._), channel_id=1, source_target_pairs={{0,8},{1,5},{2,10},{3,7},{4,12},{5,1},{6,14},{7,3},{8,0},{9,13},{1... | collective-permute-start | bytes 196616 | tf_op jit(solution)/shard_map/ppermute | solution.py:212
  28.2 6.4 %collective-permute-start.9 = (bf16[64,384]{1,0:T(8,128)(2,1)S(1)}, bf16[64,384]{1,0:T(8,128)(2,1)S(1)}, u32[]{:S(2)}, u32[]{:S(2)}) collective-permute-start(bf16[64,384]{1,0:T(8,128)(2,1)S(1)} %get-tuple-element.48), channel_id=1, source_target_pairs={{0,8},{1,5},{2,10},{3,7},{4,12},{5,1},{6,14},{7,3},{8,0},{9,13},{1... | collective-permute-start | bytes 147464 | tf_op jit(solution)/shard_map/ppermute | solution.py:212

commit v11 on v10

--- a/solution.py
+++ b/solution.py
@@ -12,8 +12,8 @@
 X, NEAR, FAR = 0, 1, 2
 PLAN = [
     (3.5, (NEAR, X, FAR), (X, FAR, NEAR)),
-    (2, (X, NEAR, FAR), (FAR, X, NEAR)),
-    (1.5, (NEAR, X, FAR), (X, FAR, NEAR)),
+    (2, (X, NEAR, FAR), (NEAR, X, FAR)),
+    (1.5, (X, NEAR, FAR), (X, NEAR, FAR)),
 ]
 ORDER = [(piece, stage) for stage in (1, 2) for piece in range(len(PLAN))]
 
@@ -56,14 +56,10 @@
     return jnp.concatenate(parts, axis=0)
 
 
-def tiles_of(width):
-    return [(at, min(TILE, width - at)) for at in range(0, width, TILE)]
-
-
-def dot_tiles(out, rows, eig, first, waits=()):
-    for i, (at, size) in enumerate(tiles_of(out.shape[1])):
-        if waits:
-            waits[i].wait()
+def dot_tiles(out, rows, eig, first):
+    width = out.shape[1]
+    for at in range(0, width, TILE):
+        size = min(TILE, width - at)
         out[:, at : at + size] = lax.dot_general(
             rows,
             eig[first + at : first + at + size, :],
@@ -123,31 +119,34 @@
     prod[...] = value.reshape(chosen.shape).astype(jnp.bfloat16)
 
 
-def first_kernel(pick, own, other, lanc16, eig, out, prod, acc):
+def first_kernel(cut, pick, own, other, lanc16, eig, eig_hbm, out, prod, eig_next, acc, sem):
+    copy = pltpu.make_async_copy(
+        eig_hbm.at[pl.ds(cut, eig_next.shape[0])], eig_next, sem.at[0]
+    )
+    copy.start()
     make_rows(prod, pick, own, other, lanc16, 0)
     dot_tiles(acc, prod[...], eig, 0)
     out[...] = acc[...].astype(out.dtype)
-
-
-def send_kernel(cuts, pick, own, other, lanc16, half, eig_hbm, *rest):
-    count = len(cuts) - 2
-    outs, (prod, eig, acc, sem) = rest[:count], rest[count:]
-    copies = []
-    for cut, end in zip(cuts[1:], cuts[2:]):
-        copies.append([])
-        for at, size in tiles_of(end - cut):
-            source = eig_hbm.at[pl.ds(cut + at, size)]
-            target = eig.at[pl.ds(cut - cuts[1] + at, size)]
-            copy = pltpu.make_async_copy(source, target, sem.at[sum(map(len, copies))])
-            copy.start()
-            copies[-1].append(copy)
+    copy.wait()
+
+
+def send_kernel(cut, pick, own, other, lanc16, half, eig, eig_hbm, *rest):
+    *outs, prod, eig_rest, acc, sem = rest
+    copy = pltpu.make_async_copy(
+        eig_hbm.at[pl.ds(cut, eig_rest.shape[0])], eig_rest, sem.at[0]
+    )
+    copy.start()
     first = half.shape[0]
     prod[:first, :] = half[...]
     make_rows(prod.at[first:, :], pick, own, other, lanc16, first)
+    at = 0
     for i, out in enumerate(outs):
         part = acc.at[:, : out.shape[1]]
-        dot_tiles(part, rows_of(prod, i + 1, False), eig, cuts[i + 1] - cuts[1], copies[i])
+        if i == 1:
+            copy.wait()
+        dot_tiles(part, rows_of(prod, i + 1, False), eig_rest if i else eig, at)
         out[...] = part[...].astype(out.dtype)
+        at += out.shape[1] if i else 0
 
 
 def keep_kernel(p, first, prod, eig, out):
@@ -228,30 +227,28 @@
         (0, 2 * widths[0] * depth),
     )
     sources = [(x, False) for x in (pick, own, other, lanc16)]
-    send, half = kernel_call(
-        first_kernel,
-        sources + [(eig, False)],
-        [((rows // 2, widths[0]), bf16), ((rows // 2, depth), bf16)],
-        [pltpu.VMEM((rows // 2, widths[0]), jnp.float32)],
+    send, half, eig_next = kernel_call(
+        functools.partial(first_kernel, cuts[1]),
+        sources + [(eig, False), (eigvecs, True)],
+        [((rows // 2, widths[0]), bf16), ((rows // 2, depth), bf16), ((widths[1], depth), bf16)],
+        [pltpu.VMEM((rows // 2, widths[0]), jnp.float32), pltpu.SemaphoreType.DMA((1,))],
         (flops(widths[0]), 2 * widths[0] * depth),
     )
     *sends, prod, eig_rest = kernel_call(
-        functools.partial(send_kernel, cuts),
-        sources + [(half, False), (eigvecs, True)],
+        functools.partial(send_kernel, cuts[2]),
+        sources + [(half, False), (eig_next, False), (eigvecs, True)],
         [((rows // 2, w), bf16) for w in widths[1:]]
-        + [((rows, depth), bf16), ((cols - widths[0], depth), bf16)],
-        [
-            pltpu.VMEM((rows // 2, max(widths[1:])), jnp.float32),
-            pltpu.SemaphoreType.DMA((sum(len(tiles_of(w)) for w in widths[1:]),)),
-        ],
+        + [((rows, depth), bf16), ((cols - cuts[2], depth), bf16)],
+        [pltpu.VMEM((rows // 2, max(widths[1:])), jnp.float32), pltpu.SemaphoreType.DMA((1,))],
         (flops(sum(widths[1:])), 2 * sum(widths[1:]) * depth),
     )
+    eigs = [eig, eig_next] + [eig_rest] * (len(PLAN) - 2)
     got = [exchange(s, p, 0) for p, s in enumerate([send, *sends])]
     value = []
     for p, width in enumerate(widths):
         value += kernel_call(
-            functools.partial(keep_kernel, p, cuts[p] - cuts[min(p, 1)]),
-            [(prod, False), (eig_rest if p else eig, False)],
+            functools.partial(keep_kernel, p, cuts[p] - cuts[min(p, 2)]),
+            [(prod, False), (eigs[p], False)],
             [((rows // 2, width), jnp.float32)],
             [],
             (flops(width), 2 * width * depth),

time: 35.5 us -> 36.2 us (1.020)
  starting transfers between devices: 14.4 us -> 16.1 us
  Pallas kernels: 11.6 us -> 9.99 us
  waiting for transfers between devices: 9.2 us -> 9.81 us
    ppermute x9, starting transfers between devices: 13.9 us -> 15.7 us  [exchange(): return lax.ppermute(value, ('grid', 'eig'), pairs)]
    pallas_call x13, Pallas kernels: 11.6 us -> 9.99 us  [kernel_call(): pl.pallas_call(body, out_shape=[jax.ShapeDtypeStruct(*out) for out in out...]
    ppermute x9, waiting for transfers between devices: 9.2 us -> 9.8 us  [exchange(): return lax.ppermute(value, ('grid', 'eig'), pairs)]
  transfers between devices with their start and end apart: 10 -> 10, of which waited for: 3 -> 4; matrix products, arithmetic and copies ran while one was open for 0% -> 0% of each run, Pallas kernels for 26% -> 21%
where the time goes in v11:
time: 36.2 us; the launch traced here: 36 us
  starting transfers between devices  16.1 us (44%)
  Pallas kernels  9.99 us (28%)
  waiting for transfers between devices  9.81 us (27%)
    ppermute x9, starting transfers between devices, exchange(): return lax.ppermute(value, ('grid', 'eig'), pairs)  15.7 us
    pallas_call x13, Pallas kernels, kernel_call(): pl.pallas_call(body, out_shape=[jax.ShapeDtypeStruct(*out) for out in out...  9.99 us
    ppermute x9, waiting for transfers between devices, exchange(): return lax.ppermute(value, ('grid', 'eig'), pairs)  9.8 us
  transfers between devices with their start and end apart: 10, of which 4 were waited for; matrix products, arithmetic and copies ran while one was open for 0% of the time, Pallas kernels for 21%

profile of v11, /device:TPU:0, one launch (start us, length us, event | category | flops | bytes accessed | tf_op | source)
XLA Modules:
  0.0 36.0 jit_solution(7200497872218631693)
XLA Ops:
  0.0 0.5 %collective-permute-start = (bf16[32,2048]{1,0:T(8,128)(2,1)}, bf16[32,2048]{1,0:T(8,128)(2,1)S(1)}, u32[]{:S(2)}, u32[]{:S(2)}) collective-permute-start(bf16[32,2048]{1,0:T(8,128)(2,1)} %own_hbm.1), channel_id=1, source_target_pairs={{0,1},{1,0},{2,3},{3,2},{4,5},{5,4},{6,7},{7,6},{8,9},{9,8},{10,11... | collective-permute-start | bytes 393224 | tf_op jit(solution)/shard_map/ppermute | solution.py:216
  0.5 2.2 %shard_map.46 = (bf16[512,64]{1,0:T(8,128)(2,1)S(1)}, bf16[32,2048]{1,0:T(8,128)(2,1)S(1)}, bf16[8,2048]{1,0:T(8,128)(2,1)S(1)}, bf16[896,2048]{1,0:T(8,128)(2,1)S(1)}) custom-call(s32[64]{0:T(128)} %order_hbm.1, bf16[32,2048]{1,0:T(8,128)(2,1)} %own_hbm.1, bf16[8,2048]{1,0:T(8,128)(2,1)} %lanc_hbm.1, bf16[1792,2048]{1,0:T(8,128)(2,1)} %eig_hbm.5), custom_call_target="tpu_custom_call" | custom-call | bytes 3670016 | tf_op jit(solution)/shard_map/pallas_call | solution.py:179
  2.6 0.0 collective-permute-done.other
  2.6 1.6 %shard_map.47 = (bf16[256,896]{1,0:T(8,128)(2,1)S(1)}, bf16[256,2048]{1,0:T(8,128)(2,1)S(1)}, bf16[512,2048]{1,0:T(8,128)(2,1)S(1)}) custom-call(bf16[512,64]{1,0:T(8,128)(2,1)S(1)} %get-tuple-element.28.pick, bf16[32,2048]{1,0:T(8,128)(2,1)S(1)} %get-tuple-element.29.own, bf16[32,2048]{1,0:T(8,128)(2,1)S(1)} %collective-permute-done.other, ...), custom_call_target="tpu_custom_call" | custom-call | flops 939524096 | bytes 3670016 | tf_op jit(solution)/shard_map/pallas_call | solution.py:179
  4.3 2.6 %collective-permute-start.1 = (bf16[256,896]{1,0:T(8,128)(2,1)S(1)}, bf16[256,896]{1,0:T(8,128)(2,1)S(1)}, u32[]{:S(2)}, u32[]{:S(2)}) collective-permute-start(bf16[256,896]{1,0:T(8,128)(2,1)S(1)} %get-tuple-element.35), channel_id=1, source_target_pairs={{0,4},{1,3},{2,6},{3,1},{4,0},{5,7},{6,2},{7,5},{8,12},{9,11},{10,... | collective-permute-start | bytes 1376264 | tf_op jit(solution)/shard_map/ppermute | solution.py:211
  6.9 2.4 %shard_map.48 = (bf16[256,512]{1,0:T(8,128)(2,1)S(1)}, bf16[256,384]{1,0:T(8,128)(2,1)S(1)}, bf16[512,2048]{1,0:T(8,128)(2,1)S(1)}, bf16[384,2048]{1,0:T(8,128)(2,1)S(1)}) custom-call(bf16[512,64]{1,0:T(8,128)(2,1)S(1)} %get-tuple-element.28.pick, bf16[32,2048]{1,0:T(8,128)(2,1)S(1)} %get-tuple-element.29.own, ...), custom_call_target="tpu_custom_call" | custom-call | flops 939524096 | bytes 3670016 | tf_op jit(solution)/shard_map/pallas_call | solution.py:179
  9.4 1.6 %collective-permute-start.4 = (bf16[256,512]{1,0:T(8,128)(2,1)S(1)}, bf16[256,512]{1,0:T(8,128)(2,1)S(1)}, u32[]{:S(2)}, u32[]{:S(2)}) collective-permute-start(bf16[256,512]{1,0:T(8,128)(2,1)S(1)} %get-tuple-element.40), channel_id=1, source_target_pairs={{0,2},{1,5},{2,0},{3,7},{4,6},{5,1},{6,4},{7,3},{8,10},{9,13},{10,... | collective-permute-start | bytes 786440 | tf_op jit(solution)/shard_map/ppermute | solution.py:211
  10.9 0.5 %collective-permute-start.3 = (bf16[256,384]{1,0:T(8,128)(2,1)S(1)}, bf16[256,384]{1,0:T(8,128)(2,1)S(1)}, u32[]{:S(2)}, u32[]{:S(2)}) collective-permute-start(bf16[256,384]{1,0:T(8,128)(2,1)S(1)} %get-tuple-element.39), channel_id=1, source_target_pairs={{0,2},{1,3},{2,0},{3,1},{4,6},{5,7},{6,4},{7,5},{8,10},{9,11},{10,... | collective-permute-start | bytes 589832 | tf_op jit(solution)/shard_map/ppermute | solution.py:211
  11.4 1.3 %shard_map.49.kept = f32[256,896]{1,0:T(8,128)S(1)} custom-call(bf16[512,2048]{1,0:T(8,128)(2,1)S(1)} %get-tuple-element.34.prod._, bf16[896,2048]{1,0:T(8,128)(2,1)S(1)} %get-tuple-element.31.eig), custom_call_target="tpu_custom_call" | custom-call | flops 939524096 | bytes 3670016 | tf_op jit(solution)/shard_map/pallas_call | solution.py:179
  12.7 1.8 %collective-permute-done.1.got = bf16[256,896]{1,0:T(8,128)(2,1)S(1)} collective-permute-done((bf16[256,896]{1,0:T(8,128)(2,1)S(1)}, bf16[256,896]{1,0:T(8,128)(2,1)S(1)}, u32[]{:S(2)}, u32[]{:S(2)}) %collective-permute-start.1) | collective-permute-done | bytes 458784 | tf_op jit(solution)/shard_map/ppermute | solution.py:211
  14.5 0.1 shard_map.50
  14.6 3.6 %collective-permute-start.2 = (bf16[128,896]{1,0:T(8,128)(2,1)S(1)}, bf16[128,896]{1,0:T(8,128)(2,1)S(1)}, u32[]{:S(2)}, u32[]{:S(2)}) collective-permute-start(bf16[128,896]{1,0:T(8,128)(2,1)S(1)} %get-tuple-element.37._), channel_id=1, source_target_pairs={{0,2},{1,9},{2,0},{3,11},{4,6},{5,13},{6,4},{7,15},{8,10},{9,1},{1... | collective-permute-start | bytes 688136 | tf_op jit(solution)/shard_map/ppermute | solution.py:211
  18.1 0.7 %shard_map.52.kept = f32[256,512]{1,0:T(8,128)S(1)} custom-call(bf16[512,2048]{1,0:T(8,128)(2,1)S(1)} %get-tuple-element.34.prod._, bf16[512,2048]{1,0:T(8,128)(2,1)S(1)} %get-tuple-element.33.eig), custom_call_target="tpu_custom_call" | custom-call | flops 536870912 | bytes 2097152 | tf_op jit(solution)/shard_map/pallas_call | solution.py:179
  18.9 0.0 collective-permute-done.4.got
  18.9 1.5 %collective-permute-start.5 = (bf16[128,512]{1,0:T(8,128)(2,1)S(1)}, bf16[128,512]{1,0:T(8,128)(2,1)S(1)}, u32[]{:S(2)}, u32[]{:S(2)}) collective-permute-start(bf16[128,512]{1,0:T(8,128)(2,1)S(1)} %get-tuple-element.41._), channel_id=1, source_target_pairs={{0,4},{1,3},{2,6},{3,1},{4,0},{5,7},{6,2},{7,5},{8,12},{9,11},{10,... | collective-permute-start | bytes 393224 | tf_op jit(solution)/shard_map/ppermute | solution.py:211
  20.4 0.7 %shard_map.51.kept = f32[256,384]{1,0:T(8,128)S(1)} custom-call(bf16[512,2048]{1,0:T(8,128)(2,1)S(1)} %get-tuple-element.34.prod._, bf16[384,2048]{1,0:T(8,128)(2,1)S(1)} %get-tuple-element.38.eig), custom_call_target="tpu_custom_call" | custom-call | flops 402653184 | bytes 1572864 | tf_op jit(solution)/shard_map/pallas_call | solution.py:179
  21.2 0.8 %collective-permute-start.6 = (bf16[128,384]{1,0:T(8,128)(2,1)S(1)}, bf16[128,384]{1,0:T(8,128)(2,1)S(1)}, u32[]{:S(2)}, u32[]{:S(2)}) collective-permute-start(bf16[128,384]{1,0:T(8,128)(2,1)S(1)} %get-tuple-element.42._), channel_id=1, source_target_pairs={{0,4},{1,5},{2,6},{3,7},{4,0},{5,1},{6,2},{7,3},{8,12},{9,13},{10,... | collective-permute-start | bytes 294920 | tf_op jit(solution)/shard_map/ppermute | solution.py:211
  22.0 1.9 %collective-permute-done.2.got = bf16[128,896]{1,0:T(8,128)(2,1)S(1)} collective-permute-done((bf16[128,896]{1,0:T(8,128)(2,1)S(1)}, bf16[128,896]{1,0:T(8,128)(2,1)S(1)}, u32[]{:S(2)}, u32[]{:S(2)}) %collective-permute-start.2) | collective-permute-done | bytes 229408 | tf_op jit(solution)/shard_map/ppermute | solution.py:211
  24.0 2.9 %collective-permute-start.7 = (bf16[64,896]{1,0:T(8,128)(2,1)S(1)}, bf16[64,896]{1,0:T(8,128)(2,1)S(1)}, u32[]{:S(2)}, u32[]{:S(2)}) collective-permute-start(bf16[64,896]{1,0:T(8,128)(2,1)S(1)} %get-tuple-element.45._), channel_id=1, source_target_pairs={{0,8},{1,5},{2,10},{3,7},{4,12},{5,1},{6,14},{7,3},{8,0},{9,13},{1... | collective-permute-start | bytes 344072 | tf_op jit(solution)/shard_map/ppermute | solution.py:211
  26.9 0.2 collective-permute-start.8
  27.1 0.9 %collective-permute-done.6.got = bf16[128,384]{1,0:T(8,128)(2,1)S(1)} collective-permute-done((bf16[128,384]{1,0:T(8,128)(2,1)S(1)}, bf16[128,384]{1,0:T(8,128)(2,1)S(1)}, u32[]{:S(2)}, u32[]{:S(2)}) %collective-permute-start.6) | collective-permute-done | bytes 98336 | tf_op jit(solution)/shard_map/ppermute | solution.py:211
  28.0 2.0 %collective-permute-start.9 = (bf16[64,384]{1,0:T(8,128)(2,1)S(1)}, bf16[64,384]{1,0:T(8,128)(2,1)S(1)}, u32[]{:S(2)}, u32[]{:S(2)}) collective-permute-start(bf16[64,384]{1,0:T(8,128)(2,1)S(1)} %get-tuple-element.50), channel_id=1, source_target_pairs={{0,8},{1,9},{2,10},{3,11},{4,12},{5,13},{6,14},{7,15},{8,0},{9,1},... | collective-permute-start | bytes 147464 | tf_op jit(solution)/shard_map/ppermute | solution.py:211
  30.0 5.2 %collective-permute-done.9.refs_5_ = bf16[64,384]{1,0:T(8,128)(2,1)S(1)} collective-permute-done((bf16[64,384]{1,0:T(8,128)(2,1)S(1)}, bf16[64,384]{1,0:T(8,128)(2,1)S(1)}, u32[]{:S(2)}, u32[]{:S(2)}) %collective-permute-start.9) | collective-permute-done | bytes 49184 | tf_op jit(solution)/shard_map/ppermute | solution.py:211
  35.2 0.8 %shard_map.58 = f32[64,1792]{1,0:T(8,128)} custom-call(f32[64,896]{1,0:T(8,128)S(1)} %get-tuple-element.43.refs_0_, f32[64,512]{1,0:T(8,128)S(1)} %get-tuple-element.46.refs_1_, f32[64,384]{1,0:T(8,128)S(1)} %get-tuple-element.49.refs_2_, bf16[64,896]{1,0:T(8,128)(2,1)S(1)} %collective-permute-done.7.refs_3_, ...), custom_call_target="tpu_custom_call" | custom-call | flops 114688 | bytes 1376256 | tf_op jit(solution)/shard_map/pallas_call | solution.py:179
  (9 shorter events, 0.2 us)
Async XLA Ops:
  0.0 2.6 %collective-permute-start = (bf16[32,2048]{1,0:T(8,128)(2,1)}, bf16[32,2048]{1,0:T(8,128)(2,1)S(1)}, u32[]{:S(2)}, u32[]{:S(2)}) collective-permute-start(bf16[32,2048]{1,0:T(8,128)(2,1)} %own_hbm.1), channel_id=1, source_target_pairs={{0,1},{1,0},{2,3},{3,2},{4,5},{5,4},{6,7},{7,6},{8,9},{9,8},{10,11... | collective-permute-start | bytes 393224 | tf_op jit(solution)/shard_map/ppermute | solution.py:216
  4.3 10.2 %collective-permute-start.1 = (bf16[256,896]{1,0:T(8,128)(2,1)S(1)}, bf16[256,896]{1,0:T(8,128)(2,1)S(1)}, u32[]{:S(2)}, u32[]{:S(2)}) collective-permute-start(bf16[256,896]{1,0:T(8,128)(2,1)S(1)} %get-tuple-element.35), channel_id=1, source_target_pairs={{0,4},{1,3},{2,6},{3,1},{4,0},{5,7},{6,2},{7,5},{8,12},{9,11},{10,... | collective-permute-start | bytes 1376264 | tf_op jit(solution)/shard_map/ppermute | solution.py:211
  9.4 9.5 %collective-permute-start.4 = (bf16[256,512]{1,0:T(8,128)(2,1)S(1)}, bf16[256,512]{1,0:T(8,128)(2,1)S(1)}, u32[]{:S(2)}, u32[]{:S(2)}) collective-permute-start(bf16[256,512]{1,0:T(8,128)(2,1)S(1)} %get-tuple-element.40), channel_id=1, source_target_pairs={{0,2},{1,5},{2,0},{3,7},{4,6},{5,1},{6,4},{7,3},{8,10},{9,13},{10,... | collective-permute-start | bytes 786440 | tf_op jit(solution)/shard_map/ppermute | solution.py:211
  10.9 10.2 %collective-permute-start.3 = (bf16[256,384]{1,0:T(8,128)(2,1)S(1)}, bf16[256,384]{1,0:T(8,128)(2,1)S(1)}, u32[]{:S(2)}, u32[]{:S(2)}) collective-permute-start(bf16[256,384]{1,0:T(8,128)(2,1)S(1)} %get-tuple-element.39), channel_id=1, source_target_pairs={{0,2},{1,3},{2,0},{3,1},{4,6},{5,7},{6,4},{7,5},{8,10},{9,11},{10,... | collective-permute-start | bytes 589832 | tf_op jit(solution)/shard_map/ppermute | solution.py:211
  14.6 9.4 %collective-permute-start.2 = (bf16[128,896]{1,0:T(8,128)(2,1)S(1)}, bf16[128,896]{1,0:T(8,128)(2,1)S(1)}, u32[]{:S(2)}, u32[]{:S(2)}) collective-permute-start(bf16[128,896]{1,0:T(8,128)(2,1)S(1)} %get-tuple-element.37._), channel_id=1, source_target_pairs={{0,2},{1,9},{2,0},{3,11},{4,6},{5,13},{6,4},{7,15},{8,10},{9,1},{1... | collective-permute-start | bytes 688136 | tf_op jit(solution)/shard_map/ppermute | solution.py:211
  18.9 8.0 %collective-permute-start.5 = (bf16[128,512]{1,0:T(8,128)(2,1)S(1)}, bf16[128,512]{1,0:T(8,128)(2,1)S(1)}, u32[]{:S(2)}, u32[]{:S(2)}) collective-permute-start(bf16[128,512]{1,0:T(8,128)(2,1)S(1)} %get-tuple-element.41._), channel_id=1, source_target_pairs={{0,4},{1,3},{2,6},{3,1},{4,0},{5,7},{6,2},{7,5},{8,12},{9,11},{10,... | collective-permute-start | bytes 393224 | tf_op jit(solution)/shard_map/ppermute | solution.py:211
  21.2 6.8 %collective-permute-start.6 = (bf16[128,384]{1,0:T(8,128)(2,1)S(1)}, bf16[128,384]{1,0:T(8,128)(2,1)S(1)}, u32[]{:S(2)}, u32[]{:S(2)}) collective-permute-start(bf16[128,384]{1,0:T(8,128)(2,1)S(1)} %get-tuple-element.42._), channel_id=1, source_target_pairs={{0,4},{1,5},{2,6},{3,7},{4,0},{5,1},{6,2},{7,3},{8,12},{9,13},{10,... | collective-permute-start | bytes 294920 | tf_op jit(solution)/shard_map/ppermute | solution.py:211
  24.0 11.2 %collective-permute-start.7 = (bf16[64,896]{1,0:T(8,128)(2,1)S(1)}, bf16[64,896]{1,0:T(8,128)(2,1)S(1)}, u32[]{:S(2)}, u32[]{:S(2)}) collective-permute-start(bf16[64,896]{1,0:T(8,128)(2,1)S(1)} %get-tuple-element.45._), channel_id=1, source_target_pairs={{0,8},{1,5},{2,10},{3,7},{4,12},{5,1},{6,14},{7,3},{8,0},{9,13},{1... | collective-permute-start | bytes 344072 | tf_op jit(solution)/shard_map/ppermute | solution.py:211
  26.9 8.3 %collective-permute-start.8 = (bf16[64,512]{1,0:T(8,128)(2,1)S(1)}, bf16[64,512]{1,0:T(8,128)(2,1)S(1)}, u32[]{:S(2)}, u32[]{:S(2)}) collective-permute-start(bf16[64,512]{1,0:T(8,128)(2,1)S(1)} %get-tuple-element.48._), channel_id=1, source_target_pairs={{0,8},{1,9},{2,10},{3,11},{4,12},{5,13},{6,14},{7,15},{8,0},{9,1},... | collective-permute-start | bytes 196616 | tf_op jit(solution)/shard_map/ppermute | solution.py:211
  28.0 7.2 %collective-permute-start.9 = (bf16[64,384]{1,0:T(8,128)(2,1)S(1)}, bf16[64,384]{1,0:T(8,128)(2,1)S(1)}, u32[]{:S(2)}, u32[]{:S(2)}) collective-permute-start(bf16[64,384]{1,0:T(8,128)(2,1)S(1)} %get-tuple-element.50), channel_id=1, source_target_pairs={{0,8},{1,9},{2,10},{3,11},{4,12},{5,13},{6,14},{7,15},{8,0},{9,1},... | collective-permute-start | bytes 147464 | tf_op jit(solution)/shard_map/ppermute | solution.py:211

commit v12 on v11

--- a/solution.py
+++ b/solution.py
@@ -12,8 +12,8 @@
 X, NEAR, FAR = 0, 1, 2
 PLAN = [
     (3.5, (NEAR, X, FAR), (X, FAR, NEAR)),
-    (2, (X, NEAR, FAR), (NEAR, X, FAR)),
-    (1.5, (X, NEAR, FAR), (X, NEAR, FAR)),
+    (2, (X, FAR, NEAR), (NEAR, X, FAR)),
+    (1.5, (X, FAR, NEAR), (NEAR, X, FAR)),
 ]
 ORDER = [(piece, stage) for stage in (1, 2) for piece in range(len(PLAN))]
 

time: 36.2 us -> 35.4 us (0.978)
  the two profiles are of different devices: /device:TPU:0 before, /device:TPU:3 now
where the time goes in v12:
time: 35.4 us; the launch traced here: 35.3 us
  starting transfers between devices  15.1 us (43%)
  waiting for transfers between devices  10.1 us (29%)
  Pallas kernels  10 us (28%)
    ppermute x9, starting transfers between devices, exchange(): return lax.ppermute(value, ('grid', 'eig'), pairs)  14.4 us
    ppermute x9, waiting for transfers between devices, exchange(): return lax.ppermute(value, ('grid', 'eig'), pairs)  10 us
    pallas_call x13, Pallas kernels, kernel_call(): pl.pallas_call(body, out_shape=[jax.ShapeDtypeStruct(*out) for out in out...  10 us
  transfers between devices with their start and end apart: 10, of which 3 were waited for; matrix products, arithmetic and copies ran while one was open for 0% of the time, Pallas kernels for 21%

profile of v12, /device:TPU:3, one launch (start us, length us, event | category | flops | bytes accessed | tf_op | source)
XLA Modules:
  0.0 35.3 jit_solution(5445719825050885498)
XLA Ops:
  0.0 0.7 %collective-permute-start = (bf16[32,2048]{1,0:T(8,128)(2,1)}, bf16[32,2048]{1,0:T(8,128)(2,1)S(1)}, u32[]{:S(2)}, u32[]{:S(2)}) collective-permute-start(bf16[32,2048]{1,0:T(8,128)(2,1)} %own_hbm.1), channel_id=1, source_target_pairs={{0,1},{1,0},{2,3},{3,2},{4,5},{5,4},{6,7},{7,6},{8,9},{9,8},{10,11... | collective-permute-start | bytes 393224 | tf_op jit(solution)/shard_map/ppermute | solution.py:216
  0.7 2.2 %shard_map.46 = (bf16[512,64]{1,0:T(8,128)(2,1)S(1)}, bf16[32,2048]{1,0:T(8,128)(2,1)S(1)}, bf16[8,2048]{1,0:T(8,128)(2,1)S(1)}, bf16[896,2048]{1,0:T(8,128)(2,1)S(1)}) custom-call(s32[64]{0:T(128)} %order_hbm.1, bf16[32,2048]{1,0:T(8,128)(2,1)} %own_hbm.1, bf16[8,2048]{1,0:T(8,128)(2,1)} %lanc_hbm.1, bf16[1792,2048]{1,0:T(8,128)(2,1)} %eig_hbm.5), custom_call_target="tpu_custom_call" | custom-call | bytes 3670016 | tf_op jit(solution)/shard_map/pallas_call | solution.py:179
  2.9 0.0 collective-permute-done.other
  2.9 1.6 %shard_map.47 = (bf16[256,896]{1,0:T(8,128)(2,1)S(1)}, bf16[256,2048]{1,0:T(8,128)(2,1)S(1)}, bf16[512,2048]{1,0:T(8,128)(2,1)S(1)}) custom-call(bf16[512,64]{1,0:T(8,128)(2,1)S(1)} %get-tuple-element.28.pick, bf16[32,2048]{1,0:T(8,128)(2,1)S(1)} %get-tuple-element.29.own, bf16[32,2048]{1,0:T(8,128)(2,1)S(1)} %collective-permute-done.other, ...), custom_call_target="tpu_custom_call" | custom-call | flops 939524096 | bytes 3670016 | tf_op jit(solution)/shard_map/pallas_call | solution.py:179
  4.5 0.1 collective-permute-start.1
  4.6 2.4 %shard_map.48 = (bf16[256,512]{1,0:T(8,128)(2,1)S(1)}, bf16[256,384]{1,0:T(8,128)(2,1)S(1)}, bf16[512,2048]{1,0:T(8,128)(2,1)S(1)}, bf16[384,2048]{1,0:T(8,128)(2,1)S(1)}) custom-call(bf16[512,64]{1,0:T(8,128)(2,1)S(1)} %get-tuple-element.28.pick, bf16[32,2048]{1,0:T(8,128)(2,1)S(1)} %get-tuple-element.29.own, ...), custom_call_target="tpu_custom_call" | custom-call | flops 939524096 | bytes 3670016 | tf_op jit(solution)/shard_map/pallas_call | solution.py:179
  7.0 1.6 %collective-permute-start.4 = (bf16[256,512]{1,0:T(8,128)(2,1)S(1)}, bf16[256,512]{1,0:T(8,128)(2,1)S(1)}, u32[]{:S(2)}, u32[]{:S(2)}) collective-permute-start(bf16[256,512]{1,0:T(8,128)(2,1)S(1)} %get-tuple-element.40), channel_id=1, source_target_pairs={{0,2},{1,5},{2,0},{3,7},{4,6},{5,1},{6,4},{7,3},{8,10},{9,13},{10,... | collective-permute-start | bytes 786440 | tf_op jit(solution)/shard_map/ppermute | solution.py:211
  8.6 0.1 collective-permute-start.3
  8.7 1.3 %shard_map.49.kept = f32[256,896]{1,0:T(8,128)S(1)} custom-call(bf16[512,2048]{1,0:T(8,128)(2,1)S(1)} %get-tuple-element.34.prod._, bf16[896,2048]{1,0:T(8,128)(2,1)S(1)} %get-tuple-element.31.eig), custom_call_target="tpu_custom_call" | custom-call | flops 939524096 | bytes 3670016 | tf_op jit(solution)/shard_map/pallas_call | solution.py:179
  10.0 2.5 %collective-permute-done.1.got = bf16[256,896]{1,0:T(8,128)(2,1)S(1)} collective-permute-done((bf16[256,896]{1,0:T(8,128)(2,1)S(1)}, bf16[256,896]{1,0:T(8,128)(2,1)S(1)}, u32[]{:S(2)}, u32[]{:S(2)}) %collective-permute-start.1) | collective-permute-done | bytes 458784 | tf_op jit(solution)/shard_map/ppermute | solution.py:211
  12.5 0.1 shard_map.50
  12.5 2.4 %collective-permute-start.2 = (bf16[128,896]{1,0:T(8,128)(2,1)S(1)}, bf16[128,896]{1,0:T(8,128)(2,1)S(1)}, u32[]{:S(2)}, u32[]{:S(2)}) collective-permute-start(bf16[128,896]{1,0:T(8,128)(2,1)S(1)} %get-tuple-element.37._), channel_id=1, source_target_pairs={{0,2},{1,9},{2,0},{3,11},{4,6},{5,13},{6,4},{7,15},{8,10},{9,1},{1... | collective-permute-start | bytes 688136 | tf_op jit(solution)/shard_map/ppermute | solution.py:211
  14.9 0.7 %shard_map.52.kept = f32[256,512]{1,0:T(8,128)S(1)} custom-call(bf16[512,2048]{1,0:T(8,128)(2,1)S(1)} %get-tuple-element.34.prod._, bf16[512,2048]{1,0:T(8,128)(2,1)S(1)} %get-tuple-element.33.eig), custom_call_target="tpu_custom_call" | custom-call | flops 536870912 | bytes 2097152 | tf_op jit(solution)/shard_map/pallas_call | solution.py:179
  15.7 0.0 collective-permute-done.4.got
  15.7 0.3 collective-permute-start.5
  16.0 0.7 %shard_map.51.kept = f32[256,384]{1,0:T(8,128)S(1)} custom-call(bf16[512,2048]{1,0:T(8,128)(2,1)S(1)} %get-tuple-element.34.prod._, bf16[384,2048]{1,0:T(8,128)(2,1)S(1)} %get-tuple-element.38.eig), custom_call_target="tpu_custom_call" | custom-call | flops 402653184 | bytes 1572864 | tf_op jit(solution)/shard_map/pallas_call | solution.py:179
  16.8 3.2 %collective-permute-done.3.got = bf16[256,384]{1,0:T(8,128)(2,1)S(1)} collective-permute-done((bf16[256,384]{1,0:T(8,128)(2,1)S(1)}, bf16[256,384]{1,0:T(8,128)(2,1)S(1)}, u32[]{:S(2)}, u32[]{:S(2)}) %collective-permute-start.3) | collective-permute-done | bytes 196640 | tf_op jit(solution)/shard_map/ppermute | solution.py:211
  20.0 0.1 collective-permute-start.6
  20.1 0.0 collective-permute-done.2.got
  20.2 6.6 %collective-permute-start.7 = (bf16[64,896]{1,0:T(8,128)(2,1)S(1)}, bf16[64,896]{1,0:T(8,128)(2,1)S(1)}, u32[]{:S(2)}, u32[]{:S(2)}) collective-permute-start(bf16[64,896]{1,0:T(8,128)(2,1)S(1)} %get-tuple-element.45._), channel_id=1, source_target_pairs={{0,8},{1,5},{2,10},{3,7},{4,12},{5,1},{6,14},{7,3},{8,0},{9,13},{1... | collective-permute-start | bytes 344072 | tf_op jit(solution)/shard_map/ppermute | solution.py:211
  26.9 3.2 %collective-permute-start.8 = (bf16[64,512]{1,0:T(8,128)(2,1)S(1)}, bf16[64,512]{1,0:T(8,128)(2,1)S(1)}, u32[]{:S(2)}, u32[]{:S(2)}) collective-permute-start(bf16[64,512]{1,0:T(8,128)(2,1)S(1)} %get-tuple-element.48._), channel_id=1, source_target_pairs={{0,4},{1,9},{2,6},{3,11},{4,0},{5,13},{6,2},{7,15},{8,12},{9,1},{1... | collective-permute-start | bytes 196616 | tf_op jit(solution)/shard_map/ppermute | solution.py:211
  30.0 0.1 collective-permute-start.9
  30.1 4.3 %collective-permute-done.9.refs_5_ = bf16[64,384]{1,0:T(8,128)(2,1)S(1)} collective-permute-done((bf16[64,384]{1,0:T(8,128)(2,1)S(1)}, bf16[64,384]{1,0:T(8,128)(2,1)S(1)}, u32[]{:S(2)}, u32[]{:S(2)}) %collective-permute-start.9) | collective-permute-done | bytes 49184 | tf_op jit(solution)/shard_map/ppermute | solution.py:211
  34.4 0.8 %shard_map.58 = f32[64,1792]{1,0:T(8,128)} custom-call(f32[64,896]{1,0:T(8,128)S(1)} %get-tuple-element.43.refs_0_, f32[64,512]{1,0:T(8,128)S(1)} %get-tuple-element.46.refs_1_, f32[64,384]{1,0:T(8,128)S(1)} %get-tuple-element.49.refs_2_, bf16[64,896]{1,0:T(8,128)(2,1)S(1)} %collective-permute-done.7.refs_3_, ...), custom_call_target="tpu_custom_call" | custom-call | flops 114688 | bytes 1376256 | tf_op jit(solution)/shard_map/pallas_call | solution.py:179
  (9 shorter events, 0.2 us)
Async XLA Ops:
  0.0 2.9 %collective-permute-start = (bf16[32,2048]{1,0:T(8,128)(2,1)}, bf16[32,2048]{1,0:T(8,128)(2,1)S(1)}, u32[]{:S(2)}, u32[]{:S(2)}) collective-permute-start(bf16[32,2048]{1,0:T(8,128)(2,1)} %own_hbm.1), channel_id=1, source_target_pairs={{0,1},{1,0},{2,3},{3,2},{4,5},{5,4},{6,7},{7,6},{8,9},{9,8},{10,11... | collective-permute-start | bytes 393224 | tf_op jit(solution)/shard_map/ppermute | solution.py:216
  4.5 8.0 %collective-permute-start.1 = (bf16[256,896]{1,0:T(8,128)(2,1)S(1)}, bf16[256,896]{1,0:T(8,128)(2,1)S(1)}, u32[]{:S(2)}, u32[]{:S(2)}) collective-permute-start(bf16[256,896]{1,0:T(8,128)(2,1)S(1)} %get-tuple-element.35), channel_id=1, source_target_pairs={{0,4},{1,3},{2,6},{3,1},{4,0},{5,7},{6,2},{7,5},{8,12},{9,11},{10,... | collective-permute-start | bytes 1376264 | tf_op jit(solution)/shard_map/ppermute | solution.py:211
  7.0 8.7 %collective-permute-start.4 = (bf16[256,512]{1,0:T(8,128)(2,1)S(1)}, bf16[256,512]{1,0:T(8,128)(2,1)S(1)}, u32[]{:S(2)}, u32[]{:S(2)}) collective-permute-start(bf16[256,512]{1,0:T(8,128)(2,1)S(1)} %get-tuple-element.40), channel_id=1, source_target_pairs={{0,2},{1,5},{2,0},{3,7},{4,6},{5,1},{6,4},{7,3},{8,10},{9,13},{10,... | collective-permute-start | bytes 786440 | tf_op jit(solution)/shard_map/ppermute | solution.py:211
  8.6 11.4 %collective-permute-start.3 = (bf16[256,384]{1,0:T(8,128)(2,1)S(1)}, bf16[256,384]{1,0:T(8,128)(2,1)S(1)}, u32[]{:S(2)}, u32[]{:S(2)}) collective-permute-start(bf16[256,384]{1,0:T(8,128)(2,1)S(1)} %get-tuple-element.39), channel_id=1, source_target_pairs={{0,2},{1,5},{2,0},{3,7},{4,6},{5,1},{6,4},{7,3},{8,10},{9,13},{10,... | collective-permute-start | bytes 589832 | tf_op jit(solution)/shard_map/ppermute | solution.py:211
  12.5 7.6 %collective-permute-start.2 = (bf16[128,896]{1,0:T(8,128)(2,1)S(1)}, bf16[128,896]{1,0:T(8,128)(2,1)S(1)}, u32[]{:S(2)}, u32[]{:S(2)}) collective-permute-start(bf16[128,896]{1,0:T(8,128)(2,1)S(1)} %get-tuple-element.37._), channel_id=1, source_target_pairs={{0,2},{1,9},{2,0},{3,11},{4,6},{5,13},{6,4},{7,15},{8,10},{9,1},{1... | collective-permute-start | bytes 688136 | tf_op jit(solution)/shard_map/ppermute | solution.py:211
  15.7 11.1 %collective-permute-start.5 = (bf16[128,512]{1,0:T(8,128)(2,1)S(1)}, bf16[128,512]{1,0:T(8,128)(2,1)S(1)}, u32[]{:S(2)}, u32[]{:S(2)}) collective-permute-start(bf16[128,512]{1,0:T(8,128)(2,1)S(1)} %get-tuple-element.41._), channel_id=1, source_target_pairs={{0,8},{1,3},{2,10},{3,1},{4,12},{5,7},{6,14},{7,5},{8,0},{9,11},{1... | collective-permute-start | bytes 393224 | tf_op jit(solution)/shard_map/ppermute | solution.py:211
  20.0 10.0 %collective-permute-start.6 = (bf16[128,384]{1,0:T(8,128)(2,1)S(1)}, bf16[128,384]{1,0:T(8,128)(2,1)S(1)}, u32[]{:S(2)}, u32[]{:S(2)}) collective-permute-start(bf16[128,384]{1,0:T(8,128)(2,1)S(1)} %get-tuple-element.42._), channel_id=1, source_target_pairs={{0,8},{1,3},{2,10},{3,1},{4,12},{5,7},{6,14},{7,5},{8,0},{9,11},{1... | collective-permute-start | bytes 294920 | tf_op jit(solution)/shard_map/ppermute | solution.py:211
  20.2 14.3 %collective-permute-start.7 = (bf16[64,896]{1,0:T(8,128)(2,1)S(1)}, bf16[64,896]{1,0:T(8,128)(2,1)S(1)}, u32[]{:S(2)}, u32[]{:S(2)}) collective-permute-start(bf16[64,896]{1,0:T(8,128)(2,1)S(1)} %get-tuple-element.45._), channel_id=1, source_target_pairs={{0,8},{1,5},{2,10},{3,7},{4,12},{5,1},{6,14},{7,3},{8,0},{9,13},{1... | collective-permute-start | bytes 344072 | tf_op jit(solution)/shard_map/ppermute | solution.py:211
  26.9 7.6 %collective-permute-start.8 = (bf16[64,512]{1,0:T(8,128)(2,1)S(1)}, bf16[64,512]{1,0:T(8,128)(2,1)S(1)}, u32[]{:S(2)}, u32[]{:S(2)}) collective-permute-start(bf16[64,512]{1,0:T(8,128)(2,1)S(1)} %get-tuple-element.48._), channel_id=1, source_target_pairs={{0,4},{1,9},{2,6},{3,11},{4,0},{5,13},{6,2},{7,15},{8,12},{9,1},{1... | collective-permute-start | bytes 196616 | tf_op jit(solution)/shard_map/ppermute | solution.py:211
  30.0 4.4 %collective-permute-start.9 = (bf16[64,384]{1,0:T(8,128)(2,1)S(1)}, bf16[64,384]{1,0:T(8,128)(2,1)S(1)}, u32[]{:S(2)}, u32[]{:S(2)}) collective-permute-start(bf16[64,384]{1,0:T(8,128)(2,1)S(1)} %get-tuple-element.50), channel_id=1, source_target_pairs={{0,4},{1,9},{2,6},{3,11},{4,0},{5,13},{6,2},{7,15},{8,12},{9,1},{1... | collective-permute-start | bytes 147464 | tf_op jit(solution)/shard_map/ppermute | solution.py:211

commit v13 on v11

--- a/solution.py
+++ b/solution.py
@@ -11,11 +11,13 @@
 VMEM_LIMIT = 32 * 1024 * 1024
 X, NEAR, FAR = 0, 1, 2
 PLAN = [
-    (3.5, (NEAR, X, FAR), (X, FAR, NEAR)),
+    (2, (NEAR, X, FAR), (X, NEAR, FAR)),
     (2, (X, NEAR, FAR), (NEAR, X, FAR)),
-    (1.5, (X, NEAR, FAR), (X, NEAR, FAR)),
+    (2, (NEAR, X, FAR), (X, NEAR, FAR)),
+    (1, (X, NEAR, FAR), (X, NEAR, FAR)),
 ]
-ORDER = [(piece, stage) for stage in (1, 2) for piece in range(len(PLAN))]
+ORDER = [(1, 0), (2, 0), (0, 1), (1, 1), (3, 0), (0, 2), (2, 1), (1, 2), (3, 1)]
+ORDER += [(0, 3), (2, 2), (1, 3), (3, 2)]
 
 
 def ranked(bits, fixed=0):
@@ -130,23 +132,22 @@
     copy.wait()
 
 
-def send_kernel(cut, pick, own, other, lanc16, half, eig, eig_hbm, *rest):
-    *outs, prod, eig_rest, acc, sem = rest
+def second_kernel(cut, pick, own, other, lanc16, half, eig, eig_hbm, out, prod, eig_next, acc, sem):
     copy = pltpu.make_async_copy(
-        eig_hbm.at[pl.ds(cut, eig_rest.shape[0])], eig_rest, sem.at[0]
+        eig_hbm.at[pl.ds(cut, eig_next.shape[0])], eig_next, sem.at[0]
     )
     copy.start()
     first = half.shape[0]
     prod[:first, :] = half[...]
     make_rows(prod.at[first:, :], pick, own, other, lanc16, first)
-    at = 0
-    for i, out in enumerate(outs):
-        part = acc.at[:, : out.shape[1]]
-        if i == 1:
-            copy.wait()
-        dot_tiles(part, rows_of(prod, i + 1, False), eig_rest if i else eig, at)
-        out[...] = part[...].astype(out.dtype)
-        at += out.shape[1] if i else 0
+    dot_tiles(acc, rows_of(prod, 1, False), eig, 0)
+    out[...] = acc[...].astype(out.dtype)
+    copy.wait()
+
+
+def send_kernel(p, first, prod, eig, _, out, acc):
+    dot_tiles(acc, rows_of(prod, p, False), eig, first)
+    out[...] = acc[...].astype(out.dtype)
 
 
 def keep_kernel(p, first, prod, eig, out):
@@ -159,11 +160,17 @@
     keep[...] = kept[mid:, :] + got[mid:, :].astype(jnp.float32)
 
 
+def last_kernel(kept, got, _, out):
+    out[...] = kept[...] + got[...].astype(jnp.float32)
+
+
 def finish_kernel(spans, *refs):
-    count = len(spans)
-    kept, came, out = refs[:count], refs[count : 2 * count], refs[-1]
-    for (at, end), a, b in zip(spans, kept, came):
-        out[:, at:end] = a[a.shape[0] - out.shape[0] :, :] + b[...].astype(jnp.float32)
+    refs, out = list(refs[:-1]), refs[-1]
+    for p, (at, end) in enumerate(spans):
+        value = refs.pop(0)[...]
+        if (p, 3) not in ORDER:
+            value += refs.pop(0)[...].astype(jnp.float32)
+        out[:, at:end] = value
 
 
 VMEM_SPEC = pl.BlockSpec(memory_space=pltpu.VMEM)
@@ -234,16 +241,15 @@
         [pltpu.VMEM((rows // 2, widths[0]), jnp.float32), pltpu.SemaphoreType.DMA((1,))],
         (flops(widths[0]), 2 * widths[0] * depth),
     )
-    *sends, prod, eig_rest = kernel_call(
-        functools.partial(send_kernel, cuts[2]),
+    second, prod, eig_rest = kernel_call(
+        functools.partial(second_kernel, cuts[2]),
         sources + [(half, False), (eig_next, False), (eigvecs, True)],
-        [((rows // 2, w), bf16) for w in widths[1:]]
-        + [((rows, depth), bf16), ((cols - cuts[2], depth), bf16)],
-        [pltpu.VMEM((rows // 2, max(widths[1:])), jnp.float32), pltpu.SemaphoreType.DMA((1,))],
-        (flops(sum(widths[1:])), 2 * sum(widths[1:]) * depth),
+        [((rows // 2, widths[1]), bf16), ((rows, depth), bf16), ((cols - cuts[2], depth), bf16)],
+        [pltpu.VMEM((rows // 2, widths[1]), jnp.float32), pltpu.SemaphoreType.DMA((1,))],
+        (flops(widths[1]), 2 * (cols - cuts[2]) * depth),
     )
     eigs = [eig, eig_next] + [eig_rest] * (len(PLAN) - 2)
-    got = [exchange(s, p, 0) for p, s in enumerate([send, *sends])]
+    got = {0: exchange(send, 0, 0)}
     value = []
     for p, width in enumerate(widths):
         value += kernel_call(
@@ -255,23 +261,53 @@
         )
     later = range(3, n.bit_length() - 1)
     token = prod
-    for p, stage in ORDER + [(p, stage) for stage in later for p in range(len(PLAN))]:
-        part = value[p].shape[0] // 2
+    events = [(p, stage) for p, stage in ORDER if stage < 3]
+    events += [(p, stage) for stage in later for p in range(len(PLAN))]
+    if not later:
+        events = ORDER
+    for p, stage in events:
+        part = rows // 2 >> stage
         size = part * widths[p]
-        leave, value[p] = kernel_call(
-            add_kernel,
-            [(value[p], False), (got[p], False), (token, None)],
-            [((part, widths[p]), bf16 if stage < 3 else jnp.float32)]
-            + [((part, widths[p]), jnp.float32)],
-            [],
-            (2 * size, 18 * size),
-        )
+        if (p, stage) == (1, 0):
+            leave = second
+        elif stage == 0:
+            (leave,) = kernel_call(
+                functools.partial(send_kernel, p, cuts[p] - cuts[2]),
+                [(prod, False), (eig_rest, False), (token, None)],
+                [((part, widths[p]), bf16)],
+                [pltpu.VMEM((part, widths[p]), jnp.float32)],
+                (flops(widths[p]), 2 * widths[p] * depth),
+            )
+        elif stage == 3 and not later:
+            (value[p],) = kernel_call(
+                last_kernel,
+                [(value[p], False), (got[p], False), (token, None)],
+                [((rows // n, widths[p]), jnp.float32)],
+                [],
+                (size, 10 * size),
+            )
+            token = value[p]
+            continue
+        else:
+            leave, value[p] = kernel_call(
+                add_kernel,
+                [(value[p], False), (got[p], False), (token, None)],
+                [((part, widths[p]), bf16 if stage < 3 else jnp.float32)]
+                + [((part, widths[p]), jnp.float32)],
+                [],
+                (2 * size, 18 * size),
+            )
         token = leave
         got[p] = exchange(leave, p, stage)
-    outs = list(zip(value, got))
+    for p in range(len(PLAN)):
+        if later and (p, 3) in ORDER:
+            value[p] += got[p]
+    parts = []
+    for p in range(len(PLAN)):
+        parts += [value[p]] if (p, 3) in ORDER else [value[p], got[p]]
     (result,) = kernel_call(
         functools.partial(finish_kernel, spans),
-        [(value, False) for value, _ in outs] + [(came, False) for _, came in outs],
+        [(part, False) for part in parts],
         [((rows // n, cols), jnp.float32)],
         [],
         (rows // n * cols, 12 * rows // n * cols),

time: 36.2 us -> 37.8 us (1.044)
  waiting for transfers between devices: 9.81 us -> 11.3 us
    ppermute x9 -> x12, waiting for transfers between devices: 9.8 us -> 11.3 us  [exchange(): return lax.ppermute(value, ('grid', 'eig'), pairs)]
    pallas_call x13 -> x20, Pallas kernels: 9.99 us -> 10.3 us  [kernel_call(): pl.pallas_call(body, out_shape=[jax.ShapeDtypeStruct(*out) for out in out...]
    ppermute x9 -> x12, starting transfers between devices: 15.7 us -> 15.4 us  [exchange(): return lax.ppermute(value, ('grid', 'eig'), pairs)]
  transfers between devices with their start and end apart: 10 -> 13, of which waited for: 4 -> 4; matrix products, arithmetic and copies ran while one was open for 0% -> 0% of each run, Pallas kernels for 21% -> 21%
where the time goes in v13:
time: 37.8 us; the launch traced here: 37.6 us
  starting transfers between devices  15.8 us (42%)
  waiting for transfers between devices  11.3 us (30%)
  Pallas kernels  10.3 us (27%)
    ppermute x12, starting transfers between devices, exchange(): return lax.ppermute(value, ('grid', 'eig'), pairs)  15.4 us
    ppermute x12, waiting for transfers between devices, exchange(): return lax.ppermute(value, ('grid', 'eig'), pairs)  11.3 us
    pallas_call x20, Pallas kernels, kernel_call(): pl.pallas_call(body, out_shape=[jax.ShapeDtypeStruct(*out) for out in out...  10.3 us
  transfers between devices with their start and end apart: 13, of which 4 were waited for; matrix products, arithmetic and copies ran while one was open for 0% of the time, Pallas kernels for 21%

profile of v13, /device:TPU:0, one launch (start us, length us, event | category | flops | bytes accessed | tf_op | source)
XLA Modules:
  0.0 37.6 jit_solution(17269245537663362348)
XLA Ops:
  0.5 1.7 %shard_map.46 = (bf16[512,64]{1,0:T(8,128)(2,1)S(1)}, bf16[32,2048]{1,0:T(8,128)(2,1)S(1)}, bf16[8,2048]{1,0:T(8,128)(2,1)S(1)}, bf16[512,2048]{1,0:T(8,128)(2,1)S(1)}) custom-call(s32[64]{0:T(128)} %order_hbm.1, bf16[32,2048]{1,0:T(8,128)(2,1)} %own_hbm.1, bf16[8,2048]{1,0:T(8,128)(2,1)} %lanc_hbm.1, bf16[1792,2048]{1,0:T(8,128)(2,1)} %eig_hbm.5), custom_call_target="tpu_custom_call" | custom-call | bytes 2097152 | tf_op jit(solution)/shard_map/pallas_call | solution.py:186
  2.2 1.6 %shard_map.47 = (bf16[256,512]{1,0:T(8,128)(2,1)S(1)}, bf16[256,2048]{1,0:T(8,128)(2,1)S(1)}, bf16[512,2048]{1,0:T(8,128)(2,1)S(1)}) custom-call(bf16[512,64]{1,0:T(8,128)(2,1)S(1)} %get-tuple-element.31.pick, bf16[32,2048]{1,0:T(8,128)(2,1)S(1)} %get-tuple-element.32.own, bf16[32,2048]{1,0:T(8,128)(2,1)S(1)} %collective-permute-done.other, ...), custom_call_target="tpu_custom_call" | custom-call | flops 536870912 | bytes 2097152 | tf_op jit(solution)/shard_map/pallas_call | solution.py:186
  3.8 2.6 %collective-permute-start.1 = (bf16[256,512]{1,0:T(8,128)(2,1)S(1)}, bf16[256,512]{1,0:T(8,128)(2,1)S(1)}, u32[]{:S(2)}, u32[]{:S(2)}) collective-permute-start(bf16[256,512]{1,0:T(8,128)(2,1)S(1)} %get-tuple-element.38), channel_id=1, source_target_pairs={{0,4},{1,3},{2,6},{3,1},{4,0},{5,7},{6,2},{7,5},{8,12},{9,11},{10,... | collective-permute-start | bytes 786440 | tf_op jit(solution)/shard_map/ppermute | solution.py:218
  6.4 2.1 %shard_map.48 = (bf16[256,512]{1,0:T(8,128)(2,1)S(1)}, bf16[512,2048]{1,0:T(8,128)(2,1)S(1)}, bf16[768,2048]{1,0:T(8,128)(2,1)S(1)}) custom-call(bf16[512,64]{1,0:T(8,128)(2,1)S(1)} %get-tuple-element.31.pick, bf16[32,2048]{1,0:T(8,128)(2,1)S(1)} %get-tuple-element.32.own, bf16[32,2048]{1,0:T(8,128)(2,1)S(1)} %collective-permute-done.other, ...), custom_call_target="tpu_custom_call" | custom-call | flops 536870912 | bytes 3145728 | tf_op jit(solution)/shard_map/pallas_call | solution.py:186
  8.5 1.6 %collective-permute-start.3 = (bf16[256,512]{1,0:T(8,128)(2,1)S(1)}, bf16[256,512]{1,0:T(8,128)(2,1)S(1)}, u32[]{:S(2)}, u32[]{:S(2)}) collective-permute-start(bf16[256,512]{1,0:T(8,128)(2,1)S(1)} %get-tuple-element.40._), channel_id=1, source_target_pairs={{0,2},{1,5},{2,0},{3,7},{4,6},{5,1},{6,4},{7,3},{8,10},{9,13},{10,... | collective-permute-start | bytes 786440 | tf_op jit(solution)/shard_map/ppermute | solution.py:218
  10.1 0.7 %shard_map.50._ = bf16[256,512]{1,0:T(8,128)(2,1)S(1)} custom-call(bf16[512,2048]{1,0:T(8,128)(2,1)S(1)} %get-tuple-element.37.prod, bf16[768,2048]{1,0:T(8,128)(2,1)S(1)} %get-tuple-element.39.eig, bf16[256,512]{1,0:T(8,128)(2,1)S(1)} %get-tuple-element.40._), custom_call_target="tpu_custom_call" | custom-call | flops 536870912 | bytes 2097152 | tf_op jit(solution)/shard_map/pallas_call | solution.py:186
  10.8 0.5 %collective-permute-start.7 = (bf16[256,512]{1,0:T(8,128)(2,1)S(1)}, bf16[256,512]{1,0:T(8,128)(2,1)S(1)}, u32[]{:S(2)}, u32[]{:S(2)}) collective-permute-start(bf16[256,512]{1,0:T(8,128)(2,1)S(1)} %shard_map.50._), channel_id=1, source_target_pairs={{0,4},{1,3},{2,6},{3,1},{4,0},{5,7},{6,2},{7,5},{8,12},{9,11},{10,... | collective-permute-start | bytes 786440 | tf_op jit(solution)/shard_map/ppermute | solution.py:218
  11.3 0.7 %shard_map.49.kept = f32[256,512]{1,0:T(8,128)S(1)} custom-call(bf16[512,2048]{1,0:T(8,128)(2,1)S(1)} %get-tuple-element.37.prod, bf16[512,2048]{1,0:T(8,128)(2,1)S(1)} %get-tuple-element.34.eig), custom_call_target="tpu_custom_call" | custom-call | flops 536870912 | bytes 2097152 | tf_op jit(solution)/shard_map/pallas_call | solution.py:186
  12.1 1.7 %collective-permute-start.2 = (bf16[128,512]{1,0:T(8,128)(2,1)S(1)}, bf16[128,512]{1,0:T(8,128)(2,1)S(1)}, u32[]{:S(2)}, u32[]{:S(2)}) collective-permute-start(bf16[128,512]{1,0:T(8,128)(2,1)S(1)} %get-tuple-element.42._), channel_id=1, source_target_pairs={{0,2},{1,5},{2,0},{3,7},{4,6},{5,1},{6,4},{7,3},{8,10},{9,13},{10,... | collective-permute-start | bytes 393224 | tf_op jit(solution)/shard_map/ppermute | solution.py:218
  13.8 0.7 %shard_map.52.kept = f32[256,512]{1,0:T(8,128)S(1)} custom-call(bf16[512,2048]{1,0:T(8,128)(2,1)S(1)} %get-tuple-element.37.prod, bf16[512,2048]{1,0:T(8,128)(2,1)S(1)} %get-tuple-element.36.eig), custom_call_target="tpu_custom_call" | custom-call | flops 536870912 | bytes 2097152 | tf_op jit(solution)/shard_map/pallas_call | solution.py:186
  14.6 1.9 %collective-permute-done.3.got = bf16[256,512]{1,0:T(8,128)(2,1)S(1)} collective-permute-done((bf16[256,512]{1,0:T(8,128)(2,1)S(1)}, bf16[256,512]{1,0:T(8,128)(2,1)S(1)}, u32[]{:S(2)}, u32[]{:S(2)}) %collective-permute-start.3) | collective-permute-done | bytes 262176 | tf_op jit(solution)/shard_map/ppermute | solution.py:218
  16.5 0.7 %collective-permute-start.6 = (bf16[128,512]{1,0:T(8,128)(2,1)S(1)}, bf16[128,512]{1,0:T(8,128)(2,1)S(1)}, u32[]{:S(2)}, u32[]{:S(2)}) collective-permute-start(bf16[128,512]{1,0:T(8,128)(2,1)S(1)} %get-tuple-element.43._), channel_id=1, source_target_pairs={{0,4},{1,3},{2,6},{3,1},{4,0},{5,7},{6,2},{7,5},{8,12},{9,11},{10,... | collective-permute-start | bytes 393224 | tf_op jit(solution)/shard_map/ppermute | solution.py:218
  17.2 0.5 %shard_map.54._ = bf16[256,256]{1,0:T(8,128)(2,1)S(1)} custom-call(bf16[512,2048]{1,0:T(8,128)(2,1)S(1)} %get-tuple-element.37.prod, bf16[768,2048]{1,0:T(8,128)(2,1)S(1)} %get-tuple-element.39.eig, bf16[128,512]{1,0:T(8,128)(2,1)S(1)} %get-tuple-element.43._), custom_call_target="tpu_custom_call" | custom-call | flops 268435456 | bytes 1048576 | tf_op jit(solution)/shard_map/pallas_call | solution.py:186
  17.6 2.5 %collective-permute-start.5 = (bf16[256,256]{1,0:T(8,128)(2,1)S(1)}, bf16[256,256]{1,0:T(8,128)(2,1)S(1)}, u32[]{:S(2)}, u32[]{:S(2)}) collective-permute-start(bf16[256,256]{1,0:T(8,128)(2,1)S(1)} %shard_map.54._), channel_id=1, source_target_pairs={{0,2},{1,3},{2,0},{3,1},{4,6},{5,7},{6,4},{7,5},{8,10},{9,11},{10,... | collective-permute-start | bytes 393224 | tf_op jit(solution)/shard_map/ppermute | solution.py:218
  20.2 0.7 %shard_map.57.kept = f32[256,512]{1,0:T(8,128)S(1)} custom-call(bf16[512,2048]{1,0:T(8,128)(2,1)S(1)} %get-tuple-element.37.prod, bf16[768,2048]{1,0:T(8,128)(2,1)S(1)} %get-tuple-element.39.eig), custom_call_target="tpu_custom_call" | custom-call | flops 536870912 | bytes 2097152 | tf_op jit(solution)/shard_map/pallas_call | solution.py:186
  21.0 0.9 %collective-permute-start.9 = (bf16[128,512]{1,0:T(8,128)(2,1)S(1)}, bf16[128,512]{1,0:T(8,128)(2,1)S(1)}, u32[]{:S(2)}, u32[]{:S(2)}) collective-permute-start(bf16[128,512]{1,0:T(8,128)(2,1)S(1)} %get-tuple-element.47._), channel_id=1, source_target_pairs={{0,2},{1,5},{2,0},{3,7},{4,6},{5,1},{6,4},{7,3},{8,10},{9,13},{10,... | collective-permute-start | bytes 393224 | tf_op jit(solution)/shard_map/ppermute | solution.py:218
  21.9 2.6 %collective-permute-start.4 = (bf16[64,512]{1,0:T(8,128)(2,1)S(1)}, bf16[64,512]{1,0:T(8,128)(2,1)S(1)}, u32[]{:S(2)}, u32[]{:S(2)}) collective-permute-start(bf16[64,512]{1,0:T(8,128)(2,1)S(1)} %get-tuple-element.45._), channel_id=1, source_target_pairs={{0,8},{1,9},{2,10},{3,11},{4,12},{5,13},{6,14},{7,15},{8,0},{9,1},... | collective-permute-start | bytes 196616 | tf_op jit(solution)/shard_map/ppermute | solution.py:218
  25.4 0.8 %collective-permute-start.11 = (bf16[128,256]{1,0:T(8,128)(2,1)S(1)}, bf16[128,256]{1,0:T(8,128)(2,1)S(1)}, u32[]{:S(2)}, u32[]{:S(2)}) collective-permute-start(bf16[128,256]{1,0:T(8,128)(2,1)S(1)} %get-tuple-element.49._), channel_id=1, source_target_pairs={{0,4},{1,5},{2,6},{3,7},{4,0},{5,1},{6,2},{7,3},{8,12},{9,13},{10,... | collective-permute-start | bytes 196616 | tf_op jit(solution)/shard_map/ppermute | solution.py:218
  26.2 3.0 %collective-permute-done.4.got = bf16[64,512]{1,0:T(8,128)(2,1)S(1)} collective-permute-done((bf16[64,512]{1,0:T(8,128)(2,1)S(1)}, bf16[64,512]{1,0:T(8,128)(2,1)S(1)}, u32[]{:S(2)}, u32[]{:S(2)}) %collective-permute-start.4) | collective-permute-done | bytes 65568 | tf_op jit(solution)/shard_map/ppermute | solution.py:218
  29.2 0.6 %collective-permute-start.10 = (bf16[64,512]{1,0:T(8,128)(2,1)S(1)}, bf16[64,512]{1,0:T(8,128)(2,1)S(1)}, u32[]{:S(2)}, u32[]{:S(2)}) collective-permute-start(bf16[64,512]{1,0:T(8,128)(2,1)S(1)} %get-tuple-element.52._), channel_id=1, source_target_pairs={{0,8},{1,9},{2,10},{3,11},{4,12},{5,13},{6,14},{7,15},{8,0},{9,1},... | collective-permute-start | bytes 196616 | tf_op jit(solution)/shard_map/ppermute | solution.py:218
  29.9 2.0 %collective-permute-done.8.got = bf16[64,512]{1,0:T(8,128)(2,1)S(1)} collective-permute-done((bf16[64,512]{1,0:T(8,128)(2,1)S(1)}, bf16[64,512]{1,0:T(8,128)(2,1)S(1)}, u32[]{:S(2)}, u32[]{:S(2)}) %collective-permute-start.8) | collective-permute-done | bytes 65568 | tf_op jit(solution)/shard_map/ppermute | solution.py:218
  31.9 0.5 %collective-permute-start.12 = (bf16[64,256]{1,0:T(8,128)(2,1)S(1)}, bf16[64,256]{1,0:T(8,128)(2,1)S(1)}, u32[]{:S(2)}, u32[]{:S(2)}) collective-permute-start(bf16[64,256]{1,0:T(8,128)(2,1)S(1)} %get-tuple-element.56), channel_id=1, source_target_pairs={{0,8},{1,9},{2,10},{3,11},{4,12},{5,13},{6,14},{7,15},{8,0},{9,1},... | collective-permute-start | bytes 98312 | tf_op jit(solution)/shard_map/ppermute | solution.py:218
  32.4 4.4 %collective-permute-done.12.refs_5_ = bf16[64,256]{1,0:T(8,128)(2,1)S(1)} collective-permute-done((bf16[64,256]{1,0:T(8,128)(2,1)S(1)}, bf16[64,256]{1,0:T(8,128)(2,1)S(1)}, u32[]{:S(2)}, u32[]{:S(2)}) %collective-permute-start.12) | collective-permute-done | bytes 32800 | tf_op jit(solution)/shard_map/ppermute | solution.py:218
  36.8 0.8 %shard_map.65 = f32[64,1792]{1,0:T(8,128)} custom-call(f32[64,512]{1,0:T(8,128)S(1)} %shard_map.61._.refs_0_, f32[64,512]{1,0:T(8,128)S(1)} %shard_map.63._.refs_1_, f32[64,512]{1,0:T(8,128)S(1)} %get-tuple-element.53.refs_2_, bf16[64,512]{1,0:T(8,128)(2,1)S(1)} %collective-permute-done.10.refs_3_, f32[64,256]{1,0:T(8,128)S(1)} %get-tuple-element.55.refs_4_, ...), custom_call_target="tpu_custom_call" | custom-call | flops 114688 | bytes 1376256 | tf_op jit(solution)/shard_map/pallas_call | solution.py:186
  (22 shorter events, 1.6 us)
Async XLA Ops:
  0.0 2.2 %collective-permute-start = (bf16[32,2048]{1,0:T(8,128)(2,1)}, bf16[32,2048]{1,0:T(8,128)(2,1)S(1)}, u32[]{:S(2)}, u32[]{:S(2)}) collective-permute-start(bf16[32,2048]{1,0:T(8,128)(2,1)} %own_hbm.1), channel_id=1, source_target_pairs={{0,1},{1,0},{2,3},{3,2},{4,5},{5,4},{6,7},{7,6},{8,9},{9,8},{10,11... | collective-permute-start | bytes 393224 | tf_op jit(solution)/shard_map/ppermute | solution.py:223
  3.8 8.3 %collective-permute-start.1 = (bf16[256,512]{1,0:T(8,128)(2,1)S(1)}, bf16[256,512]{1,0:T(8,128)(2,1)S(1)}, u32[]{:S(2)}, u32[]{:S(2)}) collective-permute-start(bf16[256,512]{1,0:T(8,128)(2,1)S(1)} %get-tuple-element.38), channel_id=1, source_target_pairs={{0,4},{1,3},{2,6},{3,1},{4,0},{5,7},{6,2},{7,5},{8,12},{9,11},{10,... | collective-permute-start | bytes 786440 | tf_op jit(solution)/shard_map/ppermute | solution.py:218
  8.5 8.0 %collective-permute-start.3 = (bf16[256,512]{1,0:T(8,128)(2,1)S(1)}, bf16[256,512]{1,0:T(8,128)(2,1)S(1)}, u32[]{:S(2)}, u32[]{:S(2)}) collective-permute-start(bf16[256,512]{1,0:T(8,128)(2,1)S(1)} %get-tuple-element.40._), channel_id=1, source_target_pairs={{0,2},{1,5},{2,0},{3,7},{4,6},{5,1},{6,4},{7,3},{8,10},{9,13},{10,... | collective-permute-start | bytes 786440 | tf_op jit(solution)/shard_map/ppermute | solution.py:218
  10.8 10.2 %collective-permute-start.7 = (bf16[256,512]{1,0:T(8,128)(2,1)S(1)}, bf16[256,512]{1,0:T(8,128)(2,1)S(1)}, u32[]{:S(2)}, u32[]{:S(2)}) collective-permute-start(bf16[256,512]{1,0:T(8,128)(2,1)S(1)} %shard_map.50._), channel_id=1, source_target_pairs={{0,4},{1,3},{2,6},{3,1},{4,0},{5,7},{6,2},{7,5},{8,12},{9,11},{10,... | collective-permute-start | bytes 786440 | tf_op jit(solution)/shard_map/ppermute | solution.py:218
  12.1 8.8 %collective-permute-start.2 = (bf16[128,512]{1,0:T(8,128)(2,1)S(1)}, bf16[128,512]{1,0:T(8,128)(2,1)S(1)}, u32[]{:S(2)}, u32[]{:S(2)}) collective-permute-start(bf16[128,512]{1,0:T(8,128)(2,1)S(1)} %get-tuple-element.42._), channel_id=1, source_target_pairs={{0,2},{1,5},{2,0},{3,7},{4,6},{5,1},{6,4},{7,3},{8,10},{9,13},{10,... | collective-permute-start | bytes 393224 | tf_op jit(solution)/shard_map/ppermute | solution.py:218
  16.5 8.4 %collective-permute-start.6 = (bf16[128,512]{1,0:T(8,128)(2,1)S(1)}, bf16[128,512]{1,0:T(8,128)(2,1)S(1)}, u32[]{:S(2)}, u32[]{:S(2)}) collective-permute-start(bf16[128,512]{1,0:T(8,128)(2,1)S(1)} %get-tuple-element.43._), channel_id=1, source_target_pairs={{0,4},{1,3},{2,6},{3,1},{4,0},{5,7},{6,2},{7,5},{8,12},{9,11},{10,... | collective-permute-start | bytes 393224 | tf_op jit(solution)/shard_map/ppermute | solution.py:218
  17.6 7.8 %collective-permute-start.5 = (bf16[256,256]{1,0:T(8,128)(2,1)S(1)}, bf16[256,256]{1,0:T(8,128)(2,1)S(1)}, u32[]{:S(2)}, u32[]{:S(2)}) collective-permute-start(bf16[256,256]{1,0:T(8,128)(2,1)S(1)} %shard_map.54._), channel_id=1, source_target_pairs={{0,2},{1,3},{2,0},{3,1},{4,6},{5,7},{6,4},{7,5},{8,10},{9,11},{10,... | collective-permute-start | bytes 393224 | tf_op jit(solution)/shard_map/ppermute | solution.py:218
  21.0 8.2 %collective-permute-start.9 = (bf16[128,512]{1,0:T(8,128)(2,1)S(1)}, bf16[128,512]{1,0:T(8,128)(2,1)S(1)}, u32[]{:S(2)}, u32[]{:S(2)}) collective-permute-start(bf16[128,512]{1,0:T(8,128)(2,1)S(1)} %get-tuple-element.47._), channel_id=1, source_target_pairs={{0,2},{1,5},{2,0},{3,7},{4,6},{5,1},{6,4},{7,3},{8,10},{9,13},{10,... | collective-permute-start | bytes 393224 | tf_op jit(solution)/shard_map/ppermute | solution.py:218
  21.9 7.3 %collective-permute-start.4 = (bf16[64,512]{1,0:T(8,128)(2,1)S(1)}, bf16[64,512]{1,0:T(8,128)(2,1)S(1)}, u32[]{:S(2)}, u32[]{:S(2)}) collective-permute-start(bf16[64,512]{1,0:T(8,128)(2,1)S(1)} %get-tuple-element.45._), channel_id=1, source_target_pairs={{0,8},{1,9},{2,10},{3,11},{4,12},{5,13},{6,14},{7,15},{8,0},{9,1},... | collective-permute-start | bytes 196616 | tf_op jit(solution)/shard_map/ppermute | solution.py:218
  25.0 6.9 %collective-permute-start.8 = (bf16[64,512]{1,0:T(8,128)(2,1)S(1)}, bf16[64,512]{1,0:T(8,128)(2,1)S(1)}, u32[]{:S(2)}, u32[]{:S(2)}) collective-permute-start(bf16[64,512]{1,0:T(8,128)(2,1)S(1)} %get-tuple-element.48._), channel_id=1, source_target_pairs={{0,8},{1,9},{2,10},{3,11},{4,12},{5,13},{6,14},{7,15},{8,0},{9,1},... | collective-permute-start | bytes 196616 | tf_op jit(solution)/shard_map/ppermute | solution.py:218
  25.4 6.5 %collective-permute-start.11 = (bf16[128,256]{1,0:T(8,128)(2,1)S(1)}, bf16[128,256]{1,0:T(8,128)(2,1)S(1)}, u32[]{:S(2)}, u32[]{:S(2)}) collective-permute-start(bf16[128,256]{1,0:T(8,128)(2,1)S(1)} %get-tuple-element.49._), channel_id=1, source_target_pairs={{0,4},{1,5},{2,6},{3,7},{4,0},{5,1},{6,2},{7,3},{8,12},{9,13},{10,... | collective-permute-start | bytes 196616 | tf_op jit(solution)/shard_map/ppermute | solution.py:218
  29.2 7.6 %collective-permute-start.10 = (bf16[64,512]{1,0:T(8,128)(2,1)S(1)}, bf16[64,512]{1,0:T(8,128)(2,1)S(1)}, u32[]{:S(2)}, u32[]{:S(2)}) collective-permute-start(bf16[64,512]{1,0:T(8,128)(2,1)S(1)} %get-tuple-element.52._), channel_id=1, source_target_pairs={{0,8},{1,9},{2,10},{3,11},{4,12},{5,13},{6,14},{7,15},{8,0},{9,1},... | collective-permute-start | bytes 196616 | tf_op jit(solution)/shard_map/ppermute | solution.py:218
  31.9 4.9 %collective-permute-start.12 = (bf16[64,256]{1,0:T(8,128)(2,1)S(1)}, bf16[64,256]{1,0:T(8,128)(2,1)S(1)}, u32[]{:S(2)}, u32[]{:S(2)}) collective-permute-start(bf16[64,256]{1,0:T(8,128)(2,1)S(1)} %get-tuple-element.56), channel_id=1, source_target_pairs={{0,8},{1,9},{2,10},{3,11},{4,12},{5,13},{6,14},{7,15},{8,0},{9,1},... | collective-permute-start | bytes 98312 | tf_op jit(solution)/shard_map/ppermute | solution.py:218

commit v14 on v12

--- a/solution.py
+++ b/solution.py
@@ -12,8 +12,8 @@
 X, NEAR, FAR = 0, 1, 2
 PLAN = [
     (3.5, (NEAR, X, FAR), (X, FAR, NEAR)),
-    (2, (X, FAR, NEAR), (NEAR, X, FAR)),
-    (1.5, (X, FAR, NEAR), (NEAR, X, FAR)),
+    (2, (X, NEAR, FAR), (FAR, X, NEAR)),
+    (1.5, (NEAR, X, FAR), (X, FAR, NEAR)),
 ]
 ORDER = [(piece, stage) for stage in (1, 2) for piece in range(len(PLAN))]
 

time: 35.4 us -> 33.2 us (0.938)
  the two profiles are of different devices: /device:TPU:3 before, /device:TPU:0 now
where the time goes in v14:
time: 33.2 us; the launch traced here: 33 us
  starting transfers between devices  16.3 us (49%)
  Pallas kernels  10 us (30%)
  waiting for transfers between devices  6.56 us (20%)
    ppermute x9, starting transfers between devices, exchange(): return lax.ppermute(value, ('grid', 'eig'), pairs)  15.9 us
    pallas_call x13, Pallas kernels, kernel_call(): pl.pallas_call(body, out_shape=[jax.ShapeDtypeStruct(*out) for out in out...  10 us
    ppermute x9, waiting for transfers between devices, exchange(): return lax.ppermute(value, ('grid', 'eig'), pairs)  6.56 us
  transfers between devices with their start and end apart: 10, of which 3 were waited for; matrix products, arithmetic and copies ran while one was open for 0% of the time, Pallas kernels for 23%

profile of v14, /device:TPU:0, one launch (start us, length us, event | category | flops | bytes accessed | tf_op | source)
XLA Modules:
  0.0 33.0 jit_solution(6102873518721716411)
XLA Ops:
  0.0 0.5 %collective-permute-start = (bf16[32,2048]{1,0:T(8,128)(2,1)}, bf16[32,2048]{1,0:T(8,128)(2,1)S(1)}, u32[]{:S(2)}, u32[]{:S(2)}) collective-permute-start(bf16[32,2048]{1,0:T(8,128)(2,1)} %own_hbm.1), channel_id=1, source_target_pairs={{0,1},{1,0},{2,3},{3,2},{4,5},{5,4},{6,7},{7,6},{8,9},{9,8},{10,11... | collective-permute-start | bytes 393224 | tf_op jit(solution)/shard_map/ppermute | solution.py:216
  0.5 2.2 %shard_map.46 = (bf16[512,64]{1,0:T(8,128)(2,1)S(1)}, bf16[32,2048]{1,0:T(8,128)(2,1)S(1)}, bf16[8,2048]{1,0:T(8,128)(2,1)S(1)}, bf16[896,2048]{1,0:T(8,128)(2,1)S(1)}) custom-call(s32[64]{0:T(128)} %order_hbm.1, bf16[32,2048]{1,0:T(8,128)(2,1)} %own_hbm.1, bf16[8,2048]{1,0:T(8,128)(2,1)} %lanc_hbm.1, bf16[1792,2048]{1,0:T(8,128)(2,1)} %eig_hbm.5), custom_call_target="tpu_custom_call" | custom-call | bytes 3670016 | tf_op jit(solution)/shard_map/pallas_call | solution.py:179
  2.6 0.0 collective-permute-done.other
  2.6 1.6 %shard_map.47 = (bf16[256,896]{1,0:T(8,128)(2,1)S(1)}, bf16[256,2048]{1,0:T(8,128)(2,1)S(1)}, bf16[512,2048]{1,0:T(8,128)(2,1)S(1)}) custom-call(bf16[512,64]{1,0:T(8,128)(2,1)S(1)} %get-tuple-element.28.pick, bf16[32,2048]{1,0:T(8,128)(2,1)S(1)} %get-tuple-element.29.own, bf16[32,2048]{1,0:T(8,128)(2,1)S(1)} %collective-permute-done.other, ...), custom_call_target="tpu_custom_call" | custom-call | flops 939524096 | bytes 3670016 | tf_op jit(solution)/shard_map/pallas_call | solution.py:179
  4.3 2.6 %collective-permute-start.1 = (bf16[256,896]{1,0:T(8,128)(2,1)S(1)}, bf16[256,896]{1,0:T(8,128)(2,1)S(1)}, u32[]{:S(2)}, u32[]{:S(2)}) collective-permute-start(bf16[256,896]{1,0:T(8,128)(2,1)S(1)} %get-tuple-element.35), channel_id=1, source_target_pairs={{0,4},{1,3},{2,6},{3,1},{4,0},{5,7},{6,2},{7,5},{8,12},{9,11},{10,... | collective-permute-start | bytes 1376264 | tf_op jit(solution)/shard_map/ppermute | solution.py:211
  6.9 2.5 %shard_map.48 = (bf16[256,512]{1,0:T(8,128)(2,1)S(1)}, bf16[256,384]{1,0:T(8,128)(2,1)S(1)}, bf16[512,2048]{1,0:T(8,128)(2,1)S(1)}, bf16[384,2048]{1,0:T(8,128)(2,1)S(1)}) custom-call(bf16[512,64]{1,0:T(8,128)(2,1)S(1)} %get-tuple-element.28.pick, bf16[32,2048]{1,0:T(8,128)(2,1)S(1)} %get-tuple-element.29.own, ...), custom_call_target="tpu_custom_call" | custom-call | flops 939524096 | bytes 3670016 | tf_op jit(solution)/shard_map/pallas_call | solution.py:179
  9.4 1.6 %collective-permute-start.4 = (bf16[256,512]{1,0:T(8,128)(2,1)S(1)}, bf16[256,512]{1,0:T(8,128)(2,1)S(1)}, u32[]{:S(2)}, u32[]{:S(2)}) collective-permute-start(bf16[256,512]{1,0:T(8,128)(2,1)S(1)} %get-tuple-element.40), channel_id=1, source_target_pairs={{0,2},{1,9},{2,0},{3,11},{4,6},{5,13},{6,4},{7,15},{8,10},{9,1},{1... | collective-permute-start | bytes 786440 | tf_op jit(solution)/shard_map/ppermute | solution.py:211
  10.9 0.4 %collective-permute-start.3 = (bf16[256,384]{1,0:T(8,128)(2,1)S(1)}, bf16[256,384]{1,0:T(8,128)(2,1)S(1)}, u32[]{:S(2)}, u32[]{:S(2)}) collective-permute-start(bf16[256,384]{1,0:T(8,128)(2,1)S(1)} %get-tuple-element.39), channel_id=1, source_target_pairs={{0,4},{1,3},{2,6},{3,1},{4,0},{5,7},{6,2},{7,5},{8,12},{9,11},{10,... | collective-permute-start | bytes 589832 | tf_op jit(solution)/shard_map/ppermute | solution.py:211
  11.4 1.3 %shard_map.49.kept = f32[256,896]{1,0:T(8,128)S(1)} custom-call(bf16[512,2048]{1,0:T(8,128)(2,1)S(1)} %get-tuple-element.34.prod._, bf16[896,2048]{1,0:T(8,128)(2,1)S(1)} %get-tuple-element.31.eig), custom_call_target="tpu_custom_call" | custom-call | flops 939524096 | bytes 3670016 | tf_op jit(solution)/shard_map/pallas_call | solution.py:179
  12.6 2.0 %collective-permute-done.1.got = bf16[256,896]{1,0:T(8,128)(2,1)S(1)} collective-permute-done((bf16[256,896]{1,0:T(8,128)(2,1)S(1)}, bf16[256,896]{1,0:T(8,128)(2,1)S(1)}, u32[]{:S(2)}, u32[]{:S(2)}) %collective-permute-start.1) | collective-permute-done | bytes 458784 | tf_op jit(solution)/shard_map/ppermute | solution.py:211
  14.6 0.1 shard_map.50
  14.7 3.5 %collective-permute-start.2 = (bf16[128,896]{1,0:T(8,128)(2,1)S(1)}, bf16[128,896]{1,0:T(8,128)(2,1)S(1)}, u32[]{:S(2)}, u32[]{:S(2)}) collective-permute-start(bf16[128,896]{1,0:T(8,128)(2,1)S(1)} %get-tuple-element.37._), channel_id=1, source_target_pairs={{0,2},{1,9},{2,0},{3,11},{4,6},{5,13},{6,4},{7,15},{8,10},{9,1},{1... | collective-permute-start | bytes 688136 | tf_op jit(solution)/shard_map/ppermute | solution.py:211
  18.2 0.7 %shard_map.52.kept = f32[256,512]{1,0:T(8,128)S(1)} custom-call(bf16[512,2048]{1,0:T(8,128)(2,1)S(1)} %get-tuple-element.34.prod._, bf16[512,2048]{1,0:T(8,128)(2,1)S(1)} %get-tuple-element.33.eig), custom_call_target="tpu_custom_call" | custom-call | flops 536870912 | bytes 2097152 | tf_op jit(solution)/shard_map/pallas_call | solution.py:179
  19.0 0.0 collective-permute-done.4.got
  19.0 0.4 %collective-permute-start.5 = (bf16[128,512]{1,0:T(8,128)(2,1)S(1)}, bf16[128,512]{1,0:T(8,128)(2,1)S(1)}, u32[]{:S(2)}, u32[]{:S(2)}) collective-permute-start(bf16[128,512]{1,0:T(8,128)(2,1)S(1)} %get-tuple-element.41._), channel_id=1, source_target_pairs={{0,4},{1,3},{2,6},{3,1},{4,0},{5,7},{6,2},{7,5},{8,12},{9,11},{10,... | collective-permute-start | bytes 393224 | tf_op jit(solution)/shard_map/ppermute | solution.py:211
  19.4 0.7 %shard_map.51.kept = f32[256,384]{1,0:T(8,128)S(1)} custom-call(bf16[512,2048]{1,0:T(8,128)(2,1)S(1)} %get-tuple-element.34.prod._, bf16[384,2048]{1,0:T(8,128)(2,1)S(1)} %get-tuple-element.38.eig), custom_call_target="tpu_custom_call" | custom-call | flops 402653184 | bytes 1572864 | tf_op jit(solution)/shard_map/pallas_call | solution.py:179
  20.1 0.0 collective-permute-done.3.got
  20.2 2.2 %collective-permute-start.6 = (bf16[128,384]{1,0:T(8,128)(2,1)S(1)}, bf16[128,384]{1,0:T(8,128)(2,1)S(1)}, u32[]{:S(2)}, u32[]{:S(2)}) collective-permute-start(bf16[128,384]{1,0:T(8,128)(2,1)S(1)} %get-tuple-element.42._), channel_id=1, source_target_pairs={{0,2},{1,9},{2,0},{3,11},{4,6},{5,13},{6,4},{7,15},{8,10},{9,1},{1... | collective-permute-start | bytes 294920 | tf_op jit(solution)/shard_map/ppermute | solution.py:211
  22.4 1.2 %collective-permute-done.2.got = bf16[128,896]{1,0:T(8,128)(2,1)S(1)} collective-permute-done((bf16[128,896]{1,0:T(8,128)(2,1)S(1)}, bf16[128,896]{1,0:T(8,128)(2,1)S(1)}, u32[]{:S(2)}, u32[]{:S(2)}) %collective-permute-start.2) | collective-permute-done | bytes 229408 | tf_op jit(solution)/shard_map/ppermute | solution.py:211
  23.7 2.0 %collective-permute-start.7 = (bf16[64,896]{1,0:T(8,128)(2,1)S(1)}, bf16[64,896]{1,0:T(8,128)(2,1)S(1)}, u32[]{:S(2)}, u32[]{:S(2)}) collective-permute-start(bf16[64,896]{1,0:T(8,128)(2,1)S(1)} %get-tuple-element.45._), channel_id=1, source_target_pairs={{0,8},{1,5},{2,10},{3,7},{4,12},{5,1},{6,14},{7,3},{8,0},{9,13},{1... | collective-permute-start | bytes 344072 | tf_op jit(solution)/shard_map/ppermute | solution.py:211
  25.8 1.0 %collective-permute-start.8 = (bf16[64,512]{1,0:T(8,128)(2,1)S(1)}, bf16[64,512]{1,0:T(8,128)(2,1)S(1)}, u32[]{:S(2)}, u32[]{:S(2)}) collective-permute-start(bf16[64,512]{1,0:T(8,128)(2,1)S(1)} %get-tuple-element.48._), channel_id=1, source_target_pairs={{0,8},{1,5},{2,10},{3,7},{4,12},{5,1},{6,14},{7,3},{8,0},{9,13},{1... | collective-permute-start | bytes 196616 | tf_op jit(solution)/shard_map/ppermute | solution.py:211
  26.8 2.0 %collective-permute-start.9 = (bf16[64,384]{1,0:T(8,128)(2,1)S(1)}, bf16[64,384]{1,0:T(8,128)(2,1)S(1)}, u32[]{:S(2)}, u32[]{:S(2)}) collective-permute-start(bf16[64,384]{1,0:T(8,128)(2,1)S(1)} %get-tuple-element.50), channel_id=1, source_target_pairs={{0,8},{1,5},{2,10},{3,7},{4,12},{5,1},{6,14},{7,3},{8,0},{9,13},{1... | collective-permute-start | bytes 147464 | tf_op jit(solution)/shard_map/ppermute | solution.py:211
  28.8 3.3 %collective-permute-done.9.refs_5_ = bf16[64,384]{1,0:T(8,128)(2,1)S(1)} collective-permute-done((bf16[64,384]{1,0:T(8,128)(2,1)S(1)}, bf16[64,384]{1,0:T(8,128)(2,1)S(1)}, u32[]{:S(2)}, u32[]{:S(2)}) %collective-permute-start.9) | collective-permute-done | bytes 49184 | tf_op jit(solution)/shard_map/ppermute | solution.py:211
  32.2 0.8 %shard_map.58 = f32[64,1792]{1,0:T(8,128)} custom-call(f32[64,896]{1,0:T(8,128)S(1)} %get-tuple-element.43.refs_0_, f32[64,512]{1,0:T(8,128)S(1)} %get-tuple-element.46.refs_1_, f32[64,384]{1,0:T(8,128)S(1)} %get-tuple-element.49.refs_2_, bf16[64,896]{1,0:T(8,128)(2,1)S(1)} %collective-permute-done.7.refs_3_, ...), custom_call_target="tpu_custom_call" | custom-call | flops 114688 | bytes 1376256 | tf_op jit(solution)/shard_map/pallas_call | solution.py:179
  (9 shorter events, 0.2 us)
Async XLA Ops:
  0.0 2.6 %collective-permute-start = (bf16[32,2048]{1,0:T(8,128)(2,1)}, bf16[32,2048]{1,0:T(8,128)(2,1)S(1)}, u32[]{:S(2)}, u32[]{:S(2)}) collective-permute-start(bf16[32,2048]{1,0:T(8,128)(2,1)} %own_hbm.1), channel_id=1, source_target_pairs={{0,1},{1,0},{2,3},{3,2},{4,5},{5,4},{6,7},{7,6},{8,9},{9,8},{10,11... | collective-permute-start | bytes 393224 | tf_op jit(solution)/shard_map/ppermute | solution.py:216
  4.3 10.4 %collective-permute-start.1 = (bf16[256,896]{1,0:T(8,128)(2,1)S(1)}, bf16[256,896]{1,0:T(8,128)(2,1)S(1)}, u32[]{:S(2)}, u32[]{:S(2)}) collective-permute-start(bf16[256,896]{1,0:T(8,128)(2,1)S(1)} %get-tuple-element.35), channel_id=1, source_target_pairs={{0,4},{1,3},{2,6},{3,1},{4,0},{5,7},{6,2},{7,5},{8,12},{9,11},{10,... | collective-permute-start | bytes 1376264 | tf_op jit(solution)/shard_map/ppermute | solution.py:211
  9.4 9.6 %collective-permute-start.4 = (bf16[256,512]{1,0:T(8,128)(2,1)S(1)}, bf16[256,512]{1,0:T(8,128)(2,1)S(1)}, u32[]{:S(2)}, u32[]{:S(2)}) collective-permute-start(bf16[256,512]{1,0:T(8,128)(2,1)S(1)} %get-tuple-element.40), channel_id=1, source_target_pairs={{0,2},{1,9},{2,0},{3,11},{4,6},{5,13},{6,4},{7,15},{8,10},{9,1},{1... | collective-permute-start | bytes 786440 | tf_op jit(solution)/shard_map/ppermute | solution.py:211
  10.9 9.2 %collective-permute-start.3 = (bf16[256,384]{1,0:T(8,128)(2,1)S(1)}, bf16[256,384]{1,0:T(8,128)(2,1)S(1)}, u32[]{:S(2)}, u32[]{:S(2)}) collective-permute-start(bf16[256,384]{1,0:T(8,128)(2,1)S(1)} %get-tuple-element.39), channel_id=1, source_target_pairs={{0,4},{1,3},{2,6},{3,1},{4,0},{5,7},{6,2},{7,5},{8,12},{9,11},{10,... | collective-permute-start | bytes 589832 | tf_op jit(solution)/shard_map/ppermute | solution.py:211
  14.7 8.9 %collective-permute-start.2 = (bf16[128,896]{1,0:T(8,128)(2,1)S(1)}, bf16[128,896]{1,0:T(8,128)(2,1)S(1)}, u32[]{:S(2)}, u32[]{:S(2)}) collective-permute-start(bf16[128,896]{1,0:T(8,128)(2,1)S(1)} %get-tuple-element.37._), channel_id=1, source_target_pairs={{0,2},{1,9},{2,0},{3,11},{4,6},{5,13},{6,4},{7,15},{8,10},{9,1},{1... | collective-permute-start | bytes 688136 | tf_op jit(solution)/shard_map/ppermute | solution.py:211
  19.0 6.7 %collective-permute-start.5 = (bf16[128,512]{1,0:T(8,128)(2,1)S(1)}, bf16[128,512]{1,0:T(8,128)(2,1)S(1)}, u32[]{:S(2)}, u32[]{:S(2)}) collective-permute-start(bf16[128,512]{1,0:T(8,128)(2,1)S(1)} %get-tuple-element.41._), channel_id=1, source_target_pairs={{0,4},{1,3},{2,6},{3,1},{4,0},{5,7},{6,2},{7,5},{8,12},{9,11},{10,... | collective-permute-start | bytes 393224 | tf_op jit(solution)/shard_map/ppermute | solution.py:211
  20.2 6.6 %collective-permute-start.6 = (bf16[128,384]{1,0:T(8,128)(2,1)S(1)}, bf16[128,384]{1,0:T(8,128)(2,1)S(1)}, u32[]{:S(2)}, u32[]{:S(2)}) collective-permute-start(bf16[128,384]{1,0:T(8,128)(2,1)S(1)} %get-tuple-element.42._), channel_id=1, source_target_pairs={{0,2},{1,9},{2,0},{3,11},{4,6},{5,13},{6,4},{7,15},{8,10},{9,1},{1... | collective-permute-start | bytes 294920 | tf_op jit(solution)/shard_map/ppermute | solution.py:211
  23.7 8.5 %collective-permute-start.7 = (bf16[64,896]{1,0:T(8,128)(2,1)S(1)}, bf16[64,896]{1,0:T(8,128)(2,1)S(1)}, u32[]{:S(2)}, u32[]{:S(2)}) collective-permute-start(bf16[64,896]{1,0:T(8,128)(2,1)S(1)} %get-tuple-element.45._), channel_id=1, source_target_pairs={{0,8},{1,5},{2,10},{3,7},{4,12},{5,1},{6,14},{7,3},{8,0},{9,13},{1... | collective-permute-start | bytes 344072 | tf_op jit(solution)/shard_map/ppermute | solution.py:211
  25.8 6.4 %collective-permute-start.8 = (bf16[64,512]{1,0:T(8,128)(2,1)S(1)}, bf16[64,512]{1,0:T(8,128)(2,1)S(1)}, u32[]{:S(2)}, u32[]{:S(2)}) collective-permute-start(bf16[64,512]{1,0:T(8,128)(2,1)S(1)} %get-tuple-element.48._), channel_id=1, source_target_pairs={{0,8},{1,5},{2,10},{3,7},{4,12},{5,1},{6,14},{7,3},{8,0},{9,13},{1... | collective-permute-start | bytes 196616 | tf_op jit(solution)/shard_map/ppermute | solution.py:211
  26.8 5.4 %collective-permute-start.9 = (bf16[64,384]{1,0:T(8,128)(2,1)S(1)}, bf16[64,384]{1,0:T(8,128)(2,1)S(1)}, u32[]{:S(2)}, u32[]{:S(2)}) collective-permute-start(bf16[64,384]{1,0:T(8,128)(2,1)S(1)} %get-tuple-element.50), channel_id=1, source_target_pairs={{0,8},{1,5},{2,10},{3,7},{4,12},{5,1},{6,14},{7,3},{8,0},{9,13},{1... | collective-permute-start | bytes 147464 | tf_op jit(solution)/shard_map/ppermute | solution.py:211

commit v15 on v14

--- a/solution.py
+++ b/solution.py
@@ -11,9 +11,9 @@
 VMEM_LIMIT = 32 * 1024 * 1024
 X, NEAR, FAR = 0, 1, 2
 PLAN = [
-    (3.5, (NEAR, X, FAR), (X, FAR, NEAR)),
+    (3, (NEAR, X, FAR), (X, FAR, NEAR)),
     (2, (X, NEAR, FAR), (FAR, X, NEAR)),
-    (1.5, (NEAR, X, FAR), (X, FAR, NEAR)),
+    (2, (NEAR, X, FAR), (X, FAR, NEAR)),
 ]
 ORDER = [(piece, stage) for stage in (1, 2) for piece in range(len(PLAN))]
 

time: 33.2 us -> 34.7 us (1.045)
  starting transfers between devices: 16.3 us -> 17.6 us
  waiting for transfers between devices: 6.56 us -> 7.04 us
    ppermute x9, starting transfers between devices: 15.9 us -> 17.1 us  [exchange(): return lax.ppermute(value, ('grid', 'eig'), pairs)]
    ppermute x9, waiting for transfers between devices: 6.56 us -> 7.03 us  [exchange(): return lax.ppermute(value, ('grid', 'eig'), pairs)]
  transfers between devices with their start and end apart: 10 -> 10, of which waited for: 3 -> 5; matrix products, arithmetic and copies ran while one was open for 0% -> 0% of each run, Pallas kernels for 23% -> 21%
where the time goes in v15:
time: 34.7 us; the launch traced here: 34.5 us
  starting transfers between devices  17.6 us (51%)
  Pallas kernels  9.79 us (28%)
  waiting for transfers between devices  7.04 us (20%)
    ppermute x9, starting transfers between devices, exchange(): return lax.ppermute(value, ('grid', 'eig'), pairs)  17.1 us
    pallas_call x13, Pallas kernels, kernel_call(): pl.pallas_call(body, out_shape=[jax.ShapeDtypeStruct(*out) for out in out...  9.79 us
    ppermute x9, waiting for transfers between devices, exchange(): return lax.ppermute(value, ('grid', 'eig'), pairs)  7.03 us
  transfers between devices with their start and end apart: 10, of which 5 were waited for; matrix products, arithmetic and copies ran while one was open for 0% of the time, Pallas kernels for 21%

profile of v15, /device:TPU:0, one launch (start us, length us, event | category | flops | bytes accessed | tf_op | source)
XLA Modules:
  0.0 34.5 jit_solution(5255334287962594818)
XLA Ops:
  0.0 0.5 %collective-permute-start = (bf16[32,2048]{1,0:T(8,128)(2,1)}, bf16[32,2048]{1,0:T(8,128)(2,1)S(1)}, u32[]{:S(2)}, u32[]{:S(2)}) collective-permute-start(bf16[32,2048]{1,0:T(8,128)(2,1)} %own_hbm.1), channel_id=1, source_target_pairs={{0,1},{1,0},{2,3},{3,2},{4,5},{5,4},{6,7},{7,6},{8,9},{9,8},{10,11... | collective-permute-start | bytes 393224 | tf_op jit(solution)/shard_map/ppermute | solution.py:216
  0.5 2.0 %shard_map.46 = (bf16[512,64]{1,0:T(8,128)(2,1)S(1)}, bf16[32,2048]{1,0:T(8,128)(2,1)S(1)}, bf16[8,2048]{1,0:T(8,128)(2,1)S(1)}, bf16[768,2048]{1,0:T(8,128)(2,1)S(1)}) custom-call(s32[64]{0:T(128)} %order_hbm.1, bf16[32,2048]{1,0:T(8,128)(2,1)} %own_hbm.1, bf16[8,2048]{1,0:T(8,128)(2,1)} %lanc_hbm.1, bf16[1792,2048]{1,0:T(8,128)(2,1)} %eig_hbm.5), custom_call_target="tpu_custom_call" | custom-call | bytes 3145728 | tf_op jit(solution)/shard_map/pallas_call | solution.py:179
  2.5 0.0 collective-permute-done.other
  2.5 1.6 %shard_map.47 = (bf16[256,768]{1,0:T(8,128)(2,1)S(1)}, bf16[256,2048]{1,0:T(8,128)(2,1)S(1)}, bf16[512,2048]{1,0:T(8,128)(2,1)S(1)}) custom-call(bf16[512,64]{1,0:T(8,128)(2,1)S(1)} %get-tuple-element.28.pick, bf16[32,2048]{1,0:T(8,128)(2,1)S(1)} %get-tuple-element.29.own, bf16[32,2048]{1,0:T(8,128)(2,1)S(1)} %collective-permute-done.other, ...), custom_call_target="tpu_custom_call" | custom-call | flops 805306368 | bytes 3145728 | tf_op jit(solution)/shard_map/pallas_call | solution.py:179
  4.1 2.6 %collective-permute-start.1 = (bf16[256,768]{1,0:T(8,128)(2,1)S(1)}, bf16[256,768]{1,0:T(8,128)(2,1)S(1)}, u32[]{:S(2)}, u32[]{:S(2)}) collective-permute-start(bf16[256,768]{1,0:T(8,128)(2,1)S(1)} %get-tuple-element.35), channel_id=1, source_target_pairs={{0,4},{1,3},{2,6},{3,1},{4,0},{5,7},{6,2},{7,5},{8,12},{9,11},{10,... | collective-permute-start | bytes 1179656 | tf_op jit(solution)/shard_map/ppermute | solution.py:211
  6.7 2.7 %shard_map.48 = (bf16[256,512]{1,0:T(8,128)(2,1)S(1)}, bf16[256,512]{1,0:T(8,128)(2,1)S(1)}, bf16[512,2048]{1,0:T(8,128)(2,1)S(1)}, bf16[512,2048]{1,0:T(8,128)(2,1)S(1)}) custom-call(bf16[512,64]{1,0:T(8,128)(2,1)S(1)} %get-tuple-element.28.pick, bf16[32,2048]{1,0:T(8,128)(2,1)S(1)} %get-tuple-element.29.own, ...), custom_call_target="tpu_custom_call" | custom-call | flops 1073741824 | bytes 4194304 | tf_op jit(solution)/shard_map/pallas_call | solution.py:179
  9.4 1.5 %collective-permute-start.4 = (bf16[256,512]{1,0:T(8,128)(2,1)S(1)}, bf16[256,512]{1,0:T(8,128)(2,1)S(1)}, u32[]{:S(2)}, u32[]{:S(2)}) collective-permute-start(bf16[256,512]{1,0:T(8,128)(2,1)S(1)} %get-tuple-element.40), channel_id=1, source_target_pairs={{0,2},{1,9},{2,0},{3,11},{4,6},{5,13},{6,4},{7,15},{8,10},{9,1},{1... | collective-permute-start | bytes 786440 | tf_op jit(solution)/shard_map/ppermute | solution.py:211
  11.0 0.5 %collective-permute-start.3 = (bf16[256,512]{1,0:T(8,128)(2,1)S(1)}, bf16[256,512]{1,0:T(8,128)(2,1)S(1)}, u32[]{:S(2)}, u32[]{:S(2)}) collective-permute-start(bf16[256,512]{1,0:T(8,128)(2,1)S(1)} %get-tuple-element.39), channel_id=1, source_target_pairs={{0,4},{1,3},{2,6},{3,1},{4,0},{5,7},{6,2},{7,5},{8,12},{9,11},{10,... | collective-permute-start | bytes 786440 | tf_op jit(solution)/shard_map/ppermute | solution.py:211
  11.4 1.0 %shard_map.49.kept = f32[256,768]{1,0:T(8,128)S(1)} custom-call(bf16[512,2048]{1,0:T(8,128)(2,1)S(1)} %get-tuple-element.34.prod._, bf16[768,2048]{1,0:T(8,128)(2,1)S(1)} %get-tuple-element.31.eig), custom_call_target="tpu_custom_call" | custom-call | flops 805306368 | bytes 3145728 | tf_op jit(solution)/shard_map/pallas_call | solution.py:179
  12.4 0.1 collective-permute-done.1.got
  12.5 0.1 shard_map.50
  12.6 3.9 %collective-permute-start.2 = (bf16[128,768]{1,0:T(8,128)(2,1)S(1)}, bf16[128,768]{1,0:T(8,128)(2,1)S(1)}, u32[]{:S(2)}, u32[]{:S(2)}) collective-permute-start(bf16[128,768]{1,0:T(8,128)(2,1)S(1)} %get-tuple-element.37._), channel_id=1, source_target_pairs={{0,2},{1,9},{2,0},{3,11},{4,6},{5,13},{6,4},{7,15},{8,10},{9,1},{1... | collective-permute-start | bytes 589832 | tf_op jit(solution)/shard_map/ppermute | solution.py:211
  16.5 0.7 %shard_map.52.kept = f32[256,512]{1,0:T(8,128)S(1)} custom-call(bf16[512,2048]{1,0:T(8,128)(2,1)S(1)} %get-tuple-element.34.prod._, bf16[512,2048]{1,0:T(8,128)(2,1)S(1)} %get-tuple-element.33.eig), custom_call_target="tpu_custom_call" | custom-call | flops 536870912 | bytes 2097152 | tf_op jit(solution)/shard_map/pallas_call | solution.py:179
  17.2 0.7 %shard_map.51.kept = f32[256,512]{1,0:T(8,128)S(1)} custom-call(bf16[512,2048]{1,0:T(8,128)(2,1)S(1)} %get-tuple-element.34.prod._, bf16[512,2048]{1,0:T(8,128)(2,1)S(1)} %get-tuple-element.38.eig), custom_call_target="tpu_custom_call" | custom-call | flops 536870912 | bytes 2097152 | tf_op jit(solution)/shard_map/pallas_call | solution.py:179
  18.0 0.4 %collective-permute-start.5 = (bf16[128,512]{1,0:T(8,128)(2,1)S(1)}, bf16[128,512]{1,0:T(8,128)(2,1)S(1)}, u32[]{:S(2)}, u32[]{:S(2)}) collective-permute-start(bf16[128,512]{1,0:T(8,128)(2,1)S(1)} %get-tuple-element.41._), channel_id=1, source_target_pairs={{0,4},{1,3},{2,6},{3,1},{4,0},{5,7},{6,2},{7,5},{8,12},{9,11},{10,... | collective-permute-start | bytes 393224 | tf_op jit(solution)/shard_map/ppermute | solution.py:211
  18.4 0.9 %collective-permute-done.3.got = bf16[256,512]{1,0:T(8,128)(2,1)S(1)} collective-permute-done((bf16[256,512]{1,0:T(8,128)(2,1)S(1)}, bf16[256,512]{1,0:T(8,128)(2,1)S(1)}, u32[]{:S(2)}, u32[]{:S(2)}) %collective-permute-start.3) | collective-permute-done | bytes 262176 | tf_op jit(solution)/shard_map/ppermute | solution.py:211
  19.3 2.6 %collective-permute-start.6 = (bf16[128,512]{1,0:T(8,128)(2,1)S(1)}, bf16[128,512]{1,0:T(8,128)(2,1)S(1)}, u32[]{:S(2)}, u32[]{:S(2)}) collective-permute-start(bf16[128,512]{1,0:T(8,128)(2,1)S(1)} %get-tuple-element.42._), channel_id=1, source_target_pairs={{0,2},{1,9},{2,0},{3,11},{4,6},{5,13},{6,4},{7,15},{8,10},{9,1},{1... | collective-permute-start | bytes 393224 | tf_op jit(solution)/shard_map/ppermute | solution.py:211
  21.9 2.7 %collective-permute-start.7 = (bf16[64,768]{1,0:T(8,128)(2,1)S(1)}, bf16[64,768]{1,0:T(8,128)(2,1)S(1)}, u32[]{:S(2)}, u32[]{:S(2)}) collective-permute-start(bf16[64,768]{1,0:T(8,128)(2,1)S(1)} %get-tuple-element.45._), channel_id=1, source_target_pairs={{0,8},{1,5},{2,10},{3,7},{4,12},{5,1},{6,14},{7,3},{8,0},{9,13},{1... | collective-permute-start | bytes 294920 | tf_op jit(solution)/shard_map/ppermute | solution.py:211
  24.6 0.4 %collective-permute-done.5.got = bf16[128,512]{1,0:T(8,128)(2,1)S(1)} collective-permute-done((bf16[128,512]{1,0:T(8,128)(2,1)S(1)}, bf16[128,512]{1,0:T(8,128)(2,1)S(1)}, u32[]{:S(2)}, u32[]{:S(2)}) %collective-permute-start.5) | collective-permute-done | bytes 131104 | tf_op jit(solution)/shard_map/ppermute | solution.py:211
  25.0 2.9 %collective-permute-start.9 = (bf16[64,512]{1,0:T(8,128)(2,1)S(1)}, bf16[64,512]{1,0:T(8,128)(2,1)S(1)}, u32[]{:S(2)}, u32[]{:S(2)}) collective-permute-start(bf16[64,512]{1,0:T(8,128)(2,1)S(1)} %get-tuple-element.50), channel_id=1, source_target_pairs={{0,8},{1,5},{2,10},{3,7},{4,12},{5,1},{6,14},{7,3},{8,0},{9,13},{1... | collective-permute-start | bytes 196616 | tf_op jit(solution)/shard_map/ppermute | solution.py:211
  28.0 0.1 collective-permute-start.8
  28.0 3.0 %collective-permute-done.9.refs_5_ = bf16[64,512]{1,0:T(8,128)(2,1)S(1)} collective-permute-done((bf16[64,512]{1,0:T(8,128)(2,1)S(1)}, bf16[64,512]{1,0:T(8,128)(2,1)S(1)}, u32[]{:S(2)}, u32[]{:S(2)}) %collective-permute-start.9) | collective-permute-done | bytes 65568 | tf_op jit(solution)/shard_map/ppermute | solution.py:211
  31.1 2.6 %collective-permute-done.8.refs_4_ = bf16[64,512]{1,0:T(8,128)(2,1)S(1)} collective-permute-done((bf16[64,512]{1,0:T(8,128)(2,1)S(1)}, bf16[64,512]{1,0:T(8,128)(2,1)S(1)}, u32[]{:S(2)}, u32[]{:S(2)}) %collective-permute-start.8) | collective-permute-done | bytes 65568 | tf_op jit(solution)/shard_map/ppermute | solution.py:211
  33.7 0.8 %shard_map.58 = f32[64,1792]{1,0:T(8,128)} custom-call(f32[64,768]{1,0:T(8,128)S(1)} %get-tuple-element.43.refs_0_, f32[64,512]{1,0:T(8,128)S(1)} %get-tuple-element.46.refs_1_, f32[64,512]{1,0:T(8,128)S(1)} %get-tuple-element.49.refs_2_, bf16[64,768]{1,0:T(8,128)(2,1)S(1)} %collective-permute-done.7.refs_3_, ...), custom_call_target="tpu_custom_call" | custom-call | flops 114688 | bytes 1376256 | tf_op jit(solution)/shard_map/pallas_call | solution.py:179
  (9 shorter events, 0.2 us)
Async XLA Ops:
  0.0 2.5 %collective-permute-start = (bf16[32,2048]{1,0:T(8,128)(2,1)}, bf16[32,2048]{1,0:T(8,128)(2,1)S(1)}, u32[]{:S(2)}, u32[]{:S(2)}) collective-permute-start(bf16[32,2048]{1,0:T(8,128)(2,1)} %own_hbm.1), channel_id=1, source_target_pairs={{0,1},{1,0},{2,3},{3,2},{4,5},{5,4},{6,7},{7,6},{8,9},{9,8},{10,11... | collective-permute-start | bytes 393224 | tf_op jit(solution)/shard_map/ppermute | solution.py:216
  4.1 8.4 %collective-permute-start.1 = (bf16[256,768]{1,0:T(8,128)(2,1)S(1)}, bf16[256,768]{1,0:T(8,128)(2,1)S(1)}, u32[]{:S(2)}, u32[]{:S(2)}) collective-permute-start(bf16[256,768]{1,0:T(8,128)(2,1)S(1)} %get-tuple-element.35), channel_id=1, source_target_pairs={{0,4},{1,3},{2,6},{3,1},{4,0},{5,7},{6,2},{7,5},{8,12},{9,11},{10,... | collective-permute-start | bytes 1179656 | tf_op jit(solution)/shard_map/ppermute | solution.py:211
  9.4 8.5 %collective-permute-start.4 = (bf16[256,512]{1,0:T(8,128)(2,1)S(1)}, bf16[256,512]{1,0:T(8,128)(2,1)S(1)}, u32[]{:S(2)}, u32[]{:S(2)}) collective-permute-start(bf16[256,512]{1,0:T(8,128)(2,1)S(1)} %get-tuple-element.40), channel_id=1, source_target_pairs={{0,2},{1,9},{2,0},{3,11},{4,6},{5,13},{6,4},{7,15},{8,10},{9,1},{1... | collective-permute-start | bytes 786440 | tf_op jit(solution)/shard_map/ppermute | solution.py:211
  11.0 8.3 %collective-permute-start.3 = (bf16[256,512]{1,0:T(8,128)(2,1)S(1)}, bf16[256,512]{1,0:T(8,128)(2,1)S(1)}, u32[]{:S(2)}, u32[]{:S(2)}) collective-permute-start(bf16[256,512]{1,0:T(8,128)(2,1)S(1)} %get-tuple-element.39), channel_id=1, source_target_pairs={{0,4},{1,3},{2,6},{3,1},{4,0},{5,7},{6,2},{7,5},{8,12},{9,11},{10,... | collective-permute-start | bytes 786440 | tf_op jit(solution)/shard_map/ppermute | solution.py:211
  12.6 9.3 %collective-permute-start.2 = (bf16[128,768]{1,0:T(8,128)(2,1)S(1)}, bf16[128,768]{1,0:T(8,128)(2,1)S(1)}, u32[]{:S(2)}, u32[]{:S(2)}) collective-permute-start(bf16[128,768]{1,0:T(8,128)(2,1)S(1)} %get-tuple-element.37._), channel_id=1, source_target_pairs={{0,2},{1,9},{2,0},{3,11},{4,6},{5,13},{6,4},{7,15},{8,10},{9,1},{1... | collective-permute-start | bytes 589832 | tf_op jit(solution)/shard_map/ppermute | solution.py:211
  18.0 7.0 %collective-permute-start.5 = (bf16[128,512]{1,0:T(8,128)(2,1)S(1)}, bf16[128,512]{1,0:T(8,128)(2,1)S(1)}, u32[]{:S(2)}, u32[]{:S(2)}) collective-permute-start(bf16[128,512]{1,0:T(8,128)(2,1)S(1)} %get-tuple-element.41._), channel_id=1, source_target_pairs={{0,4},{1,3},{2,6},{3,1},{4,0},{5,7},{6,2},{7,5},{8,12},{9,11},{10,... | collective-permute-start | bytes 393224 | tf_op jit(solution)/shard_map/ppermute | solution.py:211
  19.3 5.7 %collective-permute-start.6 = (bf16[128,512]{1,0:T(8,128)(2,1)S(1)}, bf16[128,512]{1,0:T(8,128)(2,1)S(1)}, u32[]{:S(2)}, u32[]{:S(2)}) collective-permute-start(bf16[128,512]{1,0:T(8,128)(2,1)S(1)} %get-tuple-element.42._), channel_id=1, source_target_pairs={{0,2},{1,9},{2,0},{3,11},{4,6},{5,13},{6,4},{7,15},{8,10},{9,1},{1... | collective-permute-start | bytes 393224 | tf_op jit(solution)/shard_map/ppermute | solution.py:211
  21.9 11.8 %collective-permute-start.7 = (bf16[64,768]{1,0:T(8,128)(2,1)S(1)}, bf16[64,768]{1,0:T(8,128)(2,1)S(1)}, u32[]{:S(2)}, u32[]{:S(2)}) collective-permute-start(bf16[64,768]{1,0:T(8,128)(2,1)S(1)} %get-tuple-element.45._), channel_id=1, source_target_pairs={{0,8},{1,5},{2,10},{3,7},{4,12},{5,1},{6,14},{7,3},{8,0},{9,13},{1... | collective-permute-start | bytes 294920 | tf_op jit(solution)/shard_map/ppermute | solution.py:211
  25.0 6.0 %collective-permute-start.9 = (bf16[64,512]{1,0:T(8,128)(2,1)S(1)}, bf16[64,512]{1,0:T(8,128)(2,1)S(1)}, u32[]{:S(2)}, u32[]{:S(2)}) collective-permute-start(bf16[64,512]{1,0:T(8,128)(2,1)S(1)} %get-tuple-element.50), channel_id=1, source_target_pairs={{0,8},{1,5},{2,10},{3,7},{4,12},{5,1},{6,14},{7,3},{8,0},{9,13},{1... | collective-permute-start | bytes 196616 | tf_op jit(solution)/shard_map/ppermute | solution.py:211
  28.0 5.7 %collective-permute-start.8 = (bf16[64,512]{1,0:T(8,128)(2,1)S(1)}, bf16[64,512]{1,0:T(8,128)(2,1)S(1)}, u32[]{:S(2)}, u32[]{:S(2)}) collective-permute-start(bf16[64,512]{1,0:T(8,128)(2,1)S(1)} %get-tuple-element.48._), channel_id=1, source_target_pairs={{0,8},{1,5},{2,10},{3,7},{4,12},{5,1},{6,14},{7,3},{8,0},{9,13},{1... | collective-permute-start | bytes 196616 | tf_op jit(solution)/shard_map/ppermute | solution.py:211

commit v16 on v15

--- a/solution.py
+++ b/solution.py
@@ -159,11 +159,23 @@
     keep[...] = kept[mid:, :] + got[mid:, :].astype(jnp.float32)
 
 
-def finish_kernel(spans, *refs):
-    count = len(spans)
-    kept, came, out = refs[:count], refs[count : 2 * count], refs[-1]
-    for (at, end), a, b in zip(spans, kept, came):
-        out[:, at:end] = a[a.shape[0] - out.shape[0] :, :] + b[...].astype(jnp.float32)
+def write_sums(first, kept, came, out, held, sem):
+    at = 0
+    for a, b in zip(kept, came):
+        end = at + a.shape[1]
+        held[:, at:end] = a[...] + b[...].astype(jnp.float32)
+        at = end
+    copy = pltpu.make_async_copy(held, out.at[:, pl.ds(first, at)], sem.at[0])
+    copy.start()
+    copy.wait()
+
+
+def early_kernel(count, *refs):
+    write_sums(0, refs[:count], refs[count : 2 * count], *refs[2 * count :])
+
+
+def finish_kernel(first, _, kept, came, out, held, sem):
+    write_sums(first, [kept], [came], out, held, sem)
 
 
 VMEM_SPEC = pl.BlockSpec(memory_space=pltpu.VMEM)
@@ -174,14 +186,15 @@
 }
 
 
-def kernel_call(body, ins, outs, scratch, cost):
+def kernel_call(body, ins, outs, scratch, cost, far_out=False, aliases={}):
     flops, moved = cost
     return pl.pallas_call(
         body,
         out_shape=[jax.ShapeDtypeStruct(*out) for out in outs],
         in_specs=[SPECS[far] for _, far in ins],
-        out_specs=[VMEM_SPEC] * len(outs),
+        out_specs=[SPECS[far_out]] * len(outs),
         scratch_shapes=scratch,
+        input_output_aliases=aliases,
         compiler_params=pltpu.CompilerParams(vmem_limit_bytes=VMEM_LIMIT),
         cost_estimate=pl.CostEstimate(flops=flops, bytes_accessed=moved, transcendentals=0),
     )(
@@ -268,13 +281,24 @@
         )
         token = leave
         got[p] = exchange(leave, p, stage)
-    outs = list(zip(value, got))
+    value = [v[v.shape[0] - rows // n :, :] for v in value]
+    last = len(PLAN) - 1
+    result = kernel_call(
+        functools.partial(early_kernel, last),
+        [(v, False) for v in value[:last]] + [(g, False) for g in got[:last]],
+        [((rows // n, cols), jnp.float32)],
+        [pltpu.VMEM((rows // n, cuts[last]), jnp.float32), pltpu.SemaphoreType.DMA((1,))],
+        (rows // n * cuts[last], 10 * rows // n * cuts[last]),
+        far_out=True,
+    )
     (result,) = kernel_call(
-        functools.partial(finish_kernel, spans),
-        [(value, False) for value, _ in outs] + [(came, False) for _, came in outs],
+        functools.partial(finish_kernel, cuts[last]),
+        [(result[0], True), (value[last], False), (got[last], False)],
         [((rows // n, cols), jnp.float32)],
-        [],
-        (rows // n * cols, 12 * rows // n * cols),
+        [pltpu.VMEM((rows // n, widths[last]), jnp.float32), pltpu.SemaphoreType.DMA((1,))],
+        (rows // n * widths[last], 10 * rows // n * widths[last]),
+        far_out=True,
+        aliases={0: 0},
     )
     return result.reshape(per_chunk, lanc, cols)
 

time: 34.7 us -> 32.9 us (0.948)
  waiting for transfers between devices: 7.04 us -> 4.25 us
  Pallas kernels: 9.79 us -> 10.4 us
    ppermute x9, waiting for transfers between devices: 7.03 us -> 4.25 us  [exchange(): return lax.ppermute(value, ('grid', 'eig'), pairs)]
    pallas_call x13 -> x14, Pallas kernels: 9.79 us -> 10.4 us  [kernel_call(): pl.pallas_call(body, out_shape=[jax.ShapeDtypeStruct(*out) for out in out...]
    ppermute x9, starting transfers between devices: 17.1 us -> 17.5 us  [exchange(): return lax.ppermute(value, ('grid', 'eig'), pairs)]
  transfers between devices with their start and end apart: 10 -> 10, of which waited for: 5 -> 4; matrix products, arithmetic and copies ran while one was open for 0% -> 0% of each run, Pallas kernels for 21% -> 25%
where the time goes in v16:
time: 32.9 us; the launch traced here: 32.7 us
  starting transfers between devices  17.9 us (54%)
  Pallas kernels  10.4 us (32%)
  waiting for transfers between devices  4.25 us (13%)
    ppermute x9, starting transfers between devices, exchange(): return lax.ppermute(value, ('grid', 'eig'), pairs)  17.5 us
    pallas_call x14, Pallas kernels, kernel_call(): pl.pallas_call(body, out_shape=[jax.ShapeDtypeStruct(*out) for out in out...  10.4 us
    ppermute x9, waiting for transfers between devices, exchange(): return lax.ppermute(value, ('grid', 'eig'), pairs)  4.25 us
  transfers between devices with their start and end apart: 10, of which 4 were waited for; matrix products, arithmetic and copies ran while one was open for 0% of the time, Pallas kernels for 25%

profile of v16, /device:TPU:0, one launch (start us, length us, event | category | flops | bytes accessed | tf_op | source)
XLA Modules:
  0.0 32.7 jit_solution(5329269759227324415)
XLA Ops:
  0.0 0.5 %collective-permute-start = (bf16[32,2048]{1,0:T(8,128)(2,1)}, bf16[32,2048]{1,0:T(8,128)(2,1)S(1)}, u32[]{:S(2)}, u32[]{:S(2)}) collective-permute-start(bf16[32,2048]{1,0:T(8,128)(2,1)} %own_hbm.1), channel_id=1, source_target_pairs={{0,1},{1,0},{2,3},{3,2},{4,5},{5,4},{6,7},{7,6},{8,9},{9,8},{10,11... | collective-permute-start | bytes 393224 | tf_op jit(solution)/shard_map/ppermute | solution.py:229
  0.5 2.0 %shard_map.46 = (bf16[512,64]{1,0:T(8,128)(2,1)S(1)}, bf16[32,2048]{1,0:T(8,128)(2,1)S(1)}, bf16[8,2048]{1,0:T(8,128)(2,1)S(1)}, bf16[768,2048]{1,0:T(8,128)(2,1)S(1)}) custom-call(s32[64]{0:T(128)} %order_hbm.1, bf16[32,2048]{1,0:T(8,128)(2,1)} %own_hbm.1, bf16[8,2048]{1,0:T(8,128)(2,1)} %lanc_hbm.1, bf16[1792,2048]{1,0:T(8,128)(2,1)} %eig_hbm.5), custom_call_target="tpu_custom_call" | custom-call | bytes 3145728 | tf_op jit(solution)/shard_map/pallas_call | solution.py:191
  2.5 0.0 collective-permute-done.other
  2.5 1.6 %shard_map.47 = (bf16[256,768]{1,0:T(8,128)(2,1)S(1)}, bf16[256,2048]{1,0:T(8,128)(2,1)S(1)}, bf16[512,2048]{1,0:T(8,128)(2,1)S(1)}) custom-call(bf16[512,64]{1,0:T(8,128)(2,1)S(1)} %get-tuple-element.28.pick, bf16[32,2048]{1,0:T(8,128)(2,1)S(1)} %get-tuple-element.29.own, bf16[32,2048]{1,0:T(8,128)(2,1)S(1)} %collective-permute-done.other, ...), custom_call_target="tpu_custom_call" | custom-call | flops 805306368 | bytes 3145728 | tf_op jit(solution)/shard_map/pallas_call | solution.py:191
  4.1 2.6 %collective-permute-start.1 = (bf16[256,768]{1,0:T(8,128)(2,1)S(1)}, bf16[256,768]{1,0:T(8,128)(2,1)S(1)}, u32[]{:S(2)}, u32[]{:S(2)}) collective-permute-start(bf16[256,768]{1,0:T(8,128)(2,1)S(1)} %get-tuple-element.35), channel_id=1, source_target_pairs={{0,4},{1,3},{2,6},{3,1},{4,0},{5,7},{6,2},{7,5},{8,12},{9,11},{10,... | collective-permute-start | bytes 1179656 | tf_op jit(solution)/shard_map/ppermute | solution.py:224
  6.7 2.7 %shard_map.48 = (bf16[256,512]{1,0:T(8,128)(2,1)S(1)}, bf16[256,512]{1,0:T(8,128)(2,1)S(1)}, bf16[512,2048]{1,0:T(8,128)(2,1)S(1)}, bf16[512,2048]{1,0:T(8,128)(2,1)S(1)}) custom-call(bf16[512,64]{1,0:T(8,128)(2,1)S(1)} %get-tuple-element.28.pick, bf16[32,2048]{1,0:T(8,128)(2,1)S(1)} %get-tuple-element.29.own, ...), custom_call_target="tpu_custom_call" | custom-call | flops 1073741824 | bytes 4194304 | tf_op jit(solution)/shard_map/pallas_call | solution.py:191
  9.4 1.5 %collective-permute-start.4 = (bf16[256,512]{1,0:T(8,128)(2,1)S(1)}, bf16[256,512]{1,0:T(8,128)(2,1)S(1)}, u32[]{:S(2)}, u32[]{:S(2)}) collective-permute-start(bf16[256,512]{1,0:T(8,128)(2,1)S(1)} %get-tuple-element.40), channel_id=1, source_target_pairs={{0,2},{1,9},{2,0},{3,11},{4,6},{5,13},{6,4},{7,15},{8,10},{9,1},{1... | collective-permute-start | bytes 786440 | tf_op jit(solution)/shard_map/ppermute | solution.py:224
  11.0 0.5 %collective-permute-start.3 = (bf16[256,512]{1,0:T(8,128)(2,1)S(1)}, bf16[256,512]{1,0:T(8,128)(2,1)S(1)}, u32[]{:S(2)}, u32[]{:S(2)}) collective-permute-start(bf16[256,512]{1,0:T(8,128)(2,1)S(1)} %get-tuple-element.39), channel_id=1, source_target_pairs={{0,4},{1,3},{2,6},{3,1},{4,0},{5,7},{6,2},{7,5},{8,12},{9,11},{10,... | collective-permute-start | bytes 786440 | tf_op jit(solution)/shard_map/ppermute | solution.py:224
  11.4 1.0 %shard_map.49.kept = f32[256,768]{1,0:T(8,128)S(1)} custom-call(bf16[512,2048]{1,0:T(8,128)(2,1)S(1)} %get-tuple-element.34.prod._, bf16[768,2048]{1,0:T(8,128)(2,1)S(1)} %get-tuple-element.31.eig), custom_call_target="tpu_custom_call" | custom-call | flops 805306368 | bytes 3145728 | tf_op jit(solution)/shard_map/pallas_call | solution.py:191
  12.4 0.1 collective-permute-done.1.got
  12.5 0.1 shard_map.50
  12.6 3.9 %collective-permute-start.2 = (bf16[128,768]{1,0:T(8,128)(2,1)S(1)}, bf16[128,768]{1,0:T(8,128)(2,1)S(1)}, u32[]{:S(2)}, u32[]{:S(2)}) collective-permute-start(bf16[128,768]{1,0:T(8,128)(2,1)S(1)} %get-tuple-element.37._), channel_id=1, source_target_pairs={{0,2},{1,9},{2,0},{3,11},{4,6},{5,13},{6,4},{7,15},{8,10},{9,1},{1... | collective-permute-start | bytes 589832 | tf_op jit(solution)/shard_map/ppermute | solution.py:224
  16.5 0.7 %shard_map.52.kept = f32[256,512]{1,0:T(8,128)S(1)} custom-call(bf16[512,2048]{1,0:T(8,128)(2,1)S(1)} %get-tuple-element.34.prod._, bf16[512,2048]{1,0:T(8,128)(2,1)S(1)} %get-tuple-element.33.eig), custom_call_target="tpu_custom_call" | custom-call | flops 536870912 | bytes 2097152 | tf_op jit(solution)/shard_map/pallas_call | solution.py:191
  17.3 0.4 %collective-permute-start.5 = (bf16[128,512]{1,0:T(8,128)(2,1)S(1)}, bf16[128,512]{1,0:T(8,128)(2,1)S(1)}, u32[]{:S(2)}, u32[]{:S(2)}) collective-permute-start(bf16[128,512]{1,0:T(8,128)(2,1)S(1)} %get-tuple-element.41._), channel_id=1, source_target_pairs={{0,4},{1,3},{2,6},{3,1},{4,0},{5,7},{6,2},{7,5},{8,12},{9,11},{10,... | collective-permute-start | bytes 393224 | tf_op jit(solution)/shard_map/ppermute | solution.py:224
  17.7 0.7 %shard_map.51.kept = f32[256,512]{1,0:T(8,128)S(1)} custom-call(bf16[512,2048]{1,0:T(8,128)(2,1)S(1)} %get-tuple-element.34.prod._, bf16[512,2048]{1,0:T(8,128)(2,1)S(1)} %get-tuple-element.38.eig), custom_call_target="tpu_custom_call" | custom-call | flops 536870912 | bytes 2097152 | tf_op jit(solution)/shard_map/pallas_call | solution.py:191
  18.4 0.8 %collective-permute-done.3.got = bf16[256,512]{1,0:T(8,128)(2,1)S(1)} collective-permute-done((bf16[256,512]{1,0:T(8,128)(2,1)S(1)}, bf16[256,512]{1,0:T(8,128)(2,1)S(1)}, u32[]{:S(2)}, u32[]{:S(2)}) %collective-permute-start.3) | collective-permute-done | bytes 262176 | tf_op jit(solution)/shard_map/ppermute | solution.py:224
  19.3 2.6 %collective-permute-start.8 = (bf16[128,512]{1,0:T(8,128)(2,1)S(1)}, bf16[128,512]{1,0:T(8,128)(2,1)S(1)}, u32[]{:S(2)}, u32[]{:S(2)}) collective-permute-start(bf16[128,512]{1,0:T(8,128)(2,1)S(1)} %get-tuple-element.42._), channel_id=1, source_target_pairs={{0,2},{1,9},{2,0},{3,11},{4,6},{5,13},{6,4},{7,15},{8,10},{9,1},{1... | collective-permute-start | bytes 393224 | tf_op jit(solution)/shard_map/ppermute | solution.py:224
  21.9 2.7 %collective-permute-start.6 = (bf16[64,768]{1,0:T(8,128)(2,1)S(1)}, bf16[64,768]{1,0:T(8,128)(2,1)S(1)}, u32[]{:S(2)}, u32[]{:S(2)}) collective-permute-start(bf16[64,768]{1,0:T(8,128)(2,1)S(1)} %get-tuple-element.45._), channel_id=1, source_target_pairs={{0,8},{1,5},{2,10},{3,7},{4,12},{5,1},{6,14},{7,3},{8,0},{9,13},{1... | collective-permute-start | bytes 294920 | tf_op jit(solution)/shard_map/ppermute | solution.py:224
  24.6 2.1 %collective-permute-start.7 = (bf16[64,512]{1,0:T(8,128)(2,1)S(1)}, bf16[64,512]{1,0:T(8,128)(2,1)S(1)}, u32[]{:S(2)}, u32[]{:S(2)}) collective-permute-start(bf16[64,512]{1,0:T(8,128)(2,1)S(1)} %get-tuple-element.47._), channel_id=1, source_target_pairs={{0,8},{1,5},{2,10},{3,7},{4,12},{5,1},{6,14},{7,3},{8,0},{9,13},{1... | collective-permute-start | bytes 196616 | tf_op jit(solution)/shard_map/ppermute | solution.py:224
  26.8 1.2 %collective-permute-start.9 = (bf16[64,512]{1,0:T(8,128)(2,1)S(1)}, bf16[64,512]{1,0:T(8,128)(2,1)S(1)}, u32[]{:S(2)}, u32[]{:S(2)}) collective-permute-start(bf16[64,512]{1,0:T(8,128)(2,1)S(1)} %get-tuple-element.50), channel_id=1, source_target_pairs={{0,8},{1,5},{2,10},{3,7},{4,12},{5,1},{6,14},{7,3},{8,0},{9,13},{1... | collective-permute-start | bytes 196616 | tf_op jit(solution)/shard_map/ppermute | solution.py:224
  28.0 2.6 %collective-permute-done.7.refs_3_ = bf16[64,512]{1,0:T(8,128)(2,1)S(1)} collective-permute-done((bf16[64,512]{1,0:T(8,128)(2,1)S(1)}, bf16[64,512]{1,0:T(8,128)(2,1)S(1)}, u32[]{:S(2)}, u32[]{:S(2)}) %collective-permute-start.7) | collective-permute-done | bytes 65568 | tf_op jit(solution)/shard_map/ppermute | solution.py:224
  30.6 0.8 %shard_map.57._ = f32[64,1792]{1,0:T(8,128)} custom-call(f32[64,768]{1,0:T(8,128)S(1)} %get-tuple-element.43.refs_0_, f32[64,512]{1,0:T(8,128)S(1)} %get-tuple-element.46.refs_1_, bf16[64,768]{1,0:T(8,128)(2,1)S(1)} %collective-permute-done.6.refs_2_, bf16[64,512]{1,0:T(8,128)(2,1)S(1)} %collective-permute-done.7.refs_3_), custom_call_target="tpu_custom_call" | custom-call | flops 81920 | bytes 819200 | tf_op jit(solution)/shard_map/pallas_call | solution.py:191
  31.3 0.7 %collective-permute-done.9.came = bf16[64,512]{1,0:T(8,128)(2,1)S(1)} collective-permute-done((bf16[64,512]{1,0:T(8,128)(2,1)S(1)}, bf16[64,512]{1,0:T(8,128)(2,1)S(1)}, u32[]{:S(2)}, u32[]{:S(2)}) %collective-permute-start.9) | collective-permute-done | bytes 65568 | tf_op jit(solution)/shard_map/ppermute | solution.py:224
  32.0 0.7 %shard_map.59 = f32[64,1792]{1,0:T(8,128)} custom-call(f32[64,1792]{1,0:T(8,128)} %shard_map.57._, f32[64,512]{1,0:T(8,128)S(1)} %get-tuple-element.49.kept, bf16[64,512]{1,0:T(8,128)(2,1)S(1)} %collective-permute-done.9.came), custom_call_target="tpu_custom_call", output_to_operand_aliasing={{}: (0, {})} | custom-call | flops 32768 | bytes 327680 | tf_op jit(solution)/shard_map/pallas_call | solution.py:191
  (10 shorter events, 0.2 us)
Async XLA Ops:
  0.0 2.5 %collective-permute-start = (bf16[32,2048]{1,0:T(8,128)(2,1)}, bf16[32,2048]{1,0:T(8,128)(2,1)S(1)}, u32[]{:S(2)}, u32[]{:S(2)}) collective-permute-start(bf16[32,2048]{1,0:T(8,128)(2,1)} %own_hbm.1), channel_id=1, source_target_pairs={{0,1},{1,0},{2,3},{3,2},{4,5},{5,4},{6,7},{7,6},{8,9},{9,8},{10,11... | collective-permute-start | bytes 393224 | tf_op jit(solution)/shard_map/ppermute | solution.py:229
  4.1 8.4 %collective-permute-start.1 = (bf16[256,768]{1,0:T(8,128)(2,1)S(1)}, bf16[256,768]{1,0:T(8,128)(2,1)S(1)}, u32[]{:S(2)}, u32[]{:S(2)}) collective-permute-start(bf16[256,768]{1,0:T(8,128)(2,1)S(1)} %get-tuple-element.35), channel_id=1, source_target_pairs={{0,4},{1,3},{2,6},{3,1},{4,0},{5,7},{6,2},{7,5},{8,12},{9,11},{10,... | collective-permute-start | bytes 1179656 | tf_op jit(solution)/shard_map/ppermute | solution.py:224
  9.4 7.8 %collective-permute-start.4 = (bf16[256,512]{1,0:T(8,128)(2,1)S(1)}, bf16[256,512]{1,0:T(8,128)(2,1)S(1)}, u32[]{:S(2)}, u32[]{:S(2)}) collective-permute-start(bf16[256,512]{1,0:T(8,128)(2,1)S(1)} %get-tuple-element.40), channel_id=1, source_target_pairs={{0,2},{1,9},{2,0},{3,11},{4,6},{5,13},{6,4},{7,15},{8,10},{9,1},{1... | collective-permute-start | bytes 786440 | tf_op jit(solution)/shard_map/ppermute | solution.py:224
  11.0 8.3 %collective-permute-start.3 = (bf16[256,512]{1,0:T(8,128)(2,1)S(1)}, bf16[256,512]{1,0:T(8,128)(2,1)S(1)}, u32[]{:S(2)}, u32[]{:S(2)}) collective-permute-start(bf16[256,512]{1,0:T(8,128)(2,1)S(1)} %get-tuple-element.39), channel_id=1, source_target_pairs={{0,4},{1,3},{2,6},{3,1},{4,0},{5,7},{6,2},{7,5},{8,12},{9,11},{10,... | collective-permute-start | bytes 786440 | tf_op jit(solution)/shard_map/ppermute | solution.py:224
  12.6 9.3 %collective-permute-start.2 = (bf16[128,768]{1,0:T(8,128)(2,1)S(1)}, bf16[128,768]{1,0:T(8,128)(2,1)S(1)}, u32[]{:S(2)}, u32[]{:S(2)}) collective-permute-start(bf16[128,768]{1,0:T(8,128)(2,1)S(1)} %get-tuple-element.37._), channel_id=1, source_target_pairs={{0,2},{1,9},{2,0},{3,11},{4,6},{5,13},{6,4},{7,15},{8,10},{9,1},{1... | collective-permute-start | bytes 589832 | tf_op jit(solution)/shard_map/ppermute | solution.py:224
  17.3 7.3 %collective-permute-start.5 = (bf16[128,512]{1,0:T(8,128)(2,1)S(1)}, bf16[128,512]{1,0:T(8,128)(2,1)S(1)}, u32[]{:S(2)}, u32[]{:S(2)}) collective-permute-start(bf16[128,512]{1,0:T(8,128)(2,1)S(1)} %get-tuple-element.41._), channel_id=1, source_target_pairs={{0,4},{1,3},{2,6},{3,1},{4,0},{5,7},{6,2},{7,5},{8,12},{9,11},{10,... | collective-permute-start | bytes 393224 | tf_op jit(solution)/shard_map/ppermute | solution.py:224
  19.3 7.5 %collective-permute-start.8 = (bf16[128,512]{1,0:T(8,128)(2,1)S(1)}, bf16[128,512]{1,0:T(8,128)(2,1)S(1)}, u32[]{:S(2)}, u32[]{:S(2)}) collective-permute-start(bf16[128,512]{1,0:T(8,128)(2,1)S(1)} %get-tuple-element.42._), channel_id=1, source_target_pairs={{0,2},{1,9},{2,0},{3,11},{4,6},{5,13},{6,4},{7,15},{8,10},{9,1},{1... | collective-permute-start | bytes 393224 | tf_op jit(solution)/shard_map/ppermute | solution.py:224
  21.9 8.6 %collective-permute-start.6 = (bf16[64,768]{1,0:T(8,128)(2,1)S(1)}, bf16[64,768]{1,0:T(8,128)(2,1)S(1)}, u32[]{:S(2)}, u32[]{:S(2)}) collective-permute-start(bf16[64,768]{1,0:T(8,128)(2,1)S(1)} %get-tuple-element.45._), channel_id=1, source_target_pairs={{0,8},{1,5},{2,10},{3,7},{4,12},{5,1},{6,14},{7,3},{8,0},{9,13},{1... | collective-permute-start | bytes 294920 | tf_op jit(solution)/shard_map/ppermute | solution.py:224
  24.6 5.9 %collective-permute-start.7 = (bf16[64,512]{1,0:T(8,128)(2,1)S(1)}, bf16[64,512]{1,0:T(8,128)(2,1)S(1)}, u32[]{:S(2)}, u32[]{:S(2)}) collective-permute-start(bf16[64,512]{1,0:T(8,128)(2,1)S(1)} %get-tuple-element.47._), channel_id=1, source_target_pairs={{0,8},{1,5},{2,10},{3,7},{4,12},{5,1},{6,14},{7,3},{8,0},{9,13},{1... | collective-permute-start | bytes 196616 | tf_op jit(solution)/shard_map/ppermute | solution.py:224
  26.8 5.2 %collective-permute-start.9 = (bf16[64,512]{1,0:T(8,128)(2,1)S(1)}, bf16[64,512]{1,0:T(8,128)(2,1)S(1)}, u32[]{:S(2)}, u32[]{:S(2)}) collective-permute-start(bf16[64,512]{1,0:T(8,128)(2,1)S(1)} %get-tuple-element.50), channel_id=1, source_target_pairs={{0,8},{1,5},{2,10},{3,7},{4,12},{5,1},{6,14},{7,3},{8,0},{9,13},{1... | collective-permute-start | bytes 196616 | tf_op jit(solution)/shard_map/ppermute | solution.py:224

commit v17 on v16

--- a/solution.py
+++ b/solution.py
@@ -130,8 +130,7 @@
     copy.wait()
 
 
-def send_kernel(cut, pick, own, other, lanc16, half, eig, eig_hbm, *rest):
-    *outs, prod, eig_rest, acc, sem = rest
+def second_kernel(cut, pick, own, other, lanc16, half, eig, eig_hbm, out, prod, eig_rest, acc, sem):
     copy = pltpu.make_async_copy(
         eig_hbm.at[pl.ds(cut, eig_rest.shape[0])], eig_rest, sem.at[0]
     )
@@ -139,14 +138,14 @@
     first = half.shape[0]
     prod[:first, :] = half[...]
     make_rows(prod.at[first:, :], pick, own, other, lanc16, first)
-    at = 0
-    for i, out in enumerate(outs):
-        part = acc.at[:, : out.shape[1]]
-        if i == 1:
-            copy.wait()
-        dot_tiles(part, rows_of(prod, i + 1, False), eig_rest if i else eig, at)
-        out[...] = part[...].astype(out.dtype)
-        at += out.shape[1] if i else 0
+    dot_tiles(acc, rows_of(prod, 1, False), eig, 0)
+    out[...] = acc[...].astype(out.dtype)
+    copy.wait()
+
+
+def send_kernel(p, first, prod, eig, _, out, acc):
+    dot_tiles(acc, rows_of(prod, p, False), eig, first)
+    out[...] = acc[...].astype(out.dtype)
 
 
 def keep_kernel(p, first, prod, eig, out):
@@ -247,16 +246,24 @@
         [pltpu.VMEM((rows // 2, widths[0]), jnp.float32), pltpu.SemaphoreType.DMA((1,))],
         (flops(widths[0]), 2 * widths[0] * depth),
     )
-    *sends, prod, eig_rest = kernel_call(
-        functools.partial(send_kernel, cuts[2]),
+    second, prod, eig_rest = kernel_call(
+        functools.partial(second_kernel, cuts[2]),
         sources + [(half, False), (eig_next, False), (eigvecs, True)],
-        [((rows // 2, w), bf16) for w in widths[1:]]
-        + [((rows, depth), bf16), ((cols - cuts[2], depth), bf16)],
-        [pltpu.VMEM((rows // 2, max(widths[1:])), jnp.float32), pltpu.SemaphoreType.DMA((1,))],
-        (flops(sum(widths[1:])), 2 * sum(widths[1:]) * depth),
+        [((rows // 2, widths[1]), bf16), ((rows, depth), bf16), ((cols - cuts[2], depth), bf16)],
+        [pltpu.VMEM((rows // 2, widths[1]), jnp.float32), pltpu.SemaphoreType.DMA((1,))],
+        (flops(widths[1]), 2 * (cols - cuts[2]) * depth),
     )
     eigs = [eig, eig_next] + [eig_rest] * (len(PLAN) - 2)
-    got = [exchange(s, p, 0) for p, s in enumerate([send, *sends])]
+    sends = [send, second]
+    for p in range(2, len(PLAN)):
+        sends += kernel_call(
+            functools.partial(send_kernel, p, cuts[p] - cuts[2]),
+            [(prod, False), (eig_rest, False), (sends[-1], None)],
+            [((rows // 2, widths[p]), bf16)],
+            [pltpu.VMEM((rows // 2, widths[p]), jnp.float32)],
+            (flops(widths[p]), 2 * widths[p] * depth),
+        )
+    got = [exchange(s, p, 0) for p, s in enumerate(sends)]
     value = []
     for p, width in enumerate(widths):
         value += kernel_call(
@@ -267,7 +274,7 @@
             (flops(width), 2 * width * depth),
         )
     later = range(3, n.bit_length() - 1)
-    token = prod
+    token = sends[-1]
     for p, stage in ORDER + [(p, stage) for stage in later for p in range(len(PLAN))]:
         part = value[p].shape[0] // 2
         size = part * widths[p]

time: 32.9 us -> 33.7 us (1.024)
  waiting for transfers between devices: 4.25 us -> 6.72 us
  starting transfers between devices: 17.9 us -> 16.4 us
    ppermute x9, waiting for transfers between devices: 4.25 us -> 6.72 us  [exchange(): return lax.ppermute(value, ('grid', 'eig'), pairs)]
    ppermute x9, starting transfers between devices: 17.5 us -> 16 us  [exchange(): return lax.ppermute(value, ('grid', 'eig'), pairs)]
    pallas_call x14 -> x15, Pallas kernels: 10.4 us -> 10.3 us  [kernel_call(): pl.pallas_call(body, out_shape=[jax.ShapeDtypeStruct(*out) for out in out...]
  transfers between devices with their start and end apart: 10 -> 10, of which waited for: 4 -> 5; matrix products, arithmetic and copies ran while one was open for 0% -> 0% of each run, Pallas kernels for 25% -> 24%
where the time goes in v17:
time: 33.7 us; the launch traced here: 33.5 us
  starting transfers between devices  16.4 us (49%)
  Pallas kernels  10.3 us (31%)
  waiting for transfers between devices  6.72 us (20%)
    ppermute x9, starting transfers between devices, exchange(): return lax.ppermute(value, ('grid', 'eig'), pairs)  16 us
    pallas_call x15, Pallas kernels, kernel_call(): pl.pallas_call(body, out_shape=[jax.ShapeDtypeStruct(*out) for out in out...  10.3 us
    ppermute x9, waiting for transfers between devices, exchange(): return lax.ppermute(value, ('grid', 'eig'), pairs)  6.72 us
  transfers between devices with their start and end apart: 10, of which 5 were waited for; matrix products, arithmetic and copies ran while one was open for 0% of the time, Pallas kernels for 24%

profile of v17, /device:TPU:0, one launch (start us, length us, event | category | flops | bytes accessed | tf_op | source)
XLA Modules:
  0.0 33.5 jit_solution(16759664385025677585)
XLA Ops:
  0.0 0.5 %collective-permute-start = (bf16[32,2048]{1,0:T(8,128)(2,1)}, bf16[32,2048]{1,0:T(8,128)(2,1)S(1)}, u32[]{:S(2)}, u32[]{:S(2)}) collective-permute-start(bf16[32,2048]{1,0:T(8,128)(2,1)} %own_hbm.1), channel_id=1, source_target_pairs={{0,1},{1,0},{2,3},{3,2},{4,5},{5,4},{6,7},{7,6},{8,9},{9,8},{10,11... | collective-permute-start | bytes 393224 | tf_op jit(solution)/shard_map/ppermute | solution.py:228
  0.5 2.0 %shard_map.46 = (bf16[512,64]{1,0:T(8,128)(2,1)S(1)}, bf16[32,2048]{1,0:T(8,128)(2,1)S(1)}, bf16[8,2048]{1,0:T(8,128)(2,1)S(1)}, bf16[768,2048]{1,0:T(8,128)(2,1)S(1)}) custom-call(s32[64]{0:T(128)} %order_hbm.1, bf16[32,2048]{1,0:T(8,128)(2,1)} %own_hbm.1, bf16[8,2048]{1,0:T(8,128)(2,1)} %lanc_hbm.1, bf16[1792,2048]{1,0:T(8,128)(2,1)} %eig_hbm.5), custom_call_target="tpu_custom_call" | custom-call | bytes 3145728 | tf_op jit(solution)/shard_map/pallas_call | solution.py:190
  2.5 1.6 %shard_map.47 = (bf16[256,768]{1,0:T(8,128)(2,1)S(1)}, bf16[256,2048]{1,0:T(8,128)(2,1)S(1)}, bf16[512,2048]{1,0:T(8,128)(2,1)S(1)}) custom-call(bf16[512,64]{1,0:T(8,128)(2,1)S(1)} %get-tuple-element.27.pick, bf16[32,2048]{1,0:T(8,128)(2,1)S(1)} %get-tuple-element.28.own, bf16[32,2048]{1,0:T(8,128)(2,1)S(1)} %collective-permute-done.other, ...), custom_call_target="tpu_custom_call" | custom-call | flops 805306368 | bytes 3145728 | tf_op jit(solution)/shard_map/pallas_call | solution.py:190
  4.1 2.6 %collective-permute-start.1 = (bf16[256,768]{1,0:T(8,128)(2,1)S(1)}, bf16[256,768]{1,0:T(8,128)(2,1)S(1)}, u32[]{:S(2)}, u32[]{:S(2)}) collective-permute-start(bf16[256,768]{1,0:T(8,128)(2,1)S(1)} %get-tuple-element.34), channel_id=1, source_target_pairs={{0,4},{1,3},{2,6},{3,1},{4,0},{5,7},{6,2},{7,5},{8,12},{9,11},{10,... | collective-permute-start | bytes 1179656 | tf_op jit(solution)/shard_map/ppermute | solution.py:223
  6.7 1.8 %shard_map.48 = (bf16[256,512]{1,0:T(8,128)(2,1)S(1)}, bf16[512,2048]{1,0:T(8,128)(2,1)S(1)}, bf16[512,2048]{1,0:T(8,128)(2,1)S(1)}) custom-call(bf16[512,64]{1,0:T(8,128)(2,1)S(1)} %get-tuple-element.27.pick, bf16[32,2048]{1,0:T(8,128)(2,1)S(1)} %get-tuple-element.28.own, bf16[32,2048]{1,0:T(8,128)(2,1)S(1)} %collective-permute-done.other, ...), custom_call_target="tpu_custom_call" | custom-call | flops 536870912 | bytes 2097152 | tf_op jit(solution)/shard_map/pallas_call | solution.py:190
  8.5 1.5 %collective-permute-start.4 = (bf16[256,512]{1,0:T(8,128)(2,1)S(1)}, bf16[256,512]{1,0:T(8,128)(2,1)S(1)}, u32[]{:S(2)}, u32[]{:S(2)}) collective-permute-start(bf16[256,512]{1,0:T(8,128)(2,1)S(1)} %get-tuple-element.36._), channel_id=1, source_target_pairs={{0,2},{1,9},{2,0},{3,11},{4,6},{5,13},{6,4},{7,15},{8,10},{9,1},{1... | collective-permute-start | bytes 786440 | tf_op jit(solution)/shard_map/ppermute | solution.py:223
  10.1 0.7 %shard_map.50._ = bf16[256,512]{1,0:T(8,128)(2,1)S(1)} custom-call(bf16[512,2048]{1,0:T(8,128)(2,1)S(1)} %get-tuple-element.33.prod, bf16[512,2048]{1,0:T(8,128)(2,1)S(1)} %get-tuple-element.35.eig, bf16[256,512]{1,0:T(8,128)(2,1)S(1)} %get-tuple-element.36._), custom_call_target="tpu_custom_call" | custom-call | flops 536870912 | bytes 2097152 | tf_op jit(solution)/shard_map/pallas_call | solution.py:190
  10.8 0.5 %collective-permute-start.3 = (bf16[256,512]{1,0:T(8,128)(2,1)S(1)}, bf16[256,512]{1,0:T(8,128)(2,1)S(1)}, u32[]{:S(2)}, u32[]{:S(2)}) collective-permute-start(bf16[256,512]{1,0:T(8,128)(2,1)S(1)} %shard_map.50._), channel_id=1, source_target_pairs={{0,4},{1,3},{2,6},{3,1},{4,0},{5,7},{6,2},{7,5},{8,12},{9,11},{10,... | collective-permute-start | bytes 786440 | tf_op jit(solution)/shard_map/ppermute | solution.py:223
  11.3 1.0 %shard_map.49.kept = f32[256,768]{1,0:T(8,128)S(1)} custom-call(bf16[512,2048]{1,0:T(8,128)(2,1)S(1)} %get-tuple-element.33.prod, bf16[768,2048]{1,0:T(8,128)(2,1)S(1)} %get-tuple-element.30.eig), custom_call_target="tpu_custom_call" | custom-call | flops 805306368 | bytes 3145728 | tf_op jit(solution)/shard_map/pallas_call | solution.py:190
  12.3 1.5 %collective-permute-done.1.got = bf16[256,768]{1,0:T(8,128)(2,1)S(1)} collective-permute-done((bf16[256,768]{1,0:T(8,128)(2,1)S(1)}, bf16[256,768]{1,0:T(8,128)(2,1)S(1)}, u32[]{:S(2)}, u32[]{:S(2)}) %collective-permute-start.1) | collective-permute-done | bytes 393248 | tf_op jit(solution)/shard_map/ppermute | solution.py:223
  13.9 3.5 %collective-permute-start.2 = (bf16[128,768]{1,0:T(8,128)(2,1)S(1)}, bf16[128,768]{1,0:T(8,128)(2,1)S(1)}, u32[]{:S(2)}, u32[]{:S(2)}) collective-permute-start(bf16[128,768]{1,0:T(8,128)(2,1)S(1)} %get-tuple-element.38._), channel_id=1, source_target_pairs={{0,2},{1,9},{2,0},{3,11},{4,6},{5,13},{6,4},{7,15},{8,10},{9,1},{1... | collective-permute-start | bytes 589832 | tf_op jit(solution)/shard_map/ppermute | solution.py:223
  17.4 0.7 %shard_map.53.kept = f32[256,512]{1,0:T(8,128)S(1)} custom-call(bf16[512,2048]{1,0:T(8,128)(2,1)S(1)} %get-tuple-element.33.prod, bf16[512,2048]{1,0:T(8,128)(2,1)S(1)} %get-tuple-element.32.eig), custom_call_target="tpu_custom_call" | custom-call | flops 536870912 | bytes 2097152 | tf_op jit(solution)/shard_map/pallas_call | solution.py:190
  18.2 0.4 %collective-permute-start.5 = (bf16[128,512]{1,0:T(8,128)(2,1)S(1)}, bf16[128,512]{1,0:T(8,128)(2,1)S(1)}, u32[]{:S(2)}, u32[]{:S(2)}) collective-permute-start(bf16[128,512]{1,0:T(8,128)(2,1)S(1)} %get-tuple-element.39._), channel_id=1, source_target_pairs={{0,4},{1,3},{2,6},{3,1},{4,0},{5,7},{6,2},{7,5},{8,12},{9,11},{10,... | collective-permute-start | bytes 393224 | tf_op jit(solution)/shard_map/ppermute | solution.py:223
  18.5 0.7 %shard_map.52.kept = f32[256,512]{1,0:T(8,128)S(1)} custom-call(bf16[512,2048]{1,0:T(8,128)(2,1)S(1)} %get-tuple-element.33.prod, bf16[512,2048]{1,0:T(8,128)(2,1)S(1)} %get-tuple-element.35.eig), custom_call_target="tpu_custom_call" | custom-call | flops 536870912 | bytes 2097152 | tf_op jit(solution)/shard_map/pallas_call | solution.py:190
  19.3 1.0 %collective-permute-done.3.got = bf16[256,512]{1,0:T(8,128)(2,1)S(1)} collective-permute-done((bf16[256,512]{1,0:T(8,128)(2,1)S(1)}, bf16[256,512]{1,0:T(8,128)(2,1)S(1)}, u32[]{:S(2)}, u32[]{:S(2)}) %collective-permute-start.3) | collective-permute-done | bytes 262176 | tf_op jit(solution)/shard_map/ppermute | solution.py:223
  20.3 1.9 %collective-permute-start.8 = (bf16[128,512]{1,0:T(8,128)(2,1)S(1)}, bf16[128,512]{1,0:T(8,128)(2,1)S(1)}, u32[]{:S(2)}, u32[]{:S(2)}) collective-permute-start(bf16[128,512]{1,0:T(8,128)(2,1)S(1)} %get-tuple-element.40._), channel_id=1, source_target_pairs={{0,2},{1,9},{2,0},{3,11},{4,6},{5,13},{6,4},{7,15},{8,10},{9,1},{1... | collective-permute-start | bytes 393224 | tf_op jit(solution)/shard_map/ppermute | solution.py:223
  22.3 2.4 %collective-permute-start.6 = (bf16[64,768]{1,0:T(8,128)(2,1)S(1)}, bf16[64,768]{1,0:T(8,128)(2,1)S(1)}, u32[]{:S(2)}, u32[]{:S(2)}) collective-permute-start(bf16[64,768]{1,0:T(8,128)(2,1)S(1)} %get-tuple-element.43._), channel_id=1, source_target_pairs={{0,8},{1,5},{2,10},{3,7},{4,12},{5,1},{6,14},{7,3},{8,0},{9,13},{1... | collective-permute-start | bytes 294920 | tf_op jit(solution)/shard_map/ppermute | solution.py:223
  24.7 0.2 collective-permute-done.5.got
  24.9 2.0 %collective-permute-start.7 = (bf16[64,512]{1,0:T(8,128)(2,1)S(1)}, bf16[64,512]{1,0:T(8,128)(2,1)S(1)}, u32[]{:S(2)}, u32[]{:S(2)}) collective-permute-start(bf16[64,512]{1,0:T(8,128)(2,1)S(1)} %get-tuple-element.45._), channel_id=1, source_target_pairs={{0,8},{1,5},{2,10},{3,7},{4,12},{5,1},{6,14},{7,3},{8,0},{9,13},{1... | collective-permute-start | bytes 196616 | tf_op jit(solution)/shard_map/ppermute | solution.py:223
  26.9 1.1 %collective-permute-start.9 = (bf16[64,512]{1,0:T(8,128)(2,1)S(1)}, bf16[64,512]{1,0:T(8,128)(2,1)S(1)}, u32[]{:S(2)}, u32[]{:S(2)}) collective-permute-start(bf16[64,512]{1,0:T(8,128)(2,1)S(1)} %get-tuple-element.48), channel_id=1, source_target_pairs={{0,8},{1,5},{2,10},{3,7},{4,12},{5,1},{6,14},{7,3},{8,0},{9,13},{1... | collective-permute-start | bytes 196616 | tf_op jit(solution)/shard_map/ppermute | solution.py:223
  28.0 2.8 %collective-permute-done.7.refs_3_ = bf16[64,512]{1,0:T(8,128)(2,1)S(1)} collective-permute-done((bf16[64,512]{1,0:T(8,128)(2,1)S(1)}, bf16[64,512]{1,0:T(8,128)(2,1)S(1)}, u32[]{:S(2)}, u32[]{:S(2)}) %collective-permute-start.7) | collective-permute-done | bytes 65568 | tf_op jit(solution)/shard_map/ppermute | solution.py:223
  30.8 0.8 %shard_map.58._ = f32[64,1792]{1,0:T(8,128)} custom-call(f32[64,768]{1,0:T(8,128)S(1)} %get-tuple-element.41.refs_0_, f32[64,512]{1,0:T(8,128)S(1)} %get-tuple-element.44.refs_1_, bf16[64,768]{1,0:T(8,128)(2,1)S(1)} %collective-permute-done.6.refs_2_, bf16[64,512]{1,0:T(8,128)(2,1)S(1)} %collective-permute-done.7.refs_3_), custom_call_target="tpu_custom_call" | custom-call | flops 81920 | bytes 819200 | tf_op jit(solution)/shard_map/pallas_call | solution.py:190
  31.5 1.3 %collective-permute-done.9.came = bf16[64,512]{1,0:T(8,128)(2,1)S(1)} collective-permute-done((bf16[64,512]{1,0:T(8,128)(2,1)S(1)}, bf16[64,512]{1,0:T(8,128)(2,1)S(1)}, u32[]{:S(2)}, u32[]{:S(2)}) %collective-permute-start.9) | collective-permute-done | bytes 65568 | tf_op jit(solution)/shard_map/ppermute | solution.py:223
  32.9 0.7 %shard_map.60 = f32[64,1792]{1,0:T(8,128)} custom-call(f32[64,1792]{1,0:T(8,128)} %shard_map.58._, f32[64,512]{1,0:T(8,128)S(1)} %get-tuple-element.47.kept, bf16[64,512]{1,0:T(8,128)(2,1)S(1)} %collective-permute-done.9.came), custom_call_target="tpu_custom_call", output_to_operand_aliasing={{}: (0, {})} | custom-call | flops 32768 | bytes 327680 | tf_op jit(solution)/shard_map/pallas_call | solution.py:190
  (11 shorter events, 0.2 us)
Async XLA Ops:
  0.0 2.5 %collective-permute-start = (bf16[32,2048]{1,0:T(8,128)(2,1)}, bf16[32,2048]{1,0:T(8,128)(2,1)S(1)}, u32[]{:S(2)}, u32[]{:S(2)}) collective-permute-start(bf16[32,2048]{1,0:T(8,128)(2,1)} %own_hbm.1), channel_id=1, source_target_pairs={{0,1},{1,0},{2,3},{3,2},{4,5},{5,4},{6,7},{7,6},{8,9},{9,8},{10,11... | collective-permute-start | bytes 393224 | tf_op jit(solution)/shard_map/ppermute | solution.py:228
  4.1 9.7 %collective-permute-start.1 = (bf16[256,768]{1,0:T(8,128)(2,1)S(1)}, bf16[256,768]{1,0:T(8,128)(2,1)S(1)}, u32[]{:S(2)}, u32[]{:S(2)}) collective-permute-start(bf16[256,768]{1,0:T(8,128)(2,1)S(1)} %get-tuple-element.34), channel_id=1, source_target_pairs={{0,4},{1,3},{2,6},{3,1},{4,0},{5,7},{6,2},{7,5},{8,12},{9,11},{10,... | collective-permute-start | bytes 1179656 | tf_op jit(solution)/shard_map/ppermute | solution.py:223
  8.5 9.6 %collective-permute-start.4 = (bf16[256,512]{1,0:T(8,128)(2,1)S(1)}, bf16[256,512]{1,0:T(8,128)(2,1)S(1)}, u32[]{:S(2)}, u32[]{:S(2)}) collective-permute-start(bf16[256,512]{1,0:T(8,128)(2,1)S(1)} %get-tuple-element.36._), channel_id=1, source_target_pairs={{0,2},{1,9},{2,0},{3,11},{4,6},{5,13},{6,4},{7,15},{8,10},{9,1},{1... | collective-permute-start | bytes 786440 | tf_op jit(solution)/shard_map/ppermute | solution.py:223
  10.8 9.5 %collective-permute-start.3 = (bf16[256,512]{1,0:T(8,128)(2,1)S(1)}, bf16[256,512]{1,0:T(8,128)(2,1)S(1)}, u32[]{:S(2)}, u32[]{:S(2)}) collective-permute-start(bf16[256,512]{1,0:T(8,128)(2,1)S(1)} %shard_map.50._), channel_id=1, source_target_pairs={{0,4},{1,3},{2,6},{3,1},{4,0},{5,7},{6,2},{7,5},{8,12},{9,11},{10,... | collective-permute-start | bytes 786440 | tf_op jit(solution)/shard_map/ppermute | solution.py:223
  13.9 8.4 %collective-permute-start.2 = (bf16[128,768]{1,0:T(8,128)(2,1)S(1)}, bf16[128,768]{1,0:T(8,128)(2,1)S(1)}, u32[]{:S(2)}, u32[]{:S(2)}) collective-permute-start(bf16[128,768]{1,0:T(8,128)(2,1)S(1)} %get-tuple-element.38._), channel_id=1, source_target_pairs={{0,2},{1,9},{2,0},{3,11},{4,6},{5,13},{6,4},{7,15},{8,10},{9,1},{1... | collective-permute-start | bytes 589832 | tf_op jit(solution)/shard_map/ppermute | solution.py:223
  18.2 6.7 %collective-permute-start.5 = (bf16[128,512]{1,0:T(8,128)(2,1)S(1)}, bf16[128,512]{1,0:T(8,128)(2,1)S(1)}, u32[]{:S(2)}, u32[]{:S(2)}) collective-permute-start(bf16[128,512]{1,0:T(8,128)(2,1)S(1)} %get-tuple-element.39._), channel_id=1, source_target_pairs={{0,4},{1,3},{2,6},{3,1},{4,0},{5,7},{6,2},{7,5},{8,12},{9,11},{10,... | collective-permute-start | bytes 393224 | tf_op jit(solution)/shard_map/ppermute | solution.py:223
  20.3 6.6 %collective-permute-start.8 = (bf16[128,512]{1,0:T(8,128)(2,1)S(1)}, bf16[128,512]{1,0:T(8,128)(2,1)S(1)}, u32[]{:S(2)}, u32[]{:S(2)}) collective-permute-start(bf16[128,512]{1,0:T(8,128)(2,1)S(1)} %get-tuple-element.40._), channel_id=1, source_target_pairs={{0,2},{1,9},{2,0},{3,11},{4,6},{5,13},{6,4},{7,15},{8,10},{9,1},{1... | collective-permute-start | bytes 393224 | tf_op jit(solution)/shard_map/ppermute | solution.py:223
  22.3 8.5 %collective-permute-start.6 = (bf16[64,768]{1,0:T(8,128)(2,1)S(1)}, bf16[64,768]{1,0:T(8,128)(2,1)S(1)}, u32[]{:S(2)}, u32[]{:S(2)}) collective-permute-start(bf16[64,768]{1,0:T(8,128)(2,1)S(1)} %get-tuple-element.43._), channel_id=1, source_target_pairs={{0,8},{1,5},{2,10},{3,7},{4,12},{5,1},{6,14},{7,3},{8,0},{9,13},{1... | collective-permute-start | bytes 294920 | tf_op jit(solution)/shard_map/ppermute | solution.py:223
  24.9 5.8 %collective-permute-start.7 = (bf16[64,512]{1,0:T(8,128)(2,1)S(1)}, bf16[64,512]{1,0:T(8,128)(2,1)S(1)}, u32[]{:S(2)}, u32[]{:S(2)}) collective-permute-start(bf16[64,512]{1,0:T(8,128)(2,1)S(1)} %get-tuple-element.45._), channel_id=1, source_target_pairs={{0,8},{1,5},{2,10},{3,7},{4,12},{5,1},{6,14},{7,3},{8,0},{9,13},{1... | collective-permute-start | bytes 196616 | tf_op jit(solution)/shard_map/ppermute | solution.py:223
  26.9 5.9 %collective-permute-start.9 = (bf16[64,512]{1,0:T(8,128)(2,1)S(1)}, bf16[64,512]{1,0:T(8,128)(2,1)S(1)}, u32[]{:S(2)}, u32[]{:S(2)}) collective-permute-start(bf16[64,512]{1,0:T(8,128)(2,1)S(1)} %get-tuple-element.48), channel_id=1, source_target_pairs={{0,8},{1,5},{2,10},{3,7},{4,12},{5,1},{6,14},{7,3},{8,0},{9,13},{1... | collective-permute-start | bytes 196616 | tf_op jit(solution)/shard_map/ppermute | solution.py:223

commit v18 on v17

--- a/solution.py
+++ b/solution.py
@@ -13,7 +13,7 @@
 PLAN = [
     (3, (NEAR, X, FAR), (X, FAR, NEAR)),
     (2, (X, NEAR, FAR), (FAR, X, NEAR)),
-    (2, (NEAR, X, FAR), (X, FAR, NEAR)),
+    (2, (NEAR, FAR, X), (X, NEAR, FAR)),
 ]
 ORDER = [(piece, stage) for stage in (1, 2) for piece in range(len(PLAN))]
 

time: 33.7 us -> 34.7 us (1.030)
  starting transfers between devices: 16.4 us -> 17.1 us
    ppermute x9, starting transfers between devices: 16 us -> 16.6 us  [exchange(): return lax.ppermute(value, ('grid', 'eig'), pairs)]
  transfers between devices with their start and end apart: 10 -> 10, of which waited for: 5 -> 4; matrix products, arithmetic and copies ran while one was open for 0% -> 0% of each run, Pallas kernels for 24% -> 23%
where the time goes in v18:
time: 34.7 us; the launch traced here: 34.5 us
  starting transfers between devices  17.1 us (49%)
  Pallas kernels  10.3 us (30%)
  waiting for transfers between devices  7.03 us (20%)
    ppermute x9, starting transfers between devices, exchange(): return lax.ppermute(value, ('grid', 'eig'), pairs)  16.6 us
    pallas_call x15, Pallas kernels, kernel_call(): pl.pallas_call(body, out_shape=[jax.ShapeDtypeStruct(*out) for out in out...  10.3 us
    ppermute x9, waiting for transfers between devices, exchange(): return lax.ppermute(value, ('grid', 'eig'), pairs)  7.03 us
  transfers between devices with their start and end apart: 10, of which 4 were waited for; matrix products, arithmetic and copies ran while one was open for 0% of the time, Pallas kernels for 23%

profile of v18, /device:TPU:0, one launch (start us, length us, event | category | flops | bytes accessed | tf_op | source)
XLA Modules:
  0.0 34.5 jit_solution(8909656515314113452)
XLA Ops:
  0.0 0.5 %collective-permute-start = (bf16[32,2048]{1,0:T(8,128)(2,1)}, bf16[32,2048]{1,0:T(8,128)(2,1)S(1)}, u32[]{:S(2)}, u32[]{:S(2)}) collective-permute-start(bf16[32,2048]{1,0:T(8,128)(2,1)} %own_hbm.1), channel_id=1, source_target_pairs={{0,1},{1,0},{2,3},{3,2},{4,5},{5,4},{6,7},{7,6},{8,9},{9,8},{10,11... | collective-permute-start | bytes 393224 | tf_op jit(solution)/shard_map/ppermute | solution.py:228
  0.5 2.0 %shard_map.46 = (bf16[512,64]{1,0:T(8,128)(2,1)S(1)}, bf16[32,2048]{1,0:T(8,128)(2,1)S(1)}, bf16[8,2048]{1,0:T(8,128)(2,1)S(1)}, bf16[768,2048]{1,0:T(8,128)(2,1)S(1)}) custom-call(s32[64]{0:T(128)} %order_hbm.1, bf16[32,2048]{1,0:T(8,128)(2,1)} %own_hbm.1, bf16[8,2048]{1,0:T(8,128)(2,1)} %lanc_hbm.1, bf16[1792,2048]{1,0:T(8,128)(2,1)} %eig_hbm.5), custom_call_target="tpu_custom_call" | custom-call | bytes 3145728 | tf_op jit(solution)/shard_map/pallas_call | solution.py:190
  2.5 1.6 %shard_map.47 = (bf16[256,768]{1,0:T(8,128)(2,1)S(1)}, bf16[256,2048]{1,0:T(8,128)(2,1)S(1)}, bf16[512,2048]{1,0:T(8,128)(2,1)S(1)}) custom-call(bf16[512,64]{1,0:T(8,128)(2,1)S(1)} %get-tuple-element.27.pick, bf16[32,2048]{1,0:T(8,128)(2,1)S(1)} %get-tuple-element.28.own, bf16[32,2048]{1,0:T(8,128)(2,1)S(1)} %collective-permute-done.other, ...), custom_call_target="tpu_custom_call" | custom-call | flops 805306368 | bytes 3145728 | tf_op jit(solution)/shard_map/pallas_call | solution.py:190
  4.1 2.6 %collective-permute-start.1 = (bf16[256,768]{1,0:T(8,128)(2,1)S(1)}, bf16[256,768]{1,0:T(8,128)(2,1)S(1)}, u32[]{:S(2)}, u32[]{:S(2)}) collective-permute-start(bf16[256,768]{1,0:T(8,128)(2,1)S(1)} %get-tuple-element.34), channel_id=1, source_target_pairs={{0,4},{1,3},{2,6},{3,1},{4,0},{5,7},{6,2},{7,5},{8,12},{9,11},{10,... | collective-permute-start | bytes 1179656 | tf_op jit(solution)/shard_map/ppermute | solution.py:223
  6.7 1.8 %shard_map.48 = (bf16[256,512]{1,0:T(8,128)(2,1)S(1)}, bf16[512,2048]{1,0:T(8,128)(2,1)S(1)}, bf16[512,2048]{1,0:T(8,128)(2,1)S(1)}) custom-call(bf16[512,64]{1,0:T(8,128)(2,1)S(1)} %get-tuple-element.27.pick, bf16[32,2048]{1,0:T(8,128)(2,1)S(1)} %get-tuple-element.28.own, bf16[32,2048]{1,0:T(8,128)(2,1)S(1)} %collective-permute-done.other, ...), custom_call_target="tpu_custom_call" | custom-call | flops 536870912 | bytes 2097152 | tf_op jit(solution)/shard_map/pallas_call | solution.py:190
  8.5 1.5 %collective-permute-start.4 = (bf16[256,512]{1,0:T(8,128)(2,1)S(1)}, bf16[256,512]{1,0:T(8,128)(2,1)S(1)}, u32[]{:S(2)}, u32[]{:S(2)}) collective-permute-start(bf16[256,512]{1,0:T(8,128)(2,1)S(1)} %get-tuple-element.36._), channel_id=1, source_target_pairs={{0,2},{1,9},{2,0},{3,11},{4,6},{5,13},{6,4},{7,15},{8,10},{9,1},{1... | collective-permute-start | bytes 786440 | tf_op jit(solution)/shard_map/ppermute | solution.py:223
  10.1 0.7 %shard_map.50._ = bf16[256,512]{1,0:T(8,128)(2,1)S(1)} custom-call(bf16[512,2048]{1,0:T(8,128)(2,1)S(1)} %get-tuple-element.33.prod, bf16[512,2048]{1,0:T(8,128)(2,1)S(1)} %get-tuple-element.35.eig, bf16[256,512]{1,0:T(8,128)(2,1)S(1)} %get-tuple-element.36._), custom_call_target="tpu_custom_call" | custom-call | flops 536870912 | bytes 2097152 | tf_op jit(solution)/shard_map/pallas_call | solution.py:190
  10.8 0.5 %collective-permute-start.3 = (bf16[256,512]{1,0:T(8,128)(2,1)S(1)}, bf16[256,512]{1,0:T(8,128)(2,1)S(1)}, u32[]{:S(2)}, u32[]{:S(2)}) collective-permute-start(bf16[256,512]{1,0:T(8,128)(2,1)S(1)} %shard_map.50._), channel_id=1, source_target_pairs={{0,4},{1,3},{2,6},{3,1},{4,0},{5,7},{6,2},{7,5},{8,12},{9,11},{10,... | collective-permute-start | bytes 786440 | tf_op jit(solution)/shard_map/ppermute | solution.py:223
  11.3 1.0 %shard_map.49.kept = f32[256,768]{1,0:T(8,128)S(1)} custom-call(bf16[512,2048]{1,0:T(8,128)(2,1)S(1)} %get-tuple-element.33.prod, bf16[768,2048]{1,0:T(8,128)(2,1)S(1)} %get-tuple-element.30.eig), custom_call_target="tpu_custom_call" | custom-call | flops 805306368 | bytes 3145728 | tf_op jit(solution)/shard_map/pallas_call | solution.py:190
  12.3 1.5 %collective-permute-done.1.got = bf16[256,768]{1,0:T(8,128)(2,1)S(1)} collective-permute-done((bf16[256,768]{1,0:T(8,128)(2,1)S(1)}, bf16[256,768]{1,0:T(8,128)(2,1)S(1)}, u32[]{:S(2)}, u32[]{:S(2)}) %collective-permute-start.1) | collective-permute-done | bytes 393248 | tf_op jit(solution)/shard_map/ppermute | solution.py:223
  13.8 0.1 shard_map.51
  13.9 3.5 %collective-permute-start.2 = (bf16[128,768]{1,0:T(8,128)(2,1)S(1)}, bf16[128,768]{1,0:T(8,128)(2,1)S(1)}, u32[]{:S(2)}, u32[]{:S(2)}) collective-permute-start(bf16[128,768]{1,0:T(8,128)(2,1)S(1)} %get-tuple-element.38._), channel_id=1, source_target_pairs={{0,2},{1,9},{2,0},{3,11},{4,6},{5,13},{6,4},{7,15},{8,10},{9,1},{1... | collective-permute-start | bytes 589832 | tf_op jit(solution)/shard_map/ppermute | solution.py:223
  17.4 0.7 %shard_map.53.kept = f32[256,512]{1,0:T(8,128)S(1)} custom-call(bf16[512,2048]{1,0:T(8,128)(2,1)S(1)} %get-tuple-element.33.prod, bf16[512,2048]{1,0:T(8,128)(2,1)S(1)} %get-tuple-element.32.eig), custom_call_target="tpu_custom_call" | custom-call | flops 536870912 | bytes 2097152 | tf_op jit(solution)/shard_map/pallas_call | solution.py:190
  18.2 0.4 %collective-permute-start.5 = (bf16[128,512]{1,0:T(8,128)(2,1)S(1)}, bf16[128,512]{1,0:T(8,128)(2,1)S(1)}, u32[]{:S(2)}, u32[]{:S(2)}) collective-permute-start(bf16[128,512]{1,0:T(8,128)(2,1)S(1)} %get-tuple-element.39._), channel_id=1, source_target_pairs={{0,4},{1,3},{2,6},{3,1},{4,0},{5,7},{6,2},{7,5},{8,12},{9,11},{10,... | collective-permute-start | bytes 393224 | tf_op jit(solution)/shard_map/ppermute | solution.py:223
  18.5 0.7 %shard_map.52.kept = f32[256,512]{1,0:T(8,128)S(1)} custom-call(bf16[512,2048]{1,0:T(8,128)(2,1)S(1)} %get-tuple-element.33.prod, bf16[512,2048]{1,0:T(8,128)(2,1)S(1)} %get-tuple-element.35.eig), custom_call_target="tpu_custom_call" | custom-call | flops 536870912 | bytes 2097152 | tf_op jit(solution)/shard_map/pallas_call | solution.py:190
  19.3 1.0 %collective-permute-done.3.got = bf16[256,512]{1,0:T(8,128)(2,1)S(1)} collective-permute-done((bf16[256,512]{1,0:T(8,128)(2,1)S(1)}, bf16[256,512]{1,0:T(8,128)(2,1)S(1)}, u32[]{:S(2)}, u32[]{:S(2)}) %collective-permute-start.3) | collective-permute-done | bytes 262176 | tf_op jit(solution)/shard_map/ppermute | solution.py:223
  20.3 2.4 %collective-permute-start.8 = (bf16[128,512]{1,0:T(8,128)(2,1)S(1)}, bf16[128,512]{1,0:T(8,128)(2,1)S(1)}, u32[]{:S(2)}, u32[]{:S(2)}) collective-permute-start(bf16[128,512]{1,0:T(8,128)(2,1)S(1)} %get-tuple-element.40._), channel_id=1, source_target_pairs={{0,8},{1,5},{2,10},{3,7},{4,12},{5,1},{6,14},{7,3},{8,0},{9,13},{1... | collective-permute-start | bytes 393224 | tf_op jit(solution)/shard_map/ppermute | solution.py:223
  22.8 1.7 %collective-permute-start.6 = (bf16[64,768]{1,0:T(8,128)(2,1)S(1)}, bf16[64,768]{1,0:T(8,128)(2,1)S(1)}, u32[]{:S(2)}, u32[]{:S(2)}) collective-permute-start(bf16[64,768]{1,0:T(8,128)(2,1)S(1)} %get-tuple-element.43._), channel_id=1, source_target_pairs={{0,8},{1,5},{2,10},{3,7},{4,12},{5,1},{6,14},{7,3},{8,0},{9,13},{1... | collective-permute-start | bytes 294920 | tf_op jit(solution)/shard_map/ppermute | solution.py:223
  24.5 0.1 collective-permute-done.5.got
  24.6 2.9 %collective-permute-start.7 = (bf16[64,512]{1,0:T(8,128)(2,1)S(1)}, bf16[64,512]{1,0:T(8,128)(2,1)S(1)}, u32[]{:S(2)}, u32[]{:S(2)}) collective-permute-start(bf16[64,512]{1,0:T(8,128)(2,1)S(1)} %get-tuple-element.45._), channel_id=1, source_target_pairs={{0,8},{1,5},{2,10},{3,7},{4,12},{5,1},{6,14},{7,3},{8,0},{9,13},{1... | collective-permute-start | bytes 196616 | tf_op jit(solution)/shard_map/ppermute | solution.py:223
  27.5 1.1 %collective-permute-start.9 = (bf16[64,512]{1,0:T(8,128)(2,1)S(1)}, bf16[64,512]{1,0:T(8,128)(2,1)S(1)}, u32[]{:S(2)}, u32[]{:S(2)}) collective-permute-start(bf16[64,512]{1,0:T(8,128)(2,1)S(1)} %get-tuple-element.48), channel_id=1, source_target_pairs={{0,2},{1,9},{2,0},{3,11},{4,6},{5,13},{6,4},{7,15},{8,10},{9,1},{1... | collective-permute-start | bytes 196616 | tf_op jit(solution)/shard_map/ppermute | solution.py:223
  28.6 4.5 %collective-permute-done.7.refs_3_ = bf16[64,512]{1,0:T(8,128)(2,1)S(1)} collective-permute-done((bf16[64,512]{1,0:T(8,128)(2,1)S(1)}, bf16[64,512]{1,0:T(8,128)(2,1)S(1)}, u32[]{:S(2)}, u32[]{:S(2)}) %collective-permute-start.7) | collective-permute-done | bytes 65568 | tf_op jit(solution)/shard_map/ppermute | solution.py:223
  33.1 0.8 %shard_map.58._ = f32[64,1792]{1,0:T(8,128)} custom-call(f32[64,768]{1,0:T(8,128)S(1)} %get-tuple-element.41.refs_0_, f32[64,512]{1,0:T(8,128)S(1)} %get-tuple-element.44.refs_1_, bf16[64,768]{1,0:T(8,128)(2,1)S(1)} %collective-permute-done.6.refs_2_, bf16[64,512]{1,0:T(8,128)(2,1)S(1)} %collective-permute-done.7.refs_3_), custom_call_target="tpu_custom_call" | custom-call | flops 81920 | bytes 819200 | tf_op jit(solution)/shard_map/pallas_call | solution.py:190
  33.8 0.7 %shard_map.60 = f32[64,1792]{1,0:T(8,128)} custom-call(f32[64,1792]{1,0:T(8,128)} %shard_map.58._, f32[64,512]{1,0:T(8,128)S(1)} %get-tuple-element.47.kept, bf16[64,512]{1,0:T(8,128)(2,1)S(1)} %collective-permute-done.9.came), custom_call_target="tpu_custom_call", output_to_operand_aliasing={{}: (0, {})} | custom-call | flops 32768 | bytes 327680 | tf_op jit(solution)/shard_map/pallas_call | solution.py:190
  (11 shorter events, 0.2 us)
Async XLA Ops:
  0.0 2.5 %collective-permute-start = (bf16[32,2048]{1,0:T(8,128)(2,1)}, bf16[32,2048]{1,0:T(8,128)(2,1)S(1)}, u32[]{:S(2)}, u32[]{:S(2)}) collective-permute-start(bf16[32,2048]{1,0:T(8,128)(2,1)} %own_hbm.1), channel_id=1, source_target_pairs={{0,1},{1,0},{2,3},{3,2},{4,5},{5,4},{6,7},{7,6},{8,9},{9,8},{10,11... | collective-permute-start | bytes 393224 | tf_op jit(solution)/shard_map/ppermute | solution.py:228
  4.1 9.7 %collective-permute-start.1 = (bf16[256,768]{1,0:T(8,128)(2,1)S(1)}, bf16[256,768]{1,0:T(8,128)(2,1)S(1)}, u32[]{:S(2)}, u32[]{:S(2)}) collective-permute-start(bf16[256,768]{1,0:T(8,128)(2,1)S(1)} %get-tuple-element.34), channel_id=1, source_target_pairs={{0,4},{1,3},{2,6},{3,1},{4,0},{5,7},{6,2},{7,5},{8,12},{9,11},{10,... | collective-permute-start | bytes 1179656 | tf_op jit(solution)/shard_map/ppermute | solution.py:223
  8.5 9.6 %collective-permute-start.4 = (bf16[256,512]{1,0:T(8,128)(2,1)S(1)}, bf16[256,512]{1,0:T(8,128)(2,1)S(1)}, u32[]{:S(2)}, u32[]{:S(2)}) collective-permute-start(bf16[256,512]{1,0:T(8,128)(2,1)S(1)} %get-tuple-element.36._), channel_id=1, source_target_pairs={{0,2},{1,9},{2,0},{3,11},{4,6},{5,13},{6,4},{7,15},{8,10},{9,1},{1... | collective-permute-start | bytes 786440 | tf_op jit(solution)/shard_map/ppermute | solution.py:223
  10.8 9.5 %collective-permute-start.3 = (bf16[256,512]{1,0:T(8,128)(2,1)S(1)}, bf16[256,512]{1,0:T(8,128)(2,1)S(1)}, u32[]{:S(2)}, u32[]{:S(2)}) collective-permute-start(bf16[256,512]{1,0:T(8,128)(2,1)S(1)} %shard_map.50._), channel_id=1, source_target_pairs={{0,4},{1,3},{2,6},{3,1},{4,0},{5,7},{6,2},{7,5},{8,12},{9,11},{10,... | collective-permute-start | bytes 786440 | tf_op jit(solution)/shard_map/ppermute | solution.py:223
  13.9 8.9 %collective-permute-start.2 = (bf16[128,768]{1,0:T(8,128)(2,1)S(1)}, bf16[128,768]{1,0:T(8,128)(2,1)S(1)}, u32[]{:S(2)}, u32[]{:S(2)}) collective-permute-start(bf16[128,768]{1,0:T(8,128)(2,1)S(1)} %get-tuple-element.38._), channel_id=1, source_target_pairs={{0,2},{1,9},{2,0},{3,11},{4,6},{5,13},{6,4},{7,15},{8,10},{9,1},{1... | collective-permute-start | bytes 589832 | tf_op jit(solution)/shard_map/ppermute | solution.py:223
  18.2 6.4 %collective-permute-start.5 = (bf16[128,512]{1,0:T(8,128)(2,1)S(1)}, bf16[128,512]{1,0:T(8,128)(2,1)S(1)}, u32[]{:S(2)}, u32[]{:S(2)}) collective-permute-start(bf16[128,512]{1,0:T(8,128)(2,1)S(1)} %get-tuple-element.39._), channel_id=1, source_target_pairs={{0,4},{1,3},{2,6},{3,1},{4,0},{5,7},{6,2},{7,5},{8,12},{9,11},{10,... | collective-permute-start | bytes 393224 | tf_op jit(solution)/shard_map/ppermute | solution.py:223
  20.3 7.2 %collective-permute-start.8 = (bf16[128,512]{1,0:T(8,128)(2,1)S(1)}, bf16[128,512]{1,0:T(8,128)(2,1)S(1)}, u32[]{:S(2)}, u32[]{:S(2)}) collective-permute-start(bf16[128,512]{1,0:T(8,128)(2,1)S(1)} %get-tuple-element.40._), channel_id=1, source_target_pairs={{0,8},{1,5},{2,10},{3,7},{4,12},{5,1},{6,14},{7,3},{8,0},{9,13},{1... | collective-permute-start | bytes 393224 | tf_op jit(solution)/shard_map/ppermute | solution.py:223
  22.8 10.3 %collective-permute-start.6 = (bf16[64,768]{1,0:T(8,128)(2,1)S(1)}, bf16[64,768]{1,0:T(8,128)(2,1)S(1)}, u32[]{:S(2)}, u32[]{:S(2)}) collective-permute-start(bf16[64,768]{1,0:T(8,128)(2,1)S(1)} %get-tuple-element.43._), channel_id=1, source_target_pairs={{0,8},{1,5},{2,10},{3,7},{4,12},{5,1},{6,14},{7,3},{8,0},{9,13},{1... | collective-permute-start | bytes 294920 | tf_op jit(solution)/shard_map/ppermute | solution.py:223
  24.6 8.5 %collective-permute-start.7 = (bf16[64,512]{1,0:T(8,128)(2,1)S(1)}, bf16[64,512]{1,0:T(8,128)(2,1)S(1)}, u32[]{:S(2)}, u32[]{:S(2)}) collective-permute-start(bf16[64,512]{1,0:T(8,128)(2,1)S(1)} %get-tuple-element.45._), channel_id=1, source_target_pairs={{0,8},{1,5},{2,10},{3,7},{4,12},{5,1},{6,14},{7,3},{8,0},{9,13},{1... | collective-permute-start | bytes 196616 | tf_op jit(solution)/shard_map/ppermute | solution.py:223
  27.5 6.3 %collective-permute-start.9 = (bf16[64,512]{1,0:T(8,128)(2,1)S(1)}, bf16[64,512]{1,0:T(8,128)(2,1)S(1)}, u32[]{:S(2)}, u32[]{:S(2)}) collective-permute-start(bf16[64,512]{1,0:T(8,128)(2,1)S(1)} %get-tuple-element.48), channel_id=1, source_target_pairs={{0,2},{1,9},{2,0},{3,11},{4,6},{5,13},{6,4},{7,15},{8,10},{9,1},{1... | collective-permute-start | bytes 196616 | tf_op jit(solution)/shard_map/ppermute | solution.py:223

commit v19 on v18

--- a/solution.py
+++ b/solution.py
@@ -11,9 +11,9 @@
 VMEM_LIMIT = 32 * 1024 * 1024
 X, NEAR, FAR = 0, 1, 2
 PLAN = [
-    (3, (NEAR, X, FAR), (X, FAR, NEAR)),
+    (3.5, (NEAR, X, FAR), (X, FAR, NEAR)),
     (2, (X, NEAR, FAR), (FAR, X, NEAR)),
-    (2, (NEAR, FAR, X), (X, NEAR, FAR)),
+    (1.5, (NEAR, X, FAR), (X, FAR, NEAR)),
 ]
 ORDER = [(piece, stage) for stage in (1, 2) for piece in range(len(PLAN))]
 

time: 34.7 us -> 35.5 us (1.023)
  waiting for transfers between devices: 7.03 us -> 8.51 us
  starting transfers between devices: 17.1 us -> 16.2 us
    ppermute x9, waiting for transfers between devices: 7.03 us -> 8.51 us  [exchange(): return lax.ppermute(value, ('grid', 'eig'), pairs)]
    ppermute x9, starting transfers between devices: 16.6 us -> 15.7 us  [exchange(): return lax.ppermute(value, ('grid', 'eig'), pairs)]
  transfers between devices with their start and end apart: 10 -> 10, of which waited for: 4 -> 5; matrix products, arithmetic and copies ran while one was open for 0% -> 0% of each run, Pallas kernels for 23% -> 23%
where the time goes in v19:
time: 35.5 us; the launch traced here: 35.3 us
  starting transfers between devices  16.2 us (46%)
  Pallas kernels  10.5 us (30%)
  waiting for transfers between devices  8.51 us (24%)
    ppermute x9, starting transfers between devices, exchange(): return lax.ppermute(value, ('grid', 'eig'), pairs)  15.7 us
    pallas_call x15, Pallas kernels, kernel_call(): pl.pallas_call(body, out_shape=[jax.ShapeDtypeStruct(*out) for out in out...  10.5 us
    ppermute x9, waiting for transfers between devices, exchange(): return lax.ppermute(value, ('grid', 'eig'), pairs)  8.51 us
  transfers between devices with their start and end apart: 10, of which 5 were waited for; matrix products, arithmetic and copies ran while one was open for 0% of the time, Pallas kernels for 23%

profile of v19, /device:TPU:0, one launch (start us, length us, event | category | flops | bytes accessed | tf_op | source)
XLA Modules:
  0.0 35.3 jit_solution(8280849005763683745)
XLA Ops:
  0.0 0.5 %collective-permute-start = (bf16[32,2048]{1,0:T(8,128)(2,1)}, bf16[32,2048]{1,0:T(8,128)(2,1)S(1)}, u32[]{:S(2)}, u32[]{:S(2)}) collective-permute-start(bf16[32,2048]{1,0:T(8,128)(2,1)} %own_hbm.1), channel_id=1, source_target_pairs={{0,1},{1,0},{2,3},{3,2},{4,5},{5,4},{6,7},{7,6},{8,9},{9,8},{10,11... | collective-permute-start | bytes 393224 | tf_op jit(solution)/shard_map/ppermute | solution.py:228
  0.5 2.2 %shard_map.46 = (bf16[512,64]{1,0:T(8,128)(2,1)S(1)}, bf16[32,2048]{1,0:T(8,128)(2,1)S(1)}, bf16[8,2048]{1,0:T(8,128)(2,1)S(1)}, bf16[896,2048]{1,0:T(8,128)(2,1)S(1)}) custom-call(s32[64]{0:T(128)} %order_hbm.1, bf16[32,2048]{1,0:T(8,128)(2,1)} %own_hbm.1, bf16[8,2048]{1,0:T(8,128)(2,1)} %lanc_hbm.1, bf16[1792,2048]{1,0:T(8,128)(2,1)} %eig_hbm.5), custom_call_target="tpu_custom_call" | custom-call | bytes 3670016 | tf_op jit(solution)/shard_map/pallas_call | solution.py:190
  2.6 1.6 %shard_map.47 = (bf16[256,896]{1,0:T(8,128)(2,1)S(1)}, bf16[256,2048]{1,0:T(8,128)(2,1)S(1)}, bf16[512,2048]{1,0:T(8,128)(2,1)S(1)}) custom-call(bf16[512,64]{1,0:T(8,128)(2,1)S(1)} %get-tuple-element.27.pick, bf16[32,2048]{1,0:T(8,128)(2,1)S(1)} %get-tuple-element.28.own, bf16[32,2048]{1,0:T(8,128)(2,1)S(1)} %collective-permute-done.other, ...), custom_call_target="tpu_custom_call" | custom-call | flops 939524096 | bytes 3670016 | tf_op jit(solution)/shard_map/pallas_call | solution.py:190
  4.3 2.6 %collective-permute-start.1 = (bf16[256,896]{1,0:T(8,128)(2,1)S(1)}, bf16[256,896]{1,0:T(8,128)(2,1)S(1)}, u32[]{:S(2)}, u32[]{:S(2)}) collective-permute-start(bf16[256,896]{1,0:T(8,128)(2,1)S(1)} %get-tuple-element.34), channel_id=1, source_target_pairs={{0,4},{1,3},{2,6},{3,1},{4,0},{5,7},{6,2},{7,5},{8,12},{9,11},{10,... | collective-permute-start | bytes 1376264 | tf_op jit(solution)/shard_map/ppermute | solution.py:223
  6.9 1.6 %shard_map.48 = (bf16[256,512]{1,0:T(8,128)(2,1)S(1)}, bf16[512,2048]{1,0:T(8,128)(2,1)S(1)}, bf16[384,2048]{1,0:T(8,128)(2,1)S(1)}) custom-call(bf16[512,64]{1,0:T(8,128)(2,1)S(1)} %get-tuple-element.27.pick, bf16[32,2048]{1,0:T(8,128)(2,1)S(1)} %get-tuple-element.28.own, bf16[32,2048]{1,0:T(8,128)(2,1)S(1)} %collective-permute-done.other, ...), custom_call_target="tpu_custom_call" | custom-call | flops 536870912 | bytes 1572864 | tf_op jit(solution)/shard_map/pallas_call | solution.py:190
  8.5 1.6 %collective-permute-start.4 = (bf16[256,512]{1,0:T(8,128)(2,1)S(1)}, bf16[256,512]{1,0:T(8,128)(2,1)S(1)}, u32[]{:S(2)}, u32[]{:S(2)}) collective-permute-start(bf16[256,512]{1,0:T(8,128)(2,1)S(1)} %get-tuple-element.36._), channel_id=1, source_target_pairs={{0,2},{1,9},{2,0},{3,11},{4,6},{5,13},{6,4},{7,15},{8,10},{9,1},{1... | collective-permute-start | bytes 786440 | tf_op jit(solution)/shard_map/ppermute | solution.py:223
  10.0 0.7 %shard_map.50._ = bf16[256,384]{1,0:T(8,128)(2,1)S(1)} custom-call(bf16[512,2048]{1,0:T(8,128)(2,1)S(1)} %get-tuple-element.33.prod, bf16[384,2048]{1,0:T(8,128)(2,1)S(1)} %get-tuple-element.35.eig, bf16[256,512]{1,0:T(8,128)(2,1)S(1)} %get-tuple-element.36._), custom_call_target="tpu_custom_call" | custom-call | flops 402653184 | bytes 1572864 | tf_op jit(solution)/shard_map/pallas_call | solution.py:190
  10.8 1.3 %shard_map.49.kept = f32[256,896]{1,0:T(8,128)S(1)} custom-call(bf16[512,2048]{1,0:T(8,128)(2,1)S(1)} %get-tuple-element.33.prod, bf16[896,2048]{1,0:T(8,128)(2,1)S(1)} %get-tuple-element.30.eig), custom_call_target="tpu_custom_call" | custom-call | flops 939524096 | bytes 3670016 | tf_op jit(solution)/shard_map/pallas_call | solution.py:190
  12.0 3.5 %collective-permute-done.1.got = bf16[256,896]{1,0:T(8,128)(2,1)S(1)} collective-permute-done((bf16[256,896]{1,0:T(8,128)(2,1)S(1)}, bf16[256,896]{1,0:T(8,128)(2,1)S(1)}, u32[]{:S(2)}, u32[]{:S(2)}) %collective-permute-start.1) | collective-permute-done | bytes 458784 | tf_op jit(solution)/shard_map/ppermute | solution.py:223
  15.6 2.7 %collective-permute-start.2 = (bf16[128,896]{1,0:T(8,128)(2,1)S(1)}, bf16[128,896]{1,0:T(8,128)(2,1)S(1)}, u32[]{:S(2)}, u32[]{:S(2)}) collective-permute-start(bf16[128,896]{1,0:T(8,128)(2,1)S(1)} %get-tuple-element.38._), channel_id=1, source_target_pairs={{0,2},{1,9},{2,0},{3,11},{4,6},{5,13},{6,4},{7,15},{8,10},{9,1},{1... | collective-permute-start | bytes 688136 | tf_op jit(solution)/shard_map/ppermute | solution.py:223
  18.2 1.2 %collective-permute-start.3 = (bf16[256,384]{1,0:T(8,128)(2,1)S(1)}, bf16[256,384]{1,0:T(8,128)(2,1)S(1)}, u32[]{:S(2)}, u32[]{:S(2)}) collective-permute-start(bf16[256,384]{1,0:T(8,128)(2,1)S(1)} %shard_map.50._), channel_id=1, source_target_pairs={{0,4},{1,3},{2,6},{3,1},{4,0},{5,7},{6,2},{7,5},{8,12},{9,11},{10,... | collective-permute-start | bytes 589832 | tf_op jit(solution)/shard_map/ppermute | solution.py:223
  19.4 0.7 %shard_map.53.kept = f32[256,512]{1,0:T(8,128)S(1)} custom-call(bf16[512,2048]{1,0:T(8,128)(2,1)S(1)} %get-tuple-element.33.prod, bf16[512,2048]{1,0:T(8,128)(2,1)S(1)} %get-tuple-element.32.eig), custom_call_target="tpu_custom_call" | custom-call | flops 536870912 | bytes 2097152 | tf_op jit(solution)/shard_map/pallas_call | solution.py:190
  20.2 0.9 %collective-permute-start.5 = (bf16[128,512]{1,0:T(8,128)(2,1)S(1)}, bf16[128,512]{1,0:T(8,128)(2,1)S(1)}, u32[]{:S(2)}, u32[]{:S(2)}) collective-permute-start(bf16[128,512]{1,0:T(8,128)(2,1)S(1)} %get-tuple-element.39._), channel_id=1, source_target_pairs={{0,4},{1,3},{2,6},{3,1},{4,0},{5,7},{6,2},{7,5},{8,12},{9,11},{10,... | collective-permute-start | bytes 393224 | tf_op jit(solution)/shard_map/ppermute | solution.py:223
  21.1 0.7 %shard_map.52.kept = f32[256,384]{1,0:T(8,128)S(1)} custom-call(bf16[512,2048]{1,0:T(8,128)(2,1)S(1)} %get-tuple-element.33.prod, bf16[384,2048]{1,0:T(8,128)(2,1)S(1)} %get-tuple-element.35.eig), custom_call_target="tpu_custom_call" | custom-call | flops 402653184 | bytes 1572864 | tf_op jit(solution)/shard_map/pallas_call | solution.py:190
  21.9 2.1 %collective-permute-done.3.got = bf16[256,384]{1,0:T(8,128)(2,1)S(1)} collective-permute-done((bf16[256,384]{1,0:T(8,128)(2,1)S(1)}, bf16[256,384]{1,0:T(8,128)(2,1)S(1)}, u32[]{:S(2)}, u32[]{:S(2)}) %collective-permute-start.3) | collective-permute-done | bytes 196640 | tf_op jit(solution)/shard_map/ppermute | solution.py:223
  24.0 0.2 collective-permute-start.8
  24.2 0.5 %collective-permute-done.2.got = bf16[128,896]{1,0:T(8,128)(2,1)S(1)} collective-permute-done((bf16[128,896]{1,0:T(8,128)(2,1)S(1)}, bf16[128,896]{1,0:T(8,128)(2,1)S(1)}, u32[]{:S(2)}, u32[]{:S(2)}) %collective-permute-start.2) | collective-permute-done | bytes 229408 | tf_op jit(solution)/shard_map/ppermute | solution.py:223
  24.7 3.2 %collective-permute-start.6 = (bf16[64,896]{1,0:T(8,128)(2,1)S(1)}, bf16[64,896]{1,0:T(8,128)(2,1)S(1)}, u32[]{:S(2)}, u32[]{:S(2)}) collective-permute-start(bf16[64,896]{1,0:T(8,128)(2,1)S(1)} %get-tuple-element.43._), channel_id=1, source_target_pairs={{0,8},{1,5},{2,10},{3,7},{4,12},{5,1},{6,14},{7,3},{8,0},{9,13},{1... | collective-permute-start | bytes 344072 | tf_op jit(solution)/shard_map/ppermute | solution.py:223
  27.9 0.5 %collective-permute-start.7 = (bf16[64,512]{1,0:T(8,128)(2,1)S(1)}, bf16[64,512]{1,0:T(8,128)(2,1)S(1)}, u32[]{:S(2)}, u32[]{:S(2)}) collective-permute-start(bf16[64,512]{1,0:T(8,128)(2,1)S(1)} %get-tuple-element.45._), channel_id=1, source_target_pairs={{0,8},{1,5},{2,10},{3,7},{4,12},{5,1},{6,14},{7,3},{8,0},{9,13},{1... | collective-permute-start | bytes 196616 | tf_op jit(solution)/shard_map/ppermute | solution.py:223
  28.5 0.2 collective-permute-done.8.got
  28.7 2.9 %collective-permute-start.9 = (bf16[64,384]{1,0:T(8,128)(2,1)S(1)}, bf16[64,384]{1,0:T(8,128)(2,1)S(1)}, u32[]{:S(2)}, u32[]{:S(2)}) collective-permute-start(bf16[64,384]{1,0:T(8,128)(2,1)S(1)} %get-tuple-element.48), channel_id=1, source_target_pairs={{0,8},{1,5},{2,10},{3,7},{4,12},{5,1},{6,14},{7,3},{8,0},{9,13},{1... | collective-permute-start | bytes 147464 | tf_op jit(solution)/shard_map/ppermute | solution.py:223
  31.7 2.2 %collective-permute-done.7.refs_3_ = bf16[64,512]{1,0:T(8,128)(2,1)S(1)} collective-permute-done((bf16[64,512]{1,0:T(8,128)(2,1)S(1)}, bf16[64,512]{1,0:T(8,128)(2,1)S(1)}, u32[]{:S(2)}, u32[]{:S(2)}) %collective-permute-start.7) | collective-permute-done | bytes 65568 | tf_op jit(solution)/shard_map/ppermute | solution.py:223
  33.8 0.8 %shard_map.58._ = f32[64,1792]{1,0:T(8,128)} custom-call(f32[64,896]{1,0:T(8,128)S(1)} %get-tuple-element.41.refs_0_, f32[64,512]{1,0:T(8,128)S(1)} %get-tuple-element.44.refs_1_, bf16[64,896]{1,0:T(8,128)(2,1)S(1)} %collective-permute-done.6.refs_2_, bf16[64,512]{1,0:T(8,128)(2,1)S(1)} %collective-permute-done.7.refs_3_), custom_call_target="tpu_custom_call" | custom-call | flops 90112 | bytes 901120 | tf_op jit(solution)/shard_map/pallas_call | solution.py:190
  34.6 0.7 %shard_map.60 = f32[64,1792]{1,0:T(8,128)} custom-call(f32[64,1792]{1,0:T(8,128)} %shard_map.58._, f32[64,384]{1,0:T(8,128)S(1)} %get-tuple-element.47.kept, bf16[64,384]{1,0:T(8,128)(2,1)S(1)} %collective-permute-done.9.came), custom_call_target="tpu_custom_call", output_to_operand_aliasing={{}: (0, {})} | custom-call | flops 24576 | bytes 245760 | tf_op jit(solution)/shard_map/pallas_call | solution.py:190
  (11 shorter events, 0.2 us)
Async XLA Ops:
  0.0 2.6 %collective-permute-start = (bf16[32,2048]{1,0:T(8,128)(2,1)}, bf16[32,2048]{1,0:T(8,128)(2,1)S(1)}, u32[]{:S(2)}, u32[]{:S(2)}) collective-permute-start(bf16[32,2048]{1,0:T(8,128)(2,1)} %own_hbm.1), channel_id=1, source_target_pairs={{0,1},{1,0},{2,3},{3,2},{4,5},{5,4},{6,7},{7,6},{8,9},{9,8},{10,11... | collective-permute-start | bytes 393224 | tf_op jit(solution)/shard_map/ppermute | solution.py:228
  4.3 11.3 %collective-permute-start.1 = (bf16[256,896]{1,0:T(8,128)(2,1)S(1)}, bf16[256,896]{1,0:T(8,128)(2,1)S(1)}, u32[]{:S(2)}, u32[]{:S(2)}) collective-permute-start(bf16[256,896]{1,0:T(8,128)(2,1)S(1)} %get-tuple-element.34), channel_id=1, source_target_pairs={{0,4},{1,3},{2,6},{3,1},{4,0},{5,7},{6,2},{7,5},{8,12},{9,11},{10,... | collective-permute-start | bytes 1376264 | tf_op jit(solution)/shard_map/ppermute | solution.py:223
  8.5 11.7 %collective-permute-start.4 = (bf16[256,512]{1,0:T(8,128)(2,1)S(1)}, bf16[256,512]{1,0:T(8,128)(2,1)S(1)}, u32[]{:S(2)}, u32[]{:S(2)}) collective-permute-start(bf16[256,512]{1,0:T(8,128)(2,1)S(1)} %get-tuple-element.36._), channel_id=1, source_target_pairs={{0,2},{1,9},{2,0},{3,11},{4,6},{5,13},{6,4},{7,15},{8,10},{9,1},{1... | collective-permute-start | bytes 786440 | tf_op jit(solution)/shard_map/ppermute | solution.py:223
  15.6 9.1 %collective-permute-start.2 = (bf16[128,896]{1,0:T(8,128)(2,1)S(1)}, bf16[128,896]{1,0:T(8,128)(2,1)S(1)}, u32[]{:S(2)}, u32[]{:S(2)}) collective-permute-start(bf16[128,896]{1,0:T(8,128)(2,1)S(1)} %get-tuple-element.38._), channel_id=1, source_target_pairs={{0,2},{1,9},{2,0},{3,11},{4,6},{5,13},{6,4},{7,15},{8,10},{9,1},{1... | collective-permute-start | bytes 688136 | tf_op jit(solution)/shard_map/ppermute | solution.py:223
  18.2 5.7 %collective-permute-start.3 = (bf16[256,384]{1,0:T(8,128)(2,1)S(1)}, bf16[256,384]{1,0:T(8,128)(2,1)S(1)}, u32[]{:S(2)}, u32[]{:S(2)}) collective-permute-start(bf16[256,384]{1,0:T(8,128)(2,1)S(1)} %shard_map.50._), channel_id=1, source_target_pairs={{0,4},{1,3},{2,6},{3,1},{4,0},{5,7},{6,2},{7,5},{8,12},{9,11},{10,... | collective-permute-start | bytes 589832 | tf_op jit(solution)/shard_map/ppermute | solution.py:223
  20.2 7.7 %collective-permute-start.5 = (bf16[128,512]{1,0:T(8,128)(2,1)S(1)}, bf16[128,512]{1,0:T(8,128)(2,1)S(1)}, u32[]{:S(2)}, u32[]{:S(2)}) collective-permute-start(bf16[128,512]{1,0:T(8,128)(2,1)S(1)} %get-tuple-element.39._), channel_id=1, source_target_pairs={{0,4},{1,3},{2,6},{3,1},{4,0},{5,7},{6,2},{7,5},{8,12},{9,11},{10,... | collective-permute-start | bytes 393224 | tf_op jit(solution)/shard_map/ppermute | solution.py:223
  24.0 4.7 %collective-permute-start.8 = (bf16[128,384]{1,0:T(8,128)(2,1)S(1)}, bf16[128,384]{1,0:T(8,128)(2,1)S(1)}, u32[]{:S(2)}, u32[]{:S(2)}) collective-permute-start(bf16[128,384]{1,0:T(8,128)(2,1)S(1)} %get-tuple-element.40._), channel_id=1, source_target_pairs={{0,2},{1,9},{2,0},{3,11},{4,6},{5,13},{6,4},{7,15},{8,10},{9,1},{1... | collective-permute-start | bytes 294920 | tf_op jit(solution)/shard_map/ppermute | solution.py:223
  24.7 9.1 %collective-permute-start.6 = (bf16[64,896]{1,0:T(8,128)(2,1)S(1)}, bf16[64,896]{1,0:T(8,128)(2,1)S(1)}, u32[]{:S(2)}, u32[]{:S(2)}) collective-permute-start(bf16[64,896]{1,0:T(8,128)(2,1)S(1)} %get-tuple-element.43._), channel_id=1, source_target_pairs={{0,8},{1,5},{2,10},{3,7},{4,12},{5,1},{6,14},{7,3},{8,0},{9,13},{1... | collective-permute-start | bytes 344072 | tf_op jit(solution)/shard_map/ppermute | solution.py:223
  27.9 5.9 %collective-permute-start.7 = (bf16[64,512]{1,0:T(8,128)(2,1)S(1)}, bf16[64,512]{1,0:T(8,128)(2,1)S(1)}, u32[]{:S(2)}, u32[]{:S(2)}) collective-permute-start(bf16[64,512]{1,0:T(8,128)(2,1)S(1)} %get-tuple-element.45._), channel_id=1, source_target_pairs={{0,8},{1,5},{2,10},{3,7},{4,12},{5,1},{6,14},{7,3},{8,0},{9,13},{1... | collective-permute-start | bytes 196616 | tf_op jit(solution)/shard_map/ppermute | solution.py:223
  28.7 5.9 %collective-permute-start.9 = (bf16[64,384]{1,0:T(8,128)(2,1)S(1)}, bf16[64,384]{1,0:T(8,128)(2,1)S(1)}, u32[]{:S(2)}, u32[]{:S(2)}) collective-permute-start(bf16[64,384]{1,0:T(8,128)(2,1)S(1)} %get-tuple-element.48), channel_id=1, source_target_pairs={{0,8},{1,5},{2,10},{3,7},{4,12},{5,1},{6,14},{7,3},{8,0},{9,13},{1... | collective-permute-start | bytes 147464 | tf_op jit(solution)/shard_map/ppermute | solution.py:223

commit v20 on v16

--- a/solution.py
+++ b/solution.py
@@ -13,7 +13,7 @@
 PLAN = [
     (3, (NEAR, X, FAR), (X, FAR, NEAR)),
     (2, (X, NEAR, FAR), (FAR, X, NEAR)),
-    (2, (NEAR, X, FAR), (X, FAR, NEAR)),
+    (2, (X, FAR, NEAR), (NEAR, X, FAR)),
 ]
 ORDER = [(piece, stage) for stage in (1, 2) for piece in range(len(PLAN))]
 

time: 32.9 us -> 34.1 us (1.036)
  starting transfers between devices: 17.9 us -> 21.9 us
  waiting for transfers between devices: 4.25 us -> 1.49 us
    ppermute x9, starting transfers between devices: 17.5 us -> 21.4 us  [exchange(): return lax.ppermute(value, ('grid', 'eig'), pairs)]
    ppermute x9, waiting for transfers between devices: 4.25 us -> 1.49 us  [exchange(): return lax.ppermute(value, ('grid', 'eig'), pairs)]
  transfers between devices with their start and end apart: 10 -> 10, of which waited for: 4 -> 2; matrix products, arithmetic and copies ran while one was open for 0% -> 0% of each run, Pallas kernels for 25% -> 24%
where the time goes in v20:
time: 34.1 us; the launch traced here: 33.9 us
  starting transfers between devices  21.9 us (64%)
  Pallas kernels  10.4 us (30%)
  waiting for transfers between devices  1.49 us (4%)
    ppermute x9, starting transfers between devices, exchange(): return lax.ppermute(value, ('grid', 'eig'), pairs)  21.4 us
    pallas_call x14, Pallas kernels, kernel_call(): pl.pallas_call(body, out_shape=[jax.ShapeDtypeStruct(*out) for out in out...  10.4 us
    ppermute x9, waiting for transfers between devices, exchange(): return lax.ppermute(value, ('grid', 'eig'), pairs)  1.49 us
  transfers between devices with their start and end apart: 10, of which 2 were waited for; matrix products, arithmetic and copies ran while one was open for 0% of the time, Pallas kernels for 24%

profile of v20, /device:TPU:0, one launch (start us, length us, event | category | flops | bytes accessed | tf_op | source)
XLA Modules:
  0.0 33.9 jit_solution(15125805202937984277)
XLA Ops:
  0.0 0.5 %collective-permute-start = (bf16[32,2048]{1,0:T(8,128)(2,1)}, bf16[32,2048]{1,0:T(8,128)(2,1)S(1)}, u32[]{:S(2)}, u32[]{:S(2)}) collective-permute-start(bf16[32,2048]{1,0:T(8,128)(2,1)} %own_hbm.1), channel_id=1, source_target_pairs={{0,1},{1,0},{2,3},{3,2},{4,5},{5,4},{6,7},{7,6},{8,9},{9,8},{10,11... | collective-permute-start | bytes 393224 | tf_op jit(solution)/shard_map/ppermute | solution.py:229
  0.5 2.0 %shard_map.46 = (bf16[512,64]{1,0:T(8,128)(2,1)S(1)}, bf16[32,2048]{1,0:T(8,128)(2,1)S(1)}, bf16[8,2048]{1,0:T(8,128)(2,1)S(1)}, bf16[768,2048]{1,0:T(8,128)(2,1)S(1)}) custom-call(s32[64]{0:T(128)} %order_hbm.1, bf16[32,2048]{1,0:T(8,128)(2,1)} %own_hbm.1, bf16[8,2048]{1,0:T(8,128)(2,1)} %lanc_hbm.1, bf16[1792,2048]{1,0:T(8,128)(2,1)} %eig_hbm.5), custom_call_target="tpu_custom_call" | custom-call | bytes 3145728 | tf_op jit(solution)/shard_map/pallas_call | solution.py:191
  2.5 0.0 collective-permute-done.other
  2.5 1.6 %shard_map.47 = (bf16[256,768]{1,0:T(8,128)(2,1)S(1)}, bf16[256,2048]{1,0:T(8,128)(2,1)S(1)}, bf16[512,2048]{1,0:T(8,128)(2,1)S(1)}) custom-call(bf16[512,64]{1,0:T(8,128)(2,1)S(1)} %get-tuple-element.28.pick, bf16[32,2048]{1,0:T(8,128)(2,1)S(1)} %get-tuple-element.29.own, bf16[32,2048]{1,0:T(8,128)(2,1)S(1)} %collective-permute-done.other, ...), custom_call_target="tpu_custom_call" | custom-call | flops 805306368 | bytes 3145728 | tf_op jit(solution)/shard_map/pallas_call | solution.py:191
  4.1 2.6 %collective-permute-start.1 = (bf16[256,768]{1,0:T(8,128)(2,1)S(1)}, bf16[256,768]{1,0:T(8,128)(2,1)S(1)}, u32[]{:S(2)}, u32[]{:S(2)}) collective-permute-start(bf16[256,768]{1,0:T(8,128)(2,1)S(1)} %get-tuple-element.35), channel_id=1, source_target_pairs={{0,4},{1,3},{2,6},{3,1},{4,0},{5,7},{6,2},{7,5},{8,12},{9,11},{10,... | collective-permute-start | bytes 1179656 | tf_op jit(solution)/shard_map/ppermute | solution.py:224
  6.7 2.7 %shard_map.48 = (bf16[256,512]{1,0:T(8,128)(2,1)S(1)}, bf16[256,512]{1,0:T(8,128)(2,1)S(1)}, bf16[512,2048]{1,0:T(8,128)(2,1)S(1)}, bf16[512,2048]{1,0:T(8,128)(2,1)S(1)}) custom-call(bf16[512,64]{1,0:T(8,128)(2,1)S(1)} %get-tuple-element.28.pick, bf16[32,2048]{1,0:T(8,128)(2,1)S(1)} %get-tuple-element.29.own, ...), custom_call_target="tpu_custom_call" | custom-call | flops 1073741824 | bytes 4194304 | tf_op jit(solution)/shard_map/pallas_call | solution.py:191
  9.4 1.5 %collective-permute-start.4 = (bf16[256,512]{1,0:T(8,128)(2,1)S(1)}, bf16[256,512]{1,0:T(8,128)(2,1)S(1)}, u32[]{:S(2)}, u32[]{:S(2)}) collective-permute-start(bf16[256,512]{1,0:T(8,128)(2,1)S(1)} %get-tuple-element.40), channel_id=1, source_target_pairs={{0,2},{1,9},{2,0},{3,11},{4,6},{5,13},{6,4},{7,15},{8,10},{9,1},{1... | collective-permute-start | bytes 786440 | tf_op jit(solution)/shard_map/ppermute | solution.py:224
  11.0 0.5 %collective-permute-start.3 = (bf16[256,512]{1,0:T(8,128)(2,1)S(1)}, bf16[256,512]{1,0:T(8,128)(2,1)S(1)}, u32[]{:S(2)}, u32[]{:S(2)}) collective-permute-start(bf16[256,512]{1,0:T(8,128)(2,1)S(1)} %get-tuple-element.39), channel_id=1, source_target_pairs={{0,2},{1,5},{2,0},{3,7},{4,6},{5,1},{6,4},{7,3},{8,10},{9,13},{10,... | collective-permute-start | bytes 786440 | tf_op jit(solution)/shard_map/ppermute | solution.py:224
  11.5 1.0 %shard_map.49.kept = f32[256,768]{1,0:T(8,128)S(1)} custom-call(bf16[512,2048]{1,0:T(8,128)(2,1)S(1)} %get-tuple-element.34.prod._, bf16[768,2048]{1,0:T(8,128)(2,1)S(1)} %get-tuple-element.31.eig), custom_call_target="tpu_custom_call" | custom-call | flops 805306368 | bytes 3145728 | tf_op jit(solution)/shard_map/pallas_call | solution.py:191
  12.5 0.0 collective-permute-done.1.got
  12.5 0.1 shard_map.50
  12.6 5.0 %collective-permute-start.2 = (bf16[128,768]{1,0:T(8,128)(2,1)S(1)}, bf16[128,768]{1,0:T(8,128)(2,1)S(1)}, u32[]{:S(2)}, u32[]{:S(2)}) collective-permute-start(bf16[128,768]{1,0:T(8,128)(2,1)S(1)} %get-tuple-element.37._), channel_id=1, source_target_pairs={{0,2},{1,9},{2,0},{3,11},{4,6},{5,13},{6,4},{7,15},{8,10},{9,1},{1... | collective-permute-start | bytes 589832 | tf_op jit(solution)/shard_map/ppermute | solution.py:224
  17.6 0.7 %shard_map.52.kept = f32[256,512]{1,0:T(8,128)S(1)} custom-call(bf16[512,2048]{1,0:T(8,128)(2,1)S(1)} %get-tuple-element.34.prod._, bf16[512,2048]{1,0:T(8,128)(2,1)S(1)} %get-tuple-element.33.eig), custom_call_target="tpu_custom_call" | custom-call | flops 536870912 | bytes 2097152 | tf_op jit(solution)/shard_map/pallas_call | solution.py:191
  18.4 0.0 collective-permute-done.4.got
  18.4 0.1 collective-permute-start.5
  18.5 0.7 %shard_map.51.kept = f32[256,512]{1,0:T(8,128)S(1)} custom-call(bf16[512,2048]{1,0:T(8,128)(2,1)S(1)} %get-tuple-element.34.prod._, bf16[512,2048]{1,0:T(8,128)(2,1)S(1)} %get-tuple-element.38.eig), custom_call_target="tpu_custom_call" | custom-call | flops 536870912 | bytes 2097152 | tf_op jit(solution)/shard_map/pallas_call | solution.py:191
  19.3 3.4 %collective-permute-start.8 = (bf16[128,512]{1,0:T(8,128)(2,1)S(1)}, bf16[128,512]{1,0:T(8,128)(2,1)S(1)}, u32[]{:S(2)}, u32[]{:S(2)}) collective-permute-start(bf16[128,512]{1,0:T(8,128)(2,1)S(1)} %get-tuple-element.42._), channel_id=1, source_target_pairs={{0,8},{1,3},{2,10},{3,1},{4,12},{5,7},{6,14},{7,5},{8,0},{9,11},{1... | collective-permute-start | bytes 393224 | tf_op jit(solution)/shard_map/ppermute | solution.py:224
  22.8 2.7 %collective-permute-start.6 = (bf16[64,768]{1,0:T(8,128)(2,1)S(1)}, bf16[64,768]{1,0:T(8,128)(2,1)S(1)}, u32[]{:S(2)}, u32[]{:S(2)}) collective-permute-start(bf16[64,768]{1,0:T(8,128)(2,1)S(1)} %get-tuple-element.45._), channel_id=1, source_target_pairs={{0,8},{1,5},{2,10},{3,7},{4,12},{5,1},{6,14},{7,3},{8,0},{9,13},{1... | collective-permute-start | bytes 294920 | tf_op jit(solution)/shard_map/ppermute | solution.py:224
  25.5 2.4 %collective-permute-start.7 = (bf16[64,512]{1,0:T(8,128)(2,1)S(1)}, bf16[64,512]{1,0:T(8,128)(2,1)S(1)}, u32[]{:S(2)}, u32[]{:S(2)}) collective-permute-start(bf16[64,512]{1,0:T(8,128)(2,1)S(1)} %get-tuple-element.47._), channel_id=1, source_target_pairs={{0,8},{1,5},{2,10},{3,7},{4,12},{5,1},{6,14},{7,3},{8,0},{9,13},{1... | collective-permute-start | bytes 196616 | tf_op jit(solution)/shard_map/ppermute | solution.py:224
  27.9 3.0 %collective-permute-start.9 = (bf16[64,512]{1,0:T(8,128)(2,1)S(1)}, bf16[64,512]{1,0:T(8,128)(2,1)S(1)}, u32[]{:S(2)}, u32[]{:S(2)}) collective-permute-start(bf16[64,512]{1,0:T(8,128)(2,1)S(1)} %get-tuple-element.50), channel_id=1, source_target_pairs={{0,4},{1,9},{2,6},{3,11},{4,0},{5,13},{6,2},{7,15},{8,12},{9,1},{1... | collective-permute-start | bytes 196616 | tf_op jit(solution)/shard_map/ppermute | solution.py:224
  31.0 0.3 collective-permute-done.7.refs_3_
  31.3 0.8 %shard_map.57._ = f32[64,1792]{1,0:T(8,128)} custom-call(f32[64,768]{1,0:T(8,128)S(1)} %get-tuple-element.43.refs_0_, f32[64,512]{1,0:T(8,128)S(1)} %get-tuple-element.46.refs_1_, bf16[64,768]{1,0:T(8,128)(2,1)S(1)} %collective-permute-done.6.refs_2_, bf16[64,512]{1,0:T(8,128)(2,1)S(1)} %collective-permute-done.7.refs_3_), custom_call_target="tpu_custom_call" | custom-call | flops 81920 | bytes 819200 | tf_op jit(solution)/shard_map/pallas_call | solution.py:191
  32.1 1.2 %collective-permute-done.9.came = bf16[64,512]{1,0:T(8,128)(2,1)S(1)} collective-permute-done((bf16[64,512]{1,0:T(8,128)(2,1)S(1)}, bf16[64,512]{1,0:T(8,128)(2,1)S(1)}, u32[]{:S(2)}, u32[]{:S(2)}) %collective-permute-start.9) | collective-permute-done | bytes 65568 | tf_op jit(solution)/shard_map/ppermute | solution.py:224
  33.2 0.7 %shard_map.59 = f32[64,1792]{1,0:T(8,128)} custom-call(f32[64,1792]{1,0:T(8,128)} %shard_map.57._, f32[64,512]{1,0:T(8,128)S(1)} %get-tuple-element.49.kept, bf16[64,512]{1,0:T(8,128)(2,1)S(1)} %collective-permute-done.9.came), custom_call_target="tpu_custom_call", output_to_operand_aliasing={{}: (0, {})} | custom-call | flops 32768 | bytes 327680 | tf_op jit(solution)/shard_map/pallas_call | solution.py:191
  (10 shorter events, 0.2 us)
Async XLA Ops:
  0.0 2.5 %collective-permute-start = (bf16[32,2048]{1,0:T(8,128)(2,1)}, bf16[32,2048]{1,0:T(8,128)(2,1)S(1)}, u32[]{:S(2)}, u32[]{:S(2)}) collective-permute-start(bf16[32,2048]{1,0:T(8,128)(2,1)} %own_hbm.1), channel_id=1, source_target_pairs={{0,1},{1,0},{2,3},{3,2},{4,5},{5,4},{6,7},{7,6},{8,9},{9,8},{10,11... | collective-permute-start | bytes 393224 | tf_op jit(solution)/shard_map/ppermute | solution.py:229
  4.1 8.4 %collective-permute-start.1 = (bf16[256,768]{1,0:T(8,128)(2,1)S(1)}, bf16[256,768]{1,0:T(8,128)(2,1)S(1)}, u32[]{:S(2)}, u32[]{:S(2)}) collective-permute-start(bf16[256,768]{1,0:T(8,128)(2,1)S(1)} %get-tuple-element.35), channel_id=1, source_target_pairs={{0,4},{1,3},{2,6},{3,1},{4,0},{5,7},{6,2},{7,5},{8,12},{9,11},{10,... | collective-permute-start | bytes 1179656 | tf_op jit(solution)/shard_map/ppermute | solution.py:224
  9.4 9.0 %collective-permute-start.4 = (bf16[256,512]{1,0:T(8,128)(2,1)S(1)}, bf16[256,512]{1,0:T(8,128)(2,1)S(1)}, u32[]{:S(2)}, u32[]{:S(2)}) collective-permute-start(bf16[256,512]{1,0:T(8,128)(2,1)S(1)} %get-tuple-element.40), channel_id=1, source_target_pairs={{0,2},{1,9},{2,0},{3,11},{4,6},{5,13},{6,4},{7,15},{8,10},{9,1},{1... | collective-permute-start | bytes 786440 | tf_op jit(solution)/shard_map/ppermute | solution.py:224
  11.0 8.3 %collective-permute-start.3 = (bf16[256,512]{1,0:T(8,128)(2,1)S(1)}, bf16[256,512]{1,0:T(8,128)(2,1)S(1)}, u32[]{:S(2)}, u32[]{:S(2)}) collective-permute-start(bf16[256,512]{1,0:T(8,128)(2,1)S(1)} %get-tuple-element.39), channel_id=1, source_target_pairs={{0,2},{1,5},{2,0},{3,7},{4,6},{5,1},{6,4},{7,3},{8,10},{9,13},{10,... | collective-permute-start | bytes 786440 | tf_op jit(solution)/shard_map/ppermute | solution.py:224
  12.6 10.1 %collective-permute-start.2 = (bf16[128,768]{1,0:T(8,128)(2,1)S(1)}, bf16[128,768]{1,0:T(8,128)(2,1)S(1)}, u32[]{:S(2)}, u32[]{:S(2)}) collective-permute-start(bf16[128,768]{1,0:T(8,128)(2,1)S(1)} %get-tuple-element.37._), channel_id=1, source_target_pairs={{0,2},{1,9},{2,0},{3,11},{4,6},{5,13},{6,4},{7,15},{8,10},{9,1},{1... | collective-permute-start | bytes 589832 | tf_op jit(solution)/shard_map/ppermute | solution.py:224
  18.4 7.1 %collective-permute-start.5 = (bf16[128,512]{1,0:T(8,128)(2,1)S(1)}, bf16[128,512]{1,0:T(8,128)(2,1)S(1)}, u32[]{:S(2)}, u32[]{:S(2)}) collective-permute-start(bf16[128,512]{1,0:T(8,128)(2,1)S(1)} %get-tuple-element.41._), channel_id=1, source_target_pairs={{0,4},{1,3},{2,6},{3,1},{4,0},{5,7},{6,2},{7,5},{8,12},{9,11},{10,... | collective-permute-start | bytes 393224 | tf_op jit(solution)/shard_map/ppermute | solution.py:224
  19.3 8.6 %collective-permute-start.8 = (bf16[128,512]{1,0:T(8,128)(2,1)S(1)}, bf16[128,512]{1,0:T(8,128)(2,1)S(1)}, u32[]{:S(2)}, u32[]{:S(2)}) collective-permute-start(bf16[128,512]{1,0:T(8,128)(2,1)S(1)} %get-tuple-element.42._), channel_id=1, source_target_pairs={{0,8},{1,3},{2,10},{3,1},{4,12},{5,7},{6,14},{7,5},{8,0},{9,11},{1... | collective-permute-start | bytes 393224 | tf_op jit(solution)/shard_map/ppermute | solution.py:224
  22.8 8.5 %collective-permute-start.6 = (bf16[64,768]{1,0:T(8,128)(2,1)S(1)}, bf16[64,768]{1,0:T(8,128)(2,1)S(1)}, u32[]{:S(2)}, u32[]{:S(2)}) collective-permute-start(bf16[64,768]{1,0:T(8,128)(2,1)S(1)} %get-tuple-element.45._), channel_id=1, source_target_pairs={{0,8},{1,5},{2,10},{3,7},{4,12},{5,1},{6,14},{7,3},{8,0},{9,13},{1... | collective-permute-start | bytes 294920 | tf_op jit(solution)/shard_map/ppermute | solution.py:224
  25.5 5.7 %collective-permute-start.7 = (bf16[64,512]{1,0:T(8,128)(2,1)S(1)}, bf16[64,512]{1,0:T(8,128)(2,1)S(1)}, u32[]{:S(2)}, u32[]{:S(2)}) collective-permute-start(bf16[64,512]{1,0:T(8,128)(2,1)S(1)} %get-tuple-element.47._), channel_id=1, source_target_pairs={{0,8},{1,5},{2,10},{3,7},{4,12},{5,1},{6,14},{7,3},{8,0},{9,13},{1... | collective-permute-start | bytes 196616 | tf_op jit(solution)/shard_map/ppermute | solution.py:224
  27.9 5.3 %collective-permute-start.9 = (bf16[64,512]{1,0:T(8,128)(2,1)S(1)}, bf16[64,512]{1,0:T(8,128)(2,1)S(1)}, u32[]{:S(2)}, u32[]{:S(2)}) collective-permute-start(bf16[64,512]{1,0:T(8,128)(2,1)S(1)} %get-tuple-element.50), channel_id=1, source_target_pairs={{0,4},{1,9},{2,6},{3,11},{4,0},{5,13},{6,2},{7,15},{8,12},{9,1},{1... | collective-permute-start | bytes 196616 | tf_op jit(solution)/shard_map/ppermute | solution.py:224

commit v21 on v20

--- a/solution.py
+++ b/solution.py
@@ -12,8 +12,8 @@
 X, NEAR, FAR = 0, 1, 2
 PLAN = [
     (3, (NEAR, X, FAR), (X, FAR, NEAR)),
-    (2, (X, NEAR, FAR), (FAR, X, NEAR)),
-    (2, (X, FAR, NEAR), (NEAR, X, FAR)),
+    (2, (X, NEAR, FAR), (X, FAR, NEAR)),
+    (2, (NEAR, X, FAR), (FAR, X, NEAR)),
 ]
 ORDER = [(piece, stage) for stage in (1, 2) for piece in range(len(PLAN))]
 

time: 34.1 us -> 33.6 us (0.985)
  starting transfers between devices: 21.9 us -> 15.4 us
  waiting for transfers between devices: 1.49 us -> 7.74 us
    ppermute x9, starting transfers between devices: 21.4 us -> 15 us  [exchange(): return lax.ppermute(value, ('grid', 'eig'), pairs)]
    ppermute x9, waiting for transfers between devices: 1.49 us -> 7.74 us  [exchange(): return lax.ppermute(value, ('grid', 'eig'), pairs)]
  transfers between devices with their start and end apart: 10 -> 10, of which waited for: 2 -> 5; matrix products, arithmetic and copies ran while one was open for 0% -> 0% of each run, Pallas kernels for 24% -> 23%
where the time goes in v21:
time: 33.6 us; the launch traced here: 33.4 us
  starting transfers between devices  15.4 us (46%)
  Pallas kernels  10.1 us (30%)
  waiting for transfers between devices  7.74 us (23%)
    ppermute x9, starting transfers between devices, exchange(): return lax.ppermute(value, ('grid', 'eig'), pairs)  15 us
    pallas_call x14, Pallas kernels, kernel_call(): pl.pallas_call(body, out_shape=[jax.ShapeDtypeStruct(*out) for out in out...  10.1 us
    ppermute x9, waiting for transfers between devices, exchange(): return lax.ppermute(value, ('grid', 'eig'), pairs)  7.74 us
  transfers between devices with their start and end apart: 10, of which 5 were waited for; matrix products, arithmetic and copies ran while one was open for 0% of the time, Pallas kernels for 23%

profile of v21, /device:TPU:0, one launch (start us, length us, event | category | flops | bytes accessed | tf_op | source)
XLA Modules:
  0.0 33.4 jit_solution(6107679447822975287)
XLA Ops:
  0.0 0.5 %collective-permute-start = (bf16[32,2048]{1,0:T(8,128)(2,1)}, bf16[32,2048]{1,0:T(8,128)(2,1)S(1)}, u32[]{:S(2)}, u32[]{:S(2)}) collective-permute-start(bf16[32,2048]{1,0:T(8,128)(2,1)} %own_hbm.1), channel_id=1, source_target_pairs={{0,1},{1,0},{2,3},{3,2},{4,5},{5,4},{6,7},{7,6},{8,9},{9,8},{10,11... | collective-permute-start | bytes 393224 | tf_op jit(solution)/shard_map/ppermute | solution.py:229
  0.5 2.0 %shard_map.46 = (bf16[512,64]{1,0:T(8,128)(2,1)S(1)}, bf16[32,2048]{1,0:T(8,128)(2,1)S(1)}, bf16[8,2048]{1,0:T(8,128)(2,1)S(1)}, bf16[768,2048]{1,0:T(8,128)(2,1)S(1)}) custom-call(s32[64]{0:T(128)} %order_hbm.1, bf16[32,2048]{1,0:T(8,128)(2,1)} %own_hbm.1, bf16[8,2048]{1,0:T(8,128)(2,1)} %lanc_hbm.1, bf16[1792,2048]{1,0:T(8,128)(2,1)} %eig_hbm.5), custom_call_target="tpu_custom_call" | custom-call | bytes 3145728 | tf_op jit(solution)/shard_map/pallas_call | solution.py:191
  2.5 1.6 %shard_map.47 = (bf16[256,768]{1,0:T(8,128)(2,1)S(1)}, bf16[256,2048]{1,0:T(8,128)(2,1)S(1)}, bf16[512,2048]{1,0:T(8,128)(2,1)S(1)}) custom-call(bf16[512,64]{1,0:T(8,128)(2,1)S(1)} %get-tuple-element.28.pick, bf16[32,2048]{1,0:T(8,128)(2,1)S(1)} %get-tuple-element.29.own, bf16[32,2048]{1,0:T(8,128)(2,1)S(1)} %collective-permute-done.other, ...), custom_call_target="tpu_custom_call" | custom-call | flops 805306368 | bytes 3145728 | tf_op jit(solution)/shard_map/pallas_call | solution.py:191
  4.1 2.6 %collective-permute-start.1 = (bf16[256,768]{1,0:T(8,128)(2,1)S(1)}, bf16[256,768]{1,0:T(8,128)(2,1)S(1)}, u32[]{:S(2)}, u32[]{:S(2)}) collective-permute-start(bf16[256,768]{1,0:T(8,128)(2,1)S(1)} %get-tuple-element.35), channel_id=1, source_target_pairs={{0,4},{1,3},{2,6},{3,1},{4,0},{5,7},{6,2},{7,5},{8,12},{9,11},{10,... | collective-permute-start | bytes 1179656 | tf_op jit(solution)/shard_map/ppermute | solution.py:224
  6.7 2.4 %shard_map.48 = (bf16[256,512]{1,0:T(8,128)(2,1)S(1)}, bf16[256,512]{1,0:T(8,128)(2,1)S(1)}, bf16[512,2048]{1,0:T(8,128)(2,1)S(1)}, bf16[512,2048]{1,0:T(8,128)(2,1)S(1)}) custom-call(bf16[512,64]{1,0:T(8,128)(2,1)S(1)} %get-tuple-element.28.pick, bf16[32,2048]{1,0:T(8,128)(2,1)S(1)} %get-tuple-element.29.own, ...), custom_call_target="tpu_custom_call" | custom-call | flops 1073741824 | bytes 4194304 | tf_op jit(solution)/shard_map/pallas_call | solution.py:191
  9.1 1.6 %collective-permute-start.4 = (bf16[256,512]{1,0:T(8,128)(2,1)S(1)}, bf16[256,512]{1,0:T(8,128)(2,1)S(1)}, u32[]{:S(2)}, u32[]{:S(2)}) collective-permute-start(bf16[256,512]{1,0:T(8,128)(2,1)S(1)} %get-tuple-element.40), channel_id=1, source_target_pairs={{0,2},{1,3},{2,0},{3,1},{4,6},{5,7},{6,4},{7,5},{8,10},{9,11},{10,... | collective-permute-start | bytes 786440 | tf_op jit(solution)/shard_map/ppermute | solution.py:224
  10.7 0.4 %collective-permute-start.3 = (bf16[256,512]{1,0:T(8,128)(2,1)S(1)}, bf16[256,512]{1,0:T(8,128)(2,1)S(1)}, u32[]{:S(2)}, u32[]{:S(2)}) collective-permute-start(bf16[256,512]{1,0:T(8,128)(2,1)S(1)} %get-tuple-element.39), channel_id=1, source_target_pairs={{0,4},{1,9},{2,6},{3,11},{4,0},{5,13},{6,2},{7,15},{8,12},{9,1},{1... | collective-permute-start | bytes 786440 | tf_op jit(solution)/shard_map/ppermute | solution.py:224
  11.1 1.0 %shard_map.49.kept = f32[256,768]{1,0:T(8,128)S(1)} custom-call(bf16[512,2048]{1,0:T(8,128)(2,1)S(1)} %get-tuple-element.34.prod._, bf16[768,2048]{1,0:T(8,128)(2,1)S(1)} %get-tuple-element.31.eig), custom_call_target="tpu_custom_call" | custom-call | flops 805306368 | bytes 3145728 | tf_op jit(solution)/shard_map/pallas_call | solution.py:191
  12.1 0.4 %collective-permute-done.1.got = bf16[256,768]{1,0:T(8,128)(2,1)S(1)} collective-permute-done((bf16[256,768]{1,0:T(8,128)(2,1)S(1)}, bf16[256,768]{1,0:T(8,128)(2,1)S(1)}, u32[]{:S(2)}, u32[]{:S(2)}) %collective-permute-start.1) | collective-permute-done | bytes 393248 | tf_op jit(solution)/shard_map/ppermute | solution.py:224
  12.5 0.1 shard_map.50
  12.6 2.0 %collective-permute-start.2 = (bf16[128,768]{1,0:T(8,128)(2,1)S(1)}, bf16[128,768]{1,0:T(8,128)(2,1)S(1)}, u32[]{:S(2)}, u32[]{:S(2)}) collective-permute-start(bf16[128,768]{1,0:T(8,128)(2,1)S(1)} %get-tuple-element.37._), channel_id=1, source_target_pairs={{0,2},{1,9},{2,0},{3,11},{4,6},{5,13},{6,4},{7,15},{8,10},{9,1},{1... | collective-permute-start | bytes 589832 | tf_op jit(solution)/shard_map/ppermute | solution.py:224
  14.6 0.7 %shard_map.52.kept = f32[256,512]{1,0:T(8,128)S(1)} custom-call(bf16[512,2048]{1,0:T(8,128)(2,1)S(1)} %get-tuple-element.34.prod._, bf16[512,2048]{1,0:T(8,128)(2,1)S(1)} %get-tuple-element.33.eig), custom_call_target="tpu_custom_call" | custom-call | flops 536870912 | bytes 2097152 | tf_op jit(solution)/shard_map/pallas_call | solution.py:191
  15.3 2.5 %collective-permute-done.4.got = bf16[256,512]{1,0:T(8,128)(2,1)S(1)} collective-permute-done((bf16[256,512]{1,0:T(8,128)(2,1)S(1)}, bf16[256,512]{1,0:T(8,128)(2,1)S(1)}, u32[]{:S(2)}, u32[]{:S(2)}) %collective-permute-start.4) | collective-permute-done | bytes 262176 | tf_op jit(solution)/shard_map/ppermute | solution.py:224
  17.9 0.6 %collective-permute-start.5 = (bf16[128,512]{1,0:T(8,128)(2,1)S(1)}, bf16[128,512]{1,0:T(8,128)(2,1)S(1)}, u32[]{:S(2)}, u32[]{:S(2)}) collective-permute-start(bf16[128,512]{1,0:T(8,128)(2,1)S(1)} %get-tuple-element.41._), channel_id=1, source_target_pairs={{0,4},{1,9},{2,6},{3,11},{4,0},{5,13},{6,2},{7,15},{8,12},{9,1},{1... | collective-permute-start | bytes 393224 | tf_op jit(solution)/shard_map/ppermute | solution.py:224
  18.5 0.7 %shard_map.51.kept = f32[256,512]{1,0:T(8,128)S(1)} custom-call(bf16[512,2048]{1,0:T(8,128)(2,1)S(1)} %get-tuple-element.34.prod._, bf16[512,2048]{1,0:T(8,128)(2,1)S(1)} %get-tuple-element.38.eig), custom_call_target="tpu_custom_call" | custom-call | flops 536870912 | bytes 2097152 | tf_op jit(solution)/shard_map/pallas_call | solution.py:191
  19.4 2.0 %collective-permute-start.8 = (bf16[128,512]{1,0:T(8,128)(2,1)S(1)}, bf16[128,512]{1,0:T(8,128)(2,1)S(1)}, u32[]{:S(2)}, u32[]{:S(2)}) collective-permute-start(bf16[128,512]{1,0:T(8,128)(2,1)S(1)} %get-tuple-element.42._), channel_id=1, source_target_pairs={{0,2},{1,3},{2,0},{3,1},{4,6},{5,7},{6,4},{7,5},{8,10},{9,11},{10,... | collective-permute-start | bytes 393224 | tf_op jit(solution)/shard_map/ppermute | solution.py:224
  21.4 2.6 %collective-permute-start.6 = (bf16[64,768]{1,0:T(8,128)(2,1)S(1)}, bf16[64,768]{1,0:T(8,128)(2,1)S(1)}, u32[]{:S(2)}, u32[]{:S(2)}) collective-permute-start(bf16[64,768]{1,0:T(8,128)(2,1)S(1)} %get-tuple-element.45._), channel_id=1, source_target_pairs={{0,8},{1,5},{2,10},{3,7},{4,12},{5,1},{6,14},{7,3},{8,0},{9,13},{1... | collective-permute-start | bytes 294920 | tf_op jit(solution)/shard_map/ppermute | solution.py:224
  24.0 0.6 %collective-permute-done.5.got = bf16[128,512]{1,0:T(8,128)(2,1)S(1)} collective-permute-done((bf16[128,512]{1,0:T(8,128)(2,1)S(1)}, bf16[128,512]{1,0:T(8,128)(2,1)S(1)}, u32[]{:S(2)}, u32[]{:S(2)}) %collective-permute-start.5) | collective-permute-done | bytes 131104 | tf_op jit(solution)/shard_map/ppermute | solution.py:224
  24.7 2.3 %collective-permute-start.7 = (bf16[64,512]{1,0:T(8,128)(2,1)S(1)}, bf16[64,512]{1,0:T(8,128)(2,1)S(1)}, u32[]{:S(2)}, u32[]{:S(2)}) collective-permute-start(bf16[64,512]{1,0:T(8,128)(2,1)S(1)} %get-tuple-element.47._), channel_id=1, source_target_pairs={{0,8},{1,5},{2,10},{3,7},{4,12},{5,1},{6,14},{7,3},{8,0},{9,13},{1... | collective-permute-start | bytes 196616 | tf_op jit(solution)/shard_map/ppermute | solution.py:224
  27.0 0.8 %collective-permute-start.9 = (bf16[64,512]{1,0:T(8,128)(2,1)S(1)}, bf16[64,512]{1,0:T(8,128)(2,1)S(1)}, u32[]{:S(2)}, u32[]{:S(2)}) collective-permute-start(bf16[64,512]{1,0:T(8,128)(2,1)S(1)} %get-tuple-element.50), channel_id=1, source_target_pairs={{0,8},{1,5},{2,10},{3,7},{4,12},{5,1},{6,14},{7,3},{8,0},{9,13},{1... | collective-permute-start | bytes 196616 | tf_op jit(solution)/shard_map/ppermute | solution.py:224
  27.8 2.8 %collective-permute-done.7.refs_3_ = bf16[64,512]{1,0:T(8,128)(2,1)S(1)} collective-permute-done((bf16[64,512]{1,0:T(8,128)(2,1)S(1)}, bf16[64,512]{1,0:T(8,128)(2,1)S(1)}, u32[]{:S(2)}, u32[]{:S(2)}) %collective-permute-start.7) | collective-permute-done | bytes 65568 | tf_op jit(solution)/shard_map/ppermute | solution.py:224
  30.6 0.8 %shard_map.57._ = f32[64,1792]{1,0:T(8,128)} custom-call(f32[64,768]{1,0:T(8,128)S(1)} %get-tuple-element.43.refs_0_, f32[64,512]{1,0:T(8,128)S(1)} %get-tuple-element.46.refs_1_, bf16[64,768]{1,0:T(8,128)(2,1)S(1)} %collective-permute-done.6.refs_2_, bf16[64,512]{1,0:T(8,128)(2,1)S(1)} %collective-permute-done.7.refs_3_), custom_call_target="tpu_custom_call" | custom-call | flops 81920 | bytes 819200 | tf_op jit(solution)/shard_map/pallas_call | solution.py:191
  31.4 1.3 %collective-permute-done.9.came = bf16[64,512]{1,0:T(8,128)(2,1)S(1)} collective-permute-done((bf16[64,512]{1,0:T(8,128)(2,1)S(1)}, bf16[64,512]{1,0:T(8,128)(2,1)S(1)}, u32[]{:S(2)}, u32[]{:S(2)}) %collective-permute-start.9) | collective-permute-done | bytes 65568 | tf_op jit(solution)/shard_map/ppermute | solution.py:224
  32.7 0.7 %shard_map.59 = f32[64,1792]{1,0:T(8,128)} custom-call(f32[64,1792]{1,0:T(8,128)} %shard_map.57._, f32[64,512]{1,0:T(8,128)S(1)} %get-tuple-element.49.kept, bf16[64,512]{1,0:T(8,128)(2,1)S(1)} %collective-permute-done.9.came), custom_call_target="tpu_custom_call", output_to_operand_aliasing={{}: (0, {})} | custom-call | flops 32768 | bytes 327680 | tf_op jit(solution)/shard_map/pallas_call | solution.py:191
  (10 shorter events, 0.2 us)
Async XLA Ops:
  0.0 2.5 %collective-permute-start = (bf16[32,2048]{1,0:T(8,128)(2,1)}, bf16[32,2048]{1,0:T(8,128)(2,1)S(1)}, u32[]{:S(2)}, u32[]{:S(2)}) collective-permute-start(bf16[32,2048]{1,0:T(8,128)(2,1)} %own_hbm.1), channel_id=1, source_target_pairs={{0,1},{1,0},{2,3},{3,2},{4,5},{5,4},{6,7},{7,6},{8,9},{9,8},{10,11... | collective-permute-start | bytes 393224 | tf_op jit(solution)/shard_map/ppermute | solution.py:229
  4.1 8.4 %collective-permute-start.1 = (bf16[256,768]{1,0:T(8,128)(2,1)S(1)}, bf16[256,768]{1,0:T(8,128)(2,1)S(1)}, u32[]{:S(2)}, u32[]{:S(2)}) collective-permute-start(bf16[256,768]{1,0:T(8,128)(2,1)S(1)} %get-tuple-element.35), channel_id=1, source_target_pairs={{0,4},{1,3},{2,6},{3,1},{4,0},{5,7},{6,2},{7,5},{8,12},{9,11},{10,... | collective-permute-start | bytes 1179656 | tf_op jit(solution)/shard_map/ppermute | solution.py:224
  9.1 8.7 %collective-permute-start.4 = (bf16[256,512]{1,0:T(8,128)(2,1)S(1)}, bf16[256,512]{1,0:T(8,128)(2,1)S(1)}, u32[]{:S(2)}, u32[]{:S(2)}) collective-permute-start(bf16[256,512]{1,0:T(8,128)(2,1)S(1)} %get-tuple-element.40), channel_id=1, source_target_pairs={{0,2},{1,3},{2,0},{3,1},{4,6},{5,7},{6,4},{7,5},{8,10},{9,11},{10,... | collective-permute-start | bytes 786440 | tf_op jit(solution)/shard_map/ppermute | solution.py:224
  10.7 8.7 %collective-permute-start.3 = (bf16[256,512]{1,0:T(8,128)(2,1)S(1)}, bf16[256,512]{1,0:T(8,128)(2,1)S(1)}, u32[]{:S(2)}, u32[]{:S(2)}) collective-permute-start(bf16[256,512]{1,0:T(8,128)(2,1)S(1)} %get-tuple-element.39), channel_id=1, source_target_pairs={{0,4},{1,9},{2,6},{3,11},{4,0},{5,13},{6,2},{7,15},{8,12},{9,1},{1... | collective-permute-start | bytes 786440 | tf_op jit(solution)/shard_map/ppermute | solution.py:224
  12.6 8.8 %collective-permute-start.2 = (bf16[128,768]{1,0:T(8,128)(2,1)S(1)}, bf16[128,768]{1,0:T(8,128)(2,1)S(1)}, u32[]{:S(2)}, u32[]{:S(2)}) collective-permute-start(bf16[128,768]{1,0:T(8,128)(2,1)S(1)} %get-tuple-element.37._), channel_id=1, source_target_pairs={{0,2},{1,9},{2,0},{3,11},{4,6},{5,13},{6,4},{7,15},{8,10},{9,1},{1... | collective-permute-start | bytes 589832 | tf_op jit(solution)/shard_map/ppermute | solution.py:224
  17.9 6.8 %collective-permute-start.5 = (bf16[128,512]{1,0:T(8,128)(2,1)S(1)}, bf16[128,512]{1,0:T(8,128)(2,1)S(1)}, u32[]{:S(2)}, u32[]{:S(2)}) collective-permute-start(bf16[128,512]{1,0:T(8,128)(2,1)S(1)} %get-tuple-element.41._), channel_id=1, source_target_pairs={{0,4},{1,9},{2,6},{3,11},{4,0},{5,13},{6,2},{7,15},{8,12},{9,1},{1... | collective-permute-start | bytes 393224 | tf_op jit(solution)/shard_map/ppermute | solution.py:224
  19.4 7.6 %collective-permute-start.8 = (bf16[128,512]{1,0:T(8,128)(2,1)S(1)}, bf16[128,512]{1,0:T(8,128)(2,1)S(1)}, u32[]{:S(2)}, u32[]{:S(2)}) collective-permute-start(bf16[128,512]{1,0:T(8,128)(2,1)S(1)} %get-tuple-element.42._), channel_id=1, source_target_pairs={{0,2},{1,3},{2,0},{3,1},{4,6},{5,7},{6,4},{7,5},{8,10},{9,11},{10,... | collective-permute-start | bytes 393224 | tf_op jit(solution)/shard_map/ppermute | solution.py:224
  21.4 9.2 %collective-permute-start.6 = (bf16[64,768]{1,0:T(8,128)(2,1)S(1)}, bf16[64,768]{1,0:T(8,128)(2,1)S(1)}, u32[]{:S(2)}, u32[]{:S(2)}) collective-permute-start(bf16[64,768]{1,0:T(8,128)(2,1)S(1)} %get-tuple-element.45._), channel_id=1, source_target_pairs={{0,8},{1,5},{2,10},{3,7},{4,12},{5,1},{6,14},{7,3},{8,0},{9,13},{1... | collective-permute-start | bytes 294920 | tf_op jit(solution)/shard_map/ppermute | solution.py:224
  24.7 5.9 %collective-permute-start.7 = (bf16[64,512]{1,0:T(8,128)(2,1)S(1)}, bf16[64,512]{1,0:T(8,128)(2,1)S(1)}, u32[]{:S(2)}, u32[]{:S(2)}) collective-permute-start(bf16[64,512]{1,0:T(8,128)(2,1)S(1)} %get-tuple-element.47._), channel_id=1, source_target_pairs={{0,8},{1,5},{2,10},{3,7},{4,12},{5,1},{6,14},{7,3},{8,0},{9,13},{1... | collective-permute-start | bytes 196616 | tf_op jit(solution)/shard_map/ppermute | solution.py:224
  27.0 5.7 %collective-permute-start.9 = (bf16[64,512]{1,0:T(8,128)(2,1)S(1)}, bf16[64,512]{1,0:T(8,128)(2,1)S(1)}, u32[]{:S(2)}, u32[]{:S(2)}) collective-permute-start(bf16[64,512]{1,0:T(8,128)(2,1)S(1)} %get-tuple-element.50), channel_id=1, source_target_pairs={{0,8},{1,5},{2,10},{3,7},{4,12},{5,1},{6,14},{7,3},{8,0},{9,13},{1... | collective-permute-start | bytes 196616 | tf_op jit(solution)/shard_map/ppermute | solution.py:224

commit v22 on v14

--- a/solution.py
+++ b/solution.py
@@ -12,8 +12,8 @@
 X, NEAR, FAR = 0, 1, 2
 PLAN = [
     (3.5, (NEAR, X, FAR), (X, FAR, NEAR)),
-    (2, (X, NEAR, FAR), (FAR, X, NEAR)),
-    (1.5, (NEAR, X, FAR), (X, FAR, NEAR)),
+    (2, (X, NEAR, FAR), (X, FAR, NEAR)),
+    (1.5, (NEAR, X, FAR), (FAR, X, NEAR)),
 ]
 ORDER = [(piece, stage) for stage in (1, 2) for piece in range(len(PLAN))]
 

time: 33.2 us -> 33.8 us (1.018)
  waiting for transfers between devices: 6.56 us -> 8.21 us
  starting transfers between devices: 16.3 us -> 15.6 us
    ppermute x9, waiting for transfers between devices: 6.56 us -> 8.21 us  [exchange(): return lax.ppermute(value, ('grid', 'eig'), pairs)]
    ppermute x9, starting transfers between devices: 15.9 us -> 15.2 us  [exchange(): return lax.ppermute(value, ('grid', 'eig'), pairs)]
  transfers between devices with their start and end apart: 10 -> 10, of which waited for: 3 -> 4; matrix products, arithmetic and copies ran while one was open for 0% -> 0% of each run, Pallas kernels for 23% -> 22%
where the time goes in v22:
time: 33.8 us; the launch traced here: 33.6 us
  starting transfers between devices  15.6 us (46%)
  Pallas kernels  9.71 us (29%)
  waiting for transfers between devices  8.21 us (24%)
    ppermute x9, starting transfers between devices, exchange(): return lax.ppermute(value, ('grid', 'eig'), pairs)  15.2 us
    pallas_call x13, Pallas kernels, kernel_call(): pl.pallas_call(body, out_shape=[jax.ShapeDtypeStruct(*out) for out in out...  9.71 us
    ppermute x9, waiting for transfers between devices, exchange(): return lax.ppermute(value, ('grid', 'eig'), pairs)  8.21 us
  transfers between devices with their start and end apart: 10, of which 4 were waited for; matrix products, arithmetic and copies ran while one was open for 0% of the time, Pallas kernels for 22%

profile of v22, /device:TPU:0, one launch (start us, length us, event | category | flops | bytes accessed | tf_op | source)
XLA Modules:
  0.0 33.6 jit_solution(4038948702813661154)
XLA Ops:
  0.0 0.5 %collective-permute-start = (bf16[32,2048]{1,0:T(8,128)(2,1)}, bf16[32,2048]{1,0:T(8,128)(2,1)S(1)}, u32[]{:S(2)}, u32[]{:S(2)}) collective-permute-start(bf16[32,2048]{1,0:T(8,128)(2,1)} %own_hbm.1), channel_id=1, source_target_pairs={{0,1},{1,0},{2,3},{3,2},{4,5},{5,4},{6,7},{7,6},{8,9},{9,8},{10,11... | collective-permute-start | bytes 393224 | tf_op jit(solution)/shard_map/ppermute | solution.py:216
  0.5 2.2 %shard_map.46 = (bf16[512,64]{1,0:T(8,128)(2,1)S(1)}, bf16[32,2048]{1,0:T(8,128)(2,1)S(1)}, bf16[8,2048]{1,0:T(8,128)(2,1)S(1)}, bf16[896,2048]{1,0:T(8,128)(2,1)S(1)}) custom-call(s32[64]{0:T(128)} %order_hbm.1, bf16[32,2048]{1,0:T(8,128)(2,1)} %own_hbm.1, bf16[8,2048]{1,0:T(8,128)(2,1)} %lanc_hbm.1, bf16[1792,2048]{1,0:T(8,128)(2,1)} %eig_hbm.5), custom_call_target="tpu_custom_call" | custom-call | bytes 3670016 | tf_op jit(solution)/shard_map/pallas_call | solution.py:179
  2.6 0.0 collective-permute-done.other
  2.6 1.6 %shard_map.47 = (bf16[256,896]{1,0:T(8,128)(2,1)S(1)}, bf16[256,2048]{1,0:T(8,128)(2,1)S(1)}, bf16[512,2048]{1,0:T(8,128)(2,1)S(1)}) custom-call(bf16[512,64]{1,0:T(8,128)(2,1)S(1)} %get-tuple-element.28.pick, bf16[32,2048]{1,0:T(8,128)(2,1)S(1)} %get-tuple-element.29.own, bf16[32,2048]{1,0:T(8,128)(2,1)S(1)} %collective-permute-done.other, ...), custom_call_target="tpu_custom_call" | custom-call | flops 939524096 | bytes 3670016 | tf_op jit(solution)/shard_map/pallas_call | solution.py:179
  4.3 2.6 %collective-permute-start.1 = (bf16[256,896]{1,0:T(8,128)(2,1)S(1)}, bf16[256,896]{1,0:T(8,128)(2,1)S(1)}, u32[]{:S(2)}, u32[]{:S(2)}) collective-permute-start(bf16[256,896]{1,0:T(8,128)(2,1)S(1)} %get-tuple-element.35), channel_id=1, source_target_pairs={{0,4},{1,3},{2,6},{3,1},{4,0},{5,7},{6,2},{7,5},{8,12},{9,11},{10,... | collective-permute-start | bytes 1376264 | tf_op jit(solution)/shard_map/ppermute | solution.py:211
  6.9 2.2 %shard_map.48 = (bf16[256,512]{1,0:T(8,128)(2,1)S(1)}, bf16[256,384]{1,0:T(8,128)(2,1)S(1)}, bf16[512,2048]{1,0:T(8,128)(2,1)S(1)}, bf16[384,2048]{1,0:T(8,128)(2,1)S(1)}) custom-call(bf16[512,64]{1,0:T(8,128)(2,1)S(1)} %get-tuple-element.28.pick, bf16[32,2048]{1,0:T(8,128)(2,1)S(1)} %get-tuple-element.29.own, ...), custom_call_target="tpu_custom_call" | custom-call | flops 939524096 | bytes 3670016 | tf_op jit(solution)/shard_map/pallas_call | solution.py:179
  9.1 1.6 %collective-permute-start.4 = (bf16[256,512]{1,0:T(8,128)(2,1)S(1)}, bf16[256,512]{1,0:T(8,128)(2,1)S(1)}, u32[]{:S(2)}, u32[]{:S(2)}) collective-permute-start(bf16[256,512]{1,0:T(8,128)(2,1)S(1)} %get-tuple-element.40), channel_id=1, source_target_pairs={{0,2},{1,3},{2,0},{3,1},{4,6},{5,7},{6,4},{7,5},{8,10},{9,11},{10,... | collective-permute-start | bytes 786440 | tf_op jit(solution)/shard_map/ppermute | solution.py:211
  10.6 0.4 %collective-permute-start.3 = (bf16[256,384]{1,0:T(8,128)(2,1)S(1)}, bf16[256,384]{1,0:T(8,128)(2,1)S(1)}, u32[]{:S(2)}, u32[]{:S(2)}) collective-permute-start(bf16[256,384]{1,0:T(8,128)(2,1)S(1)} %get-tuple-element.39), channel_id=1, source_target_pairs={{0,4},{1,9},{2,6},{3,11},{4,0},{5,13},{6,2},{7,15},{8,12},{9,1},{1... | collective-permute-start | bytes 589832 | tf_op jit(solution)/shard_map/ppermute | solution.py:211
  11.1 1.3 %shard_map.49.kept = f32[256,896]{1,0:T(8,128)S(1)} custom-call(bf16[512,2048]{1,0:T(8,128)(2,1)S(1)} %get-tuple-element.34.prod._, bf16[896,2048]{1,0:T(8,128)(2,1)S(1)} %get-tuple-element.31.eig), custom_call_target="tpu_custom_call" | custom-call | flops 939524096 | bytes 3670016 | tf_op jit(solution)/shard_map/pallas_call | solution.py:179
  12.4 2.4 %collective-permute-done.1.got = bf16[256,896]{1,0:T(8,128)(2,1)S(1)} collective-permute-done((bf16[256,896]{1,0:T(8,128)(2,1)S(1)}, bf16[256,896]{1,0:T(8,128)(2,1)S(1)}, u32[]{:S(2)}, u32[]{:S(2)}) %collective-permute-start.1) | collective-permute-done | bytes 458784 | tf_op jit(solution)/shard_map/ppermute | solution.py:211
  14.8 0.1 shard_map.50
  14.9 2.3 %collective-permute-start.2 = (bf16[128,896]{1,0:T(8,128)(2,1)S(1)}, bf16[128,896]{1,0:T(8,128)(2,1)S(1)}, u32[]{:S(2)}, u32[]{:S(2)}) collective-permute-start(bf16[128,896]{1,0:T(8,128)(2,1)S(1)} %get-tuple-element.37._), channel_id=1, source_target_pairs={{0,2},{1,9},{2,0},{3,11},{4,6},{5,13},{6,4},{7,15},{8,10},{9,1},{1... | collective-permute-start | bytes 688136 | tf_op jit(solution)/shard_map/ppermute | solution.py:211
  17.2 0.7 %shard_map.52.kept = f32[256,512]{1,0:T(8,128)S(1)} custom-call(bf16[512,2048]{1,0:T(8,128)(2,1)S(1)} %get-tuple-element.34.prod._, bf16[512,2048]{1,0:T(8,128)(2,1)S(1)} %get-tuple-element.33.eig), custom_call_target="tpu_custom_call" | custom-call | flops 536870912 | bytes 2097152 | tf_op jit(solution)/shard_map/pallas_call | solution.py:179
  17.9 0.4 %collective-permute-done.4.got = bf16[256,512]{1,0:T(8,128)(2,1)S(1)} collective-permute-done((bf16[256,512]{1,0:T(8,128)(2,1)S(1)}, bf16[256,512]{1,0:T(8,128)(2,1)S(1)}, u32[]{:S(2)}, u32[]{:S(2)}) %collective-permute-start.4) | collective-permute-done | bytes 262176 | tf_op jit(solution)/shard_map/ppermute | solution.py:211
  18.4 0.1 collective-permute-start.5
  18.5 0.7 %shard_map.51.kept = f32[256,384]{1,0:T(8,128)S(1)} custom-call(bf16[512,2048]{1,0:T(8,128)(2,1)S(1)} %get-tuple-element.34.prod._, bf16[384,2048]{1,0:T(8,128)(2,1)S(1)} %get-tuple-element.38.eig), custom_call_target="tpu_custom_call" | custom-call | flops 402653184 | bytes 1572864 | tf_op jit(solution)/shard_map/pallas_call | solution.py:179
  19.3 2.0 %collective-permute-start.6 = (bf16[128,384]{1,0:T(8,128)(2,1)S(1)}, bf16[128,384]{1,0:T(8,128)(2,1)S(1)}, u32[]{:S(2)}, u32[]{:S(2)}) collective-permute-start(bf16[128,384]{1,0:T(8,128)(2,1)S(1)} %get-tuple-element.42._), channel_id=1, source_target_pairs={{0,2},{1,3},{2,0},{3,1},{4,6},{5,7},{6,4},{7,5},{8,10},{9,11},{10,... | collective-permute-start | bytes 294920 | tf_op jit(solution)/shard_map/ppermute | solution.py:211
  21.3 0.0 collective-permute-done.2.got
  21.3 3.1 %collective-permute-start.7 = (bf16[64,896]{1,0:T(8,128)(2,1)S(1)}, bf16[64,896]{1,0:T(8,128)(2,1)S(1)}, u32[]{:S(2)}, u32[]{:S(2)}) collective-permute-start(bf16[64,896]{1,0:T(8,128)(2,1)S(1)} %get-tuple-element.45._), channel_id=1, source_target_pairs={{0,8},{1,5},{2,10},{3,7},{4,12},{5,1},{6,14},{7,3},{8,0},{9,13},{1... | collective-permute-start | bytes 344072 | tf_op jit(solution)/shard_map/ppermute | solution.py:211
  24.4 0.6 %collective-permute-done.5.got = bf16[128,512]{1,0:T(8,128)(2,1)S(1)} collective-permute-done((bf16[128,512]{1,0:T(8,128)(2,1)S(1)}, bf16[128,512]{1,0:T(8,128)(2,1)S(1)}, u32[]{:S(2)}, u32[]{:S(2)}) %collective-permute-start.5) | collective-permute-done | bytes 131104 | tf_op jit(solution)/shard_map/ppermute | solution.py:211
  25.0 2.3 %collective-permute-start.8 = (bf16[64,512]{1,0:T(8,128)(2,1)S(1)}, bf16[64,512]{1,0:T(8,128)(2,1)S(1)}, u32[]{:S(2)}, u32[]{:S(2)}) collective-permute-start(bf16[64,512]{1,0:T(8,128)(2,1)S(1)} %get-tuple-element.48._), channel_id=1, source_target_pairs={{0,8},{1,5},{2,10},{3,7},{4,12},{5,1},{6,14},{7,3},{8,0},{9,13},{1... | collective-permute-start | bytes 196616 | tf_op jit(solution)/shard_map/ppermute | solution.py:211
  27.3 0.8 %collective-permute-start.9 = (bf16[64,384]{1,0:T(8,128)(2,1)S(1)}, bf16[64,384]{1,0:T(8,128)(2,1)S(1)}, u32[]{:S(2)}, u32[]{:S(2)}) collective-permute-start(bf16[64,384]{1,0:T(8,128)(2,1)S(1)} %get-tuple-element.50), channel_id=1, source_target_pairs={{0,8},{1,5},{2,10},{3,7},{4,12},{5,1},{6,14},{7,3},{8,0},{9,13},{1... | collective-permute-start | bytes 147464 | tf_op jit(solution)/shard_map/ppermute | solution.py:211
  28.1 4.8 %collective-permute-done.9.refs_5_ = bf16[64,384]{1,0:T(8,128)(2,1)S(1)} collective-permute-done((bf16[64,384]{1,0:T(8,128)(2,1)S(1)}, bf16[64,384]{1,0:T(8,128)(2,1)S(1)}, u32[]{:S(2)}, u32[]{:S(2)}) %collective-permute-start.9) | collective-permute-done | bytes 49184 | tf_op jit(solution)/shard_map/ppermute | solution.py:211
  32.8 0.8 %shard_map.58 = f32[64,1792]{1,0:T(8,128)} custom-call(f32[64,896]{1,0:T(8,128)S(1)} %get-tuple-element.43.refs_0_, f32[64,512]{1,0:T(8,128)S(1)} %get-tuple-element.46.refs_1_, f32[64,384]{1,0:T(8,128)S(1)} %get-tuple-element.49.refs_2_, bf16[64,896]{1,0:T(8,128)(2,1)S(1)} %collective-permute-done.7.refs_3_, ...), custom_call_target="tpu_custom_call" | custom-call | flops 114688 | bytes 1376256 | tf_op jit(solution)/shard_map/pallas_call | solution.py:179
  (9 shorter events, 0.2 us)
Async XLA Ops:
  0.0 2.6 %collective-permute-start = (bf16[32,2048]{1,0:T(8,128)(2,1)}, bf16[32,2048]{1,0:T(8,128)(2,1)S(1)}, u32[]{:S(2)}, u32[]{:S(2)}) collective-permute-start(bf16[32,2048]{1,0:T(8,128)(2,1)} %own_hbm.1), channel_id=1, source_target_pairs={{0,1},{1,0},{2,3},{3,2},{4,5},{5,4},{6,7},{7,6},{8,9},{9,8},{10,11... | collective-permute-start | bytes 393224 | tf_op jit(solution)/shard_map/ppermute | solution.py:216
  4.3 10.5 %collective-permute-start.1 = (bf16[256,896]{1,0:T(8,128)(2,1)S(1)}, bf16[256,896]{1,0:T(8,128)(2,1)S(1)}, u32[]{:S(2)}, u32[]{:S(2)}) collective-permute-start(bf16[256,896]{1,0:T(8,128)(2,1)S(1)} %get-tuple-element.35), channel_id=1, source_target_pairs={{0,4},{1,3},{2,6},{3,1},{4,0},{5,7},{6,2},{7,5},{8,12},{9,11},{10,... | collective-permute-start | bytes 1376264 | tf_op jit(solution)/shard_map/ppermute | solution.py:211
  9.1 9.3 %collective-permute-start.4 = (bf16[256,512]{1,0:T(8,128)(2,1)S(1)}, bf16[256,512]{1,0:T(8,128)(2,1)S(1)}, u32[]{:S(2)}, u32[]{:S(2)}) collective-permute-start(bf16[256,512]{1,0:T(8,128)(2,1)S(1)} %get-tuple-element.40), channel_id=1, source_target_pairs={{0,2},{1,3},{2,0},{3,1},{4,6},{5,7},{6,4},{7,5},{8,10},{9,11},{10,... | collective-permute-start | bytes 786440 | tf_op jit(solution)/shard_map/ppermute | solution.py:211
  10.6 8.6 %collective-permute-start.3 = (bf16[256,384]{1,0:T(8,128)(2,1)S(1)}, bf16[256,384]{1,0:T(8,128)(2,1)S(1)}, u32[]{:S(2)}, u32[]{:S(2)}) collective-permute-start(bf16[256,384]{1,0:T(8,128)(2,1)S(1)} %get-tuple-element.39), channel_id=1, source_target_pairs={{0,4},{1,9},{2,6},{3,11},{4,0},{5,13},{6,2},{7,15},{8,12},{9,1},{1... | collective-permute-start | bytes 589832 | tf_op jit(solution)/shard_map/ppermute | solution.py:211
  14.9 6.4 %collective-permute-start.2 = (bf16[128,896]{1,0:T(8,128)(2,1)S(1)}, bf16[128,896]{1,0:T(8,128)(2,1)S(1)}, u32[]{:S(2)}, u32[]{:S(2)}) collective-permute-start(bf16[128,896]{1,0:T(8,128)(2,1)S(1)} %get-tuple-element.37._), channel_id=1, source_target_pairs={{0,2},{1,9},{2,0},{3,11},{4,6},{5,13},{6,4},{7,15},{8,10},{9,1},{1... | collective-permute-start | bytes 688136 | tf_op jit(solution)/shard_map/ppermute | solution.py:211
  18.4 6.5 %collective-permute-start.5 = (bf16[128,512]{1,0:T(8,128)(2,1)S(1)}, bf16[128,512]{1,0:T(8,128)(2,1)S(1)}, u32[]{:S(2)}, u32[]{:S(2)}) collective-permute-start(bf16[128,512]{1,0:T(8,128)(2,1)S(1)} %get-tuple-element.41._), channel_id=1, source_target_pairs={{0,4},{1,9},{2,6},{3,11},{4,0},{5,13},{6,2},{7,15},{8,12},{9,1},{1... | collective-permute-start | bytes 393224 | tf_op jit(solution)/shard_map/ppermute | solution.py:211
  19.3 7.9 %collective-permute-start.6 = (bf16[128,384]{1,0:T(8,128)(2,1)S(1)}, bf16[128,384]{1,0:T(8,128)(2,1)S(1)}, u32[]{:S(2)}, u32[]{:S(2)}) collective-permute-start(bf16[128,384]{1,0:T(8,128)(2,1)S(1)} %get-tuple-element.42._), channel_id=1, source_target_pairs={{0,2},{1,3},{2,0},{3,1},{4,6},{5,7},{6,4},{7,5},{8,10},{9,11},{10,... | collective-permute-start | bytes 294920 | tf_op jit(solution)/shard_map/ppermute | solution.py:211
  21.3 11.5 %collective-permute-start.7 = (bf16[64,896]{1,0:T(8,128)(2,1)S(1)}, bf16[64,896]{1,0:T(8,128)(2,1)S(1)}, u32[]{:S(2)}, u32[]{:S(2)}) collective-permute-start(bf16[64,896]{1,0:T(8,128)(2,1)S(1)} %get-tuple-element.45._), channel_id=1, source_target_pairs={{0,8},{1,5},{2,10},{3,7},{4,12},{5,1},{6,14},{7,3},{8,0},{9,13},{1... | collective-permute-start | bytes 344072 | tf_op jit(solution)/shard_map/ppermute | solution.py:211
  25.0 7.9 %collective-permute-start.8 = (bf16[64,512]{1,0:T(8,128)(2,1)S(1)}, bf16[64,512]{1,0:T(8,128)(2,1)S(1)}, u32[]{:S(2)}, u32[]{:S(2)}) collective-permute-start(bf16[64,512]{1,0:T(8,128)(2,1)S(1)} %get-tuple-element.48._), channel_id=1, source_target_pairs={{0,8},{1,5},{2,10},{3,7},{4,12},{5,1},{6,14},{7,3},{8,0},{9,13},{1... | collective-permute-start | bytes 196616 | tf_op jit(solution)/shard_map/ppermute | solution.py:211
  27.3 5.6 %collective-permute-start.9 = (bf16[64,384]{1,0:T(8,128)(2,1)S(1)}, bf16[64,384]{1,0:T(8,128)(2,1)S(1)}, u32[]{:S(2)}, u32[]{:S(2)}) collective-permute-start(bf16[64,384]{1,0:T(8,128)(2,1)S(1)} %get-tuple-element.50), channel_id=1, source_target_pairs={{0,8},{1,5},{2,10},{3,7},{4,12},{5,1},{6,14},{7,3},{8,0},{9,13},{1... | collective-permute-start | bytes 147464 | tf_op jit(solution)/shard_map/ppermute | solution.py:211

commit v23 on v21

--- a/solution.py
+++ b/solution.py
@@ -12,8 +12,8 @@
 X, NEAR, FAR = 0, 1, 2
 PLAN = [
     (3, (NEAR, X, FAR), (X, FAR, NEAR)),
+    (2, (X, NEAR, FAR), (FAR, X, NEAR)),
     (2, (X, NEAR, FAR), (X, FAR, NEAR)),
-    (2, (NEAR, X, FAR), (FAR, X, NEAR)),
 ]
 ORDER = [(piece, stage) for stage in (1, 2) for piece in range(len(PLAN))]
 

time: 33.6 us -> 36.6 us (1.089)
  waiting for transfers between devices: 7.74 us -> 12 us
  starting transfers between devices: 15.4 us -> 13.9 us
    ppermute x9, waiting for transfers between devices: 7.74 us -> 12 us  [exchange(): return lax.ppermute(value, ('grid', 'eig'), pairs)]
    ppermute x9, starting transfers between devices: 15 us -> 13.5 us  [exchange(): return lax.ppermute(value, ('grid', 'eig'), pairs)]
  transfers between devices with their start and end apart: 10 -> 10, of which waited for: 5 -> 5; matrix products, arithmetic and copies ran while one was open for 0% -> 0% of each run, Pallas kernels for 23% -> 22%
where the time goes in v23:
time: 36.6 us; the launch traced here: 36.4 us
  starting transfers between devices  13.9 us (38%)
  waiting for transfers between devices  12 us (33%)
  Pallas kernels  10.4 us (28%)
    ppermute x9, starting transfers between devices, exchange(): return lax.ppermute(value, ('grid', 'eig'), pairs)  13.5 us
    ppermute x9, waiting for transfers between devices, exchange(): return lax.ppermute(value, ('grid', 'eig'), pairs)  12 us
    pallas_call x14, Pallas kernels, kernel_call(): pl.pallas_call(body, out_shape=[jax.ShapeDtypeStruct(*out) for out in out...  10.4 us
  transfers between devices with their start and end apart: 10, of which 5 were waited for; matrix products, arithmetic and copies ran while one was open for 0% of the time, Pallas kernels for 22%

profile of v23, /device:TPU:0, one launch (start us, length us, event | category | flops | bytes accessed | tf_op | source)
XLA Modules:
  0.0 36.4 jit_solution(17054175510191247342)
XLA Ops:
  0.0 0.5 %collective-permute-start = (bf16[32,2048]{1,0:T(8,128)(2,1)}, bf16[32,2048]{1,0:T(8,128)(2,1)S(1)}, u32[]{:S(2)}, u32[]{:S(2)}) collective-permute-start(bf16[32,2048]{1,0:T(8,128)(2,1)} %own_hbm.1), channel_id=1, source_target_pairs={{0,1},{1,0},{2,3},{3,2},{4,5},{5,4},{6,7},{7,6},{8,9},{9,8},{10,11... | collective-permute-start | bytes 393224 | tf_op jit(solution)/shard_map/ppermute | solution.py:229
  0.5 2.0 %shard_map.46 = (bf16[512,64]{1,0:T(8,128)(2,1)S(1)}, bf16[32,2048]{1,0:T(8,128)(2,1)S(1)}, bf16[8,2048]{1,0:T(8,128)(2,1)S(1)}, bf16[768,2048]{1,0:T(8,128)(2,1)S(1)}) custom-call(s32[64]{0:T(128)} %order_hbm.1, bf16[32,2048]{1,0:T(8,128)(2,1)} %own_hbm.1, bf16[8,2048]{1,0:T(8,128)(2,1)} %lanc_hbm.1, bf16[1792,2048]{1,0:T(8,128)(2,1)} %eig_hbm.5), custom_call_target="tpu_custom_call" | custom-call | bytes 3145728 | tf_op jit(solution)/shard_map/pallas_call | solution.py:191
  2.5 1.6 %shard_map.47 = (bf16[256,768]{1,0:T(8,128)(2,1)S(1)}, bf16[256,2048]{1,0:T(8,128)(2,1)S(1)}, bf16[512,2048]{1,0:T(8,128)(2,1)S(1)}) custom-call(bf16[512,64]{1,0:T(8,128)(2,1)S(1)} %get-tuple-element.28.pick, bf16[32,2048]{1,0:T(8,128)(2,1)S(1)} %get-tuple-element.29.own, bf16[32,2048]{1,0:T(8,128)(2,1)S(1)} %collective-permute-done.other, ...), custom_call_target="tpu_custom_call" | custom-call | flops 805306368 | bytes 3145728 | tf_op jit(solution)/shard_map/pallas_call | solution.py:191
  4.1 2.6 %collective-permute-start.1 = (bf16[256,768]{1,0:T(8,128)(2,1)S(1)}, bf16[256,768]{1,0:T(8,128)(2,1)S(1)}, u32[]{:S(2)}, u32[]{:S(2)}) collective-permute-start(bf16[256,768]{1,0:T(8,128)(2,1)S(1)} %get-tuple-element.35), channel_id=1, source_target_pairs={{0,4},{1,3},{2,6},{3,1},{4,0},{5,7},{6,2},{7,5},{8,12},{9,11},{10,... | collective-permute-start | bytes 1179656 | tf_op jit(solution)/shard_map/ppermute | solution.py:224
  6.7 2.7 %shard_map.48 = (bf16[256,512]{1,0:T(8,128)(2,1)S(1)}, bf16[256,512]{1,0:T(8,128)(2,1)S(1)}, bf16[512,2048]{1,0:T(8,128)(2,1)S(1)}, bf16[512,2048]{1,0:T(8,128)(2,1)S(1)}) custom-call(bf16[512,64]{1,0:T(8,128)(2,1)S(1)} %get-tuple-element.28.pick, bf16[32,2048]{1,0:T(8,128)(2,1)S(1)} %get-tuple-element.29.own, ...), custom_call_target="tpu_custom_call" | custom-call | flops 1073741824 | bytes 4194304 | tf_op jit(solution)/shard_map/pallas_call | solution.py:191
  9.4 1.5 %collective-permute-start.4 = (bf16[256,512]{1,0:T(8,128)(2,1)S(1)}, bf16[256,512]{1,0:T(8,128)(2,1)S(1)}, u32[]{:S(2)}, u32[]{:S(2)}) collective-permute-start(bf16[256,512]{1,0:T(8,128)(2,1)S(1)} %get-tuple-element.40), channel_id=1, source_target_pairs={{0,2},{1,9},{2,0},{3,11},{4,6},{5,13},{6,4},{7,15},{8,10},{9,1},{1... | collective-permute-start | bytes 786440 | tf_op jit(solution)/shard_map/ppermute | solution.py:224
  11.0 0.5 %collective-permute-start.3 = (bf16[256,512]{1,0:T(8,128)(2,1)S(1)}, bf16[256,512]{1,0:T(8,128)(2,1)S(1)}, u32[]{:S(2)}, u32[]{:S(2)}) collective-permute-start(bf16[256,512]{1,0:T(8,128)(2,1)S(1)} %get-tuple-element.39), channel_id=1, source_target_pairs={{0,2},{1,3},{2,0},{3,1},{4,6},{5,7},{6,4},{7,5},{8,10},{9,11},{10,... | collective-permute-start | bytes 786440 | tf_op jit(solution)/shard_map/ppermute | solution.py:224
  11.5 1.0 %shard_map.49.kept = f32[256,768]{1,0:T(8,128)S(1)} custom-call(bf16[512,2048]{1,0:T(8,128)(2,1)S(1)} %get-tuple-element.34.prod._, bf16[768,2048]{1,0:T(8,128)(2,1)S(1)} %get-tuple-element.31.eig), custom_call_target="tpu_custom_call" | custom-call | flops 805306368 | bytes 3145728 | tf_op jit(solution)/shard_map/pallas_call | solution.py:191
  12.5 0.1 shard_map.50
  12.6 3.9 %collective-permute-start.2 = (bf16[128,768]{1,0:T(8,128)(2,1)S(1)}, bf16[128,768]{1,0:T(8,128)(2,1)S(1)}, u32[]{:S(2)}, u32[]{:S(2)}) collective-permute-start(bf16[128,768]{1,0:T(8,128)(2,1)S(1)} %get-tuple-element.37._), channel_id=1, source_target_pairs={{0,2},{1,9},{2,0},{3,11},{4,6},{5,13},{6,4},{7,15},{8,10},{9,1},{1... | collective-permute-start | bytes 589832 | tf_op jit(solution)/shard_map/ppermute | solution.py:224
  16.5 0.7 %shard_map.52.kept = f32[256,512]{1,0:T(8,128)S(1)} custom-call(bf16[512,2048]{1,0:T(8,128)(2,1)S(1)} %get-tuple-element.34.prod._, bf16[512,2048]{1,0:T(8,128)(2,1)S(1)} %get-tuple-element.33.eig), custom_call_target="tpu_custom_call" | custom-call | flops 536870912 | bytes 2097152 | tf_op jit(solution)/shard_map/pallas_call | solution.py:191
  17.3 0.4 %collective-permute-start.5 = (bf16[128,512]{1,0:T(8,128)(2,1)S(1)}, bf16[128,512]{1,0:T(8,128)(2,1)S(1)}, u32[]{:S(2)}, u32[]{:S(2)}) collective-permute-start(bf16[128,512]{1,0:T(8,128)(2,1)S(1)} %get-tuple-element.41._), channel_id=1, source_target_pairs={{0,4},{1,3},{2,6},{3,1},{4,0},{5,7},{6,2},{7,5},{8,12},{9,11},{10,... | collective-permute-start | bytes 393224 | tf_op jit(solution)/shard_map/ppermute | solution.py:224
  17.7 0.7 %shard_map.51.kept = f32[256,512]{1,0:T(8,128)S(1)} custom-call(bf16[512,2048]{1,0:T(8,128)(2,1)S(1)} %get-tuple-element.34.prod._, bf16[512,2048]{1,0:T(8,128)(2,1)S(1)} %get-tuple-element.38.eig), custom_call_target="tpu_custom_call" | custom-call | flops 536870912 | bytes 2097152 | tf_op jit(solution)/shard_map/pallas_call | solution.py:191
  18.4 3.0 %collective-permute-done.3.got = bf16[256,512]{1,0:T(8,128)(2,1)S(1)} collective-permute-done((bf16[256,512]{1,0:T(8,128)(2,1)S(1)}, bf16[256,512]{1,0:T(8,128)(2,1)S(1)}, u32[]{:S(2)}, u32[]{:S(2)}) %collective-permute-start.3) | collective-permute-done | bytes 262176 | tf_op jit(solution)/shard_map/ppermute | solution.py:224
  21.5 1.1 %collective-permute-start.8 = (bf16[128,512]{1,0:T(8,128)(2,1)S(1)}, bf16[128,512]{1,0:T(8,128)(2,1)S(1)}, u32[]{:S(2)}, u32[]{:S(2)}) collective-permute-start(bf16[128,512]{1,0:T(8,128)(2,1)S(1)} %get-tuple-element.42._), channel_id=1, source_target_pairs={{0,4},{1,9},{2,6},{3,11},{4,0},{5,13},{6,2},{7,15},{8,12},{9,1},{1... | collective-permute-start | bytes 393224 | tf_op jit(solution)/shard_map/ppermute | solution.py:224
  22.6 1.3 %collective-permute-done.2.got = bf16[128,768]{1,0:T(8,128)(2,1)S(1)} collective-permute-done((bf16[128,768]{1,0:T(8,128)(2,1)S(1)}, bf16[128,768]{1,0:T(8,128)(2,1)S(1)}, u32[]{:S(2)}, u32[]{:S(2)}) %collective-permute-start.2) | collective-permute-done | bytes 196640 | tf_op jit(solution)/shard_map/ppermute | solution.py:224
  24.0 3.2 %collective-permute-start.6 = (bf16[64,768]{1,0:T(8,128)(2,1)S(1)}, bf16[64,768]{1,0:T(8,128)(2,1)S(1)}, u32[]{:S(2)}, u32[]{:S(2)}) collective-permute-start(bf16[64,768]{1,0:T(8,128)(2,1)S(1)} %get-tuple-element.45._), channel_id=1, source_target_pairs={{0,8},{1,5},{2,10},{3,7},{4,12},{5,1},{6,14},{7,3},{8,0},{9,13},{1... | collective-permute-start | bytes 294920 | tf_op jit(solution)/shard_map/ppermute | solution.py:224
  27.1 0.1 collective-permute-start.7
  27.2 2.9 %collective-permute-done.8.got = bf16[128,512]{1,0:T(8,128)(2,1)S(1)} collective-permute-done((bf16[128,512]{1,0:T(8,128)(2,1)S(1)}, bf16[128,512]{1,0:T(8,128)(2,1)S(1)}, u32[]{:S(2)}, u32[]{:S(2)}) %collective-permute-start.8) | collective-permute-done | bytes 131104 | tf_op jit(solution)/shard_map/ppermute | solution.py:224
  30.1 0.1 collective-permute-start.9
  30.2 2.8 %collective-permute-done.7.refs_3_ = bf16[64,512]{1,0:T(8,128)(2,1)S(1)} collective-permute-done((bf16[64,512]{1,0:T(8,128)(2,1)S(1)}, bf16[64,512]{1,0:T(8,128)(2,1)S(1)}, u32[]{:S(2)}, u32[]{:S(2)}) %collective-permute-start.7) | collective-permute-done | bytes 65568 | tf_op jit(solution)/shard_map/ppermute | solution.py:224
  33.1 0.8 %shard_map.57._ = f32[64,1792]{1,0:T(8,128)} custom-call(f32[64,768]{1,0:T(8,128)S(1)} %get-tuple-element.43.refs_0_, f32[64,512]{1,0:T(8,128)S(1)} %get-tuple-element.46.refs_1_, bf16[64,768]{1,0:T(8,128)(2,1)S(1)} %collective-permute-done.6.refs_2_, bf16[64,512]{1,0:T(8,128)(2,1)S(1)} %collective-permute-done.7.refs_3_), custom_call_target="tpu_custom_call" | custom-call | flops 81920 | bytes 819200 | tf_op jit(solution)/shard_map/pallas_call | solution.py:191
  33.8 1.9 %collective-permute-done.9.came = bf16[64,512]{1,0:T(8,128)(2,1)S(1)} collective-permute-done((bf16[64,512]{1,0:T(8,128)(2,1)S(1)}, bf16[64,512]{1,0:T(8,128)(2,1)S(1)}, u32[]{:S(2)}, u32[]{:S(2)}) %collective-permute-start.9) | collective-permute-done | bytes 65568 | tf_op jit(solution)/shard_map/ppermute | solution.py:224
  35.8 0.7 %shard_map.59 = f32[64,1792]{1,0:T(8,128)} custom-call(f32[64,1792]{1,0:T(8,128)} %shard_map.57._, f32[64,512]{1,0:T(8,128)S(1)} %get-tuple-element.49.kept, bf16[64,512]{1,0:T(8,128)(2,1)S(1)} %collective-permute-done.9.came), custom_call_target="tpu_custom_call", output_to_operand_aliasing={{}: (0, {})} | custom-call | flops 32768 | bytes 327680 | tf_op jit(solution)/shard_map/pallas_call | solution.py:191
  (10 shorter events, 0.2 us)
Async XLA Ops:
  0.0 2.5 %collective-permute-start = (bf16[32,2048]{1,0:T(8,128)(2,1)}, bf16[32,2048]{1,0:T(8,128)(2,1)S(1)}, u32[]{:S(2)}, u32[]{:S(2)}) collective-permute-start(bf16[32,2048]{1,0:T(8,128)(2,1)} %own_hbm.1), channel_id=1, source_target_pairs={{0,1},{1,0},{2,3},{3,2},{4,5},{5,4},{6,7},{7,6},{8,9},{9,8},{10,11... | collective-permute-start | bytes 393224 | tf_op jit(solution)/shard_map/ppermute | solution.py:229
  4.1 8.4 %collective-permute-start.1 = (bf16[256,768]{1,0:T(8,128)(2,1)S(1)}, bf16[256,768]{1,0:T(8,128)(2,1)S(1)}, u32[]{:S(2)}, u32[]{:S(2)}) collective-permute-start(bf16[256,768]{1,0:T(8,128)(2,1)S(1)} %get-tuple-element.35), channel_id=1, source_target_pairs={{0,4},{1,3},{2,6},{3,1},{4,0},{5,7},{6,2},{7,5},{8,12},{9,11},{10,... | collective-permute-start | bytes 1179656 | tf_op jit(solution)/shard_map/ppermute | solution.py:224
  9.4 7.8 %collective-permute-start.4 = (bf16[256,512]{1,0:T(8,128)(2,1)S(1)}, bf16[256,512]{1,0:T(8,128)(2,1)S(1)}, u32[]{:S(2)}, u32[]{:S(2)}) collective-permute-start(bf16[256,512]{1,0:T(8,128)(2,1)S(1)} %get-tuple-element.40), channel_id=1, source_target_pairs={{0,2},{1,9},{2,0},{3,11},{4,6},{5,13},{6,4},{7,15},{8,10},{9,1},{1... | collective-permute-start | bytes 786440 | tf_op jit(solution)/shard_map/ppermute | solution.py:224
  11.0 10.5 %collective-permute-start.3 = (bf16[256,512]{1,0:T(8,128)(2,1)S(1)}, bf16[256,512]{1,0:T(8,128)(2,1)S(1)}, u32[]{:S(2)}, u32[]{:S(2)}) collective-permute-start(bf16[256,512]{1,0:T(8,128)(2,1)S(1)} %get-tuple-element.39), channel_id=1, source_target_pairs={{0,2},{1,3},{2,0},{3,1},{4,6},{5,7},{6,4},{7,5},{8,10},{9,11},{10,... | collective-permute-start | bytes 786440 | tf_op jit(solution)/shard_map/ppermute | solution.py:224
  12.6 11.3 %collective-permute-start.2 = (bf16[128,768]{1,0:T(8,128)(2,1)S(1)}, bf16[128,768]{1,0:T(8,128)(2,1)S(1)}, u32[]{:S(2)}, u32[]{:S(2)}) collective-permute-start(bf16[128,768]{1,0:T(8,128)(2,1)S(1)} %get-tuple-element.37._), channel_id=1, source_target_pairs={{0,2},{1,9},{2,0},{3,11},{4,6},{5,13},{6,4},{7,15},{8,10},{9,1},{1... | collective-permute-start | bytes 589832 | tf_op jit(solution)/shard_map/ppermute | solution.py:224
  17.3 9.8 %collective-permute-start.5 = (bf16[128,512]{1,0:T(8,128)(2,1)S(1)}, bf16[128,512]{1,0:T(8,128)(2,1)S(1)}, u32[]{:S(2)}, u32[]{:S(2)}) collective-permute-start(bf16[128,512]{1,0:T(8,128)(2,1)S(1)} %get-tuple-element.41._), channel_id=1, source_target_pairs={{0,4},{1,3},{2,6},{3,1},{4,0},{5,7},{6,2},{7,5},{8,12},{9,11},{10,... | collective-permute-start | bytes 393224 | tf_op jit(solution)/shard_map/ppermute | solution.py:224
  21.5 8.6 %collective-permute-start.8 = (bf16[128,512]{1,0:T(8,128)(2,1)S(1)}, bf16[128,512]{1,0:T(8,128)(2,1)S(1)}, u32[]{:S(2)}, u32[]{:S(2)}) collective-permute-start(bf16[128,512]{1,0:T(8,128)(2,1)S(1)} %get-tuple-element.42._), channel_id=1, source_target_pairs={{0,4},{1,9},{2,6},{3,11},{4,0},{5,13},{6,2},{7,15},{8,12},{9,1},{1... | collective-permute-start | bytes 393224 | tf_op jit(solution)/shard_map/ppermute | solution.py:224
  24.0 9.1 %collective-permute-start.6 = (bf16[64,768]{1,0:T(8,128)(2,1)S(1)}, bf16[64,768]{1,0:T(8,128)(2,1)S(1)}, u32[]{:S(2)}, u32[]{:S(2)}) collective-permute-start(bf16[64,768]{1,0:T(8,128)(2,1)S(1)} %get-tuple-element.45._), channel_id=1, source_target_pairs={{0,8},{1,5},{2,10},{3,7},{4,12},{5,1},{6,14},{7,3},{8,0},{9,13},{1... | collective-permute-start | bytes 294920 | tf_op jit(solution)/shard_map/ppermute | solution.py:224
  27.1 5.9 %collective-permute-start.7 = (bf16[64,512]{1,0:T(8,128)(2,1)S(1)}, bf16[64,512]{1,0:T(8,128)(2,1)S(1)}, u32[]{:S(2)}, u32[]{:S(2)}) collective-permute-start(bf16[64,512]{1,0:T(8,128)(2,1)S(1)} %get-tuple-element.47._), channel_id=1, source_target_pairs={{0,8},{1,5},{2,10},{3,7},{4,12},{5,1},{6,14},{7,3},{8,0},{9,13},{1... | collective-permute-start | bytes 196616 | tf_op jit(solution)/shard_map/ppermute | solution.py:224
  30.1 5.6 %collective-permute-start.9 = (bf16[64,512]{1,0:T(8,128)(2,1)S(1)}, bf16[64,512]{1,0:T(8,128)(2,1)S(1)}, u32[]{:S(2)}, u32[]{:S(2)}) collective-permute-start(bf16[64,512]{1,0:T(8,128)(2,1)S(1)} %get-tuple-element.50), channel_id=1, source_target_pairs={{0,8},{1,5},{2,10},{3,7},{4,12},{5,1},{6,14},{7,3},{8,0},{9,13},{1... | collective-permute-start | bytes 196616 | tf_op jit(solution)/shard_map/ppermute | solution.py:224

commit v24 on v23

--- a/solution.py
+++ b/solution.py
@@ -12,8 +12,8 @@
 X, NEAR, FAR = 0, 1, 2
 PLAN = [
     (3, (NEAR, X, FAR), (X, FAR, NEAR)),
+    (2, (NEAR, X, FAR), (X, FAR, NEAR)),
     (2, (X, NEAR, FAR), (FAR, X, NEAR)),
-    (2, (X, NEAR, FAR), (X, FAR, NEAR)),
 ]
 ORDER = [(piece, stage) for stage in (1, 2) for piece in range(len(PLAN))]
 

time: 36.6 us -> 35.2 us (0.962)
  waiting for transfers between devices: 12 us -> 9.27 us
  starting transfers between devices: 13.9 us -> 15.6 us
    ppermute x9, waiting for transfers between devices: 12 us -> 9.26 us  [exchange(): return lax.ppermute(value, ('grid', 'eig'), pairs)]
    ppermute x9, starting transfers between devices: 13.5 us -> 15.1 us  [exchange(): return lax.ppermute(value, ('grid', 'eig'), pairs)]
where the time goes in v24:
time: 35.2 us; the launch traced here: 35 us
  starting transfers between devices  15.6 us (44%)
  Pallas kernels  10.1 us (29%)
  waiting for transfers between devices  9.27 us (26%)
    ppermute x9, starting transfers between devices, exchange(): return lax.ppermute(value, ('grid', 'eig'), pairs)  15.1 us
    pallas_call x14, Pallas kernels, kernel_call(): pl.pallas_call(body, out_shape=[jax.ShapeDtypeStruct(*out) for out in out...  10.1 us
    ppermute x9, waiting for transfers between devices, exchange(): return lax.ppermute(value, ('grid', 'eig'), pairs)  9.26 us
  transfers between devices with their start and end apart: 10, of which 5 were waited for; matrix products, arithmetic and copies ran while one was open for 0% of the time, Pallas kernels for 22%

profile of v24, /device:TPU:0, one launch (start us, length us, event | category | flops | bytes accessed | tf_op | source)
XLA Modules:
  0.0 35.0 jit_solution(4023521005266614168)
XLA Ops:
  0.0 0.5 %collective-permute-start = (bf16[32,2048]{1,0:T(8,128)(2,1)}, bf16[32,2048]{1,0:T(8,128)(2,1)S(1)}, u32[]{:S(2)}, u32[]{:S(2)}) collective-permute-start(bf16[32,2048]{1,0:T(8,128)(2,1)} %own_hbm.1), channel_id=1, source_target_pairs={{0,1},{1,0},{2,3},{3,2},{4,5},{5,4},{6,7},{7,6},{8,9},{9,8},{10,11... | collective-permute-start | bytes 393224 | tf_op jit(solution)/shard_map/ppermute | solution.py:229
  0.5 2.0 %shard_map.46 = (bf16[512,64]{1,0:T(8,128)(2,1)S(1)}, bf16[32,2048]{1,0:T(8,128)(2,1)S(1)}, bf16[8,2048]{1,0:T(8,128)(2,1)S(1)}, bf16[768,2048]{1,0:T(8,128)(2,1)S(1)}) custom-call(s32[64]{0:T(128)} %order_hbm.1, bf16[32,2048]{1,0:T(8,128)(2,1)} %own_hbm.1, bf16[8,2048]{1,0:T(8,128)(2,1)} %lanc_hbm.1, bf16[1792,2048]{1,0:T(8,128)(2,1)} %eig_hbm.5), custom_call_target="tpu_custom_call" | custom-call | bytes 3145728 | tf_op jit(solution)/shard_map/pallas_call | solution.py:191
  2.5 1.6 %shard_map.47 = (bf16[256,768]{1,0:T(8,128)(2,1)S(1)}, bf16[256,2048]{1,0:T(8,128)(2,1)S(1)}, bf16[512,2048]{1,0:T(8,128)(2,1)S(1)}) custom-call(bf16[512,64]{1,0:T(8,128)(2,1)S(1)} %get-tuple-element.28.pick, bf16[32,2048]{1,0:T(8,128)(2,1)S(1)} %get-tuple-element.29.own, bf16[32,2048]{1,0:T(8,128)(2,1)S(1)} %collective-permute-done.other, ...), custom_call_target="tpu_custom_call" | custom-call | flops 805306368 | bytes 3145728 | tf_op jit(solution)/shard_map/pallas_call | solution.py:191
  4.1 2.6 %collective-permute-start.1 = (bf16[256,768]{1,0:T(8,128)(2,1)S(1)}, bf16[256,768]{1,0:T(8,128)(2,1)S(1)}, u32[]{:S(2)}, u32[]{:S(2)}) collective-permute-start(bf16[256,768]{1,0:T(8,128)(2,1)S(1)} %get-tuple-element.35), channel_id=1, source_target_pairs={{0,4},{1,3},{2,6},{3,1},{4,0},{5,7},{6,2},{7,5},{8,12},{9,11},{10,... | collective-permute-start | bytes 1179656 | tf_op jit(solution)/shard_map/ppermute | solution.py:224
  6.7 2.3 %shard_map.48 = (bf16[256,512]{1,0:T(8,128)(2,1)S(1)}, bf16[256,512]{1,0:T(8,128)(2,1)S(1)}, bf16[512,2048]{1,0:T(8,128)(2,1)S(1)}, bf16[512,2048]{1,0:T(8,128)(2,1)S(1)}) custom-call(bf16[512,64]{1,0:T(8,128)(2,1)S(1)} %get-tuple-element.28.pick, bf16[32,2048]{1,0:T(8,128)(2,1)S(1)} %get-tuple-element.29.own, ...), custom_call_target="tpu_custom_call" | custom-call | flops 1073741824 | bytes 4194304 | tf_op jit(solution)/shard_map/pallas_call | solution.py:191
  9.1 0.1 collective-permute-start.4
  9.2 1.9 %collective-permute-start.3 = (bf16[256,512]{1,0:T(8,128)(2,1)S(1)}, bf16[256,512]{1,0:T(8,128)(2,1)S(1)}, u32[]{:S(2)}, u32[]{:S(2)}) collective-permute-start(bf16[256,512]{1,0:T(8,128)(2,1)S(1)} %get-tuple-element.39), channel_id=1, source_target_pairs={{0,2},{1,9},{2,0},{3,11},{4,6},{5,13},{6,4},{7,15},{8,10},{9,1},{1... | collective-permute-start | bytes 786440 | tf_op jit(solution)/shard_map/ppermute | solution.py:224
  11.1 1.0 %shard_map.49.kept = f32[256,768]{1,0:T(8,128)S(1)} custom-call(bf16[512,2048]{1,0:T(8,128)(2,1)S(1)} %get-tuple-element.34.prod._, bf16[768,2048]{1,0:T(8,128)(2,1)S(1)} %get-tuple-element.31.eig), custom_call_target="tpu_custom_call" | custom-call | flops 805306368 | bytes 3145728 | tf_op jit(solution)/shard_map/pallas_call | solution.py:191
  12.1 0.4 %collective-permute-done.1.got = bf16[256,768]{1,0:T(8,128)(2,1)S(1)} collective-permute-done((bf16[256,768]{1,0:T(8,128)(2,1)S(1)}, bf16[256,768]{1,0:T(8,128)(2,1)S(1)}, u32[]{:S(2)}, u32[]{:S(2)}) %collective-permute-start.1) | collective-permute-done | bytes 393248 | tf_op jit(solution)/shard_map/ppermute | solution.py:224
  12.5 0.1 shard_map.50
  12.6 2.0 %collective-permute-start.2 = (bf16[128,768]{1,0:T(8,128)(2,1)S(1)}, bf16[128,768]{1,0:T(8,128)(2,1)S(1)}, u32[]{:S(2)}, u32[]{:S(2)}) collective-permute-start(bf16[128,768]{1,0:T(8,128)(2,1)S(1)} %get-tuple-element.37._), channel_id=1, source_target_pairs={{0,2},{1,9},{2,0},{3,11},{4,6},{5,13},{6,4},{7,15},{8,10},{9,1},{1... | collective-permute-start | bytes 589832 | tf_op jit(solution)/shard_map/ppermute | solution.py:224
  14.6 0.7 %shard_map.52.kept = f32[256,512]{1,0:T(8,128)S(1)} custom-call(bf16[512,2048]{1,0:T(8,128)(2,1)S(1)} %get-tuple-element.34.prod._, bf16[512,2048]{1,0:T(8,128)(2,1)S(1)} %get-tuple-element.33.eig), custom_call_target="tpu_custom_call" | custom-call | flops 536870912 | bytes 2097152 | tf_op jit(solution)/shard_map/pallas_call | solution.py:191
  15.3 3.8 %collective-permute-done.4.got = bf16[256,512]{1,0:T(8,128)(2,1)S(1)} collective-permute-done((bf16[256,512]{1,0:T(8,128)(2,1)S(1)}, bf16[256,512]{1,0:T(8,128)(2,1)S(1)}, u32[]{:S(2)}, u32[]{:S(2)}) %collective-permute-start.4) | collective-permute-done | bytes 262176 | tf_op jit(solution)/shard_map/ppermute | solution.py:224
  19.2 1.9 %collective-permute-start.5 = (bf16[128,512]{1,0:T(8,128)(2,1)S(1)}, bf16[128,512]{1,0:T(8,128)(2,1)S(1)}, u32[]{:S(2)}, u32[]{:S(2)}) collective-permute-start(bf16[128,512]{1,0:T(8,128)(2,1)S(1)} %get-tuple-element.41._), channel_id=1, source_target_pairs={{0,2},{1,9},{2,0},{3,11},{4,6},{5,13},{6,4},{7,15},{8,10},{9,1},{1... | collective-permute-start | bytes 393224 | tf_op jit(solution)/shard_map/ppermute | solution.py:224
  21.1 0.7 %shard_map.51.kept = f32[256,512]{1,0:T(8,128)S(1)} custom-call(bf16[512,2048]{1,0:T(8,128)(2,1)S(1)} %get-tuple-element.34.prod._, bf16[512,2048]{1,0:T(8,128)(2,1)S(1)} %get-tuple-element.38.eig), custom_call_target="tpu_custom_call" | custom-call | flops 536870912 | bytes 2097152 | tf_op jit(solution)/shard_map/pallas_call | solution.py:191
  21.9 0.5 %collective-permute-start.8 = (bf16[128,512]{1,0:T(8,128)(2,1)S(1)}, bf16[128,512]{1,0:T(8,128)(2,1)S(1)}, u32[]{:S(2)}, u32[]{:S(2)}) collective-permute-start(bf16[128,512]{1,0:T(8,128)(2,1)S(1)} %get-tuple-element.42._), channel_id=1, source_target_pairs={{0,4},{1,3},{2,6},{3,1},{4,0},{5,7},{6,2},{7,5},{8,12},{9,11},{10,... | collective-permute-start | bytes 393224 | tf_op jit(solution)/shard_map/ppermute | solution.py:224
  22.4 2.7 %collective-permute-start.6 = (bf16[64,768]{1,0:T(8,128)(2,1)S(1)}, bf16[64,768]{1,0:T(8,128)(2,1)S(1)}, u32[]{:S(2)}, u32[]{:S(2)}) collective-permute-start(bf16[64,768]{1,0:T(8,128)(2,1)S(1)} %get-tuple-element.45._), channel_id=1, source_target_pairs={{0,8},{1,5},{2,10},{3,7},{4,12},{5,1},{6,14},{7,3},{8,0},{9,13},{1... | collective-permute-start | bytes 294920 | tf_op jit(solution)/shard_map/ppermute | solution.py:224
  25.1 2.0 %collective-permute-start.7 = (bf16[64,512]{1,0:T(8,128)(2,1)S(1)}, bf16[64,512]{1,0:T(8,128)(2,1)S(1)}, u32[]{:S(2)}, u32[]{:S(2)}) collective-permute-start(bf16[64,512]{1,0:T(8,128)(2,1)S(1)} %get-tuple-element.47._), channel_id=1, source_target_pairs={{0,8},{1,5},{2,10},{3,7},{4,12},{5,1},{6,14},{7,3},{8,0},{9,13},{1... | collective-permute-start | bytes 196616 | tf_op jit(solution)/shard_map/ppermute | solution.py:224
  27.2 1.2 %collective-permute-done.8.got = bf16[128,512]{1,0:T(8,128)(2,1)S(1)} collective-permute-done((bf16[128,512]{1,0:T(8,128)(2,1)S(1)}, bf16[128,512]{1,0:T(8,128)(2,1)S(1)}, u32[]{:S(2)}, u32[]{:S(2)}) %collective-permute-start.8) | collective-permute-done | bytes 131104 | tf_op jit(solution)/shard_map/ppermute | solution.py:224
  28.4 1.3 %collective-permute-start.9 = (bf16[64,512]{1,0:T(8,128)(2,1)S(1)}, bf16[64,512]{1,0:T(8,128)(2,1)S(1)}, u32[]{:S(2)}, u32[]{:S(2)}) collective-permute-start(bf16[64,512]{1,0:T(8,128)(2,1)S(1)} %get-tuple-element.50), channel_id=1, source_target_pairs={{0,8},{1,5},{2,10},{3,7},{4,12},{5,1},{6,14},{7,3},{8,0},{9,13},{1... | collective-permute-start | bytes 196616 | tf_op jit(solution)/shard_map/ppermute | solution.py:224
  29.7 1.3 %collective-permute-done.7.refs_3_ = bf16[64,512]{1,0:T(8,128)(2,1)S(1)} collective-permute-done((bf16[64,512]{1,0:T(8,128)(2,1)S(1)}, bf16[64,512]{1,0:T(8,128)(2,1)S(1)}, u32[]{:S(2)}, u32[]{:S(2)}) %collective-permute-start.7) | collective-permute-done | bytes 65568 | tf_op jit(solution)/shard_map/ppermute | solution.py:224
  31.1 0.8 %shard_map.57._ = f32[64,1792]{1,0:T(8,128)} custom-call(f32[64,768]{1,0:T(8,128)S(1)} %get-tuple-element.43.refs_0_, f32[64,512]{1,0:T(8,128)S(1)} %get-tuple-element.46.refs_1_, bf16[64,768]{1,0:T(8,128)(2,1)S(1)} %collective-permute-done.6.refs_2_, bf16[64,512]{1,0:T(8,128)(2,1)S(1)} %collective-permute-done.7.refs_3_), custom_call_target="tpu_custom_call" | custom-call | flops 81920 | bytes 819200 | tf_op jit(solution)/shard_map/pallas_call | solution.py:191
  31.8 2.5 %collective-permute-done.9.came = bf16[64,512]{1,0:T(8,128)(2,1)S(1)} collective-permute-done((bf16[64,512]{1,0:T(8,128)(2,1)S(1)}, bf16[64,512]{1,0:T(8,128)(2,1)S(1)}, u32[]{:S(2)}, u32[]{:S(2)}) %collective-permute-start.9) | collective-permute-done | bytes 65568 | tf_op jit(solution)/shard_map/ppermute | solution.py:224
  34.3 0.7 %shard_map.59 = f32[64,1792]{1,0:T(8,128)} custom-call(f32[64,1792]{1,0:T(8,128)} %shard_map.57._, f32[64,512]{1,0:T(8,128)S(1)} %get-tuple-element.49.kept, bf16[64,512]{1,0:T(8,128)(2,1)S(1)} %collective-permute-done.9.came), custom_call_target="tpu_custom_call", output_to_operand_aliasing={{}: (0, {})} | custom-call | flops 32768 | bytes 327680 | tf_op jit(solution)/shard_map/pallas_call | solution.py:191
  (10 shorter events, 0.2 us)
Async XLA Ops:
  0.0 2.5 %collective-permute-start = (bf16[32,2048]{1,0:T(8,128)(2,1)}, bf16[32,2048]{1,0:T(8,128)(2,1)S(1)}, u32[]{:S(2)}, u32[]{:S(2)}) collective-permute-start(bf16[32,2048]{1,0:T(8,128)(2,1)} %own_hbm.1), channel_id=1, source_target_pairs={{0,1},{1,0},{2,3},{3,2},{4,5},{5,4},{6,7},{7,6},{8,9},{9,8},{10,11... | collective-permute-start | bytes 393224 | tf_op jit(solution)/shard_map/ppermute | solution.py:229
  4.1 8.4 %collective-permute-start.1 = (bf16[256,768]{1,0:T(8,128)(2,1)S(1)}, bf16[256,768]{1,0:T(8,128)(2,1)S(1)}, u32[]{:S(2)}, u32[]{:S(2)}) collective-permute-start(bf16[256,768]{1,0:T(8,128)(2,1)S(1)} %get-tuple-element.35), channel_id=1, source_target_pairs={{0,4},{1,3},{2,6},{3,1},{4,0},{5,7},{6,2},{7,5},{8,12},{9,11},{10,... | collective-permute-start | bytes 1179656 | tf_op jit(solution)/shard_map/ppermute | solution.py:224
  9.1 10.0 %collective-permute-start.4 = (bf16[256,512]{1,0:T(8,128)(2,1)S(1)}, bf16[256,512]{1,0:T(8,128)(2,1)S(1)}, u32[]{:S(2)}, u32[]{:S(2)}) collective-permute-start(bf16[256,512]{1,0:T(8,128)(2,1)S(1)} %get-tuple-element.40), channel_id=1, source_target_pairs={{0,4},{1,3},{2,6},{3,1},{4,0},{5,7},{6,2},{7,5},{8,12},{9,11},{10,... | collective-permute-start | bytes 786440 | tf_op jit(solution)/shard_map/ppermute | solution.py:224
  9.2 12.6 %collective-permute-start.3 = (bf16[256,512]{1,0:T(8,128)(2,1)S(1)}, bf16[256,512]{1,0:T(8,128)(2,1)S(1)}, u32[]{:S(2)}, u32[]{:S(2)}) collective-permute-start(bf16[256,512]{1,0:T(8,128)(2,1)S(1)} %get-tuple-element.39), channel_id=1, source_target_pairs={{0,2},{1,9},{2,0},{3,11},{4,6},{5,13},{6,4},{7,15},{8,10},{9,1},{1... | collective-permute-start | bytes 786440 | tf_op jit(solution)/shard_map/ppermute | solution.py:224
  12.6 9.8 %collective-permute-start.2 = (bf16[128,768]{1,0:T(8,128)(2,1)S(1)}, bf16[128,768]{1,0:T(8,128)(2,1)S(1)}, u32[]{:S(2)}, u32[]{:S(2)}) collective-permute-start(bf16[128,768]{1,0:T(8,128)(2,1)S(1)} %get-tuple-element.37._), channel_id=1, source_target_pairs={{0,2},{1,9},{2,0},{3,11},{4,6},{5,13},{6,4},{7,15},{8,10},{9,1},{1... | collective-permute-start | bytes 589832 | tf_op jit(solution)/shard_map/ppermute | solution.py:224
  19.2 5.9 %collective-permute-start.5 = (bf16[128,512]{1,0:T(8,128)(2,1)S(1)}, bf16[128,512]{1,0:T(8,128)(2,1)S(1)}, u32[]{:S(2)}, u32[]{:S(2)}) collective-permute-start(bf16[128,512]{1,0:T(8,128)(2,1)S(1)} %get-tuple-element.41._), channel_id=1, source_target_pairs={{0,2},{1,9},{2,0},{3,11},{4,6},{5,13},{6,4},{7,15},{8,10},{9,1},{1... | collective-permute-start | bytes 393224 | tf_op jit(solution)/shard_map/ppermute | solution.py:224
  21.9 6.5 %collective-permute-start.8 = (bf16[128,512]{1,0:T(8,128)(2,1)S(1)}, bf16[128,512]{1,0:T(8,128)(2,1)S(1)}, u32[]{:S(2)}, u32[]{:S(2)}) collective-permute-start(bf16[128,512]{1,0:T(8,128)(2,1)S(1)} %get-tuple-element.42._), channel_id=1, source_target_pairs={{0,4},{1,3},{2,6},{3,1},{4,0},{5,7},{6,2},{7,5},{8,12},{9,11},{10,... | collective-permute-start | bytes 393224 | tf_op jit(solution)/shard_map/ppermute | solution.py:224
  22.4 8.7 %collective-permute-start.6 = (bf16[64,768]{1,0:T(8,128)(2,1)S(1)}, bf16[64,768]{1,0:T(8,128)(2,1)S(1)}, u32[]{:S(2)}, u32[]{:S(2)}) collective-permute-start(bf16[64,768]{1,0:T(8,128)(2,1)S(1)} %get-tuple-element.45._), channel_id=1, source_target_pairs={{0,8},{1,5},{2,10},{3,7},{4,12},{5,1},{6,14},{7,3},{8,0},{9,13},{1... | collective-permute-start | bytes 294920 | tf_op jit(solution)/shard_map/ppermute | solution.py:224
  25.1 5.9 %collective-permute-start.7 = (bf16[64,512]{1,0:T(8,128)(2,1)S(1)}, bf16[64,512]{1,0:T(8,128)(2,1)S(1)}, u32[]{:S(2)}, u32[]{:S(2)}) collective-permute-start(bf16[64,512]{1,0:T(8,128)(2,1)S(1)} %get-tuple-element.47._), channel_id=1, source_target_pairs={{0,8},{1,5},{2,10},{3,7},{4,12},{5,1},{6,14},{7,3},{8,0},{9,13},{1... | collective-permute-start | bytes 196616 | tf_op jit(solution)/shard_map/ppermute | solution.py:224
  28.4 5.9 %collective-permute-start.9 = (bf16[64,512]{1,0:T(8,128)(2,1)S(1)}, bf16[64,512]{1,0:T(8,128)(2,1)S(1)}, u32[]{:S(2)}, u32[]{:S(2)}) collective-permute-start(bf16[64,512]{1,0:T(8,128)(2,1)S(1)} %get-tuple-element.50), channel_id=1, source_target_pairs={{0,8},{1,5},{2,10},{3,7},{4,12},{5,1},{6,14},{7,3},{8,0},{9,13},{1... | collective-permute-start | bytes 196616 | tf_op jit(solution)/shard_map/ppermute | solution.py:224

commit v25 on v24

--- a/solution.py
+++ b/solution.py
@@ -12,8 +12,8 @@
 X, NEAR, FAR = 0, 1, 2
 PLAN = [
     (3, (NEAR, X, FAR), (X, FAR, NEAR)),
+    (2, (X, FAR, NEAR), (FAR, X, NEAR)),
     (2, (NEAR, X, FAR), (X, FAR, NEAR)),
-    (2, (X, NEAR, FAR), (FAR, X, NEAR)),
 ]
 ORDER = [(piece, stage) for stage in (1, 2) for piece in range(len(PLAN))]
 

time: 35.2 us -> 36.2 us (1.028)
  starting transfers between devices: 15.6 us -> 19.2 us
  waiting for transfers between devices: 9.27 us -> 6.41 us
    ppermute x9, starting transfers between devices: 15.1 us -> 18.8 us  [exchange(): return lax.ppermute(value, ('grid', 'eig'), pairs)]
    ppermute x9, waiting for transfers between devices: 9.26 us -> 6.41 us  [exchange(): return lax.ppermute(value, ('grid', 'eig'), pairs)]
  transfers between devices with their start and end apart: 10 -> 10, of which waited for: 5 -> 4; matrix products, arithmetic and copies ran while one was open for 0% -> 0% of each run, Pallas kernels for 22% -> 22%
where the time goes in v25:
time: 36.2 us; the launch traced here: 36 us
  starting transfers between devices  19.2 us (53%)
  Pallas kernels  10.3 us (28%)
  waiting for transfers between devices  6.41 us (18%)
    ppermute x9, starting transfers between devices, exchange(): return lax.ppermute(value, ('grid', 'eig'), pairs)  18.8 us
    pallas_call x14, Pallas kernels, kernel_call(): pl.pallas_call(body, out_shape=[jax.ShapeDtypeStruct(*out) for out in out...  10.3 us
    ppermute x9, waiting for transfers between devices, exchange(): return lax.ppermute(value, ('grid', 'eig'), pairs)  6.41 us
  transfers between devices with their start and end apart: 10, of which 4 were waited for; matrix products, arithmetic and copies ran while one was open for 0% of the time, Pallas kernels for 22%

profile of v25, /device:TPU:0, one launch (start us, length us, event | category | flops | bytes accessed | tf_op | source)
XLA Modules:
  0.0 36.0 jit_solution(17965367812822674982)
XLA Ops:
  0.0 0.5 %collective-permute-start = (bf16[32,2048]{1,0:T(8,128)(2,1)}, bf16[32,2048]{1,0:T(8,128)(2,1)S(1)}, u32[]{:S(2)}, u32[]{:S(2)}) collective-permute-start(bf16[32,2048]{1,0:T(8,128)(2,1)} %own_hbm.1), channel_id=1, source_target_pairs={{0,1},{1,0},{2,3},{3,2},{4,5},{5,4},{6,7},{7,6},{8,9},{9,8},{10,11... | collective-permute-start | bytes 393224 | tf_op jit(solution)/shard_map/ppermute | solution.py:229
  0.5 2.0 %shard_map.46 = (bf16[512,64]{1,0:T(8,128)(2,1)S(1)}, bf16[32,2048]{1,0:T(8,128)(2,1)S(1)}, bf16[8,2048]{1,0:T(8,128)(2,1)S(1)}, bf16[768,2048]{1,0:T(8,128)(2,1)S(1)}) custom-call(s32[64]{0:T(128)} %order_hbm.1, bf16[32,2048]{1,0:T(8,128)(2,1)} %own_hbm.1, bf16[8,2048]{1,0:T(8,128)(2,1)} %lanc_hbm.1, bf16[1792,2048]{1,0:T(8,128)(2,1)} %eig_hbm.5), custom_call_target="tpu_custom_call" | custom-call | bytes 3145728 | tf_op jit(solution)/shard_map/pallas_call | solution.py:191
  2.5 0.0 collective-permute-done.other
  2.5 1.6 %shard_map.47 = (bf16[256,768]{1,0:T(8,128)(2,1)S(1)}, bf16[256,2048]{1,0:T(8,128)(2,1)S(1)}, bf16[512,2048]{1,0:T(8,128)(2,1)S(1)}) custom-call(bf16[512,64]{1,0:T(8,128)(2,1)S(1)} %get-tuple-element.28.pick, bf16[32,2048]{1,0:T(8,128)(2,1)S(1)} %get-tuple-element.29.own, bf16[32,2048]{1,0:T(8,128)(2,1)S(1)} %collective-permute-done.other, ...), custom_call_target="tpu_custom_call" | custom-call | flops 805306368 | bytes 3145728 | tf_op jit(solution)/shard_map/pallas_call | solution.py:191
  4.1 2.6 %collective-permute-start.1 = (bf16[256,768]{1,0:T(8,128)(2,1)S(1)}, bf16[256,768]{1,0:T(8,128)(2,1)S(1)}, u32[]{:S(2)}, u32[]{:S(2)}) collective-permute-start(bf16[256,768]{1,0:T(8,128)(2,1)S(1)} %get-tuple-element.35), channel_id=1, source_target_pairs={{0,4},{1,3},{2,6},{3,1},{4,0},{5,7},{6,2},{7,5},{8,12},{9,11},{10,... | collective-permute-start | bytes 1179656 | tf_op jit(solution)/shard_map/ppermute | solution.py:224
  6.7 2.5 %shard_map.48 = (bf16[256,512]{1,0:T(8,128)(2,1)S(1)}, bf16[256,512]{1,0:T(8,128)(2,1)S(1)}, bf16[512,2048]{1,0:T(8,128)(2,1)S(1)}, bf16[512,2048]{1,0:T(8,128)(2,1)S(1)}) custom-call(bf16[512,64]{1,0:T(8,128)(2,1)S(1)} %get-tuple-element.28.pick, bf16[32,2048]{1,0:T(8,128)(2,1)S(1)} %get-tuple-element.29.own, ...), custom_call_target="tpu_custom_call" | custom-call | flops 1073741824 | bytes 4194304 | tf_op jit(solution)/shard_map/pallas_call | solution.py:191
  9.3 1.5 %collective-permute-start.4 = (bf16[256,512]{1,0:T(8,128)(2,1)S(1)}, bf16[256,512]{1,0:T(8,128)(2,1)S(1)}, u32[]{:S(2)}, u32[]{:S(2)}) collective-permute-start(bf16[256,512]{1,0:T(8,128)(2,1)S(1)} %get-tuple-element.40), channel_id=1, source_target_pairs={{0,2},{1,9},{2,0},{3,11},{4,6},{5,13},{6,4},{7,15},{8,10},{9,1},{1... | collective-permute-start | bytes 786440 | tf_op jit(solution)/shard_map/ppermute | solution.py:224
  10.8 0.4 %collective-permute-start.3 = (bf16[256,512]{1,0:T(8,128)(2,1)S(1)}, bf16[256,512]{1,0:T(8,128)(2,1)S(1)}, u32[]{:S(2)}, u32[]{:S(2)}) collective-permute-start(bf16[256,512]{1,0:T(8,128)(2,1)S(1)} %get-tuple-element.39), channel_id=1, source_target_pairs={{0,4},{1,3},{2,6},{3,1},{4,0},{5,7},{6,2},{7,5},{8,12},{9,11},{10,... | collective-permute-start | bytes 786440 | tf_op jit(solution)/shard_map/ppermute | solution.py:224
  11.3 1.0 %shard_map.49.kept = f32[256,768]{1,0:T(8,128)S(1)} custom-call(bf16[512,2048]{1,0:T(8,128)(2,1)S(1)} %get-tuple-element.34.prod._, bf16[768,2048]{1,0:T(8,128)(2,1)S(1)} %get-tuple-element.31.eig), custom_call_target="tpu_custom_call" | custom-call | flops 805306368 | bytes 3145728 | tf_op jit(solution)/shard_map/pallas_call | solution.py:191
  12.3 0.2 collective-permute-done.1.got
  12.5 0.1 shard_map.50
  12.6 4.0 %collective-permute-start.2 = (bf16[128,768]{1,0:T(8,128)(2,1)S(1)}, bf16[128,768]{1,0:T(8,128)(2,1)S(1)}, u32[]{:S(2)}, u32[]{:S(2)}) collective-permute-start(bf16[128,768]{1,0:T(8,128)(2,1)S(1)} %get-tuple-element.37._), channel_id=1, source_target_pairs={{0,2},{1,9},{2,0},{3,11},{4,6},{5,13},{6,4},{7,15},{8,10},{9,1},{1... | collective-permute-start | bytes 589832 | tf_op jit(solution)/shard_map/ppermute | solution.py:224
  16.6 0.7 %shard_map.52.kept = f32[256,512]{1,0:T(8,128)S(1)} custom-call(bf16[512,2048]{1,0:T(8,128)(2,1)S(1)} %get-tuple-element.34.prod._, bf16[512,2048]{1,0:T(8,128)(2,1)S(1)} %get-tuple-element.33.eig), custom_call_target="tpu_custom_call" | custom-call | flops 536870912 | bytes 2097152 | tf_op jit(solution)/shard_map/pallas_call | solution.py:191
  17.4 3.4 %collective-permute-start.5 = (bf16[128,512]{1,0:T(8,128)(2,1)S(1)}, bf16[128,512]{1,0:T(8,128)(2,1)S(1)}, u32[]{:S(2)}, u32[]{:S(2)}) collective-permute-start(bf16[128,512]{1,0:T(8,128)(2,1)S(1)} %get-tuple-element.41._), channel_id=1, source_target_pairs={{0,8},{1,3},{2,10},{3,1},{4,12},{5,7},{6,14},{7,5},{8,0},{9,11},{1... | collective-permute-start | bytes 393224 | tf_op jit(solution)/shard_map/ppermute | solution.py:224
  20.8 0.7 %shard_map.51.kept = f32[256,512]{1,0:T(8,128)S(1)} custom-call(bf16[512,2048]{1,0:T(8,128)(2,1)S(1)} %get-tuple-element.34.prod._, bf16[512,2048]{1,0:T(8,128)(2,1)S(1)} %get-tuple-element.38.eig), custom_call_target="tpu_custom_call" | custom-call | flops 536870912 | bytes 2097152 | tf_op jit(solution)/shard_map/pallas_call | solution.py:191
  21.6 1.6 %collective-permute-start.8 = (bf16[128,512]{1,0:T(8,128)(2,1)S(1)}, bf16[128,512]{1,0:T(8,128)(2,1)S(1)}, u32[]{:S(2)}, u32[]{:S(2)}) collective-permute-start(bf16[128,512]{1,0:T(8,128)(2,1)S(1)} %get-tuple-element.42._), channel_id=1, source_target_pairs={{0,2},{1,9},{2,0},{3,11},{4,6},{5,13},{6,4},{7,15},{8,10},{9,1},{1... | collective-permute-start | bytes 393224 | tf_op jit(solution)/shard_map/ppermute | solution.py:224
  23.2 1.5 %collective-permute-start.6 = (bf16[64,768]{1,0:T(8,128)(2,1)S(1)}, bf16[64,768]{1,0:T(8,128)(2,1)S(1)}, u32[]{:S(2)}, u32[]{:S(2)}) collective-permute-start(bf16[64,768]{1,0:T(8,128)(2,1)S(1)} %get-tuple-element.45._), channel_id=1, source_target_pairs={{0,8},{1,5},{2,10},{3,7},{4,12},{5,1},{6,14},{7,3},{8,0},{9,13},{1... | collective-permute-start | bytes 294920 | tf_op jit(solution)/shard_map/ppermute | solution.py:224
  24.7 4.7 %collective-permute-done.5.got = bf16[128,512]{1,0:T(8,128)(2,1)S(1)} collective-permute-done((bf16[128,512]{1,0:T(8,128)(2,1)S(1)}, bf16[128,512]{1,0:T(8,128)(2,1)S(1)}, u32[]{:S(2)}, u32[]{:S(2)}) %collective-permute-start.5) | collective-permute-done | bytes 131104 | tf_op jit(solution)/shard_map/ppermute | solution.py:224
  29.5 0.2 collective-permute-start.7
  29.7 3.4 %collective-permute-start.9 = (bf16[64,512]{1,0:T(8,128)(2,1)S(1)}, bf16[64,512]{1,0:T(8,128)(2,1)S(1)}, u32[]{:S(2)}, u32[]{:S(2)}) collective-permute-start(bf16[64,512]{1,0:T(8,128)(2,1)S(1)} %get-tuple-element.50), channel_id=1, source_target_pairs={{0,8},{1,5},{2,10},{3,7},{4,12},{5,1},{6,14},{7,3},{8,0},{9,13},{1... | collective-permute-start | bytes 196616 | tf_op jit(solution)/shard_map/ppermute | solution.py:224
  33.1 0.7 %collective-permute-done.7.refs_3_ = bf16[64,512]{1,0:T(8,128)(2,1)S(1)} collective-permute-done((bf16[64,512]{1,0:T(8,128)(2,1)S(1)}, bf16[64,512]{1,0:T(8,128)(2,1)S(1)}, u32[]{:S(2)}, u32[]{:S(2)}) %collective-permute-start.7) | collective-permute-done | bytes 65568 | tf_op jit(solution)/shard_map/ppermute | solution.py:224
  33.8 0.8 %shard_map.57._ = f32[64,1792]{1,0:T(8,128)} custom-call(f32[64,768]{1,0:T(8,128)S(1)} %get-tuple-element.43.refs_0_, f32[64,512]{1,0:T(8,128)S(1)} %get-tuple-element.46.refs_1_, bf16[64,768]{1,0:T(8,128)(2,1)S(1)} %collective-permute-done.6.refs_2_, bf16[64,512]{1,0:T(8,128)(2,1)S(1)} %collective-permute-done.7.refs_3_), custom_call_target="tpu_custom_call" | custom-call | flops 81920 | bytes 819200 | tf_op jit(solution)/shard_map/pallas_call | solution.py:191
  34.6 0.8 %collective-permute-done.9.came = bf16[64,512]{1,0:T(8,128)(2,1)S(1)} collective-permute-done((bf16[64,512]{1,0:T(8,128)(2,1)S(1)}, bf16[64,512]{1,0:T(8,128)(2,1)S(1)}, u32[]{:S(2)}, u32[]{:S(2)}) %collective-permute-start.9) | collective-permute-done | bytes 65568 | tf_op jit(solution)/shard_map/ppermute | solution.py:224
  35.4 0.7 %shard_map.59 = f32[64,1792]{1,0:T(8,128)} custom-call(f32[64,1792]{1,0:T(8,128)} %shard_map.57._, f32[64,512]{1,0:T(8,128)S(1)} %get-tuple-element.49.kept, bf16[64,512]{1,0:T(8,128)(2,1)S(1)} %collective-permute-done.9.came), custom_call_target="tpu_custom_call", output_to_operand_aliasing={{}: (0, {})} | custom-call | flops 32768 | bytes 327680 | tf_op jit(solution)/shard_map/pallas_call | solution.py:191
  (10 shorter events, 0.2 us)
Async XLA Ops:
  0.0 2.5 %collective-permute-start = (bf16[32,2048]{1,0:T(8,128)(2,1)}, bf16[32,2048]{1,0:T(8,128)(2,1)S(1)}, u32[]{:S(2)}, u32[]{:S(2)}) collective-permute-start(bf16[32,2048]{1,0:T(8,128)(2,1)} %own_hbm.1), channel_id=1, source_target_pairs={{0,1},{1,0},{2,3},{3,2},{4,5},{5,4},{6,7},{7,6},{8,9},{9,8},{10,11... | collective-permute-start | bytes 393224 | tf_op jit(solution)/shard_map/ppermute | solution.py:229
  4.1 8.4 %collective-permute-start.1 = (bf16[256,768]{1,0:T(8,128)(2,1)S(1)}, bf16[256,768]{1,0:T(8,128)(2,1)S(1)}, u32[]{:S(2)}, u32[]{:S(2)}) collective-permute-start(bf16[256,768]{1,0:T(8,128)(2,1)S(1)} %get-tuple-element.35), channel_id=1, source_target_pairs={{0,4},{1,3},{2,6},{3,1},{4,0},{5,7},{6,2},{7,5},{8,12},{9,11},{10,... | collective-permute-start | bytes 1179656 | tf_op jit(solution)/shard_map/ppermute | solution.py:224
  9.3 8.1 %collective-permute-start.4 = (bf16[256,512]{1,0:T(8,128)(2,1)S(1)}, bf16[256,512]{1,0:T(8,128)(2,1)S(1)}, u32[]{:S(2)}, u32[]{:S(2)}) collective-permute-start(bf16[256,512]{1,0:T(8,128)(2,1)S(1)} %get-tuple-element.40), channel_id=1, source_target_pairs={{0,2},{1,9},{2,0},{3,11},{4,6},{5,13},{6,4},{7,15},{8,10},{9,1},{1... | collective-permute-start | bytes 786440 | tf_op jit(solution)/shard_map/ppermute | solution.py:224
  10.8 10.7 %collective-permute-start.3 = (bf16[256,512]{1,0:T(8,128)(2,1)S(1)}, bf16[256,512]{1,0:T(8,128)(2,1)S(1)}, u32[]{:S(2)}, u32[]{:S(2)}) collective-permute-start(bf16[256,512]{1,0:T(8,128)(2,1)S(1)} %get-tuple-element.39), channel_id=1, source_target_pairs={{0,4},{1,3},{2,6},{3,1},{4,0},{5,7},{6,2},{7,5},{8,12},{9,11},{10,... | collective-permute-start | bytes 786440 | tf_op jit(solution)/shard_map/ppermute | solution.py:224
  12.6 10.6 %collective-permute-start.2 = (bf16[128,768]{1,0:T(8,128)(2,1)S(1)}, bf16[128,768]{1,0:T(8,128)(2,1)S(1)}, u32[]{:S(2)}, u32[]{:S(2)}) collective-permute-start(bf16[128,768]{1,0:T(8,128)(2,1)S(1)} %get-tuple-element.37._), channel_id=1, source_target_pairs={{0,2},{1,9},{2,0},{3,11},{4,6},{5,13},{6,4},{7,15},{8,10},{9,1},{1... | collective-permute-start | bytes 589832 | tf_op jit(solution)/shard_map/ppermute | solution.py:224
  17.4 12.0 %collective-permute-start.5 = (bf16[128,512]{1,0:T(8,128)(2,1)S(1)}, bf16[128,512]{1,0:T(8,128)(2,1)S(1)}, u32[]{:S(2)}, u32[]{:S(2)}) collective-permute-start(bf16[128,512]{1,0:T(8,128)(2,1)S(1)} %get-tuple-element.41._), channel_id=1, source_target_pairs={{0,8},{1,3},{2,10},{3,1},{4,12},{5,7},{6,14},{7,5},{8,0},{9,11},{1... | collective-permute-start | bytes 393224 | tf_op jit(solution)/shard_map/ppermute | solution.py:224
  21.6 8.0 %collective-permute-start.8 = (bf16[128,512]{1,0:T(8,128)(2,1)S(1)}, bf16[128,512]{1,0:T(8,128)(2,1)S(1)}, u32[]{:S(2)}, u32[]{:S(2)}) collective-permute-start(bf16[128,512]{1,0:T(8,128)(2,1)S(1)} %get-tuple-element.42._), channel_id=1, source_target_pairs={{0,2},{1,9},{2,0},{3,11},{4,6},{5,13},{6,4},{7,15},{8,10},{9,1},{1... | collective-permute-start | bytes 393224 | tf_op jit(solution)/shard_map/ppermute | solution.py:224
  23.2 10.6 %collective-permute-start.6 = (bf16[64,768]{1,0:T(8,128)(2,1)S(1)}, bf16[64,768]{1,0:T(8,128)(2,1)S(1)}, u32[]{:S(2)}, u32[]{:S(2)}) collective-permute-start(bf16[64,768]{1,0:T(8,128)(2,1)S(1)} %get-tuple-element.45._), channel_id=1, source_target_pairs={{0,8},{1,5},{2,10},{3,7},{4,12},{5,1},{6,14},{7,3},{8,0},{9,13},{1... | collective-permute-start | bytes 294920 | tf_op jit(solution)/shard_map/ppermute | solution.py:224
  29.5 4.3 %collective-permute-start.7 = (bf16[64,512]{1,0:T(8,128)(2,1)S(1)}, bf16[64,512]{1,0:T(8,128)(2,1)S(1)}, u32[]{:S(2)}, u32[]{:S(2)}) collective-permute-start(bf16[64,512]{1,0:T(8,128)(2,1)S(1)} %get-tuple-element.47._), channel_id=1, source_target_pairs={{0,4},{1,5},{2,6},{3,7},{4,0},{5,1},{6,2},{7,3},{8,12},{9,13},{10,... | collective-permute-start | bytes 196616 | tf_op jit(solution)/shard_map/ppermute | solution.py:224
  29.7 5.7 %collective-permute-start.9 = (bf16[64,512]{1,0:T(8,128)(2,1)S(1)}, bf16[64,512]{1,0:T(8,128)(2,1)S(1)}, u32[]{:S(2)}, u32[]{:S(2)}) collective-permute-start(bf16[64,512]{1,0:T(8,128)(2,1)S(1)} %get-tuple-element.50), channel_id=1, source_target_pairs={{0,8},{1,5},{2,10},{3,7},{4,12},{5,1},{6,14},{7,3},{8,0},{9,13},{1... | collective-permute-start | bytes 196616 | tf_op jit(solution)/shard_map/ppermute | solution.py:224

commit v26 on v24

--- a/solution.py
+++ b/solution.py
@@ -12,8 +12,8 @@
 X, NEAR, FAR = 0, 1, 2
 PLAN = [
     (3, (NEAR, X, FAR), (X, FAR, NEAR)),
-    (2, (NEAR, X, FAR), (X, FAR, NEAR)),
     (2, (X, NEAR, FAR), (FAR, X, NEAR)),
+    (2, (NEAR, X, FAR), (X, NEAR, FAR)),
 ]
 ORDER = [(piece, stage) for stage in (1, 2) for piece in range(len(PLAN))]
 

time: 35.2 us -> 33 us (0.937)
  waiting for transfers between devices: 9.27 us -> 4.36 us
  starting transfers between devices: 15.6 us -> 17.9 us
    ppermute x9, waiting for transfers between devices: 9.26 us -> 4.36 us  [exchange(): return lax.ppermute(value, ('grid', 'eig'), pairs)]
    ppermute x9, starting transfers between devices: 15.1 us -> 17.5 us  [exchange(): return lax.ppermute(value, ('grid', 'eig'), pairs)]
  transfers between devices with their start and end apart: 10 -> 10, of which waited for: 5 -> 3; matrix products, arithmetic and copies ran while one was open for 0% -> 0% of each run, Pallas kernels for 22% -> 25%
where the time goes in v26:
time: 33 us; the launch traced here: 32.8 us
  starting transfers between devices  17.9 us (54%)
  Pallas kernels  10.4 us (32%)
  waiting for transfers between devices  4.36 us (13%)
    ppermute x9, starting transfers between devices, exchange(): return lax.ppermute(value, ('grid', 'eig'), pairs)  17.5 us
    pallas_call x14, Pallas kernels, kernel_call(): pl.pallas_call(body, out_shape=[jax.ShapeDtypeStruct(*out) for out in out...  10.4 us
    ppermute x9, waiting for transfers between devices, exchange(): return lax.ppermute(value, ('grid', 'eig'), pairs)  4.36 us
  transfers between devices with their start and end apart: 10, of which 3 were waited for; matrix products, arithmetic and copies ran while one was open for 0% of the time, Pallas kernels for 25%

profile of v26, /device:TPU:0, one launch (start us, length us, event | category | flops | bytes accessed | tf_op | source)
XLA Modules:
  0.0 32.8 jit_solution(6354359079118355986)
XLA Ops:
  0.0 0.5 %collective-permute-start = (bf16[32,2048]{1,0:T(8,128)(2,1)}, bf16[32,2048]{1,0:T(8,128)(2,1)S(1)}, u32[]{:S(2)}, u32[]{:S(2)}) collective-permute-start(bf16[32,2048]{1,0:T(8,128)(2,1)} %own_hbm.1), channel_id=1, source_target_pairs={{0,1},{1,0},{2,3},{3,2},{4,5},{5,4},{6,7},{7,6},{8,9},{9,8},{10,11... | collective-permute-start | bytes 393224 | tf_op jit(solution)/shard_map/ppermute | solution.py:229
  0.5 2.0 %shard_map.46 = (bf16[512,64]{1,0:T(8,128)(2,1)S(1)}, bf16[32,2048]{1,0:T(8,128)(2,1)S(1)}, bf16[8,2048]{1,0:T(8,128)(2,1)S(1)}, bf16[768,2048]{1,0:T(8,128)(2,1)S(1)}) custom-call(s32[64]{0:T(128)} %order_hbm.1, bf16[32,2048]{1,0:T(8,128)(2,1)} %own_hbm.1, bf16[8,2048]{1,0:T(8,128)(2,1)} %lanc_hbm.1, bf16[1792,2048]{1,0:T(8,128)(2,1)} %eig_hbm.5), custom_call_target="tpu_custom_call" | custom-call | bytes 3145728 | tf_op jit(solution)/shard_map/pallas_call | solution.py:191
  2.5 0.0 collective-permute-done.other
  2.5 1.6 %shard_map.47 = (bf16[256,768]{1,0:T(8,128)(2,1)S(1)}, bf16[256,2048]{1,0:T(8,128)(2,1)S(1)}, bf16[512,2048]{1,0:T(8,128)(2,1)S(1)}) custom-call(bf16[512,64]{1,0:T(8,128)(2,1)S(1)} %get-tuple-element.28.pick, bf16[32,2048]{1,0:T(8,128)(2,1)S(1)} %get-tuple-element.29.own, bf16[32,2048]{1,0:T(8,128)(2,1)S(1)} %collective-permute-done.other, ...), custom_call_target="tpu_custom_call" | custom-call | flops 805306368 | bytes 3145728 | tf_op jit(solution)/shard_map/pallas_call | solution.py:191
  4.1 2.6 %collective-permute-start.1 = (bf16[256,768]{1,0:T(8,128)(2,1)S(1)}, bf16[256,768]{1,0:T(8,128)(2,1)S(1)}, u32[]{:S(2)}, u32[]{:S(2)}) collective-permute-start(bf16[256,768]{1,0:T(8,128)(2,1)S(1)} %get-tuple-element.35), channel_id=1, source_target_pairs={{0,4},{1,3},{2,6},{3,1},{4,0},{5,7},{6,2},{7,5},{8,12},{9,11},{10,... | collective-permute-start | bytes 1179656 | tf_op jit(solution)/shard_map/ppermute | solution.py:224
  6.7 2.7 %shard_map.48 = (bf16[256,512]{1,0:T(8,128)(2,1)S(1)}, bf16[256,512]{1,0:T(8,128)(2,1)S(1)}, bf16[512,2048]{1,0:T(8,128)(2,1)S(1)}, bf16[512,2048]{1,0:T(8,128)(2,1)S(1)}) custom-call(bf16[512,64]{1,0:T(8,128)(2,1)S(1)} %get-tuple-element.28.pick, bf16[32,2048]{1,0:T(8,128)(2,1)S(1)} %get-tuple-element.29.own, ...), custom_call_target="tpu_custom_call" | custom-call | flops 1073741824 | bytes 4194304 | tf_op jit(solution)/shard_map/pallas_call | solution.py:191
  9.4 1.5 %collective-permute-start.4 = (bf16[256,512]{1,0:T(8,128)(2,1)S(1)}, bf16[256,512]{1,0:T(8,128)(2,1)S(1)}, u32[]{:S(2)}, u32[]{:S(2)}) collective-permute-start(bf16[256,512]{1,0:T(8,128)(2,1)S(1)} %get-tuple-element.40), channel_id=1, source_target_pairs={{0,2},{1,9},{2,0},{3,11},{4,6},{5,13},{6,4},{7,15},{8,10},{9,1},{1... | collective-permute-start | bytes 786440 | tf_op jit(solution)/shard_map/ppermute | solution.py:224
  11.0 0.5 %collective-permute-start.3 = (bf16[256,512]{1,0:T(8,128)(2,1)S(1)}, bf16[256,512]{1,0:T(8,128)(2,1)S(1)}, u32[]{:S(2)}, u32[]{:S(2)}) collective-permute-start(bf16[256,512]{1,0:T(8,128)(2,1)S(1)} %get-tuple-element.39), channel_id=1, source_target_pairs={{0,4},{1,3},{2,6},{3,1},{4,0},{5,7},{6,2},{7,5},{8,12},{9,11},{10,... | collective-permute-start | bytes 786440 | tf_op jit(solution)/shard_map/ppermute | solution.py:224
  11.4 1.0 %shard_map.49.kept = f32[256,768]{1,0:T(8,128)S(1)} custom-call(bf16[512,2048]{1,0:T(8,128)(2,1)S(1)} %get-tuple-element.34.prod._, bf16[768,2048]{1,0:T(8,128)(2,1)S(1)} %get-tuple-element.31.eig), custom_call_target="tpu_custom_call" | custom-call | flops 805306368 | bytes 3145728 | tf_op jit(solution)/shard_map/pallas_call | solution.py:191
  12.4 0.1 collective-permute-done.1.got
  12.5 0.1 shard_map.50
  12.6 3.9 %collective-permute-start.2 = (bf16[128,768]{1,0:T(8,128)(2,1)S(1)}, bf16[128,768]{1,0:T(8,128)(2,1)S(1)}, u32[]{:S(2)}, u32[]{:S(2)}) collective-permute-start(bf16[128,768]{1,0:T(8,128)(2,1)S(1)} %get-tuple-element.37._), channel_id=1, source_target_pairs={{0,2},{1,9},{2,0},{3,11},{4,6},{5,13},{6,4},{7,15},{8,10},{9,1},{1... | collective-permute-start | bytes 589832 | tf_op jit(solution)/shard_map/ppermute | solution.py:224
  16.5 0.7 %shard_map.52.kept = f32[256,512]{1,0:T(8,128)S(1)} custom-call(bf16[512,2048]{1,0:T(8,128)(2,1)S(1)} %get-tuple-element.34.prod._, bf16[512,2048]{1,0:T(8,128)(2,1)S(1)} %get-tuple-element.33.eig), custom_call_target="tpu_custom_call" | custom-call | flops 536870912 | bytes 2097152 | tf_op jit(solution)/shard_map/pallas_call | solution.py:191
  17.2 0.0 collective-permute-done.4.got
  17.3 0.4 %collective-permute-start.5 = (bf16[128,512]{1,0:T(8,128)(2,1)S(1)}, bf16[128,512]{1,0:T(8,128)(2,1)S(1)}, u32[]{:S(2)}, u32[]{:S(2)}) collective-permute-start(bf16[128,512]{1,0:T(8,128)(2,1)S(1)} %get-tuple-element.41._), channel_id=1, source_target_pairs={{0,4},{1,3},{2,6},{3,1},{4,0},{5,7},{6,2},{7,5},{8,12},{9,11},{10,... | collective-permute-start | bytes 393224 | tf_op jit(solution)/shard_map/ppermute | solution.py:224
  17.7 0.7 %shard_map.51.kept = f32[256,512]{1,0:T(8,128)S(1)} custom-call(bf16[512,2048]{1,0:T(8,128)(2,1)S(1)} %get-tuple-element.34.prod._, bf16[512,2048]{1,0:T(8,128)(2,1)S(1)} %get-tuple-element.38.eig), custom_call_target="tpu_custom_call" | custom-call | flops 536870912 | bytes 2097152 | tf_op jit(solution)/shard_map/pallas_call | solution.py:191
  18.4 0.8 %collective-permute-done.3.got = bf16[256,512]{1,0:T(8,128)(2,1)S(1)} collective-permute-done((bf16[256,512]{1,0:T(8,128)(2,1)S(1)}, bf16[256,512]{1,0:T(8,128)(2,1)S(1)}, u32[]{:S(2)}, u32[]{:S(2)}) %collective-permute-start.3) | collective-permute-done | bytes 262176 | tf_op jit(solution)/shard_map/ppermute | solution.py:224
  19.3 2.6 %collective-permute-start.8 = (bf16[128,512]{1,0:T(8,128)(2,1)S(1)}, bf16[128,512]{1,0:T(8,128)(2,1)S(1)}, u32[]{:S(2)}, u32[]{:S(2)}) collective-permute-start(bf16[128,512]{1,0:T(8,128)(2,1)S(1)} %get-tuple-element.42._), channel_id=1, source_target_pairs={{0,2},{1,5},{2,0},{3,7},{4,6},{5,1},{6,4},{7,3},{8,10},{9,13},{10,... | collective-permute-start | bytes 393224 | tf_op jit(solution)/shard_map/ppermute | solution.py:224
  21.9 2.7 %collective-permute-start.6 = (bf16[64,768]{1,0:T(8,128)(2,1)S(1)}, bf16[64,768]{1,0:T(8,128)(2,1)S(1)}, u32[]{:S(2)}, u32[]{:S(2)}) collective-permute-start(bf16[64,768]{1,0:T(8,128)(2,1)S(1)} %get-tuple-element.45._), channel_id=1, source_target_pairs={{0,8},{1,5},{2,10},{3,7},{4,12},{5,1},{6,14},{7,3},{8,0},{9,13},{1... | collective-permute-start | bytes 294920 | tf_op jit(solution)/shard_map/ppermute | solution.py:224
  24.6 2.0 %collective-permute-start.7 = (bf16[64,512]{1,0:T(8,128)(2,1)S(1)}, bf16[64,512]{1,0:T(8,128)(2,1)S(1)}, u32[]{:S(2)}, u32[]{:S(2)}) collective-permute-start(bf16[64,512]{1,0:T(8,128)(2,1)S(1)} %get-tuple-element.47._), channel_id=1, source_target_pairs={{0,8},{1,5},{2,10},{3,7},{4,12},{5,1},{6,14},{7,3},{8,0},{9,13},{1... | collective-permute-start | bytes 196616 | tf_op jit(solution)/shard_map/ppermute | solution.py:224
  26.7 1.3 %collective-permute-start.9 = (bf16[64,512]{1,0:T(8,128)(2,1)S(1)}, bf16[64,512]{1,0:T(8,128)(2,1)S(1)}, u32[]{:S(2)}, u32[]{:S(2)}) collective-permute-start(bf16[64,512]{1,0:T(8,128)(2,1)S(1)} %get-tuple-element.50), channel_id=1, source_target_pairs={{0,8},{1,9},{2,10},{3,11},{4,12},{5,13},{6,14},{7,15},{8,0},{9,1},... | collective-permute-start | bytes 196616 | tf_op jit(solution)/shard_map/ppermute | solution.py:224
  28.0 3.4 %collective-permute-done.7.refs_3_ = bf16[64,512]{1,0:T(8,128)(2,1)S(1)} collective-permute-done((bf16[64,512]{1,0:T(8,128)(2,1)S(1)}, bf16[64,512]{1,0:T(8,128)(2,1)S(1)}, u32[]{:S(2)}, u32[]{:S(2)}) %collective-permute-start.7) | collective-permute-done | bytes 65568 | tf_op jit(solution)/shard_map/ppermute | solution.py:224
  31.4 0.8 %shard_map.57._ = f32[64,1792]{1,0:T(8,128)} custom-call(f32[64,768]{1,0:T(8,128)S(1)} %get-tuple-element.43.refs_0_, f32[64,512]{1,0:T(8,128)S(1)} %get-tuple-element.46.refs_1_, bf16[64,768]{1,0:T(8,128)(2,1)S(1)} %collective-permute-done.6.refs_2_, bf16[64,512]{1,0:T(8,128)(2,1)S(1)} %collective-permute-done.7.refs_3_), custom_call_target="tpu_custom_call" | custom-call | flops 81920 | bytes 819200 | tf_op jit(solution)/shard_map/pallas_call | solution.py:191
  32.2 0.7 %shard_map.59 = f32[64,1792]{1,0:T(8,128)} custom-call(f32[64,1792]{1,0:T(8,128)} %shard_map.57._, f32[64,512]{1,0:T(8,128)S(1)} %get-tuple-element.49.kept, bf16[64,512]{1,0:T(8,128)(2,1)S(1)} %collective-permute-done.9.came), custom_call_target="tpu_custom_call", output_to_operand_aliasing={{}: (0, {})} | custom-call | flops 32768 | bytes 327680 | tf_op jit(solution)/shard_map/pallas_call | solution.py:191
  (10 shorter events, 0.2 us)
Async XLA Ops:
  0.0 2.5 %collective-permute-start = (bf16[32,2048]{1,0:T(8,128)(2,1)}, bf16[32,2048]{1,0:T(8,128)(2,1)S(1)}, u32[]{:S(2)}, u32[]{:S(2)}) collective-permute-start(bf16[32,2048]{1,0:T(8,128)(2,1)} %own_hbm.1), channel_id=1, source_target_pairs={{0,1},{1,0},{2,3},{3,2},{4,5},{5,4},{6,7},{7,6},{8,9},{9,8},{10,11... | collective-permute-start | bytes 393224 | tf_op jit(solution)/shard_map/ppermute | solution.py:229
  4.1 8.4 %collective-permute-start.1 = (bf16[256,768]{1,0:T(8,128)(2,1)S(1)}, bf16[256,768]{1,0:T(8,128)(2,1)S(1)}, u32[]{:S(2)}, u32[]{:S(2)}) collective-permute-start(bf16[256,768]{1,0:T(8,128)(2,1)S(1)} %get-tuple-element.35), channel_id=1, source_target_pairs={{0,4},{1,3},{2,6},{3,1},{4,0},{5,7},{6,2},{7,5},{8,12},{9,11},{10,... | collective-permute-start | bytes 1179656 | tf_op jit(solution)/shard_map/ppermute | solution.py:224
  9.4 7.8 %collective-permute-start.4 = (bf16[256,512]{1,0:T(8,128)(2,1)S(1)}, bf16[256,512]{1,0:T(8,128)(2,1)S(1)}, u32[]{:S(2)}, u32[]{:S(2)}) collective-permute-start(bf16[256,512]{1,0:T(8,128)(2,1)S(1)} %get-tuple-element.40), channel_id=1, source_target_pairs={{0,2},{1,9},{2,0},{3,11},{4,6},{5,13},{6,4},{7,15},{8,10},{9,1},{1... | collective-permute-start | bytes 786440 | tf_op jit(solution)/shard_map/ppermute | solution.py:224
  11.0 8.3 %collective-permute-start.3 = (bf16[256,512]{1,0:T(8,128)(2,1)S(1)}, bf16[256,512]{1,0:T(8,128)(2,1)S(1)}, u32[]{:S(2)}, u32[]{:S(2)}) collective-permute-start(bf16[256,512]{1,0:T(8,128)(2,1)S(1)} %get-tuple-element.39), channel_id=1, source_target_pairs={{0,4},{1,3},{2,6},{3,1},{4,0},{5,7},{6,2},{7,5},{8,12},{9,11},{10,... | collective-permute-start | bytes 786440 | tf_op jit(solution)/shard_map/ppermute | solution.py:224
  12.6 9.3 %collective-permute-start.2 = (bf16[128,768]{1,0:T(8,128)(2,1)S(1)}, bf16[128,768]{1,0:T(8,128)(2,1)S(1)}, u32[]{:S(2)}, u32[]{:S(2)}) collective-permute-start(bf16[128,768]{1,0:T(8,128)(2,1)S(1)} %get-tuple-element.37._), channel_id=1, source_target_pairs={{0,2},{1,9},{2,0},{3,11},{4,6},{5,13},{6,4},{7,15},{8,10},{9,1},{1... | collective-permute-start | bytes 589832 | tf_op jit(solution)/shard_map/ppermute | solution.py:224
  17.3 7.3 %collective-permute-start.5 = (bf16[128,512]{1,0:T(8,128)(2,1)S(1)}, bf16[128,512]{1,0:T(8,128)(2,1)S(1)}, u32[]{:S(2)}, u32[]{:S(2)}) collective-permute-start(bf16[128,512]{1,0:T(8,128)(2,1)S(1)} %get-tuple-element.41._), channel_id=1, source_target_pairs={{0,4},{1,3},{2,6},{3,1},{4,0},{5,7},{6,2},{7,5},{8,12},{9,11},{10,... | collective-permute-start | bytes 393224 | tf_op jit(solution)/shard_map/ppermute | solution.py:224
  19.3 7.3 %collective-permute-start.8 = (bf16[128,512]{1,0:T(8,128)(2,1)S(1)}, bf16[128,512]{1,0:T(8,128)(2,1)S(1)}, u32[]{:S(2)}, u32[]{:S(2)}) collective-permute-start(bf16[128,512]{1,0:T(8,128)(2,1)S(1)} %get-tuple-element.42._), channel_id=1, source_target_pairs={{0,2},{1,5},{2,0},{3,7},{4,6},{5,1},{6,4},{7,3},{8,10},{9,13},{10,... | collective-permute-start | bytes 393224 | tf_op jit(solution)/shard_map/ppermute | solution.py:224
  21.9 9.4 %collective-permute-start.6 = (bf16[64,768]{1,0:T(8,128)(2,1)S(1)}, bf16[64,768]{1,0:T(8,128)(2,1)S(1)}, u32[]{:S(2)}, u32[]{:S(2)}) collective-permute-start(bf16[64,768]{1,0:T(8,128)(2,1)S(1)} %get-tuple-element.45._), channel_id=1, source_target_pairs={{0,8},{1,5},{2,10},{3,7},{4,12},{5,1},{6,14},{7,3},{8,0},{9,13},{1... | collective-permute-start | bytes 294920 | tf_op jit(solution)/shard_map/ppermute | solution.py:224
  24.6 6.7 %collective-permute-start.7 = (bf16[64,512]{1,0:T(8,128)(2,1)S(1)}, bf16[64,512]{1,0:T(8,128)(2,1)S(1)}, u32[]{:S(2)}, u32[]{:S(2)}) collective-permute-start(bf16[64,512]{1,0:T(8,128)(2,1)S(1)} %get-tuple-element.47._), channel_id=1, source_target_pairs={{0,8},{1,5},{2,10},{3,7},{4,12},{5,1},{6,14},{7,3},{8,0},{9,13},{1... | collective-permute-start | bytes 196616 | tf_op jit(solution)/shard_map/ppermute | solution.py:224
  26.7 5.5 %collective-permute-start.9 = (bf16[64,512]{1,0:T(8,128)(2,1)S(1)}, bf16[64,512]{1,0:T(8,128)(2,1)S(1)}, u32[]{:S(2)}, u32[]{:S(2)}) collective-permute-start(bf16[64,512]{1,0:T(8,128)(2,1)S(1)} %get-tuple-element.50), channel_id=1, source_target_pairs={{0,8},{1,9},{2,10},{3,11},{4,12},{5,13},{6,14},{7,15},{8,0},{9,1},... | collective-permute-start | bytes 196616 | tf_op jit(solution)/shard_map/ppermute | solution.py:224
